TPU v7x, 32 devices: a whole 2x2x4 slice. The times are simulated.
32 devices in a mesh: seq: 8 (over z, x), round: 4 (over y, core).
Axes of the slice: x: 2, y: 2, z: 4, core: 2. Of those that a mesh axis runs over, the one named last changes fastest.
Arguments:
- first_half: bfloat16 [8192, 1024], P(('seq', 'round')), may hold values from -6 to 6
- second_half: bfloat16 [8192, 1024], P(('seq', 'round')), may hold values from -6 to 6
- qk_weight: bfloat16 [1024, 1024], P(('seq', 'round')), may hold values from -0.1875 to 0.1875
- value_weight: bfloat16 [1024, 1024], P(('seq', 'round')), may hold values from -0.1875 to 0.1875
- output_weight: bfloat16 [1024, 1024], P(('seq', 'round')), may hold values from -1 to 1
- inner_weight: bfloat16 [1024, 4096], P(('seq', 'round')), may hold values from -0.1875 to 0.1875
- outer_weight: bfloat16 [4096, 1024], P(('seq', 'round')), may hold values from -0.09375 to 0.09375
- attn_gain: bfloat16 [1024], P(('seq', 'round')), may hold values from 0.5 to 1.5
- attn_shift: bfloat16 [1024], P(('seq', 'round')), may hold values from -1 to 1
- ffn_gain: bfloat16 [1024], P(('seq', 'round')), may hold values from 0.5 to 1.5
- ffn_shift: bfloat16 [1024], P(('seq', 'round')), may hold values from -1 to 1
- buckets: int32 [4, 8192], P('round', 'seq'), may hold values from 0 to 256, as said below
- slots: int32 [4, 8192], P('round', 'seq'), may hold values from 0 to 16383, as said below
- first_grad: bfloat16 [8192, 1024], P(('seq', 'round')), may hold values from -6 to 6
- second_grad: bfloat16 [8192, 1024], P(('seq', 'round')), may hold values from -6 to 6
Outputs:
- first_out: bfloat16 [8192, 1024], P(('seq', 'round'))
- second_out: bfloat16 [8192, 1024], P(('seq', 'round'))
- first_back: bfloat16 [8192, 1024], P(('seq', 'round'))
- second_back: bfloat16 [8192, 1024], P(('seq', 'round'))
- qk_grad: float32 [1024, 1024], P(('seq', 'round'))
- value_grad: float32 [1024, 1024], P(('seq', 'round'))
- output_grad: float32 [1024, 1024], P(('seq', 'round'))
- inner_grad: float32 [1024, 4096], P(('seq', 'round'))
- outer_grad: float32 [4096, 1024], P(('seq', 'round'))
- attn_gain_grad: float32 [1024], P(('seq', 'round'))
- attn_shift_grad: float32 [1024], P(('seq', 'round'))
- ffn_gain_grad: float32 [1024], P(('seq', 'round'))
- ffn_shift_grad: float32 [1024], P(('seq', 'round'))
Inputs may be any that keep to these rules, and one draw needn't show every extreme that they name: `buckets`: in each round a token's bucket b lies in the range of the block slots // 2048 that it goes to: from that block's index times 32 to that index times 32 plus 32. `slots`: in each round the values are distinct. The tokens that go to one block of 2048 places fill its first places, ordered by bucket and then by token. Of the 1024 tokens of one seq index at most 256 go to one block, and in every round some block receives exactly 256 from every seq index.
All inputs are finite; a program needn't handle non-finite values.
Results may differ from a plain program's by a relative error of at most 0.03.
Values may be sent and summed in bfloat16 or wider, within the bound.
No kernel may reach another device: no remote copies, remote signals or barrier semaphores. Data moves between devices by JAX's collectives and lax.ppermute only.
A program may use at most 256 MiB of HBM per device.

v0:
```python
import math

import jax
import jax.numpy as jnp
from jax import lax
from jax.sharding import PartitionSpec as P

HEADS = 8
SPAN = 64


NORM_EPS = 1e-05
KEY_EPS = 1e-06
MASKED = -1000000000.0
BLOCK_ROWS = 1024


def from_behind(value, axis, steps):
    count = lax.axis_size(axis)
    first, last = (max(0, -steps), min(count, count - steps))
    return lax.ppermute(value, axis, [(source, source + steps) for source in range(first, last)])


def shortened(shard):

    def short(part):
        return part.astype(jnp.bfloat16) if part.dtype == jnp.float32 else part

    return jax.tree.map(short, shard)


def product(left_side, right_side):
    return jnp.dot(left_side, right_side, preferred_element_type=jnp.float32)


def against(left_side, right_side):
    return lax.dot_general(
        left_side, right_side, (((0,), (0,)), ((), ())), preferred_element_type=jnp.float32
    )


def through(left_side, right_side):
    return lax.dot_general(
        left_side, right_side, (((1,), (1,)), ((), ())), preferred_element_type=jnp.float32
    )


def layer_norm(values, norm_gain, norm_shift):
    centre = values - jnp.mean(values, axis=-1, keepdims=True)
    spread = jnp.mean(centre * centre, axis=-1, keepdims=True)
    return centre * lax.rsqrt(spread + NORM_EPS) * norm_gain + norm_shift


def exact_gelu(values):
    return jax.nn.gelu(values, approximate=False)


def unit_keys(query_rows):
    head_view = query_rows.reshape(query_rows.shape[0], HEADS, -1)
    key_scale = lax.rsqrt(jnp.mean(head_view * head_view, axis=-1, keepdims=True) + KEY_EPS)
    return (head_view * key_scale * head_view.shape[-1] ** (-0.5)).reshape(query_rows.shape)


def with_previous(current, leading):
    earlier = jnp.concatenate([leading[None], current[:-1]], axis=0)
    return jnp.concatenate([earlier, current], axis=1)


def permitted(query_bucket, key_bucket, key_valid):
    span_width = query_bucket.shape[1]
    allowed = (query_bucket[:, :, None] == key_bucket[:, None, :]) & (key_valid[:, None, :] > 0)
    itself = jnp.arange(2 * span_width)[None, :] == jnp.arange(span_width)[:, None] + span_width
    others = allowed & jnp.logical_not(itself[None])
    lonely = jnp.logical_not(jnp.any(others, axis=-1, keepdims=True))
    return others | allowed & itself[None] & lonely


def scores_of(query_spans, key_spans, query_bucket, key_bucket, key_valid):
    allowed = permitted(query_bucket, key_bucket, key_valid)[:, None]
    scores = jnp.einsum(
        "cqhd,ckhd->chqk", query_spans, key_spans, preferred_element_type=jnp.float32
    )
    return (allowed, jnp.where(allowed, scores, MASKED))


def forward_block(pieces):
    query_spans, key_spans, value_spans, query_bucket, key_bucket, key_valid = pieces
    allowed, masked = scores_of(query_spans, key_spans, query_bucket, key_bucket, key_valid)
    row_max = jnp.max(masked, axis=-1, keepdims=True)
    raised = jnp.exp(masked - row_max)
    totals = jnp.sum(raised, axis=-1, keepdims=True)
    probabilities = (raised / totals).astype(jnp.bfloat16)
    outputs = jnp.einsum(
        "chqk,ckhd->cqhd", probabilities, value_spans, preferred_element_type=jnp.float32
    )
    return (outputs, (row_max + jnp.log(totals))[..., 0])


def backward_block(pieces):
    (
        query_spans,
        key_spans,
        value_spans,
        query_bucket,
        key_bucket,
        key_valid,
        log_totals,
        d_out,
        d_lse,
    ) = pieces
    allowed, masked = scores_of(query_spans, key_spans, query_bucket, key_bucket, key_valid)
    probabilities = jnp.exp(masked - log_totals[..., None])
    probs_low = probabilities.astype(jnp.bfloat16)
    d_probs = jnp.einsum("cqhd,ckhd->chqk", d_out, value_spans, preferred_element_type=jnp.float32)
    row_delta = jnp.sum(probabilities * d_probs, axis=-1, keepdims=True)
    d_scores = jnp.where(
        allowed, probabilities * (d_probs - row_delta + d_lse[..., None]), 0.0
    ).astype(jnp.bfloat16)
    d_query = jnp.einsum("chqk,ckhd->cqhd", d_scores, key_spans, preferred_element_type=jnp.float32)
    d_keys = jnp.einsum(
        "chqk,cqhd->ckhd", d_scores, query_spans, preferred_element_type=jnp.float32
    )
    d_values = jnp.einsum("chqk,cqhd->ckhd", probs_low, d_out, preferred_element_type=jnp.float32)
    return (d_query, d_keys, d_values)


def by_blocks(function, pieces, span_total):
    per_block = math.gcd(span_total, max(1, BLOCK_ROWS // SPAN))
    grouped = jax.tree.map(
        lambda member: member.reshape((span_total // per_block, per_block) + member.shape[1:]),
        pieces,
    )
    result = lax.map(function, grouped)
    return jax.tree.map(lambda member: member.reshape((span_total,) + member.shape[2:]), result)


def per_device(
    first_half,
    second_half,
    qk_weight,
    value_weight,
    output_weight,
    inner_weight,
    outer_weight,
    attn_gain,
    attn_shift,
    ffn_gain,
    ffn_shift,
    buckets,
    slots,
    first_grad,
    second_grad,
):
    gathered = (
        lax.all_gather(qk_weight, ("seq", "round"), axis=0, tiled=True),
        lax.all_gather(value_weight, ("seq", "round"), axis=0, tiled=True),
        lax.all_gather(output_weight, ("seq", "round"), axis=0, tiled=True),
        lax.all_gather(inner_weight, ("seq", "round"), axis=0, tiled=True),
        lax.all_gather(outer_weight, ("seq", "round"), axis=0, tiled=True),
        lax.all_gather(attn_gain, ("seq", "round"), axis=0, tiled=True),
        lax.all_gather(attn_shift, ("seq", "round"), axis=0, tiled=True),
        lax.all_gather(ffn_gain, ("seq", "round"), axis=0, tiled=True),
        lax.all_gather(ffn_shift, ("seq", "round"), axis=0, tiled=True),
    )
    (
        qk_full,
        value_full,
        output_full,
        inner_full,
        outer_full,
        attn_gain_full,
        attn_shift_full,
        ffn_gain_full,
        ffn_shift_full,
    ) = gathered
    seq_count = lax.axis_size("seq")
    round_count = lax.axis_size("round")
    own_rows = first_half.shape[0]
    model_width = first_half.shape[1]
    group_rows = own_rows * round_count
    slot_rows = 2 * group_rows
    capacity = slot_rows // seq_count
    span_total = slot_rows // SPAN
    head_size = model_width // HEADS
    zero_low = jnp.zeros((), jnp.bfloat16)
    first_in = first_half.astype(jnp.float32)
    second_in = second_half.astype(jnp.float32)
    normed, attn_norm_pull = jax.vjp(
        layer_norm,
        second_in,
        attn_gain_full.astype(jnp.float32),
        attn_shift_full.astype(jnp.float32),
    )
    normed_low = normed.astype(jnp.bfloat16)
    query_own = product(normed_low, qk_full).astype(jnp.bfloat16)
    value_own = product(normed_low, value_full).astype(jnp.bfloat16)
    query_group, value_group = (
        lax.all_gather(query_own, "round", axis=0, tiled=True),
        lax.all_gather(value_own, "round", axis=0, tiled=True),
    )
    slot_row = slots[0]
    bucket_row = buckets[0]
    target = slot_row // slot_rows
    local_place = slot_row - target * slot_rows
    onehot_dest = (target[:, None] == jnp.arange(seq_count, dtype=jnp.int32)[None, :]).astype(
        jnp.int32
    )
    ranking = jnp.sum((jnp.cumsum(onehot_dest, axis=0) - onehot_dest) * onehot_dest, axis=1)
    position = target * capacity + ranking
    sender = (
        jnp.full((slot_rows,), group_rows, jnp.int32)
        .at[position]
        .set(jnp.arange(group_rows, dtype=jnp.int32))
    )
    in_use = sender < group_rows
    picked = jnp.minimum(sender, group_rows - 1)
    send_shape = (seq_count, capacity)
    send_query = jnp.where(in_use[:, None], query_group[picked], zero_low).reshape(
        send_shape + (model_width,)
    )
    send_value = jnp.where(in_use[:, None], value_group[picked], zero_low).reshape(
        send_shape + (model_width,)
    )
    send_place = jnp.where(in_use, local_place[picked], -1).reshape(send_shape)
    send_bucket = jnp.where(in_use, bucket_row[picked], -1).reshape(send_shape)
    recv_query, recv_value, recv_place, recv_bucket = (
        lax.all_to_all(send_query, "seq", split_axis=0, concat_axis=0, tiled=True),
        lax.all_to_all(send_value, "seq", split_axis=0, concat_axis=0, tiled=True),
        lax.all_to_all(send_place, "seq", split_axis=0, concat_axis=0, tiled=True),
        lax.all_to_all(send_bucket, "seq", split_axis=0, concat_axis=0, tiled=True),
    )
    arrived_place = recv_place.reshape(slot_rows)
    arrived = arrived_place >= 0
    holder = (
        jnp.full((slot_rows,), slot_rows, jnp.int32)
        .at[jnp.where(arrived, arrived_place, slot_rows)]
        .set(jnp.arange(slot_rows, dtype=jnp.int32), mode="drop")
    )
    filled = holder < slot_rows
    taken_rows = jnp.minimum(holder, slot_rows - 1)
    sorted_query = jnp.where(
        filled[:, None], recv_query.reshape(slot_rows, model_width)[taken_rows], zero_low
    )
    sorted_value = jnp.where(
        filled[:, None], recv_value.reshape(slot_rows, model_width)[taken_rows], zero_low
    )
    sorted_bucket = jnp.where(filled, recv_bucket.reshape(slot_rows)[taken_rows], -1)
    sorted_valid = filled.astype(jnp.int32)
    key_float, key_pull = jax.vjp(unit_keys, sorted_query.astype(jnp.float32))
    key_low = key_float.astype(jnp.bfloat16)
    filled_count = jnp.sum(sorted_valid)
    last_start = jnp.maximum(filled_count - 1, 0) // SPAN * SPAN
    tail_keys = lax.dynamic_slice_in_dim(key_low, last_start, SPAN, 0)
    tail_value = lax.dynamic_slice_in_dim(sorted_value, last_start, SPAN, 0)
    tail_code = lax.dynamic_slice_in_dim(sorted_bucket + 1, last_start, SPAN, 0)
    halo_keys, halo_value, halo_code = from_behind((tail_keys, tail_value, tail_code), "seq", 1)
    halo_bucket = halo_code - 1
    halo_valid = (halo_code > 0).astype(jnp.int32)
    spanned = (span_total, SPAN, HEADS, head_size)
    query_spans = sorted_query.reshape(spanned)
    key_spans = with_previous(key_low.reshape(spanned), halo_keys.reshape(spanned[1:]))
    value_spans = with_previous(sorted_value.reshape(spanned), halo_value.reshape(spanned[1:]))
    query_bucket = sorted_bucket.reshape(span_total, SPAN)
    key_bucket = with_previous(query_bucket, halo_bucket)
    key_valid = with_previous(sorted_valid.reshape(span_total, SPAN), halo_valid)
    block_input = (query_spans, key_spans, value_spans, query_bucket, key_bucket, key_valid)
    out_spans, lse_spans = by_blocks(forward_block, block_input, span_total)
    sorted_out = out_spans.reshape(slot_rows, model_width).astype(jnp.bfloat16)
    sorted_lse = jnp.transpose(lse_spans, (0, 2, 1)).reshape(slot_rows, HEADS)
    back_index = jnp.clip(arrived_place, 0, slot_rows - 1)
    back_out = jnp.where(arrived[:, None], sorted_out[back_index], zero_low).reshape(
        send_shape + (model_width,)
    )
    back_lse = jnp.where(arrived[:, None], sorted_lse[back_index], 0.0).reshape(
        send_shape + (HEADS,)
    )
    ret_out, ret_lse = (
        lax.all_to_all(back_out, "seq", split_axis=0, concat_axis=0, tiled=True),
        lax.all_to_all(
            back_lse.astype(jnp.bfloat16), "seq", split_axis=0, concat_axis=0, tiled=True
        ).astype(back_lse.dtype),
    )
    round_out = ret_out.reshape(slot_rows, model_width)[position]
    round_weight = jnp.exp(ret_lse.reshape(slot_rows, HEADS)[position])
    all_out, all_weight = (
        lax.all_to_all(
            round_out.reshape(round_count, own_rows, model_width),
            "round",
            split_axis=0,
            concat_axis=0,
            tiled=True,
        ),
        lax.all_to_all(
            round_weight.reshape(round_count, own_rows, HEADS).astype(jnp.bfloat16),
            "round",
            split_axis=0,
            concat_axis=0,
            tiled=True,
        ).astype(jnp.float32),
    )
    out_heads = all_out.reshape(round_count, own_rows, HEADS, head_size).astype(jnp.float32)
    weight_sum = jnp.sum(all_weight, axis=0)
    mixed_heads = jnp.sum(all_weight[..., None] * out_heads, axis=0) / weight_sum[..., None]
    mixed_low = mixed_heads.reshape(own_rows, model_width).astype(jnp.bfloat16)
    first_sum = first_in + product(mixed_low, output_full)
    ffn_normed, ffn_norm_pull = jax.vjp(
        layer_norm, first_sum, ffn_gain_full.astype(jnp.float32), ffn_shift_full.astype(jnp.float32)
    )
    ffn_low = ffn_normed.astype(jnp.bfloat16)
    inner_act = product(ffn_low, inner_full)
    hidden, gelu_pull = jax.vjp(exact_gelu, inner_act)
    hidden_low = hidden.astype(jnp.bfloat16)
    second_sum = second_in + product(hidden_low, outer_full)
    outer_part = against(hidden_low, second_grad)
    (inner_back,) = gelu_pull(through(second_grad, outer_full))
    inner_back_low = inner_back.astype(jnp.bfloat16)
    inner_part = against(ffn_low, inner_back_low)
    first_from_ffn, ffn_gain_part, ffn_shift_part = ffn_norm_pull(
        through(inner_back_low, inner_full)
    )
    first_carry = first_grad.astype(jnp.float32) + first_from_ffn
    carry_low = first_carry.astype(jnp.bfloat16)
    output_part = against(mixed_low, carry_low)
    mixed_back = through(carry_low, output_full).reshape(own_rows, HEADS, head_size)
    mixed_dot = jnp.sum(mixed_back * mixed_heads, axis=-1)
    scaled = all_weight / weight_sum[None]
    d_out_all = (
        (scaled[..., None] * mixed_back[None])
        .reshape(round_count, own_rows, model_width)
        .astype(jnp.bfloat16)
    )
    d_lse_all = scaled * (jnp.sum(mixed_back[None] * out_heads, axis=-1) - mixed_dot[None])
    got_out, got_lse = (
        lax.all_to_all(d_out_all, "round", split_axis=0, concat_axis=0, tiled=True),
        lax.all_to_all(
            shortened(d_lse_all), "round", split_axis=0, concat_axis=0, tiled=True
        ).astype(d_lse_all.dtype),
    )
    round_out_back = got_out.reshape(group_rows, model_width)
    round_lse_back = got_lse.reshape(group_rows, HEADS)
    send_dout = jnp.where(in_use[:, None], round_out_back[picked], zero_low).reshape(
        send_shape + (model_width,)
    )
    send_dlse = jnp.where(in_use[:, None], round_lse_back[picked], 0.0).reshape(
        send_shape + (HEADS,)
    )
    recv_dout, recv_dlse = (
        lax.all_to_all(send_dout, "seq", split_axis=0, concat_axis=0, tiled=True),
        lax.all_to_all(shortened(send_dlse), "seq", split_axis=0, concat_axis=0, tiled=True).astype(
            send_dlse.dtype
        ),
    )
    sorted_dout = jnp.where(
        filled[:, None], recv_dout.reshape(slot_rows, model_width)[taken_rows], zero_low
    )
    sorted_dlse = jnp.where(filled[:, None], recv_dlse.reshape(slot_rows, HEADS)[taken_rows], 0.0)
    back_input = block_input + (
        lse_spans,
        sorted_dout.reshape(spanned),
        jnp.transpose(sorted_dlse.reshape(span_total, SPAN, HEADS), (0, 2, 1)),
    )
    dq_spans, dk_spans, dv_spans = by_blocks(backward_block, back_input, span_total)
    key_back = dk_spans[:, SPAN:] + jnp.concatenate(
        [dk_spans[1:, :SPAN], jnp.zeros_like(dk_spans[:1, :SPAN])], axis=0
    )
    value_back = dv_spans[:, SPAN:] + jnp.concatenate(
        [dv_spans[1:, :SPAN], jnp.zeros_like(dv_spans[:1, :SPAN])], axis=0
    )
    next_keys, next_value = (
        from_behind(dk_spans[0, :SPAN].astype(jnp.bfloat16), "seq", -1).astype(jnp.float32),
        from_behind(dv_spans[0, :SPAN].astype(jnp.bfloat16), "seq", -1).astype(jnp.float32),
    )
    key_back = key_back.reshape(slot_rows, model_width)
    value_back = value_back.reshape(slot_rows, model_width)
    key_back = lax.dynamic_update_slice_in_dim(
        key_back,
        lax.dynamic_slice_in_dim(key_back, last_start, SPAN, 0)
        + next_keys.reshape(SPAN, model_width),
        last_start,
        0,
    )
    value_back = lax.dynamic_update_slice_in_dim(
        value_back,
        lax.dynamic_slice_in_dim(value_back, last_start, SPAN, 0)
        + next_value.reshape(SPAN, model_width),
        last_start,
        0,
    )
    (query_from_keys,) = key_pull(key_back)
    query_back = (dq_spans.reshape(slot_rows, model_width) + query_from_keys).astype(jnp.bfloat16)
    value_back_low = value_back.astype(jnp.bfloat16)
    back_query = jnp.where(arrived[:, None], query_back[back_index], zero_low).reshape(
        send_shape + (model_width,)
    )
    back_value = jnp.where(arrived[:, None], value_back_low[back_index], zero_low).reshape(
        send_shape + (model_width,)
    )
    ret_query, ret_value = (
        lax.all_to_all(back_query, "seq", split_axis=0, concat_axis=0, tiled=True),
        lax.all_to_all(back_value, "seq", split_axis=0, concat_axis=0, tiled=True),
    )
    group_query = ret_query.reshape(slot_rows, model_width)[position].astype(jnp.float32)
    group_value = ret_value.reshape(slot_rows, model_width)[position].astype(jnp.float32)
    query_sum, value_sum = (
        lax.psum_scatter(
            group_query.astype(jnp.bfloat16), "round", scatter_dimension=0, tiled=True
        ).astype(jnp.float32),
        lax.psum_scatter(
            group_value.astype(jnp.bfloat16), "round", scatter_dimension=0, tiled=True
        ).astype(jnp.float32),
    )
    query_low = query_sum.astype(jnp.bfloat16)
    value_low = value_sum.astype(jnp.bfloat16)
    qk_part = against(normed_low, query_low)
    value_part = against(normed_low, value_low)
    normed_back = through(query_low, qk_full) + through(value_low, value_full)
    second_from_attn, attn_gain_part, attn_shift_part = attn_norm_pull(normed_back)
    second_carry = second_grad.astype(jnp.float32) + second_from_attn
    reduced = (
        lax.psum_scatter(qk_part, ("seq", "round"), scatter_dimension=0, tiled=True),
        lax.psum_scatter(value_part, ("seq", "round"), scatter_dimension=0, tiled=True),
        lax.psum_scatter(output_part, ("seq", "round"), scatter_dimension=0, tiled=True),
        lax.psum_scatter(inner_part, ("seq", "round"), scatter_dimension=0, tiled=True),
        lax.psum_scatter(outer_part, ("seq", "round"), scatter_dimension=0, tiled=True),
        lax.psum_scatter(attn_gain_part, ("seq", "round"), scatter_dimension=0, tiled=True),
        lax.psum_scatter(attn_shift_part, ("seq", "round"), scatter_dimension=0, tiled=True),
        lax.psum_scatter(ffn_gain_part, ("seq", "round"), scatter_dimension=0, tiled=True),
        lax.psum_scatter(ffn_shift_part, ("seq", "round"), scatter_dimension=0, tiled=True),
    )
    return (
        first_sum.astype(jnp.bfloat16),
        second_sum.astype(jnp.bfloat16),
        first_carry.astype(jnp.bfloat16),
        second_carry.astype(jnp.bfloat16),
        reduced[0],
        reduced[1],
        reduced[2],
        reduced[3],
        reduced[4],
        reduced[5],
        reduced[6],
        reduced[7],
        reduced[8],
    )


def solution(mesh):
    in_specs = (
        P(("seq", "round"), None),
        P(("seq", "round"), None),
        P(("seq", "round"), None),
        P(("seq", "round"), None),
        P(("seq", "round"), None),
        P(("seq", "round"), None),
        P(("seq", "round"), None),
        P(("seq", "round")),
        P(("seq", "round")),
        P(("seq", "round")),
        P(("seq", "round")),
        P("round", "seq"),
        P("round", "seq"),
        P(("seq", "round"), None),
        P(("seq", "round"), None),
    )
    out_specs = (
        P(("seq", "round"), None),
        P(("seq", "round"), None),
        P(("seq", "round"), None),
        P(("seq", "round"), None),
        P(("seq", "round"), None),
        P(("seq", "round"), None),
        P(("seq", "round"), None),
        P(("seq", "round"), None),
        P(("seq", "round"), None),
        P(("seq", "round")),
        P(("seq", "round")),
        P(("seq", "round")),
        P(("seq", "round")),
    )
    return jax.shard_map(
        per_device, mesh=mesh, in_specs=in_specs, out_specs=out_specs, check_vma=False
    )
```

profile of v0, /device:TPU:0, one launch (start us, length us, event | category | flops | bytes accessed | tf_op | source)
XLA Modules:
  0.0 2524.7 jit_solution(6919819860387326457)
XLA Ops:
  12.1 42.2 %all-reduce.11 = (bf16[1024]{0:T(1024)(128)(2,1)S(1)}, bf16[1024]{0:T(1024)(128)(2,1)S(1)}, bf16[1024]{0:T(1024)(128)(2,1)}, bf16[1024]{0:T(1024)(128)(2,1)}) all-reduce(bf16[1024]{0:T(1024)(128)(2,1)S(1)} %dynamic-update-slice.1, bf16[1024]{0:T(1024)(128)(2,1)S(1)} %dynamic-update-slice, ...), channel_id=1, replica_groups=mesh['seq'=8,'round'=4] {'seq','round'}, use_global_device_ids=true, to_apply=%add.3 | all-reduce | flops 4096 | bytes 16384
  57.6 12.5 all-gather.8.cloned.1.call-done
  73.5 54.8 %all-gather.12.cloned.1.call-done = bf16[1024,1024]{1,0:T(8,128)(2,1)} async-done(((bf16[32,1024]{1,0:T(8,128)(2,1)}), bf16[1024,1024]{1,0:T(8,128)(2,1)}) %all-gather.12.cloned.1.call-update) | async-done | bytes 2097168 | tf_op jit(solution)/shard_map/all_gather | solution.py:155
  163.2 12.8 gather_fusion.1
  176.4 12.9 gather_fusion.5
  201.5 145.5 %all_to_all.78 = bf16[8,256,1024]{2,1,0:T(8,128)(2,1)} all-to-all(bf16[8,256,1024]{2,1,0:T(8,128)(2,1)} %get-tuple-element.224), channel_id=1, replica_groups=mesh['seq'=8,'round'=4] {'seq'}, dimensions={0} | all-to-all | bytes 8388608 | tf_op jit(solution)/shard_map/all_to_all | solution.py:228
  360.5 11.8 gather_fusion.4
  386.9 13.7 gather_fusion.2
  405.9 77.6 %all-to-all-done.3 = bf16[8,256,1024]{2,1,0:T(8,128)(2,1)} async-done(((bf16[8,256,1024]{2,1,0:T(8,128)(2,1)}), bf16[8,256,1024]{2,1,0:T(8,128)(2,1)}, u32[]{:S(2)}, u32[]{:S(2)}) %all-to-all-start.3) | async-done | bytes 4194336 | tf_op jit(solution)/shard_map/all_to_all | solution.py:227
  483.5 13.9 gather_fusion.6
  502.7 28.9 %fusion.91 = f32[2048,8]{1,0:T(8,128)S(1)} fusion(bf16[2048,8,128]{2,1,0:T(8,128)(2,1)S(1)} %bitcast.332, pred[2048]{0:T(1024)(128)(4,1)S(1)} %get-tuple-element.201), kind=kLoop, calls=%fused_computation.123 | loop fusion | flops 8372224 | bytes 4261888 | tf_op jit(solution)/shard_map/jvp()/reduce_sum | solution.py:60
  565.6 9.9 pad_maximum_fusion
  575.5 10.0 pad_maximum_fusion.1
  585.5 29.9 %while.26 = (s32[]{:T(128)}, bf16[2,16,64,8,128]{4,2,3,1,0:T(8,128)(2,1)}, f32[2,16,8,64]{3,2,1,0:T(8,128)S(1)}, bf16[2,16,128,8,128]{4,2,3,1,0:T(8,128)(2,1)}, ...) while((s32[]{:T(128)}, ...), condition=%wide.region_13.14_spmd, body=%wide.region_9.13_spmd.sunk | while | flops 547629120 | bytes 87044840 | solution.py:133
  615.5 10.3 copy.157
  629.1 13.7 gather_fusion.9
  649.9 21.4 all-to-all-start.4
  686.6 86.6 %all-to-all-done.6 = bf16[8,256,1024]{2,1,0:T(8,128)(2,1)} async-done(((bf16[8,256,1024]{2,1,0:T(8,128)(2,1)}), bf16[8,256,1024]{2,1,0:T(8,128)(2,1)}, u32[]{:S(2)}, u32[]{:S(2)}) %all-to-all-start.6) | async-done | bytes 4194336 | tf_op jit(solution)/shard_map/all_to_all | solution.py:278
  796.8 17.7 all-to-all-done.7
  834.7 16.2 add_convert_fusion
  886.3 18.5 all-to-all-done.8
  934.4 86.1 %all-to-all-done.9 = bf16[8,256,1024]{2,1,0:T(8,128)(2,1)} async-done(((bf16[8,256,1024]{2,1,0:T(8,128)(2,1)}), bf16[8,256,1024]{2,1,0:T(8,128)(2,1)}, u32[]{:S(2)}, u32[]{:S(2)}) %all-to-all-start.9) | async-done | bytes 4194336 | tf_op jit(solution)/shard_map/all_to_all | solution.py:348
  1020.4 13.7 gather_fusion.12
  1039.7 219.3 %while.27 = (s32[]{:T(128)}, f32[2,16,64,8,128]{4,3,2,1,0:T(8,128)}, f32[2,16,128,8,128]{2,4,3,1,0:T(8,128)}, f32[2,16,128,8,128]{2,4,3,1,0:T(8,128)}, bf16[2,16...) while((s32[]{:T(128)}, ...), condition=%wide.region_25.26_spmd, body=%wide.region_22.25_spmd.sunk | while | flops 1367640320 | bytes 114703040 | solution.py:133
  1056.2 37.2 %fusion.215 = f32[1,16,64,8,128]{4,2,3,1,0:T(8,128)} fusion(bf16[2,16,128,8,128]{4,2,3,1,0:T(8,128)(2,1)} %get-tuple-element.445, s32[]{:T(128)S(6)} %copy.274, f32[16,8,64,128]{3,2,1,0:T(8,128)} %fusion.211, f32[16,8,64,128]{3,2,1,0:T(8,128)} %fusion.212, f32[16,8,64]{2,1,0:T(8,128)S(1)} %get-tuple-element.379, ...), kind=kOutput, calls=%fused_computation.71.clone.1 | convolution fusion | flops 278929536 | bytes 25624580 | tf_op jit(solution)/shard_map/while/body/eval_jaxpr/chqk,ckhd->cqhd/dot_general | solution.py:119
  1100.9 40.0 %bitcast_dynamic-update-slice_fusion.10 = f32[2,16,128,8,128]{2,4,3,1,0:T(8,128)} fusion(f32[2,16,128,8,128]{2,4,3,1,0:T(8,128)} %get-tuple-element.429, s32[]{:T(128)S(6)} %copy.274, f32[16,8,64,128]{3,2,1,0:T(8,128)} %fusion.211, f32[16,8,64,128]{3,2,1,0:T(8,128)} %fusion.212, f32[16,8,64]{2,1,0:T(8,128)S(1)} %get-tuple-element.379, ...), kind=kOutput, calls=%fused_computation.55.clone.1 | convolution fusion | flops 278929536 | bytes 27722752 | tf_op jit(solution)/shard_map/while/body/eval_jaxpr/chqk,cqhd->ckhd/dot_general | solution.py:120
  1165.8 37.2 %fusion.215 = f32[1,16,64,8,128]{4,2,3,1,0:T(8,128)} fusion(bf16[2,16,128,8,128]{4,2,3,1,0:T(8,128)(2,1)} %get-tuple-element.445, s32[]{:T(128)S(6)} %copy.274, f32[16,8,64,128]{3,2,1,0:T(8,128)} %fusion.211, f32[16,8,64,128]{3,2,1,0:T(8,128)} %fusion.212, f32[16,8,64]{2,1,0:T(8,128)S(1)} %get-tuple-element.379, ...), kind=kOutput, calls=%fused_computation.71.clone.1 | convolution fusion | flops 278929536 | bytes 25624580 | tf_op jit(solution)/shard_map/while/body/eval_jaxpr/chqk,ckhd->cqhd/dot_general | solution.py:119
  1210.4 39.8 %bitcast_dynamic-update-slice_fusion.10 = f32[2,16,128,8,128]{2,4,3,1,0:T(8,128)} fusion(f32[2,16,128,8,128]{2,4,3,1,0:T(8,128)} %get-tuple-element.429, s32[]{:T(128)S(6)} %copy.274, f32[16,8,64,128]{3,2,1,0:T(8,128)} %fusion.211, f32[16,8,64,128]{3,2,1,0:T(8,128)} %fusion.212, f32[16,8,64]{2,1,0:T(8,128)S(1)} %get-tuple-element.379, ...), kind=kOutput, calls=%fused_computation.55.clone.1 | convolution fusion | flops 278929536 | bytes 27722752 | tf_op jit(solution)/shard_map/while/body/eval_jaxpr/chqk,cqhd->ckhd/dot_general | solution.py:120
  1260.4 13.5 slice.129
  1302.7 12.6 copy.203
  1315.3 12.7 copy.202
  1328.0 12.5 copy.200
  1340.5 12.8 copy.199
  1353.3 10.2 pad_add_fusion
  1363.5 10.2 pad_add_fusion.1
  1389.4 14.1 gather_fusion.17
  1410.1 28.9 %fusion.92 = f32[2048,8]{1,0:T(8,128)S(1)} fusion(f32[2048,8,128]{2,1,0:T(8,128)S(1)} %bitcast.351, bf16[2048,8,128]{2,1,0:T(8,128)(2,1)S(1)} %bitcast.334, pred[2048]{0:T(1024)(128)(4,1)S(1)} %copy-done.49), kind=kLoop, calls=%fused_computation.124 | loop fusion | flops 8372224 | bytes 12650496 | tf_op jit(solution)/shard_map/transpose(jvp())/reduce_sum | solution.py:61
  1452.8 18.6 fusion.94
  1471.4 13.8 gather_fusion.15
  1490.3 99.5 %all_to_all.79 = bf16[8,256,1024]{2,1,0:T(8,128)(2,1)} all-to-all(bf16[8,256,1024]{2,1,0:T(8,128)(2,1)S(1)} %get-tuple-element.221), channel_id=1, replica_groups=mesh['seq'=8,'round'=4] {'seq'}, dimensions={0} | all-to-all | bytes 8388608 | tf_op jit(solution)/shard_map/all_to_all | solution.py:400
  1603.4 83.2 %all-to-all-done.12 = bf16[8,256,1024]{2,1,0:T(8,128)(2,1)} async-done(((bf16[8,256,1024]{2,1,0:T(8,128)(2,1)}), bf16[8,256,1024]{2,1,0:T(8,128)(2,1)}, u32[]{:S(2)}, u32[]{:S(2)}) %all-to-all-start.12) | async-done | bytes 4194336 | tf_op jit(solution)/shard_map/all_to_all | solution.py:399
  1703.8 21.5 reduce-scatter.8.cloned.1.call-done
  1762.1 40.1 %all-reduce.10 = (f32[1024]{0:T(1024)S(1)}, f32[1024]{0:T(1024)S(1)}, f32[1024]{0:T(1024)S(1)}, f32[1024]{0:T(1024)S(1)}) all-reduce(f32[1024]{0:T(1024)S(1)} %get-tuple-element.137, f32[1024]{0:T(1024)S(1)} %get-tuple-element.140, f32[1024]{0:T(1024)S(1)} %copy-done.71, ...), channel_id=9, replica_groups=mesh['seq'=8,'round'=4] {'seq','round'}, use_global_device_ids=true, to_apply=%region_37.38.clone | all-reduce | flops 4096 | bytes 32768
  1805.8 63.3 %reduce-scatter.16.cloned.1.call-done = f32[32,1024]{1,0:T(8,128)} async-done(((f32[1024,1024]{1,0:T(8,128)}), f32[32,1024]{1,0:T(8,128)}) %reduce-scatter.16.cloned.1.call-update) | async-done | bytes 131088 | tf_op jit(solution)/shard_map/reduce_scatter | solution.py:422
  1869.1 139.8 %reduce-scatter.14.cloned.1.call-done = f32[32,1024]{1,0:T(8,128)} async-done(((f32[1024,1024]{1,0:T(8,128)}), f32[32,1024]{1,0:T(8,128)}) %reduce-scatter.14.cloned.1.call-update) | async-done | bytes 131088 | tf_op jit(solution)/shard_map/reduce_scatter | solution.py:421
  2008.9 139.9 %reduce-scatter.12.cloned.1.call-done = f32[32,1024]{1,0:T(8,128)} async-done(((f32[1024,1024]{1,0:T(8,128)}), f32[32,1024]{1,0:T(8,128)}) %reduce-scatter.12.cloned.1.call-update) | async-done | bytes 131088 | tf_op jit(solution)/shard_map/reduce_scatter | solution.py:420
  2148.8 181.8 %reduce-scatter.18.cloned.1.call-done = f32[32,4096]{1,0:T(8,128)} async-done(((f32[1024,4096]{1,0:T(8,128)}), f32[32,4096]{1,0:T(8,128)}) %reduce-scatter.18.cloned.1.call-update) | async-done | bytes 524304 | tf_op jit(solution)/shard_map/reduce_scatter | solution.py:423
  2330.6 187.3 %reduce-scatter.20.cloned.1.call-done = f32[128,1024]{1,0:T(8,128)} async-done(((f32[4096,1024]{1,0:T(8,128)}), f32[128,1024]{1,0:T(8,128)}) %reduce-scatter.20.cloned.1.call-update) | async-done | bytes 524304 | tf_op jit(solution)/shard_map/reduce_scatter | solution.py:424
  (480 shorter events, 506.4 us)
Async XLA Ops:
  7.2 141.9 %copy-start = (s32[1,1024]{1,0:T(1,128)S(1)}, s32[1,1024]{1,0:T(1,128)}, u32[]{:S(2)}) copy-start(s32[1,1024]{1,0:T(1,128)} %param.30) | copy-start | bytes 12292
  7.2 121.0 %copy-start.8 = (bf16[256,1024]{1,0:T(8,128)(2,1)S(1)}, bf16[256,1024]{1,0:T(8,128)(2,1)}, u32[]{:S(2)}) copy-start(bf16[256,1024]{1,0:T(8,128)(2,1)} %param.20) | copy-start | bytes 1572868
  7.2 62.9 %all-gather.8.cloned.1.call-start = ((), (), s32[]{:S(2)}) async-start(), calls=%async_computation.21 | async-start | bytes 2162688 | tf_op jit(solution)/shard_map/all_gather | solution.py:156
  7.9 120.3 %all-gather.12.cloned.1.call-start = ((), (), s32[]{:S(2)}) async-start(), calls=%async_computation.23 | async-start | bytes 2162688 | tf_op jit(solution)/shard_map/all_gather | solution.py:155
  8.7 154.5 %all-gather.10.cloned.1.call-start = ((), (), s32[]{:S(2)}) async-start(), calls=%async_computation.22 | async-start | bytes 2621440 | tf_op jit(solution)/shard_map/all_gather | solution.py:199
  54.3 77.1 %copy-start.37 = (f32[1024]{0:T(1024)}, f32[1024]{0:T(1024)S(1)}, u32[]{:S(2)}) copy-start(f32[1024]{0:T(1024)S(1)} %convert_element_type.165) | copy-start | bytes 12292
  54.3 77.1 %copy-start.29 = (f32[1024]{0:T(1024)}, f32[1024]{0:T(1024)S(1)}, u32[]{:S(2)}) copy-start(f32[1024]{0:T(1024)S(1)} %convert_element_type.164) | copy-start | bytes 12292
  55.7 75.7 %copy-start.52 = (f32[256]{0:T(256)}, f32[256]{0:T(256)S(1)}, u32[]{:S(2)}) copy-start(f32[256]{0:T(256)S(1)} %broadcast_multiply_fusion.2) | copy-start | bytes 3076
  57.6 73.8 %copy-start.56 = (f32[256]{0:T(256)}, f32[256]{0:T(256)S(1)}, u32[]{:S(2)}) copy-start(f32[256]{0:T(256)S(1)} %fusion.133) | copy-start | bytes 3076
  57.6 75.0 %copy-start.58 = (s32[1,1024]{1,0:T(1,128)S(1)}, s32[1,1024]{1,0:T(1,128)}, u32[]{:S(2)}) copy-start(s32[1,1024]{1,0:T(1,128)} %param.31) | copy-start | bytes 12292
  73.4 103.0 %all-gather.14.cloned.1.call-start = ((), (), s32[]{:S(2)}) async-start(), calls=%async_computation.24 | async-start | bytes 2621440 | tf_op jit(solution)/shard_map/all_gather | solution.py:198
  131.4 690.8 %all-gather.16.cloned.1.call-start = ((), (), s32[]{:S(2)}) async-start(), calls=%async_computation.25 | async-start | bytes 2162688 | tf_op jit(solution)/shard_map/all_gather | solution.py:157
  132.0 694.8 %all-gather.18.cloned.1.call-start = ((), (), s32[]{:S(2)}) async-start(), calls=%async_computation.26 | async-start | bytes 8650752 | tf_op jit(solution)/shard_map/all_gather | solution.py:158
  140.4 36.0 %copy-start.35 = (s32[2048]{0:T(1024)}, s32[2048]{0:T(1024)S(1)}, u32[]{:S(2)}) copy-start(s32[2048]{0:T(1024)S(1)} %fusion.122) | copy-start | bytes 24580
  158.8 30.5 %all-to-all-start = ((s32[8,1,256]{2,1,0:T(1,128)}), s32[8,1,256]{2,1,0:T(1,128)S(1)}, u32[]{:S(2)}, u32[]{:S(2)}) async-start(s32[8,1,256]{2,1,0:T(1,128)} %bitcast.30), calls=%async_computation | async-start | bytes 16384 | tf_op jit(solution)/shard_map/all_to_all | solution.py:229
  189.3 12.1 all-to-all-start.2
  346.9 136.6 %all-to-all-start.3 = ((bf16[8,256,1024]{2,1,0:T(8,128)(2,1)}), bf16[8,256,1024]{2,1,0:T(8,128)(2,1)}, u32[]{:S(2)}, u32[]{:S(2)}) async-start(bf16[8,256,1024]{2,1,0:T(8,128)(2,1)} %get-tuple-element.223), calls=%async_computation.3 | async-start | bytes 8388608 | tf_op jit(solution)/shard_map/all_to_all | solution.py:227
  351.5 483.1 %all-gather.20.cloned.1.call-start = ((), (), s32[]{:S(2)}) async-start(), calls=%async_computation.27 | async-start | bytes 8650752 | tf_op jit(solution)/shard_map/all_gather | solution.py:159
  360.4 123.1 %copy-start.39 = (s32[2048]{0:T(1024)}, s32[2048]{0:T(1024)S(1)}, u32[]{:S(2)}) copy-start(s32[2048]{0:T(1024)S(1)} %fusion.123) | copy-start | bytes 24580
  372.3 168.7 %copy-start.47 = (pred[2048]{0:T(1024)(128)(4,1)}, pred[2048]{0:T(1024)(128)(4,1)S(1)}, u32[]{:S(2)}) copy-start(pred[2048]{0:T(1024)(128)(4,1)S(1)} %get-tuple-element.201) | copy-start | bytes 6148
  373.6 174.0 %copy-start.54 = (pred[2,16,64]{2,1,0:T(8,128)(4,1)}, pred[2,16,64]{2,1,0:T(8,128)(4,1)S(1)}, u32[]{:S(2)}) copy-start(pred[2,16,64]{2,1,0:T(8,128)(4,1)S(1)} %broadcast_in_dim.254) | copy-start | bytes 6148
  373.8 12.9 collective-permute-start.1
  377.8 293.5 %copy-start.61 = (pred[8,256]{1,0:T(8,128)(4,1)}, pred[8,256]{1,0:T(8,128)(4,1)S(1)}, u32[]{:S(2)}) copy-start(pred[8,256]{1,0:T(8,128)(4,1)S(1)} %fusion.124) | copy-start | bytes 6148
  377.8 265.1 %copy-start.43 = (s32[2048]{0:T(1024)}, s32[2048]{0:T(1024)S(1)}, u32[]{:S(2)}) copy-start(s32[2048]{0:T(1024)S(1)} %broadcast_clamp_fusion) | copy-start | bytes 24580
  532.3 26.0 %collective-permute-start = (bf16[64,1024]{1,0:T(8,128)(2,1)S(1)}, bf16[64,1024]{1,0:T(8,128)(2,1)S(1)}, u32[]{:S(2)}, u32[]{:S(2)}) collective-permute-start(bf16[64,1024]{1,0:T(8,128)(2,1)S(1)} %constant_dynamic-slice_fusion.1), channel_id=1, source_target_pairs={{0,4},{4,8},{8,12},{12,16},{16,20},{20,24},{24,28},{1,5},{5,9},{9,... | collective-permute-start | bytes 393224 | tf_op jit(solution)/shard_map/ppermute | solution.py:21
  542.8 19.2 collective-permute-start.2
  649.9 28.1 %all-to-all-start.4 = ((bf16[8,256,8]{1,2,0:T(8,128)(2,1)}), bf16[8,256,8]{1,2,0:T(8,128)(2,1)S(1)}, u32[]{:S(2)}, u32[]{:S(2)}) async-start(bf16[8,256,8]{1,2,0:T(8,128)(2,1)} %select_convert_fusion.2), calls=%async_computation.4 | async-start | bytes 65536 | tf_op jit(solution)/shard_map/all_to_all | solution.py:279
  678.0 95.3 %all-to-all-start.6 = ((bf16[8,256,1024]{2,1,0:T(8,128)(2,1)}), bf16[8,256,1024]{2,1,0:T(8,128)(2,1)}, u32[]{:S(2)}, u32[]{:S(2)}) async-start(bf16[8,256,1024]{2,1,0:T(8,128)(2,1)} %broadcast_select_fusion.5), calls=%async_computation.6 | async-start | bytes 8388608 | tf_op jit(solution)/shard_map/all_to_all | solution.py:278
  682.8 102.5 %copy-start.50 = (s32[1024]{0:T(1024)}, s32[1024]{0:T(1024)S(1)}, u32[]{:S(2)}) copy-start(s32[1024]{0:T(1024)S(1)} %broadcast_clamp_fusion.1) | copy-start | bytes 12292
  773.2 12.0 all-to-all-start.5
  785.3 29.3 %all-to-all-start.7 = ((bf16[4,256,1024]{2,1,0:T(8,128)(2,1)}), bf16[4,256,1024]{2,1,0:T(8,128)(2,1)S(1)}, u32[]{:S(2)}, u32[]{:S(2)}) async-start(bf16[4,256,1024]{2,1,0:T(8,128)(2,1)} %bitcast.376), calls=%async_computation.7 | async-start | bytes 4194304 | tf_op jit(solution)/shard_map/all_to_all | solution.py:286
  788.9 65.2 %copy-start.41 = (f32[1024]{0:T(1024)}, f32[1024]{0:T(1024)S(1)}, u32[]{:S(2)}) copy-start(f32[1024]{0:T(1024)S(1)} %convert_element_type.184) | copy-start | bytes 12292
  789.0 37.8 %copy-start.45 = (f32[1024]{0:T(1024)}, f32[1024]{0:T(1024)S(1)}, u32[]{:S(2)}) copy-start(f32[1024]{0:T(1024)S(1)} %convert_element_type.185) | copy-start | bytes 12292
  860.2 15.2 all-to-all-start.10
  875.4 29.3 %all-to-all-start.8 = ((bf16[4,256,1024]{2,1,0:T(8,128)(2,1)}), bf16[4,256,1024]{2,1,0:T(8,128)(2,1)S(1)}, u32[]{:S(2)}, u32[]{:S(2)}) async-start(bf16[4,256,1024]{2,1,0:T(8,128)(2,1)} %multiply_convert_fusion.1), calls=%async_computation.8 | async-start | bytes 4194304 | tf_op jit(solution)/shard_map/all_to_all | solution.py:334
  904.7 17.2 all-to-all-start.11
  921.9 98.5 %all-to-all-start.9 = ((bf16[8,256,1024]{2,1,0:T(8,128)(2,1)}), bf16[8,256,1024]{2,1,0:T(8,128)(2,1)}, u32[]{:S(2)}, u32[]{:S(2)}) async-start(bf16[8,256,1024]{2,1,0:T(8,128)(2,1)} %broadcast_select_fusion.6), calls=%async_computation.9 | async-start | bytes 8388608 | tf_op jit(solution)/shard_map/all_to_all | solution.py:348
  1300.0 84.9 %collective-permute-start.4 = (bf16[64,8,128]{2,1,0:T(8,128)(2,1)S(1)}, bf16[64,8,128]{2,1,0:T(8,128)(2,1)S(1)}, u32[]{:S(2)}, u32[]{:S(2)}) collective-permute-start(bf16[64,8,128]{2,1,0:T(8,128)(2,1)S(1)} %bitcast.387), channel_id=1, source_target_pairs={{4,0},{8,4},{12,8},{16,12},{20,16},{24,20},{28,24},{5,1},{9,5},{13... | collective-permute-start | bytes 393224 | tf_op jit(solution)/shard_map/ppermute | solution.py:21
  1301.4 83.5 %collective-permute-start.3 = (bf16[64,8,128]{2,1,0:T(8,128)(2,1)S(1)}, bf16[64,8,128]{2,1,0:T(8,128)(2,1)S(1)}, u32[]{:S(2)}, u32[]{:S(2)}) collective-permute-start(bf16[64,8,128]{2,1,0:T(8,128)(2,1)S(1)} %bitcast.389), channel_id=1, source_target_pairs={{4,0},{8,4},{12,8},{16,12},{20,16},{24,20},{28,24},{5,1},{9,5},{13... | collective-permute-start | bytes 393224 | tf_op jit(solution)/shard_map/ppermute | solution.py:21
  1589.8 96.8 %all-to-all-start.12 = ((bf16[8,256,1024]{2,1,0:T(8,128)(2,1)}), bf16[8,256,1024]{2,1,0:T(8,128)(2,1)}, u32[]{:S(2)}, u32[]{:S(2)}) async-start(bf16[8,256,1024]{2,1,0:T(8,128)(2,1)} %get-tuple-element.222), calls=%async_computation.12 | async-start | bytes 8388608 | tf_op jit(solution)/shard_map/all_to_all | solution.py:399
  1594.5 103.9 %reduce-scatter.10.cloned.1.call-start = ((), (), s32[]{:S(2)}) async-start(), calls=%async_computation.29 | async-start | bytes 2621440 | tf_op jit(solution)/shard_map/reduce_scatter | solution.py:408
  1603.4 121.9 %reduce-scatter.8.cloned.1.call-start = ((), (), s32[]{:S(2)}) async-start(), calls=%async_computation.28 | async-start | bytes 2621440 | tf_op jit(solution)/shard_map/reduce_scatter | solution.py:405
  1695.5 173.6 %reduce-scatter.16.cloned.1.call-start = ((), (), s32[]{:S(2)}) async-start(), calls=%async_computation.32 | async-start | bytes 4325376 | tf_op jit(solution)/shard_map/reduce_scatter | solution.py:422
  1698.4 310.5 %reduce-scatter.14.cloned.1.call-start = ((), (), s32[]{:S(2)}) async-start(), calls=%async_computation.31 | async-start | bytes 4325376 | tf_op jit(solution)/shard_map/reduce_scatter | solution.py:421
  1703.5 445.2 %reduce-scatter.12.cloned.1.call-start = ((), (), s32[]{:S(2)}) async-start(), calls=%async_computation.30 | async-start | bytes 4325376 | tf_op jit(solution)/shard_map/reduce_scatter | solution.py:420
  1729.2 601.3 %reduce-scatter.18.cloned.1.call-start = ((), (), s32[]{:S(2)}) async-start(), calls=%async_computation.33 | async-start | bytes 17301504 | tf_op jit(solution)/shard_map/reduce_scatter | solution.py:423
  1740.4 777.5 %reduce-scatter.20.cloned.1.call-start = ((), (), s32[]{:S(2)}) async-start(), calls=%async_computation.34 | async-start | bytes 17301504 | tf_op jit(solution)/shard_map/reduce_scatter | solution.py:424
  1759.8 758.1 %copy-start.1 = (s32[1,1024]{1,0:T(1,128)S(1)}, s32[1,1024]{1,0:T(1,128)}, u32[]{:S(2)}) copy-start(s32[1,1024]{1,0:T(1,128)} %param.30) | copy-start | bytes 12292
  (74 other events, 560.1 us)
Sparse Core Ops, SparseCore 0:
  10.9 59.1 all-gather.7
  72.9 55.2 all-gather.11
  130.4 21.4 all-gather.9
  153.9 22.5 all-gather.13
  179.2 63.4 all-gather.15
  245.4 101.7 all-gather.17
  355.3 130.0 all-gather.19
  1603.5 31.8 reduce-scatter.9
  1695.7 29.5 reduce-scatter.7
  1728.0 141.0 reduce-scatter.15
  1872.0 136.9 reduce-scatter.13
  2011.6 137.1 reduce-scatter.11
  2151.6 178.8 reduce-scatter.17
  2333.3 184.5 reduce-scatter.19
where the time goes:
time: 2540 us; the launch traced here: 2520 us
  waiting for transfers between devices  1190 us (47%)
  local copies, waits for them, and re-layouts  421 us (17%)
  blocking collectives  327 us (13%)
  matrix products  295 us (12%)
  other arithmetic  197 us (8%)
  starting transfers between devices  81.3 us (3%)
    reduce_scatter x1, waiting for transfers between devices, per_device(): lax.psum_scatter(outer_part, ('seq', 'round'), scatter_dimension=0, tiled...  187 us
    reduce_scatter x1, waiting for transfers between devices, per_device(): lax.psum_scatter(inner_part, ('seq', 'round'), scatter_dimension=0, tiled...  182 us
    all_to_all x1, blocking collectives, per_device(): lax.all_to_all(send_value, 'seq', split_axis=0, concat_axis=0, tiled=True)  145 us
    reduce_scatter x1, waiting for transfers between devices, per_device(): lax.psum_scatter(qk_part, ('seq', 'round'), scatter_dimension=0, tiled=True)  140 us
    reduce_scatter x1, waiting for transfers between devices, per_device(): lax.psum_scatter(value_part, ('seq', 'round'), scatter_dimension=0, tiled...  140 us
    unnamed x196, local copies, waits for them, and re-layouts  105 us
    all_to_all x1, blocking collectives, per_device(): lax.all_to_all(back_value, 'seq', split_axis=0, concat_axis=0, tiled=True)  99.5 us
    all_to_all x1, waiting for transfers between devices, per_device(): lax.all_to_all(back_out, 'seq', split_axis=0, concat_axis=0, tiled=True)  86.6 us
  transfers between devices with their start and end apart: 31, of which 18 were waited for; matrix products, arithmetic and copies ran while one was open for 19% of the time, Pallas kernels for 0%

commit v1 on v0

v1 whole, which is shorter than its diff:
```python
import functools
import math

import jax
import jax.numpy as jnp
from jax import lax
from jax.experimental import pallas as pl
from jax.experimental.pallas import tpu as pltpu
from jax.sharding import Mesh
from jax.sharding import PartitionSpec as P

HEADS = 8
NORM_EPS = 1e-05
MASKED = -1000000000.0
SPAN = 64
HEADD = 128
PAD = 16
UNROLL = 17
TOKB = 128
CHUNK = 4096
VMEM_LIMIT = 60 * 2**20
KEY_EPS = 1e-06
bf = jnp.bfloat16
f32 = jnp.float32


def product(left_side, right_side):
    return jnp.dot(left_side, right_side, preferred_element_type=f32)


def against(left_side, right_side):
    return lax.dot_general(
        left_side, right_side, (((0,), (0,)), ((), ())), preferred_element_type=f32
    )


def through(left_side, right_side):
    return lax.dot_general(
        left_side, right_side, (((1,), (1,)), ((), ())), preferred_element_type=f32
    )


def aligned(start, size, step=SPAN):
    return pl.ds(pl.multiple_of(start, step), size)


def fill_zero(ref, first=0, rows=None):
    rows = ref.shape[0] if rows is None else rows

    def body(step, carry):
        ref[aligned(first + step * SPAN, SPAN), :] = jnp.zeros((SPAN, ref.shape[1]), ref.dtype)
        return carry

    lax.fori_loop(0, rows // SPAN, body, 0)


def diagonal():
    rows = lax.broadcasted_iota(jnp.int32, (TOKB, TOKB), 0)
    return rows == lax.broadcasted_iota(jnp.int32, (TOKB, TOKB), 1)


def forward_kernel(
    own_rows,
    load_steps,
    place_ref,
    token_ref,
    bias_ref,
    pay_ref,
    query_ref,
    key_ref,
    value_ref,
    prob_ref,
    sum_ref,
    wide_a,
    wide_b,
    stage_a,
    stage_b,
):
    step = pl.program_id(0)
    own_spans = bias_ref.shape[0] // SPAN
    tail = SPAN * (own_spans + 1)

    @pl.when(step == 0)
    def _():
        fill_zero(wide_a)
        fill_zero(wide_b)

    @pl.when(step < load_steps)
    def _():
        def scatter(block, carry):
            both = token_ref[aligned(block * TOKB, TOKB, TOKB), :].astype(f32)
            stage_a[...] = both[:, :HEADD]
            stage_b[...] = both[:, HEADD:]
            for row in range(TOKB):
                place = place_ref[step * CHUNK + block * TOKB + row]
                wide_a[pl.ds(place, 1), :] = stage_a[row : row + 1, :]
                wide_b[pl.ds(place, 1), :] = stage_b[row : row + 1, :]
            return carry

        lax.fori_loop(0, CHUNK // TOKB, scatter, 0)

    def unit_keys(query):
        square = jnp.sum(query * query, axis=-1, keepdims=True)
        scale = lax.rsqrt(square * (1.0 / HEADD) + KEY_EPS) * HEADD**-0.5
        return (query * scale).astype(bf)

    @pl.when(step == load_steps)
    def _():
        query_ref[:SPAN, :] = wide_a[:SPAN, :].astype(bf)
        key_ref[:SPAN, :] = unit_keys(wide_a[:SPAN, :])
        value_ref[:SPAN, :] = wide_b[:SPAN, :].astype(bf)
        wide_a[:SPAN, :] = jnp.zeros((SPAN, HEADD), f32)
        wide_b[:SPAN, :] = jnp.zeros((SPAN, HEADD), f32)
        for ref in (query_ref, key_ref, value_ref):
            ref[pl.ds(tail, SPAN), :] = jnp.zeros((SPAN, HEADD), bf)
        ones = jnp.ones((2 * SPAN, HEADD), bf)

        def spans(group, carry):
            first = group * (UNROLL * SPAN)
            prev = aligned(first, SPAN)
            own = aligned(first, UNROLL * SPAN)
            here = aligned(first + SPAN, UNROLL * SPAN)
            query_wide = wide_a[here, :]
            values = wide_b[here, :].astype(bf)
            bias = bias_ref[own, :]
            keys = jnp.concatenate([key_ref[prev, :], unit_keys(query_wide)], axis=0)
            seen = jnp.concatenate([value_ref[prev, :], values], axis=0)
            query = query_wide.astype(bf)
            results = []
            for span in range(UNROLL):
                mine = slice(span * SPAN, (span + 1) * SPAN)
                both = slice(span * SPAN, (span + 2) * SPAN)
                raised = jnp.exp(through(query[mine], keys[both]) + bias[mine])
                low = raised.astype(bf)
                total = product(low, ones)
                inverse = jnp.where(total > 0.0, 1.0 / total, 0.0)
                results.append((product(low, seen[both]), total, (raised * inverse).astype(bf)))
            query_ref[here, :] = query
            key_ref[here, :] = keys[SPAN:]
            value_ref[here, :] = values
            for span, (weighted, total, probs) in enumerate(results):
                at = aligned(first + (span + 1) * SPAN, SPAN)
                wide_a[at, :] = weighted
                wide_b[at, :] = total
                prob_ref[aligned(first + span * SPAN, SPAN), :] = probs
            return carry

        lax.fori_loop(0, own_spans // UNROLL, spans, 0)
        wide_a[pl.ds(tail, SPAN), :] = jnp.zeros((SPAN, HEADD), f32)
        wide_b[pl.ds(tail, SPAN), :] = jnp.zeros((SPAN, HEADD), f32)

    @pl.when(step > load_steps)
    def _():
        blocks = own_rows // TOKB
        per_step = CHUNK // own_rows
        eye = diagonal()
        sum_rows = lax.broadcasted_iota(jnp.int32, (PAD, TOKB), 0)
        offset = (step - load_steps - 1) * CHUNK

        def collect(chunk, carry):
            first = chunk * (own_rows + PAD)
            sums = jnp.zeros((PAD, TOKB), f32)
            for block in range(blocks):
                start = offset + chunk * own_rows + block * TOKB
                for row in range(TOKB):
                    place = place_ref[start + row]
                    stage_a[row : row + 1, :] = wide_a[pl.ds(place, 1), :]
                    stage_b[row : row + 1, :] = wide_b[pl.ds(place, 1), :]
                pay_ref[aligned(first + block * TOKB, TOKB, PAD), :] = stage_a[...].astype(bf)
                packed = jnp.sum(jnp.where(eye, stage_b[...], 0.0), axis=0, keepdims=True)
                sum_ref[pl.ds(chunk * blocks + block, 1), :] = packed
                sums = jnp.where(sum_rows == block, packed, sums)
            pay_ref[aligned(first + own_rows, PAD, PAD), :] = sums.astype(bf)
            return carry

        lax.fori_loop(0, per_step, collect, 0)


def attend_forward(place, tokens_in, bias, own_rows):
    tokens = tokens_in.shape[0]
    steps = tokens // CHUNK
    own_spans = bias.shape[0] // SPAN
    rows = SPAN * (own_spans + 2)
    pay_rows = CHUNK // own_rows * (own_rows + PAD)
    once = pl.Buffered(1)

    def whole(shape):
        return pl.BlockSpec(shape, lambda step: (0, 0), pipeline_mode=once)

    def first_part(shape):
        return pl.BlockSpec(shape, lambda step: (jnp.minimum(step, steps - 1), 0))

    def last_part(shape):
        return pl.BlockSpec(shape, lambda step: (jnp.maximum(step - steps - 1, 0), 0))

    sorted_rows = jax.ShapeDtypeStruct((rows, HEADD), bf)
    return pl.pallas_call(
        functools.partial(forward_kernel, own_rows, steps),
        grid=(2 * steps + 1,),
        out_shape=(
            jax.ShapeDtypeStruct((steps * pay_rows, HEADD), bf),
            sorted_rows,
            sorted_rows,
            sorted_rows,
            jax.ShapeDtypeStruct((own_spans * SPAN, 2 * SPAN), bf),
            jax.ShapeDtypeStruct((tokens // TOKB, TOKB), f32),
        ),
        in_specs=[
            pl.BlockSpec(memory_space=pltpu.SMEM),
            first_part((CHUNK, 2 * HEADD)),
            whole(bias.shape),
        ],
        out_specs=(
            last_part((pay_rows, HEADD)),
            whole((rows, HEADD)),
            whole((rows, HEADD)),
            whole((rows, HEADD)),
            whole((own_spans * SPAN, 2 * SPAN)),
            last_part((CHUNK // TOKB, TOKB)),
        ),
        scratch_shapes=[pltpu.VMEM((rows, HEADD), f32)] * 2 + [pltpu.VMEM((TOKB, HEADD), f32)] * 2,
        compiler_params=pltpu.CompilerParams(vmem_limit_bytes=VMEM_LIMIT),
        name="attend_forward",
    )(place, tokens_in, bias)


def backward_kernel(
    own_rows,
    load_steps,
    place_ref,
    pay_ref,
    sum_ref,
    query_ref,
    key_ref,
    value_ref,
    prob_ref,
    out_ref,
    wide_a,
    wide_b,
    wide_c,
    stage_a,
    stage_b,
):
    step = pl.program_id(0)
    own_spans = prob_ref.shape[0] // SPAN
    tail = SPAN * (own_spans + 1)

    @pl.when(step == 0)
    def _():
        fill_zero(wide_a)
        fill_zero(wide_b)

    @pl.when(step < load_steps)
    def _():
        blocks = own_rows // TOKB
        eye = diagonal()
        ones = jnp.ones((2 * TOKB, TOKB), bf)

        def lanes(row):
            high = row.astype(bf).astype(f32)
            parts = [jnp.where(eye, high, 0.0), jnp.where(eye, row - high, 0.0)]
            return product(jnp.concatenate(parts, axis=1).astype(bf), ones)

        def scatter(chunk, carry):
            first = chunk * (own_rows + PAD)
            extra = pay_ref[aligned(first + own_rows, PAD, PAD), :].astype(f32)
            for block in range(blocks):
                share = sum_ref[pl.ds(chunk * blocks + block, 1), :]
                share = share / extra[blocks + block : blocks + block + 1, :]
                rows = pay_ref[aligned(first + block * TOKB, TOKB, PAD), :].astype(f32)
                stage_a[...] = rows * lanes(share)
                stage_b[...] = lanes(share * extra[block : block + 1, :])
                start = step * CHUNK + chunk * own_rows + block * TOKB
                for row in range(TOKB):
                    place = place_ref[start + row]
                    wide_a[pl.ds(place, 1), :] = stage_a[row : row + 1, :]
                    wide_b[pl.ds(place, 1), :] = stage_b[row : row + 1, :]
            return carry

        lax.fori_loop(0, CHUNK // own_rows, scatter, 0)

    def pulled(query_low, d_query, d_keys):
        query = query_low.astype(f32)
        inverse = lax.rsqrt(
            jnp.sum(query * query, axis=-1, keepdims=True) * (1.0 / HEADD) + KEY_EPS
        )
        along = jnp.sum(query * d_keys, axis=-1, keepdims=True)
        scale = inverse * HEADD**-0.5
        return d_query + scale * d_keys - (scale * inverse * inverse * along * (1.0 / HEADD)) * query

    @pl.when(step == load_steps)
    def _():
        for ref in (wide_a, wide_b, wide_c):
            ref[:SPAN, :] = jnp.zeros((SPAN, HEADD), f32)
        zero = jnp.zeros((SPAN, HEADD), bf)

        def spans(group, carry):
            first = group * (UNROLL * SPAN)
            prev = aligned(first, SPAN)
            own = aligned(first, UNROLL * SPAN)
            here = aligned(first + SPAN, UNROLL * SPAN)
            around = aligned(first, (UNROLL + 1) * SPAN)
            query = query_ref[around, :]
            keys = key_ref[around, :]
            values = value_ref[around, :]
            probs = prob_ref[own, :]
            d_out = wide_a[here, :].astype(bf)
            delta = wide_b[here, :]
            d_query = [wide_a[prev, :]]
            d_keys = [wide_b[prev, :]]
            d_values = [wide_c[prev, :]]
            for span in range(UNROLL):
                mine = slice(span * SPAN, (span + 1) * SPAN)
                after = slice((span + 1) * SPAN, (span + 2) * SPAN)
                both = slice(span * SPAN, (span + 2) * SPAN)
                d_probs = through(d_out[mine], values[both])
                prob = probs[mine]
                d_scores = (prob.astype(f32) * (d_probs - delta[mine])).astype(bf)
                d_query.append(product(d_scores, keys[both]))
                right = jnp.concatenate(
                    [
                        jnp.concatenate([query[after], zero], axis=1),
                        jnp.concatenate([zero, d_out[mine]], axis=1),
                    ],
                    axis=0,
                )
                pair = against(jnp.concatenate([d_scores, prob], axis=0), right)
                d_keys[-1] = d_keys[-1] + pair[:SPAN, :HEADD]
                d_values[-1] = d_values[-1] + pair[:SPAN, HEADD:]
                d_keys.append(pair[SPAN:, :HEADD])
                d_values.append(pair[SPAN:, HEADD:])
            for span in range(UNROLL + 1):
                at = aligned(first + span * SPAN, SPAN)
                wide_c[at, :] = d_values[span]
                if span < UNROLL:
                    rows = slice(span * SPAN, (span + 1) * SPAN)
                    wide_a[at, :] = pulled(query[rows], d_query[span], d_keys[span])
                else:
                    wide_a[at, :] = d_query[span]
                    wide_b[at, :] = d_keys[span]
            return carry

        lax.fori_loop(0, own_spans // UNROLL, spans, 0)
        last = pl.ds(tail - SPAN, SPAN)
        wide_a[last, :] = pulled(query_ref[last, :], wide_a[last, :], wide_b[last, :])
        wide_a[pl.ds(tail, SPAN), :] = jnp.zeros((SPAN, HEADD), f32)
        wide_c[pl.ds(tail, SPAN), :] = jnp.zeros((SPAN, HEADD), f32)

    @pl.when(step > load_steps)
    def _():
        offset = (step - load_steps - 1) * CHUNK

        def collect(block, carry):
            for row in range(TOKB):
                place = place_ref[offset + block * TOKB + row]
                stage_a[row : row + 1, :] = wide_a[pl.ds(place, 1), :]
                stage_b[row : row + 1, :] = wide_c[pl.ds(place, 1), :]
            here = aligned(block * TOKB, TOKB, TOKB)
            out_ref[here, :HEADD] = stage_a[...].astype(bf)
            out_ref[here, HEADD:] = stage_b[...].astype(bf)
            return carry

        lax.fori_loop(0, CHUNK // TOKB, collect, 0)


def attend_backward(place, pay, sums, query, keys, values, probs, own_rows):
    tokens = place.shape[0]
    steps = tokens // CHUNK
    rows = query.shape[0]
    pay_rows = CHUNK // own_rows * (own_rows + PAD)
    once = pl.Buffered(1)

    def whole(shape):
        return pl.BlockSpec(shape, lambda step: (0, 0), pipeline_mode=once)

    def first_part(shape):
        return pl.BlockSpec(shape, lambda step: (jnp.minimum(step, steps - 1), 0))

    def last_part(shape):
        return pl.BlockSpec(shape, lambda step: (jnp.maximum(step - steps - 1, 0), 0))

    return pl.pallas_call(
        functools.partial(backward_kernel, own_rows, steps),
        grid=(2 * steps + 1,),
        out_shape=jax.ShapeDtypeStruct((tokens, 2 * HEADD), bf),
        in_specs=[
            pl.BlockSpec(memory_space=pltpu.SMEM),
            first_part((pay_rows, HEADD)),
            first_part((CHUNK // TOKB, TOKB)),
            whole((rows, HEADD)),
            whole((rows, HEADD)),
            whole((rows, HEADD)),
            whole(probs.shape),
        ],
        out_specs=last_part((CHUNK, 2 * HEADD)),
        scratch_shapes=[pltpu.VMEM((rows, HEADD), f32)] * 3 + [pltpu.VMEM((TOKB, HEADD), f32)] * 2,
        compiler_params=pltpu.CompilerParams(vmem_limit_bytes=VMEM_LIMIT),
        name="attend_backward",
    )(place, pay, sums, query, keys, values, probs)


ALL = ("hd", "kk", "ry", "rc")
SWAP = [(0, 1), (1, 0)]


def layer_norm(values, norm_gain, norm_shift):
    centre = values - jnp.mean(values, axis=-1, keepdims=True)
    spread = jnp.mean(centre * centre, axis=-1, keepdims=True)
    return centre * lax.rsqrt(spread + NORM_EPS) * norm_gain + norm_shift


def exact_gelu(values):
    return jax.nn.gelu(values, approximate=False)


def exchange(parts):
    return lax.all_to_all(parts, "hd", split_axis=0, concat_axis=0, tiled=True)


def spread_round(mine):
    if lax.axis_size("kk") > 1:
        mine = lax.all_gather(mine, "kk", axis=0, tiled=False)
    else:
        mine = mine[None]
    pair = jnp.stack([mine, lax.ppermute(mine, "ry", SWAP)])
    return jnp.stack([pair, lax.ppermute(pair, "rc", SWAP)])


def sum_round(parts):
    def folded(both, axis):
        got = lax.ppermute(both[1], axis, SWAP)
        return (both[0].astype(f32) + got.astype(f32)).astype(bf)

    total = folded(folded(parts, "rc"), "ry")
    if lax.axis_size("kk") > 1:
        return lax.psum_scatter(total, "kk", scatter_dimension=0, tiled=False)
    return total[0]


def reduce_rows(part):
    return lax.psum_scatter(part.astype(bf), ALL, scatter_dimension=0, tiled=True).astype(f32)


def per_device(
    first_half,
    second_half,
    qk_weight,
    value_weight,
    output_weight,
    inner_weight,
    outer_weight,
    attn_gain,
    attn_shift,
    ffn_gain,
    ffn_shift,
    buckets,
    slots,
    first_grad,
    second_grad,
):
    heads = lax.axis_size("hd")
    groups = lax.axis_size("kk")
    seq_count = heads * groups
    round_count = lax.axis_size("ry") * lax.axis_size("rc")
    own_rows, model_width = first_half.shape
    group_rows = own_rows * round_count
    slot_rows = 2 * group_rows
    tokens = group_rows * seq_count
    own_spans = min((tokens + (SPAN - 1) * heads) // SPAN, heads * slot_rows // SPAN)
    own_spans = -(-own_spans // UNROLL) * UNROLL

    vectors = jnp.stack([attn_gain, attn_shift, ffn_gain, ffn_shift], axis=1)
    vectors = jnp.pad(vectors, ((0, 0), (0, 124)))
    qkv_shard = jnp.concatenate([qk_weight, value_weight, vectors], axis=1)
    qkv_all = lax.all_gather(qkv_shard, ALL, axis=0, tiled=True)
    qkv_full = qkv_all[:, : 2 * model_width]
    vectors_full = qkv_all[:, 2 * model_width : 2 * model_width + 4].astype(f32).T
    output_full = lax.all_gather(output_weight, ALL, axis=0, tiled=True)
    inner_full = lax.all_gather(inner_weight, ALL, axis=0, tiled=True)
    outer_full = lax.all_gather(outer_weight, ALL, axis=0, tiled=True)

    index_rows = jnp.stack([slots[0], buckets[0]])
    index_all = exchange(jnp.broadcast_to(index_rows[None], (heads,) + index_rows.shape))
    if groups > 1:
        index_all = lax.all_gather(index_all, "kk", axis=1, tiled=False)
    else:
        index_all = index_all[:, None]
    index_all = index_all.reshape(heads, groups, 2, 2, 2, own_rows)
    index_all = jnp.where(lax.axis_index("ry") == 0, index_all, jnp.flip(index_all, 3))
    index_all = jnp.where(lax.axis_index("rc") == 0, index_all, jnp.flip(index_all, 4))
    index_all = jnp.transpose(index_all, (2, 4, 3, 1, 0, 5)).reshape(2, tokens)
    slot_row, bucket_row = index_all[0], index_all[1]
    target = slot_row // slot_rows
    local_place = slot_row - target * slot_rows
    onehot = (target[None, :] == jnp.arange(seq_count, dtype=jnp.int32)[:, None]).astype(jnp.int32)
    counts = jnp.sum(onehot, axis=1)
    first_block = lax.axis_index("kk") * heads
    block_ids = jnp.arange(seq_count, dtype=jnp.int32)
    is_own = (block_ids >= first_block) & (block_ids < first_block + heads)
    span_counts = jnp.where(is_own, -(-counts // SPAN), 0)
    shift = (1 + jnp.cumsum(span_counts) - span_counts) * SPAN
    last_start = jnp.maximum(counts - 1, 0) // SPAN * SPAN
    is_halo = block_ids == first_block - 1
    shift = jnp.where(is_halo, -last_start, shift)
    lowest = jnp.where(is_own, 0, jnp.where(is_halo, last_start, slot_rows))
    token_shift = jnp.sum(onehot * shift[:, None], axis=0)
    token_lowest = jnp.sum(onehot * lowest[:, None], axis=0)
    dump = (own_spans + 1) * SPAN
    place = jnp.where(local_place >= token_lowest, local_place + token_shift, dump)
    place_bucket = jnp.full((dump + SPAN,), -1, jnp.int32).at[place].set(bucket_row)
    span_bucket = place_bucket.reshape(-1, SPAN)[: own_spans + 1]
    key_bucket = jnp.concatenate([span_bucket[:-1], span_bucket[1:]], axis=1)
    query_bucket = span_bucket[1:]
    matching = (query_bucket[:, :, None] == key_bucket[:, None, :]) & (key_bucket[:, None, :] >= 0)
    itself = jnp.arange(2 * SPAN)[None, :] == jnp.arange(SPAN)[:, None] + SPAN
    others = matching & jnp.logical_not(itself[None])
    lonely = jnp.logical_not(jnp.any(others, axis=-1, keepdims=True))
    allowed = others | matching & itself[None] & lonely
    bias = jnp.where(allowed, 0.0, MASKED).astype(f32).reshape(own_spans * SPAN, 2 * SPAN)

    first_in = first_half.astype(f32)
    second_in = second_half.astype(f32)
    normed, attn_norm_pull = jax.vjp(layer_norm, second_in, vectors_full[0], vectors_full[1])
    normed_low = normed.astype(bf)
    qkv_own = product(normed_low, qkv_full).astype(bf)
    head_rows = jnp.transpose(qkv_own.reshape(own_rows, 2, heads, HEADD), (2, 0, 1, 3))
    qkv_group = spread_round(exchange(head_rows.reshape(heads, own_rows, 2 * HEADD)))
    payload, sorted_q, sorted_k, sorted_v, probs, token_sums = attend_forward(
        place, qkv_group.reshape(tokens, 2 * HEADD), bias, own_rows
    )
    packed_rows = own_rows + PAD
    packed = (2, 2, groups, heads, packed_rows, HEADD)
    mixed_parts = exchange(sum_round(payload.reshape(packed)))
    blocks = own_rows // TOKB
    weight_sum = mixed_parts[:, own_rows : own_rows + blocks].reshape(heads, own_rows)
    mixed_heads = mixed_parts[:, :own_rows].astype(f32) / weight_sum.astype(f32)[..., None]
    mixed_low = jnp.transpose(mixed_heads, (1, 0, 2)).reshape(own_rows, model_width).astype(bf)

    first_sum = first_in + product(mixed_low, output_full)
    ffn_normed, ffn_norm_pull = jax.vjp(layer_norm, first_sum, vectors_full[2], vectors_full[3])
    ffn_low = ffn_normed.astype(bf)
    inner_act = product(ffn_low, inner_full)
    hidden, gelu_pull = jax.vjp(exact_gelu, inner_act)
    hidden_low = hidden.astype(bf)
    second_sum = second_in + product(hidden_low, outer_full)
    outer_part = against(hidden_low, second_grad)
    (inner_back,) = gelu_pull(through(second_grad, outer_full))
    inner_back_low = inner_back.astype(bf)
    inner_part = against(ffn_low, inner_back_low)
    first_from_ffn, ffn_gain_part, ffn_shift_part = ffn_norm_pull(
        through(inner_back_low, inner_full)
    )
    first_carry = first_grad.astype(f32) + first_from_ffn
    carry_low = first_carry.astype(bf)
    output_part = against(mixed_low, carry_low)
    mixed_back = through(carry_low, output_full).reshape(own_rows, heads, HEADD)
    mixed_back = jnp.transpose(mixed_back, (1, 0, 2))
    mixed_dot = jnp.sum(mixed_back * mixed_heads, axis=-1).astype(bf)
    tails = jnp.concatenate(
        [
            mixed_dot.reshape(heads, blocks, TOKB),
            weight_sum.reshape(heads, blocks, TOKB),
            jnp.zeros((heads, PAD - 2 * blocks, TOKB), bf),
        ],
        axis=1,
    )
    back_parts = jnp.concatenate([mixed_back.astype(bf), tails], axis=1)
    back_group = spread_round(exchange(back_parts)).reshape(-1, HEADD)
    query_value_back = attend_backward(
        place, back_group, token_sums, sorted_q, sorted_k, sorted_v, probs, own_rows
    )
    back_shape = (2, 2, groups, heads, own_rows, 2 * HEADD)
    own_back = exchange(sum_round(query_value_back.reshape(back_shape)))
    own_back = jnp.transpose(own_back.reshape(heads, own_rows, 2, HEADD), (1, 2, 0, 3))
    own_back = own_back.reshape(own_rows, 2 * model_width)
    qkv_part = against(normed_low, own_back)
    normed_back = through(own_back, qkv_full)
    second_from_attn, attn_gain_part, attn_shift_part = attn_norm_pull(normed_back)
    second_carry = second_grad.astype(f32) + second_from_attn

    inner_grad = reduce_rows(inner_part)
    outer_grad = reduce_rows(outer_part)
    output_grad = reduce_rows(output_part)
    qkv_grad = reduce_rows(qkv_part)
    vector_parts = jnp.stack([attn_gain_part, attn_shift_part, ffn_gain_part, ffn_shift_part])
    device_count = seq_count * round_count
    vector_parts = jnp.transpose(vector_parts.reshape(4, device_count, -1), (1, 0, 2))
    vector_rows = lax.all_to_all(
        vector_parts.reshape(device_count, -1), ALL, split_axis=0, concat_axis=0, tiled=True
    )
    vector_grads = jnp.sum(vector_rows, axis=0).reshape(4, -1)
    return (
        first_sum.astype(bf),
        second_sum.astype(bf),
        carry_low,
        second_carry.astype(bf),
        qkv_grad[:, :model_width],
        qkv_grad[:, model_width:],
        output_grad,
        inner_grad,
        outer_grad,
        vector_grads[0],
        vector_grads[1],
        vector_grads[2],
        vector_grads[3],
    )


def solution(mesh):
    seq_count, round_count = mesh.devices.shape
    shape = (HEADS, seq_count // HEADS, round_count // 2, 2)
    split_mesh = Mesh(mesh.devices.reshape(shape), ALL)
    rows = P(ALL, None)
    vector = P(ALL)
    table = P(("ry", "rc"), ("hd", "kk"))
    in_specs = (rows,) * 7 + (vector,) * 4 + (table,) * 2 + (rows,) * 2
    out_specs = (rows,) * 9 + (vector,) * 4
    return jax.shard_map(
        per_device, mesh=split_mesh, in_specs=in_specs, out_specs=out_specs, check_vma=False
    )
```

time: 2540 us -> 1020 us (0.40)
  waiting for transfers between devices: 1190 us -> 669 us
  local copies, waits for them, and re-layouts: 421 us -> 58.7 us
  blocking collectives: 327 us -> 52.8 us
  matrix products: 295 us -> 62.7 us
  other arithmetic: 197 us -> 49.8 us
  Pallas kernels: 0 us -> 75.5 us
  starting transfers between devices: 81.3 us -> 25.4 us
    all_to_all x12 -> x4, waiting for transfers between devices: 373 us -> 54.6 us  [the longest x3 48.8 us: exchange(): return lax.all_to_all(parts, 'hd', split_axis=0, concat_axis=0, tiled=True)]
    reduce_scatter x7 -> x4, waiting for transfers between devices: 734 us -> 452 us  [reduce_rows(): lax.psum_scatter(part.astype(bf), ALL, scatter_dimension=0, tiled=True)]
    dot_general x19 -> x4, matrix products: 244 us -> 20.3 us  [product(): return jnp.dot(left_side, right_side, preferred_element_type=f32)]
    gather x21 -> x0, local copies, waits for them, and re-layouts: 195 us -> none  [the longest x1 14.1 us: per_device(): value_back_low[back_index]]
    all_to_all x2, blocking collectives: 245 us -> 52.8 us  [exchange(): return lax.all_to_all(parts, 'hd', split_axis=0, concat_axis=0, tiled=True)]
    unnamed x196 -> x30, local copies, waits for them, and re-layouts: 105 us -> 3.01 us
    unnamed x2 -> x0, blocking collectives: 82.3 us -> none
    ppermute x5 -> x8, waiting for transfers between devices: 8.69 us -> 85.1 us  [the longest x4 44.7 us: folded(): got = lax.ppermute(both[1], axis, SWAP)]
  transfers between devices with their start and end apart: 31 -> 20, of which waited for: 18 -> 15; matrix products, arithmetic and copies ran while one was open for 19% -> 13% of each run, Pallas kernels for 0% -> 3%
where the time goes in v1:
time: 1020 us; the launch traced here: 1010 us
  waiting for transfers between devices  669 us (66%)
  Pallas kernels  75.5 us (7%)
  matrix products  62.7 us (6%)
  local copies, waits for them, and re-layouts  58.7 us (6%)
  blocking collectives  52.8 us (5%)
  other arithmetic  49.8 us (5%)
  starting transfers between devices  25.4 us (2%)
  between operations  15.1 us (1%)
    reduce_scatter x4, waiting for transfers between devices, reduce_rows(): lax.psum_scatter(part.astype(bf), ALL, scatter_dimension=0, tiled=True)  452 us
    all_gather x1, waiting for transfers between devices, per_device(): qkv_all = lax.all_gather(qkv_shard, ALL, axis=0, tiled=True)  54.3 us
    all_to_all x2, blocking collectives, exchange(): return lax.all_to_all(parts, 'hd', split_axis=0, concat_axis=0, tiled=True)  52.8 us
    all_to_all x3, waiting for transfers between devices, exchange(): return lax.all_to_all(parts, 'hd', split_axis=0, concat_axis=0, tiled=True)  48.8 us
    ppermute x4, waiting for transfers between devices, folded(): got = lax.ppermute(both[1], axis, SWAP)  44.7 us
    pallas_call x1, Pallas kernels, attend_backward(): pl.pallas_call(functools.partial(backward_kernel, own_rows, steps), grid=...  40.6 us
    ppermute x2, waiting for transfers between devices, spread_round(): pair = jnp.stack([mine, lax.ppermute(mine, 'ry', SWAP)])  37.6 us
    pallas_call x1, Pallas kernels, attend_forward(): pl.pallas_call(functools.partial(forward_kernel, own_rows, steps), grid=(...  34.9 us
  transfers between devices with their start and end apart: 20, of which 15 were waited for; matrix products, arithmetic and copies ran while one was open for 13% of the time, Pallas kernels for 3%

profile of v1, /device:TPU:0, one launch (start us, length us, event | category | flops | bytes accessed | tf_op | source)
XLA Modules:
  0.0 1008.8 jit_solution(15377982518851167263)
XLA Ops:
  13.1 7.3 all-to-all-start
  22.9 54.3 %all-gather.5.cloned.1.call-done = bf16[1024,2176]{1,0:T(8,128)(2,1)} async-done(((bf16[32,2176]{1,0:T(8,128)(2,1)}), bf16[1024,2176]{1,0:T(8,128)(2,1)}) %all-gather.5.cloned.1.call-update) | async-done | bytes 4456464 | tf_op jit(solution)/shard_map/all_gather | solution.py:475
  79.3 3.6 fusion.23
  85.4 3.8 all-to-all-start.1
  89.8 28.1 %all-to-all-done.1 = bf16[8,256,256]{2,1,0:T(8,128)(2,1)S(1)} async-done(((bf16[8,256,256]{2,1,0:T(8,128)(2,1)}), bf16[8,256,256]{2,1,0:T(8,128)(2,1)S(1)}, u32[]{:S(2)}, u32[]{:S(2)}) %all-to-all-start.1) | async-done | bytes 1048608 | tf_op jit(solution)/shard_map/all_to_all | solution.py:417
  120.1 25.5 %collective-permute-done = bf16[1,8,256,256]{3,2,1,0:T(8,128)(2,1)S(1)} collective-permute-done((bf16[1,8,256,256]{3,2,1,0:T(8,128)(2,1)S(1)}, bf16[1,8,256,256]{3,2,1,0:T(8,128)(2,1)S(1)}, u32[]{:S(2)}, u32[]{:S(2)}) %collective-permute-start) | collective-permute-done | bytes 1048608 | tf_op jit(solution)/shard_map/ppermute | solution.py:425
  146.6 3.2 fusion.55
  150.0 30.5 %scatter_custom_fusion = s32[8832]{0:T(1024)S(1)} fusion(s32[8192]{0:T(1024)S(1)} %bitcast.177, s32[8192]{0:T(1024)S(1)} %bitcast.176, s32[]{:T(128)} %constant.57.clone.1), kind=kCustom, calls=%fused_computation.114 | custom fusion | bytes 35332 | tf_op jit(solution)/shard_map/scatter | solution.py:510
  180.8 4.4 and_reduce_fusion
  185.3 7.7 fusion.3.bias_ref
  193.6 4.4 pad_maximum_fusion
  197.9 34.9 %attend_forward.1 = (bf16[8704,128]{1,0:T(8,128)(2,1)}, bf16[8832,128]{1,0:T(8,128)(2,1)}, bf16[8832,128]{1,0:T(8,128)(2,1)}, bf16[8832,128]{1,0:T(8,128)(2,1)},...) custom-call(s32[8192]{0:T(1024)} %add_select_fusion.1.place_ref, bf16[8192,256]{1,0:T(8,128)(2,1)} %bitcast.148, ...), custom_call_target="tpu_custom_call" | custom-call | tf_op jit(solution)/shard_map/attend_forward/pallas_call | solution.py:197
  232.8 1.8 fusion.60
  235.4 2.4 collective-permute-done.2
  238.2 1.8 collective-permute-start.3
  240.0 13.2 %collective-permute-done.3 = bf16[1,8,272,128]{3,2,1,0:T(8,128)(2,1)S(1)} collective-permute-done((bf16[1,8,272,128]{3,2,1,0:T(8,128)(2,1)S(1)}, bf16[1,8,272,128]{3,2,1,0:T(8,128)(2,1)S(1)}, u32[]{:S(2)}, u32[]{:S(2)}) %collective-permute-start.3) | collective-permute-done | bytes 557088 | tf_op jit(solution)/shard_map/ppermute | solution.py:431
  254.2 4.1 all-to-all-start.2
  258.5 20.7 %all-to-all-done.2 = bf16[8,272,128]{2,1,0:T(8,128)(2,1)S(1)} async-done(((bf16[8,272,128]{2,1,0:T(8,128)(2,1)}), bf16[8,272,128]{2,1,0:T(8,128)(2,1)S(1)}, u32[]{:S(2)}, u32[]{:S(2)}) %all-to-all-start.2) | async-done | bytes 557088 | tf_op jit(solution)/shard_map/all_to_all | solution.py:417
  279.9 2.4 fusion.65
  282.6 7.8 fusion.54
  290.4 21.1 %all-gather.11.cloned.1.call-done = bf16[4096,1024]{1,0:T(8,128)(2,1)} async-done(((bf16[128,1024]{1,0:T(8,128)(2,1)}), bf16[4096,1024]{1,0:T(8,128)(2,1)}) %all-gather.11.cloned.1.call-update) | async-done | bytes 8388624 | tf_op jit(solution)/shard_map/all_gather | solution.py:480
  311.5 15.7 %add_convert_fusion.1 = (bf16[256,4096]{1,0:T(8,128)(2,1)S(1)}, f32[256,4096]{1,0:T(8,128)}) fusion(f32[256,4096]{1,0:T(8,128)} %fusion.54, bf16[256,1024]{1,0:T(8,128)(2,1)S(1)} %copy-done.5, bf16[4096,1024]{1,0:T(8,128)(2,1)} %all-gather.11.cloned.1.call-done), kind=kOutput, calls=%fused_computation.15 | convolution fusion | flops 2222981120 | bytes 19398656 | tf_op jit(solution)/shard_map/dot_general | solution.py:38
  327.3 2.7 multiply_reduce_fusion
  333.5 2.2 maximum_maximum_fusion
  335.7 2.2 copy.123
  337.9 20.6 %all_to_all.34 = bf16[8,272,128]{2,1,0:T(8,128)(2,1)S(1)} all-to-all(bf16[8,272,128]{2,1,0:T(8,128)(2,1)} %copy.123), channel_id=1, replica_groups=mesh['hd'=8,'kk'=1,'ry'=2,'rc'=2] {'hd'}, dimensions={0} | all-to-all | bytes 1114112 | tf_op jit(solution)/shard_map/all_to_all | solution.py:417
  359.7 12.1 %collective-permute-done.4 = bf16[1,8,272,128]{3,2,1,0:T(8,128)(2,1)S(1)} collective-permute-done((bf16[1,8,272,128]{3,2,1,0:T(8,128)(2,1)S(1)}, bf16[1,8,272,128]{3,2,1,0:T(8,128)(2,1)S(1)}, u32[]{:S(2)}, u32[]{:S(2)}) %collective-permute-start.4) | collective-permute-done | bytes 557088 | tf_op jit(solution)/shard_map/ppermute | solution.py:425
  372.1 2.7 collective-permute-done.5
  376.4 40.6 %attend_backward.1 = bf16[8192,256]{1,0:T(8,128)(2,1)} custom-call(s32[8192]{0:T(1024)} %add_select_fusion.1.place_ref, bf16[8704,128]{1,0:T(8,128)(2,1)} %bitcast.149, f32[64,128]{1,0:T(8,128)} %get-tuple-element.20.sum_ref, bf16[8832,128]{1,0:T(8,128)(2,1)} %get-tuple-element.21.query_ref, bf16[8832,128]{1,0:T(8,128)(2,1)} %get-tuple-element.22.key_ref, ...), custom_call_target="tpu_custom_call" | custom-call | tf_op jit(solution)/shard_map/attend_backward/pallas_call | solution.py:382
  417.0 4.4 fusion.59
  421.4 4.0 copy.124
  425.5 2.1 convolution_convert_fusion.3
  427.7 4.1 copy.125
  431.8 3.5 add_convert_fusion
  436.9 29.2 %collective-permute-done.7 = bf16[1,8,256,256]{2,3,1,0:T(8,128)(2,1)S(1)} collective-permute-done((bf16[1,8,256,256]{2,3,1,0:T(8,128)(2,1)S(1)}, bf16[1,8,256,256]{2,3,1,0:T(8,128)(2,1)S(1)}, u32[]{:S(2)}, u32[]{:S(2)}) %collective-permute-start.7) | collective-permute-done | bytes 1048608 | tf_op jit(solution)/shard_map/ppermute | solution.py:431
  466.3 32.2 %all_to_all.35 = bf16[8,256,256]{1,2,0:T(8,128)(2,1)S(1)} all-to-all(bf16[8,256,256]{1,2,0:T(8,128)(2,1)S(1)} %fusion.35), channel_id=1, replica_groups=mesh['hd'=8,'kk'=1,'ry'=2,'rc'=2] {'hd'}, dimensions={0} | all-to-all | bytes 2097152 | tf_op jit(solution)/shard_map/all_to_all | solution.py:417
  499.6 3.6 convolution_convert_fusion.2
  503.2 7.3 convolution_convert_fusion.1
  510.9 4.2 multiply_convert_fusion
  515.2 5.6 convolution_convert_fusion
  521.0 6.5 fusion.26
  527.5 37.9 %reduce-scatter.7.cloned.1.call-done = bf16[32,1024]{1,0:T(8,128)(2,1)} async-done(((bf16[1024,1024]{1,0:T(8,128)(2,1)}), bf16[32,1024]{1,0:T(8,128)(2,1)}) %reduce-scatter.7.cloned.1.call-update) | async-done | bytes 65552 | tf_op jit(solution)/shard_map/reduce_scatter | solution.py:441
  566.9 3.9 fusion.34
  572.4 2.5 all-to-all-start.5
  576.2 5.8 all-to-all-done.5
  582.7 122.5 %reduce-scatter.5.cloned.1.call-done = bf16[32,2048]{1,0:T(8,128)(2,1)} async-done(((bf16[1024,2048]{1,0:T(8,128)(2,1)}), bf16[32,2048]{1,0:T(8,128)(2,1)}) %reduce-scatter.5.cloned.1.call-update) | async-done | bytes 131088 | tf_op jit(solution)/shard_map/reduce_scatter | solution.py:441
  706.8 145.7 %reduce-scatter.9.cloned.1.call-done = bf16[32,4096]{1,0:T(8,128)(2,1)} async-done(((bf16[1024,4096]{1,0:T(8,128)(2,1)}), bf16[32,4096]{1,0:T(8,128)(2,1)}) %reduce-scatter.9.cloned.1.call-update) | async-done | bytes 262160 | tf_op jit(solution)/shard_map/reduce_scatter | solution.py:441
  854.3 145.5 %reduce-scatter.11.cloned.1.call-done = bf16[128,1024]{1,0:T(8,128)(2,1)} async-done(((bf16[4096,1024]{1,0:T(8,128)(2,1)}), bf16[128,1024]{1,0:T(8,128)(2,1)}) %reduce-scatter.11.cloned.1.call-update) | async-done | bytes 262160 | tf_op jit(solution)/shard_map/reduce_scatter | solution.py:441
  (135 shorter events, 41.5 us)
Async XLA Ops:
  7.2 72.1 %copy-start = (bf16[256,1024]{1,0:T(8,128)(2,1)S(1)}, bf16[256,1024]{1,0:T(8,128)(2,1)}, u32[]{:S(2)}) copy-start(bf16[256,1024]{1,0:T(8,128)(2,1)} %param.16) | copy-start | bytes 1572868
  7.2 70.0 %all-gather.5.cloned.1.call-start = ((), (), s32[]{:S(2)}) async-start(), calls=%async_computation.10 | async-start | bytes 4595712 | tf_op jit(solution)/shard_map/all_gather | solution.py:475
  9.7 270.2 %all-gather.7.cloned.1.call-start = ((), (), s32[]{:S(2)}) async-start(), calls=%async_computation.11 | async-start | bytes 2162688 | tf_op jit(solution)/shard_map/all_gather | solution.py:478
  10.4 272.1 %all-gather.9.cloned.1.call-start = ((), (), s32[]{:S(2)}) async-start(), calls=%async_computation.12 | async-start | bytes 8650752 | tf_op jit(solution)/shard_map/all_gather | solution.py:479
  11.2 300.4 %all-gather.11.cloned.1.call-start = ((), (), s32[]{:S(2)}) async-start(), calls=%async_computation.13 | async-start | bytes 8650752 | tf_op jit(solution)/shard_map/all_gather | solution.py:480
  13.1 72.3 %all-to-all-start = ((s32[8,2,1024]{2,1,0:T(2,128)}), s32[8,2,1024]{2,1,0:T(2,128)S(1)}, u32[]{:S(2)}, u32[]{:S(2)}) async-start(s32[8,2,1024]{2,1,0:T(2,128)} %broadcast_in_dim.39), calls=%async_computation | async-start | bytes 131072 | tf_op jit(solution)/shard_map/all_to_all | solution.py:417
  85.4 32.5 %all-to-all-start.1 = ((bf16[8,256,256]{2,1,0:T(8,128)(2,1)}), bf16[8,256,256]{2,1,0:T(8,128)(2,1)S(1)}, u32[]{:S(2)}, u32[]{:S(2)}) async-start(bf16[8,256,256]{2,1,0:T(8,128)(2,1)} %reshape.565), calls=%async_computation.1 | async-start | bytes 2097152 | tf_op jit(solution)/shard_map/all_to_all | solution.py:417
  117.9 27.7 %copy-start.3 = (bf16[8,256,256]{2,1,0:T(8,128)(2,1)}, bf16[8,256,256]{2,1,0:T(8,128)(2,1)S(1)}, u32[]{:S(2)}) copy-start(bf16[8,256,256]{2,1,0:T(8,128)(2,1)S(1)} %all-to-all-done.1) | copy-start | bytes 3145732
  117.9 27.7 %collective-permute-start = (bf16[1,8,256,256]{3,2,1,0:T(8,128)(2,1)S(1)}, bf16[1,8,256,256]{3,2,1,0:T(8,128)(2,1)S(1)}, u32[]{:S(2)}, u32[]{:S(2)}) collective-permute-start(bf16[1,8,256,256]{3,2,1,0:T(8,128)(2,1)S(1)} %bitcast.157), channel_id=1, source_target_pairs={{0,2},{2,0},{1,3},{3,1},{4,6},{6,4},{5,7},{7,5},{8,10},{10,8},{9,1... | collective-permute-start | bytes 3145736 | tf_op jit(solution)/shard_map/ppermute | solution.py:425
  145.6 1.0 copy-start.8
  149.8 43.8 %collective-permute-start.1 = (bf16[2,1,8,256,256]{4,3,2,0,1:T(8,128)(2,1)}, bf16[2,1,8,256,256]{4,3,2,0,1:T(8,128)(2,1)}, u32[]{:S(2)}, u32[]{:S(2)}) collective-permute-start(bf16[2,1,8,256,256]{4,3,2,0,1:T(8,128)(2,1)} %get-tuple-element.50), channel_id=1, source_target_pairs={{0,1},{1,0},{2,3},{3,2},{4,5},{5,4},{6,7},{7,6},{8,9},{9,8},{10,11... | collective-permute-start | bytes 6291464 | tf_op jit(solution)/shard_map/ppermute | solution.py:426
  234.6 3.1 collective-permute-start.2
  238.1 41.7 %copy-start.9 = (bf16[256,1024]{1,0:T(8,128)(2,1)S(1)}, bf16[256,1024]{1,0:T(8,128)(2,1)}, u32[]{:S(2)}) copy-start(bf16[256,1024]{1,0:T(8,128)(2,1)} %param.15) | copy-start | bytes 1572868
  238.2 15.0 %collective-permute-start.3 = (bf16[1,8,272,128]{3,2,1,0:T(8,128)(2,1)S(1)}, bf16[1,8,272,128]{3,2,1,0:T(8,128)(2,1)S(1)}, u32[]{:S(2)}, u32[]{:S(2)}) collective-permute-start(bf16[1,8,272,128]{3,2,1,0:T(8,128)(2,1)S(1)} %slice_bitcast_fusion.2), channel_id=1, source_target_pairs={{0,2},{2,0},{1,3},{3,1},{4,6},{6,4},{5,7},{7,5},{8,10},{10,8},{9,1... | collective-permute-start | bytes 1671176 | tf_op jit(solution)/shard_map/ppermute | solution.py:431
  254.2 25.1 %all-to-all-start.2 = ((bf16[8,272,128]{2,1,0:T(8,128)(2,1)}), bf16[8,272,128]{2,1,0:T(8,128)(2,1)S(1)}, u32[]{:S(2)}, u32[]{:S(2)}) async-start(bf16[8,272,128]{2,1,0:T(8,128)(2,1)} %fusion.37), calls=%async_computation.2 | async-start | bytes 1114112 | tf_op jit(solution)/shard_map/all_to_all | solution.py:417
  258.2 307.2 %reduce-scatter.7.cloned.1.call-start = ((), (), s32[]{:S(2)}) async-start(), calls=%async_computation.15 | async-start | bytes 2162688 | tf_op jit(solution)/shard_map/reduce_scatter | solution.py:441
  282.6 29.0 %copy-start.5 = (bf16[256,1024]{1,0:T(8,128)(2,1)S(1)}, bf16[256,1024]{1,0:T(8,128)(2,1)}, u32[]{:S(2)}) copy-start(bf16[256,1024]{1,0:T(8,128)(2,1)} %param.29) | copy-start | bytes 1572868
  311.5 15.7 %copy-start.11 = (bf16[1024,4096]{1,0:T(8,128)(2,1)S(1)}, bf16[1024,4096]{1,0:T(8,128)(2,1)}, u32[]{:S(2)}) copy-start(bf16[1024,4096]{1,0:T(8,128)(2,1)} %all-gather.9.cloned.1.call-done) | copy-start | bytes 25165828
  327.2 2.7 copy-start.7
  327.3 3.9 copy-start.10
  329.9 1.8 copy-start.1
  331.7 93.8 %copy-start.2 = (bf16[256,1024]{1,0:T(8,128)(2,1)}, bf16[256,1024]{1,0:T(8,128)(2,1)S(1)}, u32[]{:S(2)}) copy-start(bf16[256,1024]{1,0:T(8,128)(2,1)S(1)} %add_convert_fusion.3) | copy-start | bytes 1572868
  358.5 13.3 %collective-permute-start.4 = (bf16[1,8,272,128]{3,2,1,0:T(8,128)(2,1)S(1)}, bf16[1,8,272,128]{3,2,1,0:T(8,128)(2,1)S(1)}, u32[]{:S(2)}, u32[]{:S(2)}) collective-permute-start(bf16[1,8,272,128]{3,2,1,0:T(8,128)(2,1)S(1)} %bitcast.161), channel_id=1, source_target_pairs={{0,2},{2,0},{1,3},{3,1},{4,6},{6,4},{5,7},{7,5},{8,10},{10,8},{9,1... | collective-permute-start | bytes 1671176 | tf_op jit(solution)/shard_map/ppermute | solution.py:425
  372.0 2.8 collective-permute-start.5
  425.4 6.4 collective-permute-start.6
  427.6 277.6 %reduce-scatter.5.cloned.1.call-start = ((), (), s32[]{:S(2)}) async-start(), calls=%async_computation.14 | async-start | bytes 4325376 | tf_op jit(solution)/shard_map/reduce_scatter | solution.py:441
  435.3 30.7 %collective-permute-start.7 = (bf16[1,8,256,256]{2,3,1,0:T(8,128)(2,1)S(1)}, bf16[1,8,256,256]{2,3,1,0:T(8,128)(2,1)S(1)}, u32[]{:S(2)}, u32[]{:S(2)}) collective-permute-start(bf16[1,8,256,256]{2,3,1,0:T(8,128)(2,1)S(1)} %slice_bitcast_fusion), channel_id=1, source_target_pairs={{0,2},{2,0},{1,3},{3,1},{4,6},{6,4},{5,7},{7,5},{8,10},{10,8},{9,1... | collective-permute-start | bytes 3145736 | tf_op jit(solution)/shard_map/ppermute | solution.py:431
  498.6 1.0 copy-start.4
  503.2 349.3 %reduce-scatter.9.cloned.1.call-start = ((), (), s32[]{:S(2)}) async-start(), calls=%async_computation.16 | async-start | bytes 8650752 | tf_op jit(solution)/shard_map/reduce_scatter | solution.py:441
  510.6 489.1 %reduce-scatter.11.cloned.1.call-start = ((), (), s32[]{:S(2)}) async-start(), calls=%async_computation.17 | async-start | bytes 8650752 | tf_op jit(solution)/shard_map/reduce_scatter | solution.py:441
  510.9 4.3 copy-start.6
  572.4 9.6 all-to-all-start.5
Sparse Core Ops, SparseCore 0:
  11.4 65.7 all-gather.4
  80.1 65.0 all-gather.6
  148.0 76.3 all-gather.8
  227.2 84.3 all-gather.10
  427.7 137.6 reduce-scatter.6
  567.6 137.5 reduce-scatter.4
  707.6 144.8 reduce-scatter.8
  854.9 144.8 reduce-scatter.10

commit v2 on v1

--- a/solution.py
+++ b/solution.py
@@ -1,5 +1,4 @@
 import functools
-import math
 
 import jax
 import jax.numpy as jnp
@@ -400,6 +399,8 @@
 
 
 ALL = ("hd", "kk", "ry", "rc")
+SEQ = ("hd", "kk")
+ROUND = ("ry", "rc")
 SWAP = [(0, 1), (1, 0)]
 
 
@@ -413,72 +414,57 @@
     return jax.nn.gelu(values, approximate=False)
 
 
-def exchange(parts):
-    return lax.all_to_all(parts, "hd", split_axis=0, concat_axis=0, tiled=True)
+def exchange(parts, axes="hd"):
+    return lax.all_to_all(parts, axes, split_axis=0, concat_axis=0, tiled=True)
+
+
+def swapped(value, axis):
+    return lax.ppermute(value, axis, SWAP)
+
+
+def spread_pair(mine):
+    pair = jnp.stack([mine, swapped(mine, "ry")])
+    return jnp.stack([pair, swapped(pair, "rc")])
+
+
+def sum_pair(parts):
+    def folded(both, axis):
+        got = swapped(both[1], axis)
+        return (both[0].astype(f32) + got.astype(f32)).astype(bf)
+
+    return folded(folded(parts, "rc"), "ry")
 
 
 def spread_round(mine):
     if lax.axis_size("kk") > 1:
         mine = lax.all_gather(mine, "kk", axis=0, tiled=False)
-    else:
-        mine = mine[None]
-    pair = jnp.stack([mine, lax.ppermute(mine, "ry", SWAP)])
-    return jnp.stack([pair, lax.ppermute(pair, "rc", SWAP)])
+    return spread_pair(mine)
 
 
 def sum_round(parts):
-    def folded(both, axis):
-        got = lax.ppermute(both[1], axis, SWAP)
-        return (both[0].astype(f32) + got.astype(f32)).astype(bf)
-
-    total = folded(folded(parts, "rc"), "ry")
+    total = sum_pair(parts)
     if lax.axis_size("kk") > 1:
         return lax.psum_scatter(total, "kk", scatter_dimension=0, tiled=False)
     return total[0]
 
 
-def reduce_rows(part):
-    return lax.psum_scatter(part.astype(bf), ALL, scatter_dimension=0, tiled=True).astype(f32)
-
-
-def per_device(
-    first_half,
-    second_half,
-    qk_weight,
-    value_weight,
-    output_weight,
-    inner_weight,
-    outer_weight,
-    attn_gain,
-    attn_shift,
-    ffn_gain,
-    ffn_shift,
-    buckets,
-    slots,
-    first_grad,
-    second_grad,
-):
+def ordered(mine, axis, dim):
+    got = swapped(mine, axis)
+    is_first = lax.axis_index(axis) == 0
+    return jnp.stack([jnp.where(is_first, mine, got), jnp.where(is_first, got, mine)], axis=dim)
+
+
+def scattered(parts, axis, dim):
+    me = lax.axis_index(axis)
+    keep = lax.dynamic_index_in_dim(parts, me, dim, keepdims=False)
+    give = lax.dynamic_index_in_dim(parts, 1 - me, dim, keepdims=False)
+    return (keep.astype(f32) + swapped(give, axis).astype(f32)).astype(bf)
+
+
+def sorted_places(slots, buckets, own_rows, slot_rows, own_spans):
     heads = lax.axis_size("hd")
     groups = lax.axis_size("kk")
     seq_count = heads * groups
-    round_count = lax.axis_size("ry") * lax.axis_size("rc")
-    own_rows, model_width = first_half.shape
-    group_rows = own_rows * round_count
-    slot_rows = 2 * group_rows
-    tokens = group_rows * seq_count
-    own_spans = min((tokens + (SPAN - 1) * heads) // SPAN, heads * slot_rows // SPAN)
-    own_spans = -(-own_spans // UNROLL) * UNROLL
-
-    vectors = jnp.stack([attn_gain, attn_shift, ffn_gain, ffn_shift], axis=1)
-    vectors = jnp.pad(vectors, ((0, 0), (0, 124)))
-    qkv_shard = jnp.concatenate([qk_weight, value_weight, vectors], axis=1)
-    qkv_all = lax.all_gather(qkv_shard, ALL, axis=0, tiled=True)
-    qkv_full = qkv_all[:, : 2 * model_width]
-    vectors_full = qkv_all[:, 2 * model_width : 2 * model_width + 4].astype(f32).T
-    output_full = lax.all_gather(output_weight, ALL, axis=0, tiled=True)
-    inner_full = lax.all_gather(inner_weight, ALL, axis=0, tiled=True)
-    outer_full = lax.all_gather(outer_weight, ALL, axis=0, tiled=True)
-
     index_rows = jnp.stack([slots[0], buckets[0]])
     index_all = exchange(jnp.broadcast_to(index_rows[None], (heads,) + index_rows.shape))
     if groups > 1:
@@ -488,7 +474,7 @@
     index_all = index_all.reshape(heads, groups, 2, 2, 2, own_rows)
     index_all = jnp.where(lax.axis_index("ry") == 0, index_all, jnp.flip(index_all, 3))
     index_all = jnp.where(lax.axis_index("rc") == 0, index_all, jnp.flip(index_all, 4))
-    index_all = jnp.transpose(index_all, (2, 4, 3, 1, 0, 5)).reshape(2, tokens)
+    index_all = jnp.transpose(index_all, (2, 4, 3, 1, 0, 5)).reshape(2, -1)
     slot_row, bucket_row = index_all[0], index_all[1]
     target = slot_row // slot_rows
     local_place = slot_row - target * slot_rows
@@ -517,11 +503,72 @@
     lonely = jnp.logical_not(jnp.any(others, axis=-1, keepdims=True))
     allowed = others | matching & itself[None] & lonely
     bias = jnp.where(allowed, 0.0, MASKED).astype(f32).reshape(own_spans * SPAN, 2 * SPAN)
+    return place, bias
+
+
+def per_device(
+    first_half,
+    second_half,
+    qk_weight,
+    value_weight,
+    output_weight,
+    inner_weight,
+    outer_weight,
+    attn_gain,
+    attn_shift,
+    ffn_gain,
+    ffn_shift,
+    buckets,
+    slots,
+    first_grad,
+    second_grad,
+):
+    heads = lax.axis_size("hd")
+    groups = lax.axis_size("kk")
+    seq_count = heads * groups
+    round_count = lax.axis_size("ry") * lax.axis_size("rc")
+    device_count = seq_count * round_count
+    own_rows, model_width = first_half.shape
+    weight_rows, hidden_width = inner_weight.shape
+    group_rows = own_rows * round_count
+    slot_rows = 2 * group_rows
+    tokens = group_rows * seq_count
+    own_spans = min((tokens + (SPAN - 1) * heads) // SPAN, heads * slot_rows // SPAN)
+    own_spans = -(-own_spans // UNROLL) * UNROLL
+    piece = hidden_width // device_count
+    blocks = own_rows // TOKB
+
+    vectors = jnp.stack([attn_gain, attn_shift, ffn_gain, ffn_shift], axis=1)
+    vectors = jnp.pad(vectors, ((0, 0), (0, 124)))
+    qkv_shard = jnp.concatenate([qk_weight, value_weight, vectors], axis=1)
+    qkv_all = lax.all_gather(qkv_shard, ALL, axis=0, tiled=True)
+    qkv_full = qkv_all[:, : 2 * model_width]
+    vectors_full = qkv_all[:, 2 * model_width : 2 * model_width + 4].astype(f32).T
+
+    place, bias = sorted_places(slots, buckets, own_rows, slot_rows, own_spans)
+
+    inner_split = inner_weight.reshape(weight_rows, seq_count, round_count, piece)
+    inner_split = jnp.transpose(inner_split, (2, 0, 1, 3)).reshape(round_count, weight_rows, -1)
+    inner_rows = exchange(inner_split, ROUND).reshape(round_count * weight_rows, -1)
+    grad_group = spread_pair(second_grad).reshape(group_rows, model_width)
 
     first_in = first_half.astype(f32)
     second_in = second_half.astype(f32)
     normed, attn_norm_pull = jax.vjp(layer_norm, second_in, vectors_full[0], vectors_full[1])
     normed_low = normed.astype(bf)
+    normed_low, bias, place = lax.optimization_barrier((normed_low, bias, place))
+    shard = jnp.concatenate([inner_rows, outer_weight, output_weight, normed_low], axis=0)
+    shards = lax.all_gather(shard, SEQ, axis=0, tiled=False)
+    cuts = [inner_rows.shape[0], outer_weight.shape[0], weight_rows]
+    ends = [cuts[0], cuts[0] + cuts[1], sum(cuts)]
+    inner_part_weight = shards[:, : ends[0]].reshape(model_width, -1)
+    outer_part_weight = shards[:, ends[0] : ends[1]].reshape(-1, model_width)
+    output_full = ordered(ordered(shards[:, ends[1] : ends[2]], "ry", 1), "rc", 2)
+    output_full = output_full.reshape(model_width, model_width)
+    normed_seq = shards[:, ends[2] :].reshape(heads, groups, own_rows, model_width)
+    normed_seq = lax.dynamic_index_in_dim(normed_seq, lax.axis_index("kk"), 1, keepdims=False)
+    normed_seq = normed_seq.reshape(heads * own_rows, model_width)
+
     qkv_own = product(normed_low, qkv_full).astype(bf)
     head_rows = jnp.transpose(qkv_own.reshape(own_rows, 2, heads, HEADD), (2, 0, 1, 3))
     qkv_group = spread_round(exchange(head_rows.reshape(heads, own_rows, 2 * HEADD)))
@@ -531,28 +578,31 @@
     packed_rows = own_rows + PAD
     packed = (2, 2, groups, heads, packed_rows, HEADD)
     mixed_parts = exchange(sum_round(payload.reshape(packed)))
-    blocks = own_rows // TOKB
+    d_hidden = through(grad_group, outer_part_weight)
+    mixed_parts, d_hidden = lax.optimization_barrier((mixed_parts, d_hidden))
     weight_sum = mixed_parts[:, own_rows : own_rows + blocks].reshape(heads, own_rows)
     mixed_heads = mixed_parts[:, :own_rows].astype(f32) / weight_sum.astype(f32)[..., None]
     mixed_low = jnp.transpose(mixed_heads, (1, 0, 2)).reshape(own_rows, model_width).astype(bf)
 
     first_sum = first_in + product(mixed_low, output_full)
     ffn_normed, ffn_norm_pull = jax.vjp(layer_norm, first_sum, vectors_full[2], vectors_full[3])
-    ffn_low = ffn_normed.astype(bf)
-    inner_act = product(ffn_low, inner_full)
+    ffn_group = spread_pair(ffn_normed.astype(bf)).reshape(group_rows, model_width)
+    inner_act = product(ffn_group, inner_part_weight)
     hidden, gelu_pull = jax.vjp(exact_gelu, inner_act)
     hidden_low = hidden.astype(bf)
-    second_sum = second_in + product(hidden_low, outer_full)
-    outer_part = against(hidden_low, second_grad)
-    (inner_back,) = gelu_pull(through(second_grad, outer_full))
+    (inner_back,) = gelu_pull(d_hidden)
     inner_back_low = inner_back.astype(bf)
-    inner_part = against(ffn_low, inner_back_low)
-    first_from_ffn, ffn_gain_part, ffn_shift_part = ffn_norm_pull(
-        through(inner_back_low, inner_full)
-    )
+    pairs = (2, 2, own_rows, model_width)
+    ffn_back = through(inner_back_low, inner_part_weight).astype(bf)
+    ffn_back = sum_pair(ffn_back.reshape(pairs)).astype(f32)
+    second_part = product(hidden_low, outer_part_weight).astype(bf)
+    second_sum = second_in + sum_pair(second_part.reshape(pairs)).astype(f32)
+    outer_part = against(hidden_low, grad_group).astype(bf).reshape(seq_count, -1, model_width)
+    inner_part = against(ffn_group, inner_back_low).astype(bf).reshape(seq_count, cuts[0], -1)
+    first_from_ffn, ffn_gain_part, ffn_shift_part = ffn_norm_pull(ffn_back)
     first_carry = first_grad.astype(f32) + first_from_ffn
     carry_low = first_carry.astype(bf)
-    output_part = against(mixed_low, carry_low)
+    output_part = against(mixed_low, carry_low).astype(bf)
     mixed_back = through(carry_low, output_full).reshape(own_rows, heads, HEADD)
     mixed_back = jnp.transpose(mixed_back, (1, 0, 2))
     mixed_dot = jnp.sum(mixed_back * mixed_heads, axis=-1).astype(bf)
@@ -564,41 +614,57 @@
         ],
         axis=1,
     )
-    back_parts = jnp.concatenate([mixed_back.astype(bf), tails], axis=1)
-    back_group = spread_round(exchange(back_parts)).reshape(-1, HEADD)
+    back_parts = exchange(jnp.concatenate([mixed_back.astype(bf), tails], axis=1))
+    ffn_parts = jnp.concatenate([inner_part, outer_part], axis=1)
+    back_parts, ffn_parts, output_part = lax.optimization_barrier(
+        (back_parts, ffn_parts, output_part)
+    )
+    ffn_grads = lax.psum_scatter(ffn_parts, SEQ, scatter_dimension=0, tiled=False)
+    inner_cols = ffn_grads[: cuts[0]].reshape(round_count, weight_rows, -1)
+    inner_cols = exchange(inner_cols, ROUND)
+    inner_cols = inner_cols.reshape(round_count, weight_rows, seq_count, piece)
+    inner_grad = jnp.transpose(inner_cols, (1, 2, 0, 3)).reshape(weight_rows, hidden_width)
+    outer_grad = ffn_grads[cuts[0] :]
+
+    def rows_of(part):
+        part = part.reshape(heads, groups, 2, 2, weight_rows, -1)
+        part = scattered(scattered(part, "rc", 3), "ry", 2)
+        if groups > 1:
+            return lax.psum_scatter(part, "kk", scatter_dimension=1, tiled=False)
+        return part[:, 0]
+
+    output_grad = jnp.sum(exchange(rows_of(output_part)).astype(f32), axis=0)
+
+    back_group = spread_round(back_parts).reshape(-1, HEADD)
     query_value_back = attend_backward(
         place, back_group, token_sums, sorted_q, sorted_k, sorted_v, probs, own_rows
     )
     back_shape = (2, 2, groups, heads, own_rows, 2 * HEADD)
-    own_back = exchange(sum_round(query_value_back.reshape(back_shape)))
+    head_back = sum_round(query_value_back.reshape(back_shape))
+    qkv_part = against(normed_seq, head_back.reshape(heads * own_rows, 2 * HEADD)).astype(bf)
+    qkv_rows = exchange(rows_of(qkv_part)).reshape(heads, weight_rows, 2, HEADD)
+    qkv_grad = jnp.transpose(qkv_rows, (2, 1, 0, 3)).reshape(2, weight_rows, model_width)
+    own_back = exchange(head_back)
     own_back = jnp.transpose(own_back.reshape(heads, own_rows, 2, HEADD), (1, 2, 0, 3))
     own_back = own_back.reshape(own_rows, 2 * model_width)
-    qkv_part = against(normed_low, own_back)
     normed_back = through(own_back, qkv_full)
     second_from_attn, attn_gain_part, attn_shift_part = attn_norm_pull(normed_back)
     second_carry = second_grad.astype(f32) + second_from_attn
 
-    inner_grad = reduce_rows(inner_part)
-    outer_grad = reduce_rows(outer_part)
-    output_grad = reduce_rows(output_part)
-    qkv_grad = reduce_rows(qkv_part)
     vector_parts = jnp.stack([attn_gain_part, attn_shift_part, ffn_gain_part, ffn_shift_part])
-    device_count = seq_count * round_count
     vector_parts = jnp.transpose(vector_parts.reshape(4, device_count, -1), (1, 0, 2))
-    vector_rows = lax.all_to_all(
-        vector_parts.reshape(device_count, -1), ALL, split_axis=0, concat_axis=0, tiled=True
-    )
+    vector_rows = exchange(vector_parts.reshape(device_count, -1), ALL)
     vector_grads = jnp.sum(vector_rows, axis=0).reshape(4, -1)
     return (
         first_sum.astype(bf),
         second_sum.astype(bf),
         carry_low,
         second_carry.astype(bf),
-        qkv_grad[:, :model_width],
-        qkv_grad[:, model_width:],
+        qkv_grad[0].astype(f32),
+        qkv_grad[1].astype(f32),
         output_grad,
-        inner_grad,
-        outer_grad,
+        inner_grad.astype(f32),
+        outer_grad.astype(f32),
         vector_grads[0],
         vector_grads[1],
         vector_grads[2],
@@ -612,7 +678,7 @@
     split_mesh = Mesh(mesh.devices.reshape(shape), ALL)
     rows = P(ALL, None)
     vector = P(ALL)
-    table = P(("ry", "rc"), ("hd", "kk"))
+    table = P(ROUND, SEQ)
     in_specs = (rows,) * 7 + (vector,) * 4 + (table,) * 2 + (rows,) * 2
     out_specs = (rows,) * 9 + (vector,) * 4
     return jax.shard_map(

time: 1020 us -> 578 us (0.57)
  waiting for transfers between devices: 669 us -> 174 us
  matrix products: 62.7 us -> 34.2 us
  blocking collectives: 52.8 us -> 74.9 us
  starting transfers between devices: 25.4 us -> 46.9 us
  other arithmetic: 49.8 us -> 71 us
  local copies, waits for them, and re-layouts: 58.7 us -> 78.3 us
    reduce_scatter x4 -> x1, waiting for transfers between devices: 452 us -> 0.01 us  [per_device(): lax.psum_scatter(ffn_parts, SEQ, scatter_dimension=0, tiled=False)]
    all_gather x1, waiting for transfers between devices: 54.3 us -> 3.55 us  [per_device(): qkv_all = lax.all_gather(qkv_shard, ALL, axis=0, tiled=True)]
    ppermute x8 -> x22, waiting for transfers between devices: 85.1 us -> 124 us  [swapped(): return lax.ppermute(value, axis, SWAP)]
    all_to_all x2, blocking collectives: 52.8 us -> 74.9 us  [exchange(): return lax.all_to_all(parts, axes, split_axis=0, concat_axis=0, tiled=True)]
    all_gather x3 -> x1, waiting for transfers between devices: 21.2 us -> 3.2 us  [per_device(): shards = lax.all_gather(shard, SEQ, axis=0, tiled=False)]
    all_to_all x4 -> x8, starting transfers between devices: 17.7 us -> 34.2 us  [exchange(): return lax.all_to_all(parts, axes, split_axis=0, concat_axis=0, tiled=True)]
    dot_general x4, matrix products: 20.3 us -> 8.95 us  [product(): return jnp.dot(left_side, right_side, preferred_element_type=f32)]
    all_to_all x4 -> x8, waiting for transfers between devices: 54.6 us -> 43.8 us  [exchange(): return lax.all_to_all(parts, axes, split_axis=0, concat_axis=0, tiled=True)]
  transfers between devices with their start and end apart: 20 -> 33, of which waited for: 15 -> 20; matrix products, arithmetic and copies ran while one was open for 13% -> 24% of each run, Pallas kernels for 3% -> 6%
where the time goes in v2:
time: 578 us; the launch traced here: 570 us
  waiting for transfers between devices  174 us (30%)
  local copies, waits for them, and re-layouts  78.3 us (14%)
  Pallas kernels  75.6 us (13%)
  blocking collectives  74.9 us (13%)
  other arithmetic  71 us (12%)
  starting transfers between devices  46.9 us (8%)
  matrix products  34.2 us (6%)
  between operations  15 us (3%)
    ppermute x22, waiting for transfers between devices, swapped(): return lax.ppermute(value, axis, SWAP)  124 us
    all_to_all x2, blocking collectives, exchange(): return lax.all_to_all(parts, axes, split_axis=0, concat_axis=0, tiled=True)  74.9 us
    all_to_all x8, waiting for transfers between devices, exchange(): return lax.all_to_all(parts, axes, split_axis=0, concat_axis=0, tiled=True)  43.8 us
    pallas_call x1, Pallas kernels, attend_backward(): pl.pallas_call(functools.partial(backward_kernel, own_rows, steps), grid=...  40.6 us
    pallas_call x1, Pallas kernels, attend_forward(): pl.pallas_call(functools.partial(forward_kernel, own_rows, steps), grid=(...  35 us
    all_to_all x8, starting transfers between devices, exchange(): return lax.all_to_all(parts, axes, split_axis=0, concat_axis=0, tiled=True)  34.2 us
    scatter x1, local copies, waits for them, and re-layouts, sorted_places(): jnp.full((dump + SPAN,), -1, jnp.int32).at[place].set(bucket_row)  30.5 us
    dot_general x4, matrix products, against(): lax.dot_general(left_side, right_side, (((0,), (0,)), ((), ())), preferre...  13.3 us
  transfers between devices with their start and end apart: 33, of which 20 were waited for; matrix products, arithmetic and copies ran while one was open for 24% of the time, Pallas kernels for 6%

profile of v2, /device:TPU:0, one launch (start us, length us, event | category | flops | bytes accessed | tf_op | source)
XLA Modules:
  0.0 570.1 jit_solution(17453364220967184609)
XLA Ops:
  11.0 7.3 %all-to-all-start = ((s32[8,2,1024]{2,1,0:T(2,128)}), s32[8,2,1024]{2,1,0:T(2,128)S(1)}, u32[]{:S(2)}, u32[]{:S(2)}) async-start(s32[8,2,1024]{2,1,0:T(2,128)} %broadcast_in_dim.36), calls=%async_computation | async-start | bytes 131072 | tf_op jit(solution)/shard_map/all_to_all | solution.py:418
  20.8 4.4 all-to-all-done
  25.2 3.4 all-to-all-start.3
  30.1 30.5 %scatter_custom_fusion = s32[8832]{0:T(1024)S(1)} fusion(s32[8192]{0:T(1024)S(1)} %bitcast.319, s32[8192]{0:T(1024)S(1)} %bitcast.318, s32[]{:T(128)} %constant.147.clone.1), kind=kCustom, calls=%fused_computation.170 | custom fusion | bytes 35332 | tf_op jit(solution)/shard_map/scatter | solution.py:496
  60.9 4.4 and_reduce_fusion
  65.4 7.7 %fusion.3.bias_ref = f32[8704,128]{1,0:T(8,128)} fusion(s32[136,128]{1,0:T(8,128)S(1)} %get-tuple-element.58, s32[8704]{0:T(1024)S(1)} %get-tuple-element.98, pred[8704]{0:T(1024)(128)(4,1)S(1)} %not.23, pred[64,128]{1,0:T(8,128)(4,1)S(1)} %get-tuple-element.103, pred[64,128]{1,0:T(8,128)(4,1)S(1)} %get-tuple-element.104, ...), kind=kLoop, calls=%fused_computation.7 | loop fusion | flops 7798784 | bytes 4603392 | tf_op jit(solution)/shard_map/jit(_where)/select_n | solution.py:505
  73.7 3.5 all-gather.4.cloned.1.call-done
  80.7 3.5 fusion.26
  85.9 58.6 %all_to_all.54 = bf16[8,256,256]{2,1,0:T(8,128)(2,1)S(1)} all-to-all(bf16[8,256,256]{2,1,0:T(8,128)(2,1)S(1)} %reshape.709), channel_id=1, replica_groups=mesh['hd'=8,'kk'=1,'ry'=2,'rc'=2] {'hd'}, dimensions={0} | all-to-all | bytes 2097152 | tf_op jit(solution)/shard_map/all_to_all | solution.py:418
  144.5 23.5 %collective-permute-done = bf16[8,256,256]{2,1,0:T(8,128)(2,1)S(1)} collective-permute-done((bf16[8,256,256]{2,1,0:T(8,128)(2,1)S(1)}, bf16[8,256,256]{2,1,0:T(8,128)(2,1)S(1)}, u32[]{:S(2)}, u32[]{:S(2)}) %collective-permute-start) | collective-permute-done | bytes 1048608 | tf_op jit(solution)/shard_map/ppermute | solution.py:422
  168.4 4.1 collective-permute-done.1
  174.9 35.0 %attend_forward.1 = (bf16[8704,128]{1,0:T(8,128)(2,1)}, bf16[8832,128]{1,0:T(8,128)(2,1)}, bf16[8832,128]{1,0:T(8,128)(2,1)}, bf16[8832,128]{1,0:T(8,128)(2,1)},...) custom-call(s32[8192]{0:T(1024)} %add_select_fusion.1.place_ref, bf16[8192,256]{1,0:T(8,128)(2,1)} %bitcast.255, ...), custom_call_target="tpu_custom_call" | custom-call | tf_op jit(solution)/shard_map/attend_forward/pallas_call | solution.py:196
  213.0 13.1 %collective-permute-done.4 = bf16[256,1024]{1,0:T(8,128)(2,1)S(1)} collective-permute-done((bf16[256,1024]{1,0:T(8,128)(2,1)S(1)}, bf16[256,1024]{1,0:T(8,128)(2,1)S(1)}, u32[]{:S(2)}, u32[]{:S(2)}) %collective-permute-start.4) | collective-permute-done | bytes 524320 | tf_op jit(solution)/shard_map/ppermute | solution.py:422
  229.5 3.2 all-gather.6.cloned.1.call-done
  236.1 2.7 pad_maximum_fusion.4
  238.8 5.3 collective-permute-done.3
  245.0 3.5 all-to-all-start.2
  248.6 6.5 %collective-permute-done.6 = bf16[8,32,1024]{2,1,0:T(8,128)(2,1)} collective-permute-done((bf16[8,32,1024]{2,1,0:T(8,128)(2,1)}, bf16[8,32,1024]{2,1,0:T(8,128)(2,1)}, u32[]{:S(2)}, u32[]{:S(2)}) %collective-permute-start.6) | collective-permute-done | bytes 524320 | tf_op jit(solution)/shard_map/ppermute | solution.py:422
  257.4 4.2 fusion.74
  262.9 4.3 fusion.85
  274.8 12.8 %collective-permute-done.8 = bf16[256,1024]{1,0:T(8,128)(2,1)S(1)} collective-permute-done((bf16[256,1024]{1,0:T(8,128)(2,1)S(1)}, bf16[256,1024]{1,0:T(8,128)(2,1)S(1)}, u32[]{:S(2)}, u32[]{:S(2)}) %collective-permute-start.8) | collective-permute-done | bytes 524320 | tf_op jit(solution)/shard_map/ppermute | solution.py:422
  287.9 2.6 collective-permute-done.9
  293.1 10.0 %add_convert_fusion.1 = (bf16[1024,1024]{1,0:T(8,128)(2,1)S(1)}, f32[1024,1024]{1,0:T(8,128)S(1)}) fusion(f32[1024,1024]{1,0:T(8,128)S(1)} %copy-done.3, f32[1024,1024]{1,0:T(8,128)S(1)} %fusion.86), kind=kLoop, calls=%fused_computation.14 | loop fusion | flops 75497472 | bytes 14680064 | tf_op jit(solution)/shard_map/convert_element_type | solution.py:594
  310.0 3.8 convolution_convert_fusion.2
  314.9 8.0 %collective-permute-done.13 = bf16[256,1024]{1,0:T(8,128)(2,1)S(1)} collective-permute-done((bf16[256,1024]{1,0:T(8,128)(2,1)S(1)}, bf16[256,1024]{1,0:T(8,128)(2,1)S(1)}, u32[]{:S(2)}, u32[]{:S(2)}) %collective-permute-start.13) | collective-permute-done | bytes 524320 | tf_op jit(solution)/shard_map/ppermute | solution.py:422
  328.8 4.2 all-to-all-start.4
  333.3 4.1 convolution_convert_fusion.1
  341.6 6.4 %all-to-all-done.4 = bf16[8,272,128]{2,1,0:T(8,128)(2,1)} async-done(((bf16[8,272,128]{2,1,0:T(8,128)(2,1)}), bf16[8,272,128]{2,1,0:T(8,128)(2,1)}, u32[]{:S(2)}, u32[]{:S(2)}) %all-to-all-start.4) | async-done | bytes 557088 | tf_op jit(solution)/shard_map/all_to_all | solution.py:418
  349.1 11.9 %collective-permute-done.14 = bf16[8,272,128]{2,1,0:T(8,128)(2,1)S(1)} collective-permute-done((bf16[8,272,128]{2,1,0:T(8,128)(2,1)}, bf16[8,272,128]{2,1,0:T(8,128)(2,1)S(1)}, u32[]{:S(2)}, u32[]{:S(2)}) %collective-permute-start.14) | collective-permute-done | bytes 557088 | tf_op jit(solution)/shard_map/ppermute | solution.py:422
  362.3 2.7 collective-permute-done.15
  366.6 40.6 %attend_backward.1 = bf16[8192,256]{1,0:T(8,128)(2,1)} custom-call(s32[8192]{0:T(1024)} %add_select_fusion.1.place_ref, bf16[8704,128]{1,0:T(8,128)(2,1)} %bitcast.260, f32[64,128]{1,0:T(8,128)} %get-tuple-element.34.sum_ref, bf16[8832,128]{1,0:T(8,128)(2,1)} %get-tuple-element.35.query_ref, bf16[8832,128]{1,0:T(8,128)(2,1)} %get-tuple-element.36.key_ref, ...), custom_call_target="tpu_custom_call" | custom-call | tf_op jit(solution)/shard_map/attend_backward/pallas_call | solution.py:381
  407.2 4.5 fusion.75
  411.6 4.0 copy.113
  417.2 4.2 copy.114
  421.4 3.8 add_convert_fusion
  431.1 4.7 slice.241
  435.8 27.1 %collective-permute-done.21 = bf16[8,1,32,1024]{3,2,0,1:T(8,128)(2,1)S(1)} collective-permute-done((bf16[8,1,32,1024]{3,2,0,1:T(8,128)(2,1)}, bf16[8,1,32,1024]{3,2,0,1:T(8,128)(2,1)S(1)}, u32[]{:S(2)}, u32[]{:S(2)}) %collective-permute-start.21) | collective-permute-done | bytes 524320 | tf_op jit(solution)/shard_map/ppermute | solution.py:422
  463.9 5.3 all-to-all-start.7
  473.2 3.6 convolution_convert_fusion.5
  481.9 3.5 collective-permute-done.19
  485.5 16.3 %all_to_all.55 = bf16[8,32,256]{2,1,0:T(8,128)(2,1)S(1)} all-to-all(bf16[8,32,256]{2,1,0:T(8,128)(2,1)S(1)} %fusion.55), channel_id=1, replica_groups=mesh['hd'=8,'kk'=1,'ry'=2,'rc'=2] {'hd'}, dimensions={0} | all-to-all | bytes 262144 | tf_op jit(solution)/shard_map/all_to_all | solution.py:418
  501.9 3.6 all-to-all-start.5
  511.5 23.0 %all-to-all-done.5 = bf16[8,256,256]{1,2,0:T(8,128)(2,1)S(1)} async-done(((bf16[8,256,256]{1,2,0:T(8,128)(2,1)}), bf16[8,256,256]{1,2,0:T(8,128)(2,1)S(1)}, u32[]{:S(2)}, u32[]{:S(2)}) %all-to-all-start.5) | async-done | bytes 1048608 | tf_op jit(solution)/shard_map/all_to_all | solution.py:418
  534.6 3.6 fusion.39
  539.8 3.6 all-to-all-start.9
  545.9 4.6 all-to-all-done.9
  552.5 3.4 all-to-all-start.8
  556.5 5.4 all-to-all-done.8
  (218 shorter events, 95.3 us)
Async XLA Ops:
  7.2 13.1 %copy-start = (bf16[256,1024]{1,0:T(8,128)(2,1)S(1)}, bf16[256,1024]{1,0:T(8,128)(2,1)}, u32[]{:S(2)}) copy-start(bf16[256,1024]{1,0:T(8,128)(2,1)} %param.16) | copy-start | bytes 1572868
  7.2 70.1 %all-gather.4.cloned.1.call-start = ((), (), s32[]{:S(2)}) async-start(), calls=%async_computation.11 | async-start | bytes 4595712 | tf_op jit(solution)/shard_map/all_gather | solution.py:544
  11.0 14.2 %all-to-all-start = ((s32[8,2,1024]{2,1,0:T(2,128)}), s32[8,2,1024]{2,1,0:T(2,128)S(1)}, u32[]{:S(2)}, u32[]{:S(2)}) async-start(s32[8,2,1024]{2,1,0:T(2,128)} %broadcast_in_dim.36), calls=%async_computation | async-start | bytes 131072 | tf_op jit(solution)/shard_map/all_to_all | solution.py:418
  25.2 54.4 %all-to-all-start.3 = ((bf16[4,32,1024]{2,1,0:T(8,128)(2,1)}), bf16[4,32,1024]{2,1,0:T(8,128)(2,1)S(1)}, u32[]{:S(2)}, u32[]{:S(2)}) async-start(bf16[4,32,1024]{2,1,0:T(8,128)(2,1)} %reshape.713), calls=%async_computation.3 | async-start | bytes 524288 | tf_op jit(solution)/shard_map/all_to_all | solution.py:418
  28.6 204.1 %all-gather.6.cloned.1.call-start = ((), (), s32[]{:S(2)}) async-start(), calls=%async_computation.13 | async-start | bytes 10027008 | tf_op jit(solution)/shard_map/all_gather | solution.py:561
  73.1 6.5 %copy-start.22 = (bf16[128,1024]{1,0:T(8,128)(2,1)S(1)}, bf16[128,1024]{1,0:T(8,128)(2,1)}, u32[]{:S(2)}) copy-start(bf16[128,1024]{1,0:T(8,128)(2,1)} %param.21) | copy-start | bytes 786436
  73.1 6.5 %copy-start.23 = (bf16[32,1024]{1,0:T(8,128)(2,1)S(1)}, bf16[32,1024]{1,0:T(8,128)(2,1)}, u32[]{:S(2)}) copy-start(bf16[32,1024]{1,0:T(8,128)(2,1)} %param.19) | copy-start | bytes 196612
  144.5 23.5 %collective-permute-start = (bf16[8,256,256]{2,1,0:T(8,128)(2,1)S(1)}, bf16[8,256,256]{2,1,0:T(8,128)(2,1)S(1)}, u32[]{:S(2)}, u32[]{:S(2)}) collective-permute-start(bf16[8,256,256]{2,1,0:T(8,128)(2,1)S(1)} %all_to_all.54), channel_id=1, source_target_pairs={{0,2},{2,0},{1,3},{3,1},{4,6},{6,4},{5,7},{7,5},{8,10},{10,8},{9,1... | collective-permute-start | bytes 3145736 | tf_op jit(solution)/shard_map/ppermute | solution.py:422
  168.3 4.2 collective-permute-start.1
  211.7 15.6 %collective-permute-start.2 = (bf16[2,1,8,272,128]{4,3,2,1,0:T(8,128)(2,1)S(1)}, bf16[2,1,8,272,128]{4,3,2,1,0:T(8,128)(2,1)S(1)}, u32[]{:S(2)}, u32[]{:S(2)}) collective-permute-start(bf16[2,1,8,272,128]{4,3,2,1,0:T(8,128)(2,1)S(1)} %bitcast.290), channel_id=1, source_target_pairs={{0,1},{1,0},{2,3},{3,2},{4,5},{5,4},{6,7},{7,6},{8,9},{9,8},{10,11... | collective-permute-start | bytes 3342344 | tf_op jit(solution)/shard_map/ppermute | solution.py:422
  211.9 14.2 %collective-permute-start.4 = (bf16[256,1024]{1,0:T(8,128)(2,1)S(1)}, bf16[256,1024]{1,0:T(8,128)(2,1)S(1)}, u32[]{:S(2)}, u32[]{:S(2)}) collective-permute-start(bf16[256,1024]{1,0:T(8,128)(2,1)S(1)} %copy-done.18), channel_id=1, source_target_pairs={{0,2},{2,0},{1,3},{3,1},{4,6},{6,4},{5,7},{7,5},{8,10},{10,8},{9,1... | collective-permute-start | bytes 1572872 | tf_op jit(solution)/shard_map/ppermute | solution.py:422
  227.2 8.8 %collective-permute-start.5 = (bf16[2,256,1024]{2,1,0:T(8,128)(2,1)}, bf16[2,256,1024]{2,1,0:T(8,128)(2,1)}, u32[]{:S(2)}, u32[]{:S(2)}) collective-permute-start(bf16[2,256,1024]{2,1,0:T(8,128)(2,1)} %get-tuple-element.86), channel_id=1, source_target_pairs={{0,1},{1,0},{2,3},{3,2},{4,5},{5,4},{6,7},{7,6},{8,9},{9,8},{10,11... | collective-permute-start | bytes 3145736 | tf_op jit(solution)/shard_map/ppermute | solution.py:422
  228.4 15.6 %collective-permute-start.3 = (bf16[1,8,272,128]{3,2,1,0:T(8,128)(2,1)}, bf16[1,8,272,128]{3,2,1,0:T(8,128)(2,1)S(1)}, u32[]{:S(2)}, u32[]{:S(2)}) collective-permute-start(bf16[1,8,272,128]{3,2,1,0:T(8,128)(2,1)} %slice_bitcast_fusion.2), channel_id=1, source_target_pairs={{0,2},{2,0},{1,3},{3,1},{4,6},{6,4},{5,7},{7,5},{8,10},{10,8},{9,1... | collective-permute-start | bytes 1671176 | tf_op jit(solution)/shard_map/ppermute | solution.py:422
  234.6 20.4 %collective-permute-start.6 = (bf16[8,32,1024]{2,1,0:T(8,128)(2,1)}, bf16[8,32,1024]{2,1,0:T(8,128)(2,1)}, u32[]{:S(2)}, u32[]{:S(2)}) collective-permute-start(bf16[8,32,1024]{2,1,0:T(8,128)(2,1)} %slice.225), channel_id=1, source_target_pairs={{0,2},{2,0},{1,3},{3,1},{4,6},{6,4},{5,7},{7,5},{8,10},{10,8},{9,1... | collective-permute-start | bytes 1572872 | tf_op jit(solution)/shard_map/ppermute | solution.py:422
  245.0 22.2 %all-to-all-start.2 = ((bf16[8,272,128]{2,1,0:T(8,128)(2,1)}), bf16[8,272,128]{2,1,0:T(8,128)(2,1)S(1)}, u32[]{:S(2)}, u32[]{:S(2)}) async-start(bf16[8,272,128]{2,1,0:T(8,128)(2,1)} %fusion.46), calls=%async_computation.2 | async-start | bytes 1114112 | tf_op jit(solution)/shard_map/all_to_all | solution.py:418
  257.4 5.5 copy-start.12
  257.4 12.2 %collective-permute-start.7 = (bf16[8,2,32,1024]{3,2,1,0:T(8,128)(2,1)}, bf16[8,2,32,1024]{3,2,1,0:T(8,128)(2,1)}, u32[]{:S(2)}, u32[]{:S(2)}) collective-permute-start(bf16[8,2,32,1024]{3,2,1,0:T(8,128)(2,1)} %pad_maximum_fusion.10), channel_id=1, source_target_pairs={{0,1},{1,0},{2,3},{3,2},{4,5},{5,4},{6,7},{7,6},{8,9},{9,8},{10,11... | collective-permute-start | bytes 3145736 | tf_op jit(solution)/shard_map/ppermute | solution.py:422
  273.4 14.3 %collective-permute-start.8 = (bf16[256,1024]{1,0:T(8,128)(2,1)S(1)}, bf16[256,1024]{1,0:T(8,128)(2,1)S(1)}, u32[]{:S(2)}, u32[]{:S(2)}) collective-permute-start(bf16[256,1024]{1,0:T(8,128)(2,1)S(1)} %add_convert_fusion.4), channel_id=1, source_target_pairs={{0,2},{2,0},{1,3},{3,1},{4,6},{6,4},{5,7},{7,5},{8,10},{10,8},{9,1... | collective-permute-start | bytes 1572872 | tf_op jit(solution)/shard_map/ppermute | solution.py:422
  287.8 2.9 copy-start.15
  287.8 2.7 collective-permute-start.9
  305.7 2.7 collective-permute-start.12
  308.8 14.0 %collective-permute-start.13 = (bf16[256,1024]{1,0:T(8,128)(2,1)S(1)}, bf16[256,1024]{1,0:T(8,128)(2,1)S(1)}, u32[]{:S(2)}, u32[]{:S(2)}) collective-permute-start(bf16[256,1024]{1,0:T(8,128)(2,1)S(1)} %slice_bitcast_fusion.4), channel_id=1, source_target_pairs={{0,2},{2,0},{1,3},{3,1},{4,6},{6,4},{5,7},{7,5},{8,10},{10,8},{9,1... | collective-permute-start | bytes 1572872 | tf_op jit(solution)/shard_map/ppermute | solution.py:422
  314.9 18.4 %copy-start.10 = (bf16[1024,1024]{1,0:T(8,128)(2,1)}, bf16[1024,1024]{1,0:T(8,128)(2,1)S(1)}, u32[]{:S(2)}) copy-start(bf16[1024,1024]{1,0:T(8,128)(2,1)S(1)} %multiply_convert_fusion) | copy-start | bytes 6291460
  314.9 8.9 %copy-start.21 = (bf16[256,1024]{1,0:T(8,128)(2,1)S(1)}, bf16[256,1024]{1,0:T(8,128)(2,1)}, u32[]{:S(2)}) copy-start(bf16[256,1024]{1,0:T(8,128)(2,1)} %param.28) | copy-start | bytes 1572868
  328.8 19.2 %all-to-all-start.4 = ((bf16[8,272,128]{2,1,0:T(8,128)(2,1)}), bf16[8,272,128]{2,1,0:T(8,128)(2,1)}, u32[]{:S(2)}, u32[]{:S(2)}) async-start(bf16[8,272,128]{2,1,0:T(8,128)(2,1)} %maximum_maximum_fusion), calls=%async_computation.4 | async-start | bytes 1114112 | tf_op jit(solution)/shard_map/all_to_all | solution.py:418
  333.0 217.5 %reduce-scatter.2.cloned.1.call-start = ((), (), s32[]{:S(2)}) async-start(), calls=%async_computation.12 | async-start | bytes 4718592 | tf_op jit(solution)/shard_map/reduce_scatter | solution.py:622
  333.3 4.1 copy-start.16
  348.0 13.0 %collective-permute-start.14 = (bf16[8,272,128]{2,1,0:T(8,128)(2,1)}, bf16[8,272,128]{2,1,0:T(8,128)(2,1)S(1)}, u32[]{:S(2)}, u32[]{:S(2)}) collective-permute-start(bf16[8,272,128]{2,1,0:T(8,128)(2,1)} %all-to-all-done.4), channel_id=1, source_target_pairs={{0,2},{2,0},{1,3},{3,1},{4,6},{6,4},{5,7},{7,5},{8,10},{10,8},{9,1... | collective-permute-start | bytes 1671176 | tf_op jit(solution)/shard_map/ppermute | solution.py:422
  362.2 2.8 collective-permute-start.15
  415.6 5.8 %collective-permute-start.16 = (bf16[2,1,8,256,256]{3,4,2,1,0:T(8,128)(2,1)}, bf16[2,1,8,256,256]{3,4,2,1,0:T(8,128)(2,1)}, u32[]{:S(2)}, u32[]{:S(2)}) collective-permute-start(bf16[2,1,8,256,256]{3,4,2,1,0:T(8,128)(2,1)} %copy.113), channel_id=1, source_target_pairs={{0,1},{1,0},{2,3},{3,2},{4,5},{5,4},{6,7},{7,6},{8,9},{9,8},{10,11... | collective-permute-start | bytes 6291464 | tf_op jit(solution)/shard_map/ppermute | solution.py:422
  416.8 10.2 %collective-permute-start.20 = (bf16[8,1,2,32,1024]{4,3,2,0,1:T(8,128)(2,1)}, bf16[8,1,2,32,1024]{4,3,2,0,1:T(8,128)(2,1)}, u32[]{:S(2)}, u32[]{:S(2)}) collective-permute-start(bf16[8,1,2,32,1024]{4,3,2,0,1:T(8,128)(2,1)} %dynamic-slice_bitcast_fusion), channel_id=1, source_target_pairs={{0,1},{1,0},{2,3},{3,2},{4,5},{5,4},{6,7},{7,6},{8,9},{9,8},{10,11... | collective-permute-start | bytes 3145736 | tf_op jit(solution)/shard_map/ppermute | solution.py:422
  425.2 3.5 copy-start.1
  426.3 42.9 %collective-permute-start.17 = (bf16[1,8,256,256]{2,3,1,0:T(8,128)(2,1)}, bf16[1,8,256,256]{2,3,1,0:T(8,128)(2,1)}, u32[]{:S(2)}, u32[]{:S(2)}) collective-permute-start(bf16[1,8,256,256]{2,3,1,0:T(8,128)(2,1)} %slice_bitcast_fusion), channel_id=1, source_target_pairs={{0,2},{2,0},{1,3},{3,1},{4,6},{6,4},{5,7},{7,5},{8,10},{10,8},{9,1... | collective-permute-start | bytes 3145736 | tf_op jit(solution)/shard_map/ppermute | solution.py:422
  429.9 33.1 %collective-permute-start.21 = (bf16[8,1,32,1024]{3,2,0,1:T(8,128)(2,1)}, bf16[8,1,32,1024]{3,2,0,1:T(8,128)(2,1)S(1)}, u32[]{:S(2)}, u32[]{:S(2)}) collective-permute-start(bf16[8,1,32,1024]{3,2,0,1:T(8,128)(2,1)} %dynamic-slice_bitcast_fusion.1), channel_id=1, source_target_pairs={{0,2},{2,0},{1,3},{3,1},{4,6},{6,4},{5,7},{7,5},{8,10},{10,8},{9,1... | collective-permute-start | bytes 1572872 | tf_op jit(solution)/shard_map/ppermute | solution.py:422
  431.1 31.8 %copy-start.5 = (bf16[8,1,2,32,1024]{4,3,2,0,1:T(8,128)(2,1)S(1)}, bf16[8,1,2,32,1024]{4,3,2,0,1:T(8,128)(2,1)}, u32[]{:S(2)}) copy-start(bf16[8,1,2,32,1024]{4,3,2,0,1:T(8,128)(2,1)} %copy-done.4) | copy-start | bytes 3145732
  435.8 33.4 %copy-start.2 = (bf16[2,1,8,256,256]{3,4,2,1,0:T(8,128)(2,1)S(1)}, bf16[2,1,8,256,256]{3,4,2,1,0:T(8,128)(2,1)}, u32[]{:S(2)}) copy-start(bf16[2,1,8,256,256]{3,4,2,1,0:T(8,128)(2,1)} %copy-done.1) | copy-start | bytes 6291460
  463.9 21.6 %all-to-all-start.7 = ((bf16[8,32,1024]{2,1,0:T(8,128)(2,1)}), bf16[8,32,1024]{2,1,0:T(8,128)(2,1)S(1)}, u32[]{:S(2)}, u32[]{:S(2)}) async-start(bf16[8,32,1024]{2,1,0:T(8,128)(2,1)} %fusion.48), calls=%async_computation.7 | async-start | bytes 1048576 | tf_op jit(solution)/shard_map/all_to_all | solution.py:418
  473.2 3.8 copy-start.11
  473.2 3.8 copy-start.14
  476.9 2.5 collective-permute-start.18
  479.5 5.9 %collective-permute-start.19 = (bf16[8,1,32,256]{3,2,0,1:T(8,128)(2,1)S(1)}, bf16[8,1,32,256]{3,2,0,1:T(8,128)(2,1)S(1)}, u32[]{:S(2)}, u32[]{:S(2)}) collective-permute-start(bf16[8,1,32,256]{3,2,0,1:T(8,128)(2,1)S(1)} %dynamic-slice_bitcast_fusion.3), channel_id=1, source_target_pairs={{0,2},{2,0},{1,3},{3,1},{4,6},{6,4},{5,7},{7,5},{8,10},{10,8},{9,1... | collective-permute-start | bytes 393224 | tf_op jit(solution)/shard_map/ppermute | solution.py:422
  481.7 23.7 %collective-permute-start.10 = (bf16[2,256,1024]{2,1,0:T(8,128)(2,1)}, bf16[2,256,1024]{2,1,0:T(8,128)(2,1)}, u32[]{:S(2)}, u32[]{:S(2)}) collective-permute-start(bf16[2,256,1024]{2,1,0:T(8,128)(2,1)} %bitcast.53), channel_id=1, source_target_pairs={{0,1},{1,0},{2,3},{3,2},{4,5},{5,4},{6,7},{7,6},{8,9},{9,8},{10,11... | collective-permute-start | bytes 3145736 | tf_op jit(solution)/shard_map/ppermute | solution.py:422
  501.9 32.7 %all-to-all-start.5 = ((bf16[8,256,256]{1,2,0:T(8,128)(2,1)}), bf16[8,256,256]{1,2,0:T(8,128)(2,1)S(1)}, u32[]{:S(2)}, u32[]{:S(2)}) async-start(bf16[8,256,256]{1,2,0:T(8,128)(2,1)} %bitcast.74), calls=%async_computation.5 | async-start | bytes 2097152 | tf_op jit(solution)/shard_map/all_to_all | solution.py:418
  508.9 34.5 %collective-permute-start.11 = (bf16[256,1024]{1,0:T(8,128)(2,1)}, bf16[256,1024]{1,0:T(8,128)(2,1)}, u32[]{:S(2)}, u32[]{:S(2)}) collective-permute-start(bf16[256,1024]{1,0:T(8,128)(2,1)} %slice_bitcast_fusion.6), channel_id=1, source_target_pairs={{0,2},{2,0},{1,3},{3,1},{4,6},{6,4},{5,7},{7,5},{8,10},{10,8},{9,1... | collective-permute-start | bytes 1572872 | tf_op jit(solution)/shard_map/ppermute | solution.py:422
  538.2 5.2 copy-start.7
  538.2 5.2 copy-start.19
  539.8 10.7 %all-to-all-start.9 = ((f32[32,1,128]{2,1,0:T(1,128)}), f32[32,1,128]{2,1,0:T(1,128)S(1)}, u32[]{:S(2)}, u32[]{:S(2)}) async-start(f32[32,1,128]{2,1,0:T(1,128)} %bitcast.97), calls=%async_computation.10 | async-start | bytes 32768 | tf_op jit(solution)/shard_map/all_to_all | solution.py:418
  552.5 9.4 %all-to-all-start.8 = ((bf16[4,32,1024]{2,1,0:T(8,128)(2,1)}), bf16[4,32,1024]{2,1,0:T(8,128)(2,1)S(1)}, u32[]{:S(2)}, u32[]{:S(2)}) async-start(bf16[4,32,1024]{2,1,0:T(8,128)(2,1)} %bitcast.93), calls=%async_computation.9 | async-start | bytes 524288 | tf_op jit(solution)/shard_map/all_to_all | solution.py:418
  (9 other events, 14.8 us)
Sparse Core Ops, SparseCore 0:
  11.4 65.7 all-gather.3
  80.8 151.8 all-gather.5
  415.9 99.2 reduce-scatter.1

commit v3 on v1

v3 whole, which is shorter than its diff:
```python
import functools
import math

import jax
import jax.numpy as jnp
from jax import lax
from jax.experimental import pallas as pl
from jax.experimental.pallas import tpu as pltpu
from jax.sharding import Mesh
from jax.sharding import PartitionSpec as P

HEADS = 8
NORM_EPS = 1e-05
SPAN = 64
HEADD = 128
PAD = 16
UNROLL = 17
TOKB = 128
CHUNK = 4096
VMEM_LIMIT = 60 * 2**20
KEY_EPS = 1e-06
bf = jnp.bfloat16
f32 = jnp.float32


def product(left_side, right_side):
    return jnp.dot(left_side, right_side, preferred_element_type=f32)


def against(left_side, right_side):
    return lax.dot_general(
        left_side, right_side, (((0,), (0,)), ((), ())), preferred_element_type=f32
    )


def through(left_side, right_side):
    return lax.dot_general(
        left_side, right_side, (((1,), (1,)), ((), ())), preferred_element_type=f32
    )


def takes(microseconds):
    return pl.CostEstimate(
        flops=int(microseconds * 1e8), bytes_accessed=int(microseconds * 3e6), transcendentals=0
    )


def aligned(start, size, step=SPAN):
    return pl.ds(pl.multiple_of(start, step), size)


def fill(ref, value):
    def body(step, carry):
        ref[aligned(step * SPAN, SPAN), :] = jnp.full((SPAN, ref.shape[1]), value, ref.dtype)
        return carry

    lax.fori_loop(0, ref.shape[0] // SPAN, body, 0)


def diagonal():
    rows = lax.broadcasted_iota(jnp.int32, (TOKB, TOKB), 0)
    return rows == lax.broadcasted_iota(jnp.int32, (TOKB, TOKB), 1)


def chunk_start(table_ref, own_rows, position):
    return table_ref[position // own_rows] * own_rows + position % own_rows


def lanes(row, eye, ones):
    high = row.astype(bf).astype(f32)
    parts = [jnp.where(eye, high, 0.0), jnp.where(eye, row - high, 0.0)]
    return product(jnp.concatenate(parts, axis=1).astype(bf), ones)


def forward_kernel(
    own_rows,
    load_steps,
    in_ref,
    out_ref,
    place_ref,
    bucket_ref,
    own_ref,
    peer_ref,
    pay_own_ref,
    pay_peer_ref,
    query_ref,
    key_ref,
    value_ref,
    prob_ref,
    sum_ref,
    wide_a,
    wide_b,
    stage_a,
    stage_b,
):
    step = pl.program_id(0)
    own_spans = prob_ref.shape[0] // SPAN
    tail = SPAN * (own_spans + 1)

    @pl.when(step == 0)
    def _():
        fill(wide_a, 0.0)
        fill(wide_b, 0.0)

    def scatter_from(token_ref):
        def scatter(block, carry):
            both = token_ref[aligned(block * TOKB, TOKB, TOKB), :].astype(f32)
            stage_a[...] = both[:, :HEADD]
            stage_b[...] = both[:, HEADD:]
            first = chunk_start(in_ref, own_rows, step * CHUNK + block * TOKB)
            for row in range(TOKB):
                place = place_ref[first + row]
                wide_a[pl.ds(place, 1), :] = stage_a[row : row + 1, :]
                wide_b[pl.ds(place, 1), :] = stage_b[row : row + 1, :]
            return carry

        lax.fori_loop(0, CHUNK // TOKB, scatter, 0)

    pl.when(step < load_steps // 2)(lambda: scatter_from(own_ref))
    pl.when((step >= load_steps // 2) & (step < load_steps))(lambda: scatter_from(peer_ref))

    def unit_keys(query):
        square = jnp.sum(query * query, axis=-1, keepdims=True)
        scale = lax.rsqrt(square * (1.0 / HEADD) + KEY_EPS) * HEADD**-0.5
        return (query * scale).astype(bf)

    @pl.when(step == load_steps)
    def _():
        query_ref[:SPAN, :] = wide_a[:SPAN, :].astype(bf)
        key_ref[:SPAN, :] = unit_keys(wide_a[:SPAN, :])
        value_ref[:SPAN, :] = wide_b[:SPAN, :].astype(bf)
        wide_a[:SPAN, :] = jnp.zeros((SPAN, HEADD), f32)
        wide_b[:SPAN, :] = jnp.zeros((SPAN, HEADD), f32)
        for ref in (query_ref, key_ref, value_ref):
            ref[pl.ds(tail, SPAN), :] = jnp.zeros((SPAN, HEADD), bf)
        ones = jnp.ones((2 * SPAN, HEADD), bf)
        row_ids = lax.broadcasted_iota(jnp.int32, (SPAN, 2 * SPAN), 0)
        lane_ids = lax.broadcasted_iota(jnp.int32, (SPAN, 2 * SPAN), 1)
        before, itself = lane_ids == row_ids, lane_ids == row_ids + SPAN

        def spans(group, carry):
            first = group * (UNROLL * SPAN)
            prev = aligned(first, SPAN)
            here = aligned(first + SPAN, UNROLL * SPAN)
            query_wide = wide_a[here, :]
            values = wide_b[here, :].astype(bf)
            keys = jnp.concatenate([key_ref[prev, :], unit_keys(query_wide)], axis=0)
            seen = jnp.concatenate([value_ref[prev, :], values], axis=0)
            query = query_wide.astype(bf)
            key_buckets, columns = [], []
            for span in range(UNROLL):
                row = bucket_ref[pl.ds(group * UNROLL + span, 1), :]
                high = row.astype(bf).astype(f32)
                low = pltpu.roll(row - high, SPAN, 1)
                key_buckets.append(row)
                columns.append(jnp.where(itself, high, jnp.where(before, low, 0.0)).astype(bf))
            columns = product(jnp.concatenate(columns, axis=0), ones)
            raised = []
            for span in range(UNROLL):
                mine = slice(span * SPAN, (span + 1) * SPAN)
                both = slice(span * SPAN, (span + 2) * SPAN)
                same = columns[mine] == key_buckets[span]
                matches = jnp.sum(jnp.where(same, 1.0, 0.0), axis=-1, keepdims=True)
                allowed = same & (jnp.logical_not(itself) | (matches < 1.5))
                scores = through(query[mine], keys[both])
                raised.append(jnp.where(allowed, jnp.exp(scores), 0.0))
            lows = [member.astype(bf) for member in raised]
            totals = product(jnp.concatenate(lows, axis=0), ones)
            results = []
            for span in range(UNROLL):
                mine = slice(span * SPAN, (span + 1) * SPAN)
                both = slice(span * SPAN, (span + 2) * SPAN)
                total = totals[mine]
                inverse = jnp.where(total > 0.0, 1.0 / total, 0.0)
                probs = (raised[span] * inverse).astype(bf)
                results.append((product(lows[span], seen[both]), total, probs))
            query_ref[here, :] = query
            key_ref[here, :] = keys[SPAN:]
            value_ref[here, :] = values
            for span, (weighted, total, probs) in enumerate(results):
                at = aligned(first + (span + 1) * SPAN, SPAN)
                wide_a[at, :] = weighted
                wide_b[at, :] = total
                prob_ref[aligned(first + span * SPAN, SPAN), :] = probs
            return carry

        lax.fori_loop(0, own_spans // UNROLL, spans, 0)
        wide_a[pl.ds(tail, SPAN), :] = jnp.zeros((SPAN, HEADD), f32)
        wide_b[pl.ds(tail, SPAN), :] = jnp.zeros((SPAN, HEADD), f32)

    def collect_to(pay_ref):
        blocks = own_rows // TOKB
        per_step = CHUNK // own_rows
        eye = diagonal()
        sum_rows = lax.broadcasted_iota(jnp.int32, (PAD, TOKB), 0)
        offset = (step - load_steps - 1) * CHUNK

        def collect(chunk, carry):
            first = chunk * (own_rows + PAD)
            sums = jnp.zeros((PAD, TOKB), f32)
            for block in range(blocks):
                start = chunk_start(out_ref, own_rows, offset + chunk * own_rows + block * TOKB)
                for row in range(TOKB):
                    place = place_ref[start + row]
                    stage_a[row : row + 1, :] = wide_a[pl.ds(place, 1), :]
                    stage_b[row : row + 1, :] = wide_b[pl.ds(place, 1), :]
                pay_ref[aligned(first + block * TOKB, TOKB, PAD), :] = stage_a[...].astype(bf)
                packed = jnp.sum(jnp.where(eye, stage_b[...], 0.0), axis=0, keepdims=True)
                sum_ref[pl.ds(chunk * blocks + block, 1), :] = packed
                sums = jnp.where(sum_rows == block, packed, sums)
            pay_ref[aligned(first + own_rows, PAD, PAD), :] = sums.astype(bf)
            return carry

        lax.fori_loop(0, per_step, collect, 0)

    half = load_steps + 1 + load_steps // 2
    pl.when((step > load_steps) & (step < half))(lambda: collect_to(pay_own_ref))
    pl.when(step >= half)(lambda: collect_to(pay_peer_ref))


def part_spec(shape, first, count):
    return pl.BlockSpec(shape, lambda step: (jnp.clip(step - first, 0, count - 1), 0))


def attend_forward(in_table, out_table, place, key_bucket, own, peer, own_rows):
    tokens = place.shape[0]
    steps = tokens // CHUNK
    half = steps // 2
    own_spans = key_bucket.shape[0]
    rows = SPAN * (own_spans + 2)
    pay_rows = CHUNK // own_rows * (own_rows + PAD)
    once = pl.Buffered(1)

    def whole(shape):
        return pl.BlockSpec(shape, lambda step: (0, 0), pipeline_mode=once)

    sorted_rows = jax.ShapeDtypeStruct((rows, HEADD), bf)
    return pl.pallas_call(
        functools.partial(forward_kernel, own_rows, steps),
        grid=(2 * steps + 1,),
        out_shape=(
            jax.ShapeDtypeStruct((half * pay_rows, HEADD), bf),
            jax.ShapeDtypeStruct((half * pay_rows, HEADD), bf),
            sorted_rows,
            sorted_rows,
            sorted_rows,
            jax.ShapeDtypeStruct((own_spans * SPAN, 2 * SPAN), bf),
            jax.ShapeDtypeStruct((tokens // TOKB, TOKB), f32),
        ),
        in_specs=[
            pl.BlockSpec(memory_space=pltpu.SMEM),
            pl.BlockSpec(memory_space=pltpu.SMEM),
            pl.BlockSpec(memory_space=pltpu.SMEM),
            whole(key_bucket.shape),
            part_spec((CHUNK, 2 * HEADD), 0, half),
            part_spec((CHUNK, 2 * HEADD), half, half),
        ],
        out_specs=(
            part_spec((pay_rows, HEADD), steps + 1, half),
            part_spec((pay_rows, HEADD), steps + 1 + half, half),
            whole((rows, HEADD)),
            whole((rows, HEADD)),
            whole((rows, HEADD)),
            whole((own_spans * SPAN, 2 * SPAN)),
            part_spec((CHUNK // TOKB, TOKB), steps + 1, steps),
        ),
        scratch_shapes=[pltpu.VMEM((rows, HEADD), f32)] * 2 + [pltpu.VMEM((TOKB, HEADD), f32)] * 2,
        compiler_params=pltpu.CompilerParams(vmem_limit_bytes=VMEM_LIMIT),
        name="attend_forward",
        cost_estimate=takes(35),
    )(in_table, out_table, place, key_bucket, own, peer)


def backward_kernel(
    own_rows,
    load_steps,
    table_ref,
    place_ref,
    pay_own_ref,
    pay_peer_ref,
    sum_ref,
    query_ref,
    key_ref,
    value_ref,
    prob_ref,
    out_own_ref,
    out_peer_ref,
    wide_a,
    wide_b,
    wide_c,
    stage_a,
    stage_b,
):
    step = pl.program_id(0)
    own_spans = prob_ref.shape[0] // SPAN
    tail = SPAN * (own_spans + 1)

    @pl.when(step == 0)
    def _():
        fill(wide_a, 0.0)
        fill(wide_b, 0.0)

    def scatter_from(pay_ref):
        blocks = own_rows // TOKB
        eye = diagonal()
        ones = jnp.ones((2 * TOKB, TOKB), bf)

        def scatter(chunk, carry):
            first = chunk * (own_rows + PAD)
            extra = pay_ref[aligned(first + own_rows, PAD, PAD), :].astype(f32)
            for block in range(blocks):
                share = sum_ref[pl.ds(chunk * blocks + block, 1), :]
                share = share / extra[blocks + block : blocks + block + 1, :]
                rows = pay_ref[aligned(first + block * TOKB, TOKB, PAD), :].astype(f32)
                stage_a[...] = rows * lanes(share, eye, ones)
                stage_b[...] = lanes(share * extra[block : block + 1, :], eye, ones)
                start = step * CHUNK + chunk * own_rows + block * TOKB
                start = chunk_start(table_ref, own_rows, start)
                for row in range(TOKB):
                    place = place_ref[start + row]
                    wide_a[pl.ds(place, 1), :] = stage_a[row : row + 1, :]
                    wide_b[pl.ds(place, 1), :] = stage_b[row : row + 1, :]
            return carry

        lax.fori_loop(0, CHUNK // own_rows, scatter, 0)

    pl.when(step < load_steps // 2)(lambda: scatter_from(pay_own_ref))
    pl.when((step >= load_steps // 2) & (step < load_steps))(lambda: scatter_from(pay_peer_ref))

    def pulled(query_low, d_query, d_keys):
        query = query_low.astype(f32)
        inverse = lax.rsqrt(
            jnp.sum(query * query, axis=-1, keepdims=True) * (1.0 / HEADD) + KEY_EPS
        )
        along = jnp.sum(query * d_keys, axis=-1, keepdims=True)
        scale = inverse * HEADD**-0.5
        return d_query + scale * d_keys - (scale * inverse * inverse * along * (1.0 / HEADD)) * query

    @pl.when(step == load_steps)
    def _():
        for ref in (wide_a, wide_b, wide_c):
            ref[:SPAN, :] = jnp.zeros((SPAN, HEADD), f32)
        zero = jnp.zeros((SPAN, HEADD), bf)

        def spans(group, carry):
            first = group * (UNROLL * SPAN)
            prev = aligned(first, SPAN)
            own = aligned(first, UNROLL * SPAN)
            here = aligned(first + SPAN, UNROLL * SPAN)
            around = aligned(first, (UNROLL + 1) * SPAN)
            query = query_ref[around, :]
            keys = key_ref[around, :]
            values = value_ref[around, :]
            probs = prob_ref[own, :]
            d_out = wide_a[here, :].astype(bf)
            delta = wide_b[here, :]
            d_query = [wide_a[prev, :]]
            d_keys = [wide_b[prev, :]]
            d_values = [wide_c[prev, :]]
            for span in range(UNROLL):
                mine = slice(span * SPAN, (span + 1) * SPAN)
                after = slice((span + 1) * SPAN, (span + 2) * SPAN)
                both = slice(span * SPAN, (span + 2) * SPAN)
                d_probs = through(d_out[mine], values[both])
                prob = probs[mine]
                d_scores = (prob.astype(f32) * (d_probs - delta[mine])).astype(bf)
                d_query.append(product(d_scores, keys[both]))
                right = jnp.concatenate(
                    [
                        jnp.concatenate([query[after], zero], axis=1),
                        jnp.concatenate([zero, d_out[mine]], axis=1),
                    ],
                    axis=0,
                )
                pair = against(jnp.concatenate([d_scores, prob], axis=0), right)
                d_keys[-1] = d_keys[-1] + pair[:SPAN, :HEADD]
                d_values[-1] = d_values[-1] + pair[:SPAN, HEADD:]
                d_keys.append(pair[SPAN:, :HEADD])
                d_values.append(pair[SPAN:, HEADD:])
            for span in range(UNROLL + 1):
                at = aligned(first + span * SPAN, SPAN)
                wide_c[at, :] = d_values[span]
                if span < UNROLL:
                    rows = slice(span * SPAN, (span + 1) * SPAN)
                    wide_a[at, :] = pulled(query[rows], d_query[span], d_keys[span])
                else:
                    wide_a[at, :] = d_query[span]
                    wide_b[at, :] = d_keys[span]
            return carry

        lax.fori_loop(0, own_spans // UNROLL, spans, 0)
        last = pl.ds(tail - SPAN, SPAN)
        wide_a[last, :] = pulled(query_ref[last, :], wide_a[last, :], wide_b[last, :])
        wide_a[pl.ds(tail, SPAN), :] = jnp.zeros((SPAN, HEADD), f32)
        wide_c[pl.ds(tail, SPAN), :] = jnp.zeros((SPAN, HEADD), f32)

    def collect_to(out_ref):
        offset = (step - load_steps - 1) * CHUNK

        def collect(block, carry):
            start = chunk_start(table_ref, own_rows, offset + block * TOKB)
            for row in range(TOKB):
                place = place_ref[start + row]
                stage_a[row : row + 1, :] = wide_a[pl.ds(place, 1), :]
                stage_b[row : row + 1, :] = wide_c[pl.ds(place, 1), :]
            here = aligned(block * TOKB, TOKB, TOKB)
            out_ref[here, :HEADD] = stage_a[...].astype(bf)
            out_ref[here, HEADD:] = stage_b[...].astype(bf)
            return carry

        lax.fori_loop(0, CHUNK // TOKB, collect, 0)

    half = load_steps + 1 + load_steps // 2
    pl.when((step > load_steps) & (step < half))(lambda: collect_to(out_own_ref))
    pl.when(step >= half)(lambda: collect_to(out_peer_ref))


def attend_backward(out_table, place, pay_own, pay_peer, sums, query, keys, values, probs, own_rows):
    tokens = place.shape[0]
    steps = tokens // CHUNK
    half = steps // 2
    rows = query.shape[0]
    pay_rows = CHUNK // own_rows * (own_rows + PAD)
    once = pl.Buffered(1)

    def whole(shape):
        return pl.BlockSpec(shape, lambda step: (0, 0), pipeline_mode=once)

    out_half = jax.ShapeDtypeStruct((tokens // 2, 2 * HEADD), bf)
    return pl.pallas_call(
        functools.partial(backward_kernel, own_rows, steps),
        grid=(2 * steps + 1,),
        out_shape=(out_half, out_half),
        in_specs=[
            pl.BlockSpec(memory_space=pltpu.SMEM),
            pl.BlockSpec(memory_space=pltpu.SMEM),
            part_spec((pay_rows, HEADD), 0, half),
            part_spec((pay_rows, HEADD), half, half),
            part_spec((CHUNK // TOKB, TOKB), 0, steps),
            whole((rows, HEADD)),
            whole((rows, HEADD)),
            whole((rows, HEADD)),
            whole(probs.shape),
        ],
        out_specs=(
            part_spec((CHUNK, 2 * HEADD), steps + 1, half),
            part_spec((CHUNK, 2 * HEADD), steps + 1 + half, half),
        ),
        scratch_shapes=[pltpu.VMEM((rows, HEADD), f32)] * 3 + [pltpu.VMEM((TOKB, HEADD), f32)] * 2,
        compiler_params=pltpu.CompilerParams(vmem_limit_bytes=VMEM_LIMIT),
        name="attend_backward",
        cost_estimate=takes(44),
    )(out_table, place, pay_own, pay_peer, sums, query, keys, values, probs)


def shard_spec(shards, number):
    block = (shards.shape[0], 1) + shards.shape[2:]
    return pl.BlockSpec(block, lambda *_: (0, number, 0, 0), pipeline_mode=pl.Buffered(1))


def whole_weight(ref):
    value = ref[...]
    return value.reshape(-1, value.shape[-1])


def feed_kernel(
    own_ref, peer_ref, grad_own_ref, grad_peer_ref, inner_weight_ref, outer_weight_ref,
    row_ref, grad_ref, hidden_ref, inner_ref,
    back_own_ref, back_peer_ref, second_own_ref, second_peer_ref,
):
    step = pl.program_id(0)

    @pl.when(step == 0)
    def _():
        row_ref[...] = own_ref[...]
        grad_ref[...] = grad_own_ref[...]

    @pl.when(step == 1)
    def _():
        row_ref[...] = peer_ref[...]
        grad_ref[...] = grad_peer_ref[...]

    weight = whole_weight(inner_weight_ref)
    outer_weight = whole_weight(outer_weight_ref)
    act = product(row_ref[...], weight)
    size = jnp.abs(act)
    bell = jnp.exp(act * act * -0.5)
    near = 1.0 / (1.0 + size * (0.3275911 * 0.5**0.5))
    tail = near * (0.254829592 + near * (-0.284496736 + near * (
        1.421413741 + near * (-1.453152027 + near * 1.061405429))))
    tail = tail * bell * 0.5
    normal = jnp.where(act >= 0.0, 1.0 - tail, tail)
    hidden = (act * normal).astype(bf)
    hidden_ref[...] = hidden
    slope = normal + act * bell * (2.0 * math.pi) ** -0.5
    inner = (through(grad_ref[...], outer_weight) * slope).astype(bf)
    inner_ref[...] = inner
    back = through(inner, weight).astype(bf)
    second = product(hidden, outer_weight).astype(bf)

    @pl.when(step == 0)
    def _():
        back_own_ref[...] = back
        second_own_ref[...] = second

    @pl.when(step == 1)
    def _():
        back_peer_ref[...] = back
        second_peer_ref[...] = second


def feed_forward(own, peer, grad_own, grad_peer, shards):
    count, width = own.shape
    units = shards.shape[3]

    def part(columns):
        return pl.BlockSpec((count, columns), lambda i: (i, 0))

    whole = pl.BlockSpec((count, width), lambda i: (0, 0), pipeline_mode=pl.Buffered(1))
    by_width = jax.ShapeDtypeStruct((2 * count, width), bf)
    by_units = jax.ShapeDtypeStruct((2 * count, units), bf)
    half = jax.ShapeDtypeStruct((count, width), bf)
    return pl.pallas_call(
        feed_kernel,
        grid=(2,),
        out_shape=(by_width, by_width, by_units, by_units, half, half, half, half),
        in_specs=[whole] * 4 + [shard_spec(shards, 0), shard_spec(shards, 1)],
        out_specs=(
            part(width), part(width), part(units), part(units), whole, whole, whole, whole
        ),
        compiler_params=pltpu.CompilerParams(vmem_limit_bytes=VMEM_LIMIT),
        name="feed_forward",
        cost_estimate=takes(9),
    )(own, peer, grad_own, grad_peer, shards, shards)


def mix_kernel(
    parts_ref, weight_ref, first_ref, gain_ref, shift_ref,
    mixed_ref, low_ref, sum_ref, unit_ref, scale_ref, feed_ref,
):
    heads, rows = parts_ref.shape[0], first_ref.shape[0]
    eye = diagonal()
    ones = jnp.ones((2 * TOKB, TOKB), bf)
    for head in range(heads):
        columns = slice(head * HEADD, (head + 1) * HEADD)
        for block in range(rows // TOKB):
            here = slice(block * TOKB, (block + 1) * TOKB)
            sums = parts_ref[head, rows : rows + PAD, :].astype(f32)[block : block + 1]
            mixed = parts_ref[head, here, :].astype(f32) / lanes(sums, eye, ones)
            mixed_ref[here, columns] = mixed
            low_ref[here, columns] = mixed.astype(bf)
    total = first_ref[...].astype(f32) + product(low_ref[...], whole_weight(weight_ref))
    sum_ref[...] = total.astype(bf)
    centre = total - jnp.mean(total, axis=-1, keepdims=True)
    scale = lax.rsqrt(jnp.mean(centre * centre, axis=-1, keepdims=True) + NORM_EPS)
    unit = centre * scale
    unit_ref[...] = unit
    scale_ref[...] = scale
    feed_ref[...] = (unit * gain_ref[...] + shift_ref[...]).astype(bf)


def mix_rows(parts, shards, first_half, gain, shift):
    rows, width = first_half.shape
    vm = pl.BlockSpec(memory_space=pltpu.VMEM)
    wide, low = jax.ShapeDtypeStruct((rows, width), f32), jax.ShapeDtypeStruct((rows, width), bf)
    return pl.pallas_call(
        mix_kernel,
        out_shape=(wide, low, low, wide, jax.ShapeDtypeStruct((rows, 1), f32), low),
        grid=(1,),
        in_specs=[vm, shard_spec(shards, 2), vm, vm, vm],
        out_specs=(vm,) * 6,
        compiler_params=pltpu.CompilerParams(vmem_limit_bytes=VMEM_LIMIT),
        name="mix_rows",
        cost_estimate=takes(5),
    )(parts, shards, first_half, gain, shift)


def carry_kernel(
    near_ref, far_ref, gain_ref, unit_ref, scale_ref, grad_ref, weight_ref, mixed_ref, parts_ref,
    carry_ref, pay_ref, wide_ref,
):
    heads, rows = parts_ref.shape[0], grad_ref.shape[0]
    blocks = rows // TOKB
    back = near_ref[...].astype(f32) + far_ref[...].astype(f32)
    unit = unit_ref[...]
    gain_sum = jnp.sum(back * unit, axis=0, keepdims=True)
    shift_sum = jnp.sum(back, axis=0, keepdims=True)
    grad = back * gain_ref[...]
    along = jnp.mean(grad * unit, axis=-1, keepdims=True)
    grad = scale_ref[...] * (grad - jnp.mean(grad, axis=-1, keepdims=True) - unit * along)
    carry_ref[...] = (grad_ref[...].astype(f32) + grad).astype(bf)
    wide_ref[...] = through(carry_ref[...], whole_weight(weight_ref))
    eye = diagonal()
    pad_rows = lax.broadcasted_iota(jnp.int32, (PAD, TOKB), 0)
    for head in range(heads):
        columns = slice(head * HEADD, (head + 1) * HEADD)
        sums = parts_ref[head, rows : rows + PAD, :].astype(f32)
        tails = jnp.zeros((PAD, TOKB), f32)
        for block in range(blocks):
            here = slice(block * TOKB, (block + 1) * TOKB)
            wide = wide_ref[here, columns]
            pay_ref[head, here, :] = wide.astype(bf)
            dot = jnp.sum(wide * mixed_ref[here, columns], axis=-1, keepdims=True)
            packed = jnp.sum(jnp.where(eye, dot, 0.0), axis=0, keepdims=True)
            tails = jnp.where(pad_rows == block, packed, tails)
            tails = jnp.where(pad_rows == blocks + block, sums[block : block + 1], tails)
        tails = jnp.where(pad_rows == 2 * blocks, gain_sum[:, columns], tails)
        tails = jnp.where(pad_rows == 2 * blocks + 1, shift_sum[:, columns], tails)
        pay_ref[head, rows : rows + PAD, :] = tails.astype(bf)


def carry_rows(near, far, gain, unit, scale, first_grad, shards, mixed, parts):
    rows, width = near.shape
    vm = pl.BlockSpec(memory_space=pltpu.VMEM)
    return pl.pallas_call(
        carry_kernel,
        out_shape=(
            jax.ShapeDtypeStruct((rows, width), bf),
            jax.ShapeDtypeStruct(parts.shape, bf),
        ),
        grid=(1,),
        in_specs=[vm] * 6 + [shard_spec(shards, 2)] + [vm] * 2,
        out_specs=(vm,) * 2,
        scratch_shapes=[pltpu.VMEM((rows, width), f32)],
        compiler_params=pltpu.CompilerParams(vmem_limit_bytes=VMEM_LIMIT),
        name="carry_rows",
        cost_estimate=takes(5),
    )(near, far, gain, unit, scale, first_grad, shards, mixed, parts)


def add_kernel(left_ref, right_ref, out_ref):
    total = left_ref[...].astype(f32) + right_ref[...].astype(f32)
    out_ref[...] = total.astype(out_ref.dtype)


def add_rows(left, right):
    shape = left.shape
    left, right = left.reshape(-1, shape[-1]), right.reshape(-1, shape[-1])
    step = math.gcd(left.shape[0], 1024)
    spec = pl.BlockSpec((step, shape[-1]), lambda i: (i, 0))
    out = pl.pallas_call(
        add_kernel,
        grid=(left.shape[0] // step,),
        out_shape=jax.ShapeDtypeStruct(left.shape, left.dtype),
        in_specs=[spec, spec],
        out_specs=spec,
        name="add_rows",
        cost_estimate=takes(3),
    )(left, right)
    return out.reshape(shape)


def last_kernel(
    back_ref, weight_ref, gain_ref, unit_ref, scale_ref, grad_ref, out_ref, query_ref, value_ref,
):
    for head in range(back_ref.shape[0]):
        columns = slice(head * HEADD, (head + 1) * HEADD)
        query_ref[:, columns] = back_ref[head, :, :HEADD]
        value_ref[:, columns] = back_ref[head, :, HEADD:]
    total = through(query_ref[...], weight_ref[0]) + through(value_ref[...], weight_ref[1])
    grad = total * gain_ref[...]
    unit = unit_ref[...]
    along = jnp.mean(grad * unit, axis=-1, keepdims=True)
    centred = grad - jnp.mean(grad, axis=-1, keepdims=True) - unit * along
    out_ref[...] = (grad_ref[...].astype(f32) + scale_ref[...] * centred).astype(bf)


def last_rows(own_back, weights, gain, unit, scale, second_grad):
    rows, width = unit.shape
    vm = pl.BlockSpec(memory_space=pltpu.VMEM)
    return pl.pallas_call(
        last_kernel,
        out_shape=jax.ShapeDtypeStruct((rows, width), bf),
        in_specs=[vm] * 6,
        out_specs=vm,
        scratch_shapes=[pltpu.VMEM((rows, width), bf)] * 2,
        compiler_params=pltpu.CompilerParams(vmem_limit_bytes=VMEM_LIMIT),
        name="last_rows",
        cost_estimate=takes(6),
    )(own_back, weights, gain, unit, scale, second_grad)


def weight_kernel(order_ref, back_ref, *refs):
    pieces, (part_ref, column_ref) = refs[:-2], refs[-2:]
    half = pieces[-1].shape[0]
    total = None
    for number, piece in enumerate(pieces[:-1]):
        back = back_ref[order_ref[number]]
        if piece.shape[0] == half:
            term = against(piece[...], back[:half]) + against(pieces[-1][...], back[half:])
        else:
            term = against(piece[...], back)
        total = term if total is None else total + term
    part_ref[...] = total
    columns = jnp.sum(back_ref[...].astype(f32), axis=(0, 1), keepdims=True)[0]
    column_ref[...] = jnp.broadcast_to(columns, column_ref.shape)


def weight_part(order, back, pieces):
    width = pieces[0].shape[1]
    vm = pl.BlockSpec(memory_space=pltpu.VMEM)
    return pl.pallas_call(
        weight_kernel,
        out_shape=(
            jax.ShapeDtypeStruct((width, back.shape[2]), f32),
            jax.ShapeDtypeStruct((8, back.shape[2]), f32),
        ),
        in_specs=[pl.BlockSpec(memory_space=pltpu.SMEM)] + [vm] * (1 + len(pieces)),
        out_specs=(vm, vm),
        compiler_params=pltpu.CompilerParams(vmem_limit_bytes=VMEM_LIMIT),
        name="weight_part",
        cost_estimate=takes(5),
    )(order, back, *pieces)


ALL = ("hd", "kk", "ry", "rc")
SEQ = ("hd", "kk")
ROUND = ("ry", "rc")
SWAP = [(0, 1), (1, 0)]
RING = (0, 2, 4, 6, 7, 5, 3, 1)
UP = [(RING[i], RING[(i + 1) % HEADS]) for i in range(HEADS)]
DOWN = [(RING[(i + 1) % HEADS], RING[i]) for i in range(HEADS)]
STEPS = ((0, -1, 1, -2, 2), (-3, 3, 4))
BUCKETS = 32


def normalised(values):
    centre = values - jnp.mean(values, axis=-1, keepdims=True)
    spread = jnp.mean(centre * centre, axis=-1, keepdims=True)
    inverse = lax.rsqrt(spread + NORM_EPS)
    return centre * inverse, inverse


def norm_back(unit, inverse, grad):
    along = jnp.mean(grad * unit, axis=-1, keepdims=True)
    return inverse * (grad - jnp.mean(grad, axis=-1, keepdims=True) - unit * along)


def together(*values):
    return lax.optimization_barrier(values)


def exchange(parts, axes="hd"):
    return lax.all_to_all(parts, axes, split_axis=0, concat_axis=0, tiled=True)


def swapped(value, axis):
    return lax.ppermute(value, axis, SWAP)


def over_groups(mine):
    if lax.axis_size("kk") > 1:
        return lax.all_gather(mine, "kk", axis=0, tiled=False)
    return mine[None]


def sum_groups(parts):
    if lax.axis_size("kk") > 1:
        return lax.psum_scatter(parts, "kk", scatter_dimension=0, tiled=False)
    return parts[0]


def pair_sum(keep, give, axis):
    return (keep.astype(f32) + swapped(give, axis).astype(f32)).astype(bf)


def spread_pair(mine):
    pair = jnp.stack([mine, swapped(mine, "ry")])
    return pair, swapped(pair, "rc")


def chip_pair(mine):
    return jnp.concatenate([mine, swapped(mine, "rc")], axis=0)


def sum_pair(own, peer):
    total = pair_sum(own, peer, "rc")
    return pair_sum(total[0], total[1], "ry")


def ordered(mine, axis, dim):
    return pair_order(mine, swapped(mine, axis), axis, dim)


def pair_order(mine, got, axis, dim):
    is_first = lax.axis_index(axis) == 0
    return jnp.stack([jnp.where(is_first, mine, got), jnp.where(is_first, got, mine)], axis=dim)


def scattered(parts, axis, dim):
    me = lax.axis_index(axis)
    keep = lax.dynamic_index_in_dim(parts, me, dim, keepdims=False)
    give = lax.dynamic_index_in_dim(parts, 1 - me, dim, keepdims=False)
    return pair_sum(keep, give, axis)


def ring_step(up, down):
    return lax.ppermute(up, "hd", UP), lax.ppermute(down, "hd", DOWN)


def ring_order():
    position = jnp.array([RING.index(i) for i in range(HEADS)], jnp.int32)[lax.axis_index("hd")]
    offsets = jnp.array([o for step in STEPS for o in step], jnp.int32)
    return jnp.array(RING, jnp.int32)[(position + offsets) % HEADS]


def wide_scattered(parts, axis, dim):
    me = lax.axis_index(axis)
    keep = lax.dynamic_index_in_dim(parts, me, dim, keepdims=False)
    return keep + swapped(lax.dynamic_index_in_dim(parts, 1 - me, dim, keepdims=False), axis)


def traded(parts, axis, dim):
    me = lax.axis_index(axis)
    got = swapped(lax.dynamic_index_in_dim(parts, 1 - me, dim, keepdims=True), axis)
    return lax.dynamic_update_slice_in_dim(parts, got, 1 - me, dim)


def index_codes(slots, buckets, slot_rows):
    first_bucket = slots // slot_rows * BUCKETS
    return jnp.concatenate([slots // 256, slots % 256, buckets - first_bucket]).astype(bf)


def sorted_layout(codes, slot_rows, own_spans):
    heads = lax.axis_size("hd")
    codes = codes.astype(jnp.int32)
    slot_grid = codes[:, :, 0] * 256 + codes[:, :, 1]
    before = lax.axis_index("kk") * heads - 1
    target = slot_grid // slot_rows
    block = target - before
    local_place = slot_grid - target * slot_rows
    category = (block * (BUCKETS + 1) + codes[:, :, 2]).reshape(1, -1)
    categories = jnp.arange((heads + 1) * (BUCKETS + 1), dtype=jnp.int32)[:, None]
    members = jnp.sum((category == categories).astype(jnp.int32), axis=1)
    members = members.reshape(heads + 1, BUCKETS + 1)
    counts = jnp.sum(members, axis=1)
    last_start = jnp.maximum(counts[:1] - 1, 0) // SPAN * SPAN
    span_counts = -(-counts[1:] // SPAN)
    own_start = (1 + jnp.cumsum(span_counts) - span_counts) * SPAN
    start = jnp.concatenate([-last_start, own_start])
    lowest = jnp.concatenate([last_start, jnp.zeros_like(own_start)])
    dump = (own_spans + 1) * SPAN
    numbers = jnp.arange(heads + 1, dtype=jnp.int32)[:, None]
    local_place, block = local_place.reshape(1, -1), block.reshape(1, -1)
    here = (block == numbers) & (local_place >= lowest[:, None])
    place = jnp.sum(jnp.where(here, local_place + start[:, None] - dump, 0), axis=0) + dump
    ends = (start[:, None] + jnp.cumsum(members, axis=1)).reshape(-1, 1)
    rows = jnp.arange(dump, dtype=jnp.int32)[None, :]
    passed = jnp.sum((ends <= rows).astype(jnp.int32), axis=0)
    row_block = jnp.sum((own_start[:, None] <= rows).astype(jnp.int32), axis=0)
    local_bucket = passed - row_block * (BUCKETS + 1)
    row_bucket = jnp.where(
        local_bucket <= BUCKETS, (before + row_block) * BUCKETS + local_bucket, -1
    )
    span_bucket = row_bucket.astype(f32).reshape(-1, SPAN)
    return place, jnp.concatenate([span_bucket[:-1], span_bucket[1:]], axis=1)


def chunk_tables(groups):
    order = ring_order()
    flip = jnp.stack([lax.axis_index("rc"), lax.axis_index("ry")])

    def number(dc, dy, kk, hd):
        return ((hd * groups + kk) * 2 + (dy ^ flip[1])) * 2 + (dc ^ flip[0])

    def column(values):
        return jnp.array(values, jnp.int32)

    offsets = [list(range(sum(map(len, STEPS[:i])), sum(map(len, STEPS[: i + 1])))) for i in range(len(STEPS))]
    coming = [
        (dc, dy, kk, at)
        for dc in range(2)
        for part in offsets
        for dy in range(2)
        for kk in range(groups)
        for at in part
    ]
    going = [
        (dc, dy, kk, hd)
        for dc in range(2)
        for dy in range(2)
        for kk in range(groups)
        for hd in range(HEADS)
    ]
    dc, dy, kk, at = map(column, zip(*coming))
    in_table = number(dc, dy, kk, order[at])
    return in_table, number(*map(column, zip(*going)))


def per_device(
    first_half,
    second_half,
    qk_weight,
    value_weight,
    output_weight,
    inner_weight,
    outer_weight,
    attn_gain,
    attn_shift,
    ffn_gain,
    ffn_shift,
    buckets,
    slots,
    first_grad,
    second_grad,
):
    heads = lax.axis_size("hd")
    groups = lax.axis_size("kk")
    seq_count = heads * groups
    round_count = lax.axis_size("ry") * lax.axis_size("rc")
    device_count = seq_count * round_count
    own_rows, model_width = first_half.shape
    weight_rows, hidden_width = inner_weight.shape
    group_rows = own_rows * round_count
    slot_rows = 2 * group_rows
    tokens = group_rows * seq_count
    own_spans = min((tokens + (SPAN - 1) * heads) // SPAN, heads * slot_rows // SPAN)
    own_spans = -(-own_spans // UNROLL) * UNROLL
    piece = hidden_width // device_count
    blocks = own_rows // TOKB
    both = 2 * HEADD

    second_in = second_half.astype(f32)
    unit, unit_scale = normalised(second_in)
    unit_low = unit.astype(bf)
    vectors = jnp.stack([attn_gain, attn_shift, ffn_gain, ffn_shift], axis=1)
    vectors = jnp.pad(vectors, ((0, 0), (0, HEADD - 4)))
    wide = both + HEADD
    head_shard = jnp.concatenate(
        [
            qk_weight.reshape(weight_rows, heads, HEADD),
            value_weight.reshape(weight_rows, heads, HEADD),
            jnp.broadcast_to(vectors[:, None], (weight_rows, heads, HEADD)),
        ],
        axis=2,
    )
    code_rows = 3 * group_rows // wide
    codes = index_codes(slots, buckets, slot_rows).reshape(code_rows, wide)
    codes = jnp.pad(codes, ((0, -code_rows % PAD), (0, 0)))
    codes = jnp.broadcast_to(codes[None], (heads,) + codes.shape)
    starter = jnp.concatenate([jnp.transpose(head_shard, (1, 0, 2)), codes], axis=1)

    inner_split = inner_weight.reshape(weight_rows, seq_count, round_count, piece)
    inner_split = jnp.transpose(inner_split, (2, 0, 1, 3)).reshape(2, 2, weight_rows, -1)
    unit_low, starter = together(unit_low, starter)
    ring = [(unit_low,)]
    up, down = ring_step(unit_low, unit_low)
    up, down, starter, inner_split = together(up, down, exchange(starter), inner_split)
    ring.append((up, down))

    up, down = ring_step(up, down)
    starter = jnp.transpose(over_groups(starter), (1, 0, 2, 3))
    codes = starter[:, :, weight_rows : weight_rows + code_rows].reshape(heads, groups, 3, -1)
    head_weight = ordered(ordered(starter[:, :, :weight_rows], "ry", 2), "rc", 3)
    head_weight = head_weight.reshape(model_width, wide)
    vectors_full = head_weight[:, both : both + 4].astype(f32)
    attn_gain_col, attn_shift_col = vectors_full[:, :1], vectors_full[:, 1:2]
    ffn_gain_row, ffn_shift_row = vectors_full[:, 2][None], vectors_full[:, 3][None]
    head_float = head_weight[:, :both].astype(f32)
    head_scaled = (head_float * attn_gain_col).astype(bf)
    head_offset = jnp.sum(head_float * attn_shift_col, axis=0, keepdims=True)
    inner_rows = traded(traded(inner_split, "rc", 1), "ry", 0)
    cut = round_count * weight_rows
    output_rows = ordered(ordered(output_weight, "rc", 0), "ry", 0).reshape(cut, model_width)
    shard = jnp.stack([inner_rows.reshape(cut, -1), outer_weight, output_rows])
    up, down, head_scaled, head_offset, shard, second_later = together(
        up, down, head_scaled, head_offset, shard, second_grad
    )
    ring.append((up, down))

    def head_part(parts):
        rows = [product(part, head_scaled) + head_offset for part in parts]
        return over_groups(jnp.concatenate(rows, axis=0).astype(bf))

    up, down = ring_step(up, down)
    first_heads = head_part([part for step in ring for part in step])
    up, down, first_heads, codes, shard = together(up, down, first_heads, codes, shard)
    ring.append((up, down))

    half = own_rows // 2
    up, down = ring_step(up[:half], down[half:])
    ring.append((up, down))
    last_heads = head_part(ring[3] + ring[4])
    head_own = []
    for rows in (first_heads, last_heads):
        head_own += [rows, swapped(rows, "ry")]
    head_own = jnp.concatenate([part.reshape(-1, both) for part in head_own], axis=0)
    place, key_bucket = sorted_layout(codes, slot_rows, own_spans)
    in_table, out_table = chunk_tables(groups)
    head_own, place, key_bucket, in_table, out_table = together(
        head_own, place, key_bucket, in_table, out_table
    )
    head_peer = swapped(head_own, "rc")

    grad_peer = swapped(second_later, "rc")
    grad_far = swapped(second_later, "ry")
    grad_last = swapped(grad_far, "rc")
    shards = lax.all_gather(shard, SEQ, axis=0, tiled=False)

    payload_own, payload_peer, sorted_q, sorted_k, sorted_v, probs, token_sums = attend_forward(
        in_table,
        out_table,
        place,
        key_bucket,
        head_own,
        head_peer,
        own_rows,
    )
    packed = (2, groups, heads, own_rows + PAD, HEADD)
    head_sums = sum_pair(payload_own.reshape(packed), payload_peer.reshape(packed))
    mixed_parts = exchange(sum_groups(head_sums))
    mixed_parts, shards = together(mixed_parts, shards)
    mixed, mixed_low, first_sum, ffn_unit, ffn_scale, ffn_low = mix_rows(
        mixed_parts, shards, first_half, ffn_gain_row, ffn_shift_row
    )
    ffn_low, qkv_rows = together(ffn_low, jnp.stack([qk_weight, value_weight]))
    qkv_rows = exchange(jnp.broadcast_to(qkv_rows[None], (heads,) + qkv_rows.shape))
    ffn_far = swapped(ffn_low, "ry")
    pair = feed_forward(ffn_low, swapped(ffn_low, "rc"), second_later, grad_peer, shards)
    ffn_far, pair = together(ffn_far, pair)
    far = feed_forward(ffn_far, swapped(ffn_far, "rc"), grad_far, grad_last, shards)
    pair, far = together(pair, far)
    ffn_pair, grad_pair, hidden_pair, inner_pair, *back_pair = pair
    ffn_far, grad_far, hidden_far, inner_far, *back_far = far
    far_sum = swapped(pair_sum(back_far[0], back_far[1], "rc"), "ry")
    near_sum = pair_sum(back_pair[0], back_pair[1], "rc")
    second_far = pair_sum(back_far[2], back_far[3], "rc")
    second_pair = pair_sum(back_pair[2], back_pair[3], "rc")
    outer_part = (against(hidden_pair, grad_pair) + against(hidden_far, grad_far)).astype(bf)
    inner_part = (against(ffn_pair, inner_pair) + against(ffn_far, inner_far)).astype(bf)
    part_sums = jnp.stack(
        [
            inner_part.reshape(seq_count, cut, -1),
            outer_part.reshape(seq_count, -1, model_width),
        ],
        axis=1,
    )
    near_sum, far_sum, part_sums, qkv_rows = together(near_sum, far_sum, part_sums, qkv_rows)
    part_grads = lax.psum_scatter(part_sums, SEQ, scatter_dimension=0, tiled=False)
    carry_low, back_parts = carry_rows(
        near_sum,
        far_sum,
        ffn_gain_row,
        ffn_unit,
        ffn_scale,
        first_grad,
        shards,
        mixed,
        mixed_parts,
    )
    back_parts = exchange(back_parts)
    output_part = against(mixed_low, carry_low).astype(bf)
    output_part = output_part.reshape(heads, groups, 2, 2, weight_rows, model_width)
    output_part = scattered(scattered(output_part, "rc", 3), "ry", 2)
    back_parts, output_part, second_pair, second_far, qkv_rows = together(
        back_parts, output_part, second_pair, second_far, qkv_rows
    )
    qkv_rows = jnp.transpose(over_groups(qkv_rows), (2, 1, 0, 3, 4))
    back_own, back_peer = spread_pair(over_groups(back_parts))
    back_own, second_far, qkv_rows = together(back_own, second_far, qkv_rows)
    second_far = swapped(second_far, "ry")
    qkv_got = swapped(qkv_rows, "ry")
    query_value_own, query_value_peer = attend_backward(
        out_table,
        place,
        back_own.reshape(-1, HEADD),
        back_peer.reshape(-1, HEADD),
        token_sums,
        sorted_q,
        sorted_k,
        sorted_v,
        probs,
        own_rows,
    )
    vector_rows = back_parts[:, own_rows + 2 * blocks : own_rows + 2 * blocks + 2]
    packed = (2, groups, heads, own_rows, both)
    vector_rows = back_parts[:, own_rows + 2 * blocks : own_rows + 2 * blocks + 2]
    packed = (2, groups, heads, own_rows, both)
    query_value_peer, qkv_got, second_far = together(query_value_peer, qkv_got, second_far)
    second_sum = second_in + second_pair.astype(f32) + second_far.astype(f32)
    head_back = pair_sum(query_value_own.reshape(packed), query_value_peer.reshape(packed), "rc")
    head_back, output_part, vector_rows, qkv_rows, qkv_got = together(
        head_back, output_part, vector_rows, qkv_rows, qkv_got
    )
    qkv_rows = pair_order(qkv_rows, qkv_got, "ry", 3)
    qkv_full = ordered(qkv_rows, "rc", 4).reshape(2, model_width, model_width)
    output_rows = exchange(sum_groups(jnp.transpose(output_part, (1, 0, 2, 3))))
    head_got, output_rows, qkv_full = together(
        swapped(head_back[1], "ry"), output_rows, qkv_full
    )
    output_grad = jnp.sum(output_rows.astype(f32), axis=0)
    head_back = sum_groups(add_rows(head_back[0], head_got))
    own_back = exchange(head_back)
    vector_sums = jnp.sum(vector_rows.astype(f32), axis=0)
    if groups > 1:
        vector_sums = lax.psum_scatter(
            vector_sums.reshape(2, groups, -1), "kk", scatter_dimension=1, tiled=False
        )
    vector_sums = jnp.pad(
        vector_sums.reshape(2, 2, 2, weight_rows), ((0, 6), (0, 0), (0, 0), (0, HEADD - weight_rows))
    )
    pieces = [part for step in ring for part in step]
    qkv_part, col_part = weight_part(ring_order(), head_back, pieces)
    qkv_part = qkv_part.reshape(heads, groups, 2, 2, weight_rows, both)
    col_part = jnp.broadcast_to(col_part[0], (heads, groups, 2, 2, PAD, both))
    qkv_part = jnp.concatenate([qkv_part, col_part], axis=4).astype(bf)
    qkv_part = scattered(scattered(qkv_part, "rc", 3), "ry", 2)
    qkv_part = sum_groups(jnp.transpose(qkv_part, (1, 0, 2, 3)))
    outer_grad = part_grads[1].astype(f32)
    turned = part_grads[0].reshape(2, 2, weight_rows, -1)
    turned = traded(traded(turned, "ry", 0), "rc", 1)
    vector_sums = wide_scattered(wide_scattered(vector_sums, "rc", 2), "ry", 1)
    vector_grads = vector_sums[:2, :weight_rows]
    own_back, qkv_part, turned = together(own_back, qkv_part, turned)
    inner_cols = turned.reshape(round_count, weight_rows, seq_count, piece)
    inner_grad = jnp.transpose(inner_cols, (1, 2, 0, 3)).reshape(weight_rows, hidden_width)
    qkv_rows = exchange(qkv_part).astype(f32)
    qkv_rows = qkv_rows.reshape(heads, weight_rows + PAD, 2, HEADD)
    qkv_rows = jnp.transpose(qkv_rows, (2, 1, 0, 3)).reshape(2, weight_rows + PAD, model_width)
    unit_grads, col_sums = qkv_rows[:, :weight_rows], qkv_rows[:, weight_rows]
    own_weights = jnp.stack([qk_weight, value_weight]).astype(f32)
    gain_own = attn_gain.astype(f32)[:, None]
    shift_own = attn_shift.astype(f32)[:, None]
    qkv_grads = unit_grads * gain_own + shift_own * col_sums[:, None]
    attn_gain_grad = jnp.sum(own_weights * unit_grads, axis=(0, 2))
    attn_shift_grad = jnp.sum(own_weights * col_sums[:, None], axis=(0, 2))

    second_carry = last_rows(
        own_back, qkv_full, attn_gain_col.reshape(1, -1), unit, unit_scale, second_grad
    )

    return (
        first_sum,
        second_sum.astype(bf),
        carry_low,
        second_carry,
        qkv_grads[0],
        qkv_grads[1],
        output_grad,
        inner_grad.astype(f32),
        outer_grad,
        attn_gain_grad,
        attn_shift_grad,
        vector_grads[0],
        vector_grads[1],
    )


def solution(mesh):
    seq_count, round_count = mesh.devices.shape
    shape = (HEADS, seq_count // HEADS, round_count // 2, 2)
    split_mesh = Mesh(mesh.devices.reshape(shape), ALL)
    rows = P(ALL, None)
    vector = P(ALL)
    table = P(ROUND, SEQ)
    in_specs = (rows,) * 7 + (vector,) * 4 + (table,) * 2 + (rows,) * 2
    out_specs = (rows,) * 9 + (vector,) * 4
    return jax.shard_map(
        per_device, mesh=split_mesh, in_specs=in_specs, out_specs=out_specs, check_vma=False
    )
```

time: 1020 us -> 445 us (0.44)
  waiting for transfers between devices: 669 us -> 141 us
  blocking collectives: 52.8 us -> 0 us
  matrix products: 62.7 us -> 11.8 us
  Pallas kernels: 75.5 us -> 123 us
  starting transfers between devices: 25.4 us -> 69.5 us
  local copies, waits for them, and re-layouts: 58.7 us -> 28.4 us
    reduce_scatter x4 -> x1, waiting for transfers between devices: 452 us -> 0.01 us  [per_device(): lax.psum_scatter(part_sums, SEQ, scatter_dimension=0, tiled=False)]
    all_gather x4 -> x1, waiting for transfers between devices: 75.5 us -> 0.01 us  [per_device(): shards = lax.all_gather(shard, SEQ, axis=0, tiled=False)]
    all_to_all x2 -> x0, blocking collectives: 52.8 us -> none  [exchange(): return lax.all_to_all(parts, 'hd', split_axis=0, concat_axis=0, tiled=True)]
    pallas_call x0 -> x7, Pallas kernels: none -> 42.7 us  [the longest x2 20.6 us: feed_forward(): pl.pallas_call(feed_kernel, grid=(2,), out_shape=(by_width, by_width, by_...]
    scatter x1 -> x0, local copies, waits for them, and re-layouts: 30.5 us -> none  [per_device(): jnp.full((dump + SPAN,), -1, jnp.int32).at[place].set(bucket_row)]
    ppermute x8 -> x45, starting transfers between devices: 6.95 us -> 34.3 us  [the longest x37 24.8 us: swapped(): return lax.ppermute(value, axis, SWAP)]
    dot_general x3 -> x0, matrix products: 22.3 us -> none  [through(): lax.dot_general(left_side, right_side, (((1,), (1,)), ((), ())), preferre...]
    all_to_all x4 -> x7, starting transfers between devices: 17.7 us -> 34.9 us  [exchange(): return lax.all_to_all(parts, axes, split_axis=0, concat_axis=0, tiled=True)]
  transfers between devices with their start and end apart: 20 -> 54, of which waited for: 15 -> 25; matrix products, arithmetic and copies ran while one was open for 13% -> 16% of each run, Pallas kernels for 3% -> 27%
where the time goes in v3:
time: 445 us; the launch traced here: 436 us
  waiting for transfers between devices  141 us (32%)
  Pallas kernels  123 us (28%)
  starting transfers between devices  69.5 us (16%)
  other arithmetic  46.9 us (11%)
  local copies, waits for them, and re-layouts  28.4 us (6%)
  between operations  15.9 us (4%)
  matrix products  11.8 us (3%)
    ppermute x37, waiting for transfers between devices, swapped(): return lax.ppermute(value, axis, SWAP)  79.6 us
    all_to_all x7, waiting for transfers between devices, exchange(): return lax.all_to_all(parts, axes, split_axis=0, concat_axis=0, tiled=True)  45.1 us
    pallas_call x1, Pallas kernels, attend_backward(): pl.pallas_call(functools.partial(backward_kernel, own_rows, steps), grid=...  44.4 us
    pallas_call x1, Pallas kernels, attend_forward(): pl.pallas_call(functools.partial(forward_kernel, own_rows, steps), grid=(...  35.3 us
    all_to_all x7, starting transfers between devices, exchange(): return lax.all_to_all(parts, axes, split_axis=0, concat_axis=0, tiled=True)  34.9 us
    ppermute x37, starting transfers between devices, swapped(): return lax.ppermute(value, axis, SWAP)  24.8 us
    pallas_call x2, Pallas kernels, feed_forward(): pl.pallas_call(feed_kernel, grid=(2,), out_shape=(by_width, by_width, by_...  20.6 us
    ppermute x8, waiting for transfers between devices, ring_step(): return (lax.ppermute(up, 'hd', UP), lax.ppermute(down, 'hd', DOWN))  16.4 us
  transfers between devices with their start and end apart: 54, of which 25 were waited for; matrix products, arithmetic and copies ran while one was open for 16% of the time, Pallas kernels for 27%

profile of v3, /device:TPU:0, one launch (start us, length us, event | category | flops | bytes accessed | tf_op | source)
XLA Modules:
  0.0 436.2 jit_solution(1235832900531433392)
XLA Ops:
  13.1 2.3 fusion.3
  15.6 3.0 collective-permute-start.1
  19.5 6.2 %all-to-all-start = ((bf16[8,48,384]{2,1,0:T(8,128)(2,1)}), bf16[8,48,384]{2,1,0:T(8,128)(2,1)S(1)}, u32[]{:S(2)}, u32[]{:S(2)}) async-start(bf16[8,48,384]{2,1,0:T(8,128)(2,1)} %copy.92), calls=%async_computation | async-start | bytes 589824 | tf_op jit(solution)/shard_map/all_to_all | solution.py:744
  26.8 12.6 %all-to-all-done = bf16[8,48,384]{2,1,0:T(8,128)(2,1)S(1)} async-done(((bf16[8,48,384]{2,1,0:T(8,128)(2,1)}), bf16[8,48,384]{2,1,0:T(8,128)(2,1)S(1)}, u32[]{:S(2)}, u32[]{:S(2)}) %all-to-all-start) | async-done | bytes 294944 | tf_op jit(solution)/shard_map/all_to_all | solution.py:744
  43.9 6.2 %collective-permute-done.4 = bf16[8,1,32,384]{3,2,0,1:T(8,128)(2,1)S(1)} collective-permute-done((bf16[8,1,32,384]{3,2,0,1:T(8,128)(2,1)S(1)}, bf16[8,1,32,384]{3,2,0,1:T(8,128)(2,1)S(1)}, u32[]{:S(2)}, u32[]{:S(2)}) %collective-permute-start.4) | collective-permute-done | bytes 196640 | tf_op jit(solution)/shard_map/ppermute | solution.py:748
  57.9 7.6 %collective-permute-done.2.refs_3_ = bf16[256,1024]{1,0:T(8,128)(2,1)} collective-permute-done((bf16[256,1024]{1,0:T(8,128)(2,1)S(1)}, bf16[256,1024]{1,0:T(8,128)(2,1)}, u32[]{:S(2)}, u32[]{:S(2)}) %collective-permute-start.2) | collective-permute-done | bytes 524320 | tf_op jit(solution)/shard_map/ppermute | solution.py:798
  72.1 7.6 %collective-permute-done.10.refs_5_ = bf16[256,1024]{1,0:T(8,128)(2,1)S(1)} collective-permute-done((bf16[256,1024]{1,0:T(8,128)(2,1)}, bf16[256,1024]{1,0:T(8,128)(2,1)S(1)}, u32[]{:S(2)}, u32[]{:S(2)}) %collective-permute-start.10) | collective-permute-done | bytes 524320 | tf_op jit(solution)/shard_map/ppermute | solution.py:798
  83.6 1.8 convert_reduce_fusion
  93.2 10.2 %collective-permute-done.12 = bf16[1,1280,256]{2,1,0:T(8,128)(2,1)S(1)} collective-permute-done((bf16[1,1280,256]{2,1,0:T(8,128)(2,1)}, bf16[1,1280,256]{2,1,0:T(8,128)(2,1)S(1)}, u32[]{:S(2)}, u32[]{:S(2)}) %collective-permute-start.12) | collective-permute-done | bytes 655392 | tf_op jit(solution)/shard_map/ppermute | solution.py:748
  107.9 5.0 %collective-permute-done.15 = bf16[1,768,256]{2,1,0:T(8,128)(2,1)S(1)} collective-permute-done((bf16[1,768,256]{2,1,0:T(8,128)(2,1)S(1)}, bf16[1,768,256]{2,1,0:T(8,128)(2,1)S(1)}, u32[]{:S(2)}, u32[]{:S(2)}) %collective-permute-start.15) | collective-permute-done | bytes 393248 | tf_op jit(solution)/shard_map/ppermute | solution.py:748
  114.3 4.3 collective-permute-done.16.peer_ref
  118.6 35.3 %attend_forward.1 = (bf16[4352,128]{1,0:T(8,128)(2,1)}, bf16[4352,128]{1,0:T(8,128)(2,1)}, bf16[8832,128]{1,0:T(8,128)(2,1)}, bf16[8832,128]{1,0:T(8,128)(2,1)},...) custom-call(s32[32]{0:T(128)} %get-tuple-element.140.in_ref, ...), custom_call_target="tpu_custom_call" | custom-call | flops 3500000000 | bytes 105000000 | tf_op jit(solution)/shard_map/attend_forward/pallas_call | solution.py:238
  154.2 2.8 collective-permute-done.17
  160.2 13.1 %collective-permute-done.18 = bf16[1,8,272,128]{3,2,1,0:T(8,128)(2,1)S(1)} collective-permute-done((bf16[1,8,272,128]{3,2,1,0:T(8,128)(2,1)S(1)}, bf16[1,8,272,128]{3,2,1,0:T(8,128)(2,1)S(1)}, u32[]{:S(2)}, u32[]{:S(2)}) %collective-permute-start.18) | collective-permute-done | bytes 557088 | tf_op jit(solution)/shard_map/ppermute | solution.py:748
  174.3 5.1 %all-to-all-start.1 = ((bf16[8,272,128]{2,1,0:T(8,128)(2,1)}), bf16[8,272,128]{2,1,0:T(8,128)(2,1)S(1)}, u32[]{:S(2)}, u32[]{:S(2)}) async-start(bf16[8,272,128]{2,1,0:T(8,128)(2,1)} %fusion.32), calls=%async_computation.1 | async-start | bytes 1114112 | tf_op jit(solution)/shard_map/all_to_all | solution.py:744
  181.1 13.2 %all-to-all-done.1.parts_ref = bf16[8,272,128]{2,1,0:T(8,128)(2,1)S(1)} async-done(((bf16[8,272,128]{2,1,0:T(8,128)(2,1)}), bf16[8,272,128]{2,1,0:T(8,128)(2,1)S(1)}, u32[]{:S(2)}, u32[]{:S(2)}) %all-to-all-start.1) | async-done | bytes 557088 | tf_op jit(solution)/shard_map/all_to_all | solution.py:744
  195.1 4.3 mix_rows.1
  202.7 10.2 %feed_forward.2 = (bf16[512,1024]{1,0:T(8,128)(2,1)}, bf16[512,1024]{1,0:T(8,128)(2,1)}, bf16[512,1024]{1,0:T(8,128)(2,1)}, bf16[512,1024]{1,0:T(8,128)(2,1)}, b...) custom-call(bf16[256,1024]{1,0:T(8,128)(2,1)} %get-tuple-element.152, ...), custom_call_target="tpu_custom_call" | custom-call | flops 900000000 | bytes 27000000 | tf_op jit(solution)/shard_map/feed_forward/pallas_call | solution.py:523
  215.2 3.9 all-to-all-start.2
  219.1 10.4 %feed_forward.3 = (bf16[512,1024]{1,0:T(8,128)(2,1)}, bf16[512,1024]{1,0:T(8,128)(2,1)}, bf16[512,1024]{1,0:T(8,128)(2,1)}, bf16[512,1024]{1,0:T(8,128)(2,1)}, b...) custom-call(bf16[256,1024]{1,0:T(8,128)(2,1)} %collective-permute-do, ...), custom_call_target="tpu_custom_call" | custom-call | flops 900000000 | bytes 27000000 | tf_op jit(solution)/shard_map/feed_forward/pallas_call | solution.py:523
  237.7 2.4 pad_maximum_fusion
  240.1 2.0 add_convert_fusion.5.near_ref
  242.1 3.5 all-to-all-done.2
  245.6 3.4 collective-permute-done.27.far_ref
  249.8 5.2 %carry_rows.1 = (bf16[256,1024]{1,0:T(8,128)(2,1)}, bf16[8,272,128]{2,1,0:T(8,128)(2,1)}) custom-call(bf16[256,1024]{1,0:T(8,128)(2,1)} %add_convert_fusion.5.near_ref, bf16[256,1024]{1,0:T(8,128)(2,1)} %copy-done.30, f32[1,1024]{1,0:T(1,128)} %bitcast.280, f32[256,1024]{1,0:T(8,128)} %get-tuple-element.194.unit_ref, f32[256,1]{1,0:T(8,128)} %get-tuple-element.195.scale_ref, ...), custom_call_target="tpu_custom_call" | custom-call | flops 500000000 | bytes 15000000 | tf_op jit(solution)/shard_map/carry_rows/pallas_call | solution.py:615
  254.9 1.8 convolution_convert_fusion
  258.3 5.7 %all-to-all-start.3 = ((bf16[8,272,128]{2,1,0:T(8,128)(2,1)}), bf16[8,272,128]{2,1,0:T(8,128)(2,1)}, u32[]{:S(2)}, u32[]{:S(2)}) async-start(bf16[8,272,128]{2,1,0:T(8,128)(2,1)} %get-tuple-element.197), calls=%async_computation.3 | async-start | bytes 1114112 | tf_op jit(solution)/shard_map/all_to_all | solution.py:744
  267.6 2.0 add_convert_fusion.3
  269.7 2.0 add_convert_fusion.2
  271.7 8.4 %collective-permute-done.29 = bf16[8,1,32,1024]{3,2,0,1:T(8,128)(2,1)S(1)} collective-permute-done((bf16[8,1,32,1024]{3,2,0,1:T(8,128)(2,1)S(1)}, bf16[8,1,32,1024]{3,2,0,1:T(8,128)(2,1)S(1)}, u32[]{:S(2)}, u32[]{:S(2)}) %collective-permute-start.29) | collective-permute-done | bytes 524320 | tf_op jit(solution)/shard_map/ppermute | solution.py:748
  282.7 12.7 %collective-permute-done.32 = bf16[1,8,272,128]{3,2,1,0:T(8,128)(2,1)S(1)} collective-permute-done((bf16[1,8,272,128]{3,2,1,0:T(8,128)(2,1)}, bf16[1,8,272,128]{3,2,1,0:T(8,128)(2,1)S(1)}, u32[]{:S(2)}, u32[]{:S(2)}) %collective-permute-start.32) | collective-permute-done | bytes 557088 | tf_op jit(solution)/shard_map/ppermute | solution.py:748
  300.4 44.4 %attend_backward.1 = (bf16[4096,256]{1,0:T(8,128)(2,1)}, bf16[4096,256]{1,0:T(8,128)(2,1)}) custom-call(s32[32]{0:T(128)} %get-tuple-element.141.out_ref.table_ref, s32[8192]{0:T(1024)} %broadcast_add_fusion.place_ref, bf16[4352,128]{1,0:T(8,128)(2,1)} %bitcast.259, bf16[4352,128]{1,0:T(8,128)(2,1)} %bitcast.296, f32[64,128]{1,0:T(8,128)} %get-tuple-element.210.sum_ref, ...), custom_call_target="tpu_custom_call" | custom-call | flops 4400000000 | bytes 132000000 | tf_op jit(solution)/shard_map/attend_backward/pallas_call | solution.py:430
  345.8 3.5 collective-permute-done.36
  349.3 2.2 fusion
  357.6 5.2 %all-to-all-start.4 = ((bf16[8,32,1024]{2,1,0:T(8,128)(2,1)}), bf16[8,32,1024]{2,1,0:T(8,128)(2,1)S(1)}, u32[]{:S(2)}, u32[]{:S(2)}) async-start(bf16[8,32,1024]{2,1,0:T(8,128)(2,1)} %bitcast.70), calls=%async_computation.4 | async-start | bytes 1048576 | tf_op jit(solution)/shard_map/all_to_all | solution.py:744
  364.9 1.9 select_bitcast_fusion.1
  367.2 2.5 copy.100
  369.7 12.3 %all-to-all-done.4 = bf16[8,32,1024]{2,1,0:T(8,128)(2,1)S(1)} async-done(((bf16[8,32,1024]{2,1,0:T(8,128)(2,1)}), bf16[8,32,1024]{2,1,0:T(8,128)(2,1)S(1)}, u32[]{:S(2)}, u32[]{:S(2)}) %all-to-all-start.4) | async-done | bytes 524320 | tf_op jit(solution)/shard_map/all_to_all | solution.py:744
  381.9 2.4 add_rows.1
  384.4 5.1 %all-to-all-start.5 = ((bf16[8,256,256]{2,1,0:T(8,128)(2,1)}), bf16[8,256,256]{2,1,0:T(8,128)(2,1)S(1)}, u32[]{:S(2)}, u32[]{:S(2)}) async-start(bf16[8,256,256]{2,1,0:T(8,128)(2,1)} %bitcast.235), calls=%async_computation.5 | async-start | bytes 2097152 | tf_op jit(solution)/shard_map/all_to_all | solution.py:744
  389.5 4.9 %weight_part.1 = (f32[1024,256]{1,0:T(8,128)}, f32[8,256]{1,0:T(8,128)}) custom-call(s32[8]{0:T(128)} %copy-done, bf16[8,256,256]{2,1,0:T(8,128)(2,1)} %bitcast.236, bf16[256,1024]{1,0:T(8,128)(2,1)} %copy-done.9, bf16[256,1024]{1,0:T(8,128)(2,1)} %copy-done.35, bf16[256,1024]{1,0:T(8,128)(2,1)} %copy-done.34, ...), custom_call_target="tpu_custom_call" | custom-call | flops 500000000 | bytes 15000000 | tf_op jit(solution)/shard_map/weight_part/pallas_call | solution.py:702
  396.6 2.1 fusion.29
  398.8 1.9 fusion.41
  403.0 4.1 collective-permute-done.41
  407.2 3.7 collective-permute-done.40
  411.6 3.5 all-to-all-done.5.back_ref
  415.1 3.7 all-to-all-start.6
  421.5 5.3 %last_rows.1 = bf16[256,1024]{1,0:T(8,128)(2,1)} custom-call(bf16[8,256,256]{2,1,0:T(8,128)(2,1)} %copy-done.4, bf16[2,1024,1024]{2,1,0:T(8,128)(2,1)} %bitcast.234, f32[1,1024]{1,0:T(1,128)} %bitcast.281, f32[256,1024]{1,0:T(8,128)} %get-tuple-element.255.unit_ref, f32[256,1]{1,0:T(8,128)} %copy.101.scale_ref, bf16[256,1024]{1,0:T(8,128)(2,1)} %grad_ref.3), custom_call_target="tpu_custom_call" | custom-call | flops 600000000 | bytes 18000000 | tf_op jit(solution)/shard_map/last_rows/pallas_call | solution.py:671
  (325 shorter events, 97.3 us)
Async XLA Ops:
  15.6 23.8 %collective-permute-start.1 = (bf16[256,1024]{1,0:T(8,128)(2,1)S(1)}, bf16[256,1024]{1,0:T(8,128)(2,1)S(1)}, u32[]{:S(2)}, u32[]{:S(2)}) collective-permute-start(bf16[256,1024]{1,0:T(8,128)(2,1)S(1)} %get-tuple-element.125.refs_0_), channel_id=1, source_target_pairs={{8,0},{16,8},{24,16},{28,24},{20,28},{12,20},{4,12},{0,4},{9,1},{1... | collective-permute-start | bytes 1572872 | tf_op jit(solution)/shard_map/ppermute | solution.py:798
  18.6 20.8 %collective-permute-start = (bf16[256,1024]{1,0:T(8,128)(2,1)S(1)}, bf16[256,1024]{1,0:T(8,128)(2,1)S(1)}, u32[]{:S(2)}, u32[]{:S(2)}) collective-permute-start(bf16[256,1024]{1,0:T(8,128)(2,1)S(1)} %get-tuple-element.125.refs_0_), channel_id=1, source_target_pairs={{0,8},{8,16},{16,24},{24,28},{28,20},{20,12},{12,4},{4,0},{1,9},{9... | collective-permute-start | bytes 1572872 | tf_op jit(solution)/shard_map/ppermute | solution.py:798
  19.5 19.9 %all-to-all-start = ((bf16[8,48,384]{2,1,0:T(8,128)(2,1)}), bf16[8,48,384]{2,1,0:T(8,128)(2,1)S(1)}, u32[]{:S(2)}, u32[]{:S(2)}) async-start(bf16[8,48,384]{2,1,0:T(8,128)(2,1)} %copy.92), calls=%async_computation | async-start | bytes 589824 | tf_op jit(solution)/shard_map/all_to_all | solution.py:744
  25.7 168.6 %all-gather.3.cloned.1.call-start = ((), (), s32[]{:S(2)}) async-start(), calls=%async_computation.9 | async-start | bytes 7077888 | tf_op jit(solution)/shard_map/all_gather | solution.py:998
  25.7 13.8 %collective-permute-start.8 = (bf16[32,1024]{1,0:T(8,128)(2,1)S(1)}, bf16[32,1024]{1,0:T(8,128)(2,1)S(1)}, u32[]{:S(2)}, u32[]{:S(2)}) collective-permute-start(bf16[32,1024]{1,0:T(8,128)(2,1)S(1)} %copy-done.40), channel_id=1, source_target_pairs={{0,1},{1,0},{2,3},{3,2},{4,5},{5,4},{6,7},{7,6},{8,9},{9,8},{10,11... | collective-permute-start | bytes 196616 | tf_op jit(solution)/shard_map/ppermute | solution.py:748
  39.5 10.8 %collective-permute-start.9 = (bf16[2,32,1024]{2,1,0:T(8,128)(2,1)S(1)}, bf16[2,32,1024]{2,1,0:T(8,128)(2,1)S(1)}, u32[]{:S(2)}, u32[]{:S(2)}) collective-permute-start(bf16[2,32,1024]{2,1,0:T(8,128)(2,1)S(1)} %pad_maximum_fusion.10), channel_id=1, source_target_pairs={{0,2},{2,0},{1,3},{3,1},{4,6},{6,4},{5,7},{7,5},{8,10},{10,8},{9,1... | collective-permute-start | bytes 393224 | tf_op jit(solution)/shard_map/ppermute | solution.py:748
  41.1 9.0 %collective-permute-start.4 = (bf16[8,1,32,384]{3,2,0,1:T(8,128)(2,1)S(1)}, bf16[8,1,32,384]{3,2,0,1:T(8,128)(2,1)S(1)}, u32[]{:S(2)}, u32[]{:S(2)}) collective-permute-start(bf16[8,1,32,384]{3,2,0,1:T(8,128)(2,1)S(1)} %slice.139), channel_id=1, source_target_pairs={{0,2},{2,0},{1,3},{3,1},{4,6},{6,4},{5,7},{7,5},{8,10},{10,8},{9,1... | collective-permute-start | bytes 589832 | tf_op jit(solution)/shard_map/ppermute | solution.py:748
  42.4 10.7 %collective-permute-start.7 = (bf16[1,2,32,1024]{3,2,1,0:T(8,128)(2,1)}, bf16[1,2,32,1024]{3,2,1,0:T(8,128)(2,1)}, u32[]{:S(2)}, u32[]{:S(2)}) collective-permute-start(bf16[1,2,32,1024]{3,2,1,0:T(8,128)(2,1)} %constant_dynamic-slice_fusion.3), channel_id=1, source_target_pairs={{0,2},{2,0},{1,3},{3,1},{4,6},{6,4},{5,7},{7,5},{8,10},{10,8},{9,1... | collective-permute-start | bytes 393224 | tf_op jit(solution)/shard_map/ppermute | solution.py:748
  50.2 4.8 %collective-permute-start.5 = (bf16[8,1,2,32,384]{4,3,2,0,1:T(8,128)(2,1)S(1)}, bf16[8,1,2,32,384]{4,3,2,0,1:T(8,128)(2,1)}, u32[]{:S(2)}, u32[]{:S(2)}) collective-permute-start(bf16[8,1,2,32,384]{4,3,2,0,1:T(8,128)(2,1)S(1)} %pad_maximum_fusion.6), channel_id=1, source_target_pairs={{0,1},{1,0},{2,3},{3,2},{4,5},{5,4},{6,7},{7,6},{8,9},{9,8},{10,11... | collective-permute-start | bytes 1179656 | tf_op jit(solution)/shard_map/ppermute | solution.py:748
  51.0 14.4 %collective-permute-start.2 = (bf16[256,1024]{1,0:T(8,128)(2,1)S(1)}, bf16[256,1024]{1,0:T(8,128)(2,1)}, u32[]{:S(2)}, u32[]{:S(2)}) collective-permute-start(bf16[256,1024]{1,0:T(8,128)(2,1)S(1)} %collective-permute-done.refs_1_), channel_id=1, source_target_pairs={{0,8},{8,16},{16,24},{24,28},{28,20},{20,12},{12,4},{4,0},{1,9},{9... | collective-permute-start | bytes 1572872 | tf_op jit(solution)/shard_map/ppermute | solution.py:798
  52.2 14.1 %collective-permute-start.3 = (bf16[256,1024]{1,0:T(8,128)(2,1)S(1)}, bf16[256,1024]{1,0:T(8,128)(2,1)}, u32[]{:S(2)}, u32[]{:S(2)}) collective-permute-start(bf16[256,1024]{1,0:T(8,128)(2,1)S(1)} %collective-permute-done.1.refs_2_), channel_id=1, source_target_pairs={{8,0},{16,8},{24,16},{28,24},{20,28},{12,20},{4,12},{0,4},{9,1},{1... | collective-permute-start | bytes 1572872 | tf_op jit(solution)/shard_map/ppermute | solution.py:798
  66.3 13.4 %collective-permute-start.10 = (bf16[256,1024]{1,0:T(8,128)(2,1)}, bf16[256,1024]{1,0:T(8,128)(2,1)S(1)}, u32[]{:S(2)}, u32[]{:S(2)}) collective-permute-start(bf16[256,1024]{1,0:T(8,128)(2,1)} %collective-permute-done.2.refs_3_), channel_id=1, source_target_pairs={{0,8},{8,16},{16,24},{24,28},{28,20},{20,12},{12,4},{4,0},{1,9},{9... | collective-permute-start | bytes 1572872 | tf_op jit(solution)/shard_map/ppermute | solution.py:798
  66.6 13.5 %collective-permute-start.11 = (bf16[256,1024]{1,0:T(8,128)(2,1)}, bf16[256,1024]{1,0:T(8,128)(2,1)S(1)}, u32[]{:S(2)}, u32[]{:S(2)}) collective-permute-start(bf16[256,1024]{1,0:T(8,128)(2,1)} %collective-permute-done.3.refs_4_), channel_id=1, source_target_pairs={{8,0},{16,8},{24,16},{28,24},{20,28},{12,20},{4,12},{0,4},{9,1},{1... | collective-permute-start | bytes 1572872 | tf_op jit(solution)/shard_map/ppermute | solution.py:798
  86.4 18.0 %collective-permute-start.14 = (bf16[128,1024]{1,0:T(8,128)(2,1)S(1)}, bf16[128,1024]{1,0:T(8,128)(2,1)S(1)}, u32[]{:S(2)}, u32[]{:S(2)}) collective-permute-start(bf16[128,1024]{1,0:T(8,128)(2,1)S(1)} %slice.109), channel_id=1, source_target_pairs={{8,0},{16,8},{24,16},{28,24},{20,28},{12,20},{4,12},{0,4},{9,1},{1... | collective-permute-start | bytes 786440 | tf_op jit(solution)/shard_map/ppermute | solution.py:798
  87.9 16.2 %collective-permute-start.13 = (bf16[128,1024]{1,0:T(8,128)(2,1)}, bf16[128,1024]{1,0:T(8,128)(2,1)S(1)}, u32[]{:S(2)}, u32[]{:S(2)}) collective-permute-start(bf16[128,1024]{1,0:T(8,128)(2,1)} %slice.108), channel_id=1, source_target_pairs={{0,8},{8,16},{16,24},{24,28},{28,20},{20,12},{12,4},{4,0},{1,9},{9... | collective-permute-start | bytes 786440 | tf_op jit(solution)/shard_map/ppermute | solution.py:798
  88.6 14.8 %collective-permute-start.12 = (bf16[1,1280,256]{2,1,0:T(8,128)(2,1)}, bf16[1,1280,256]{2,1,0:T(8,128)(2,1)S(1)}, u32[]{:S(2)}, u32[]{:S(2)}) collective-permute-start(bf16[1,1280,256]{2,1,0:T(8,128)(2,1)} %copy-done.22), channel_id=1, source_target_pairs={{0,2},{2,0},{1,3},{3,1},{4,6},{6,4},{5,7},{7,5},{8,10},{10,8},{9,1... | collective-permute-start | bytes 1966088 | tf_op jit(solution)/shard_map/ppermute | solution.py:748
  104.7 8.2 %collective-permute-start.15 = (bf16[1,768,256]{2,1,0:T(8,128)(2,1)S(1)}, bf16[1,768,256]{2,1,0:T(8,128)(2,1)S(1)}, u32[]{:S(2)}, u32[]{:S(2)}) collective-permute-start(bf16[1,768,256]{2,1,0:T(8,128)(2,1)S(1)} %pad_maximum_fusion.7), channel_id=1, source_target_pairs={{0,2},{2,0},{1,3},{3,1},{4,6},{6,4},{5,7},{7,5},{8,10},{10,8},{9,1... | collective-permute-start | bytes 1179656 | tf_op jit(solution)/shard_map/ppermute | solution.py:748
  158.6 14.7 %collective-permute-start.18 = (bf16[1,8,272,128]{3,2,1,0:T(8,128)(2,1)S(1)}, bf16[1,8,272,128]{3,2,1,0:T(8,128)(2,1)S(1)}, u32[]{:S(2)}, u32[]{:S(2)}) collective-permute-start(bf16[1,8,272,128]{3,2,1,0:T(8,128)(2,1)S(1)} %slice_bitcast_fusion.1), channel_id=1, source_target_pairs={{0,2},{2,0},{1,3},{3,1},{4,6},{6,4},{5,7},{7,5},{8,10},{10,8},{9,1... | collective-permute-start | bytes 1671176 | tf_op jit(solution)/shard_map/ppermute | solution.py:748
  174.3 19.9 %all-to-all-start.1 = ((bf16[8,272,128]{2,1,0:T(8,128)(2,1)}), bf16[8,272,128]{2,1,0:T(8,128)(2,1)S(1)}, u32[]{:S(2)}, u32[]{:S(2)}) async-start(bf16[8,272,128]{2,1,0:T(8,128)(2,1)} %fusion.32), calls=%async_computation.1 | async-start | bytes 1114112 | tf_op jit(solution)/shard_map/all_to_all | solution.py:744
  179.5 21.4 %collective-permute-start.23 = (bf16[256,1024]{1,0:T(8,128)(2,1)S(1)}, bf16[256,1024]{1,0:T(8,128)(2,1)}, u32[]{:S(2)}, u32[]{:S(2)}) collective-permute-start(bf16[256,1024]{1,0:T(8,128)(2,1)S(1)} %copy-done.7), channel_id=1, source_target_pairs={{0,2},{2,0},{1,3},{3,1},{4,6},{6,4},{5,7},{7,5},{8,10},{10,8},{9,1... | collective-permute-start | bytes 1572872 | tf_op jit(solution)/shard_map/ppermute | solution.py:748
  181.1 20.1 %collective-permute-start.21 = (bf16[256,1024]{1,0:T(8,128)(2,1)S(1)}, bf16[256,1024]{1,0:T(8,128)(2,1)S(1)}, u32[]{:S(2)}, u32[]{:S(2)}) collective-permute-start(bf16[256,1024]{1,0:T(8,128)(2,1)S(1)} %copy-done.7), channel_id=1, source_target_pairs={{0,1},{1,0},{2,3},{3,2},{4,5},{5,4},{6,7},{7,6},{8,9},{9,8},{10,11... | collective-permute-start | bytes 1572872 | tf_op jit(solution)/shard_map/ppermute | solution.py:748
  199.4 14.7 %collective-permute-start.19 = (bf16[256,1024]{1,0:T(8,128)(2,1)}, bf16[256,1024]{1,0:T(8,128)(2,1)}, u32[]{:S(2)}, u32[]{:S(2)}) collective-permute-start(bf16[256,1024]{1,0:T(8,128)(2,1)} %get-tuple-element.152.own_ref), channel_id=1, source_target_pairs={{0,2},{2,0},{1,3},{3,1},{4,6},{6,4},{5,7},{7,5},{8,10},{10,8},{9,1... | collective-permute-start | bytes 1572872 | tf_op jit(solution)/shard_map/ppermute | solution.py:748
  200.9 18.2 %collective-permute-start.24 = (bf16[256,1024]{1,0:T(8,128)(2,1)}, bf16[256,1024]{1,0:T(8,128)(2,1)}, u32[]{:S(2)}, u32[]{:S(2)}) collective-permute-start(bf16[256,1024]{1,0:T(8,128)(2,1)} %collective-permute-done.23.grad_own_ref), channel_id=1, source_target_pairs={{0,1},{1,0},{2,3},{3,2},{4,5},{5,4},{6,7},{7,6},{8,9},{9,8},{10,11... | collective-permute-start | bytes 1572872 | tf_op jit(solution)/shard_map/ppermute | solution.py:748
  214.0 5.1 %collective-permute-start.22 = (bf16[256,1024]{1,0:T(8,128)(2,1)}, bf16[256,1024]{1,0:T(8,128)(2,1)}, u32[]{:S(2)}, u32[]{:S(2)}) collective-permute-start(bf16[256,1024]{1,0:T(8,128)(2,1)} %collective-permute-done.19.own_ref), channel_id=1, source_target_pairs={{0,1},{1,0},{2,3},{3,2},{4,5},{5,4},{6,7},{7,6},{8,9},{9,8},{10,11... | collective-permute-start | bytes 1572872 | tf_op jit(solution)/shard_map/ppermute | solution.py:748
  215.2 30.4 %all-to-all-start.2 = ((bf16[8,2,32,1024]{3,2,1,0:T(8,128)(2,1)}), bf16[8,2,32,1024]{3,2,1,0:T(8,128)(2,1)S(1)}, u32[]{:S(2)}, u32[]{:S(2)}) async-start(bf16[8,2,32,1024]{3,2,1,0:T(8,128)(2,1)} %broadcast_in_dim.32), calls=%async_computation.2 | async-start | bytes 2097152 | tf_op jit(solution)/shard_map/all_to_all | solution.py:744
  229.6 10.5 %collective-permute-start.25 = (bf16[256,1024]{1,0:T(8,128)(2,1)}, bf16[256,1024]{1,0:T(8,128)(2,1)}, u32[]{:S(2)}, u32[]{:S(2)}) collective-permute-start(bf16[256,1024]{1,0:T(8,128)(2,1)} %get-tuple-element.180), channel_id=1, source_target_pairs={{0,1},{1,0},{2,3},{3,2},{4,5},{5,4},{6,7},{7,6},{8,9},{9,8},{10,11... | collective-permute-start | bytes 1572872 | tf_op jit(solution)/shard_map/ppermute | solution.py:748
  230.0 4.4 %collective-permute-start.26 = (bf16[256,1024]{1,0:T(8,128)(2,1)}, bf16[256,1024]{1,0:T(8,128)(2,1)S(1)}, u32[]{:S(2)}, u32[]{:S(2)}) collective-permute-start(bf16[256,1024]{1,0:T(8,128)(2,1)} %get-tuple-element.182), channel_id=1, source_target_pairs={{0,1},{1,0},{2,3},{3,2},{4,5},{5,4},{6,7},{7,6},{8,9},{9,8},{10,11... | collective-permute-start | bytes 1572872 | tf_op jit(solution)/shard_map/ppermute | solution.py:748
  234.6 14.3 %collective-permute-start.27 = (bf16[256,1024]{1,0:T(8,128)(2,1)S(1)}, bf16[256,1024]{1,0:T(8,128)(2,1)S(1)}, u32[]{:S(2)}, u32[]{:S(2)}) collective-permute-start(bf16[256,1024]{1,0:T(8,128)(2,1)S(1)} %add_convert_fusion.4), channel_id=1, source_target_pairs={{0,2},{2,0},{1,3},{3,1},{4,6},{6,4},{5,7},{7,5},{8,10},{10,8},{9,1... | collective-permute-start | bytes 1572872 | tf_op jit(solution)/shard_map/ppermute | solution.py:748
  257.8 6.5 %collective-permute-start.28 = (bf16[8,1,2,32,1024]{4,3,2,0,1:T(8,128)(2,1)}, bf16[8,1,2,32,1024]{4,3,2,0,1:T(8,128)(2,1)}, u32[]{:S(2)}, u32[]{:S(2)}) collective-permute-start(bf16[8,1,2,32,1024]{4,3,2,0,1:T(8,128)(2,1)} %dynamic-slice_bitcast_fusion), channel_id=1, source_target_pairs={{0,1},{1,0},{2,3},{3,2},{4,5},{5,4},{6,7},{7,6},{8,9},{9,8},{10,11... | collective-permute-start | bytes 3145736 | tf_op jit(solution)/shard_map/ppermute | solution.py:748
  257.8 9.8 %collective-permute-start.30 = (bf16[256,1024]{1,0:T(8,128)(2,1)}, bf16[256,1024]{1,0:T(8,128)(2,1)}, u32[]{:S(2)}, u32[]{:S(2)}) collective-permute-start(bf16[256,1024]{1,0:T(8,128)(2,1)} %get-tuple-element.201), channel_id=1, source_target_pairs={{0,1},{1,0},{2,3},{3,2},{4,5},{5,4},{6,7},{7,6},{8,9},{9,8},{10,11... | collective-permute-start | bytes 1572872 | tf_op jit(solution)/shard_map/ppermute | solution.py:748
  258.3 11.4 %collective-permute-start.31 = (bf16[256,1024]{1,0:T(8,128)(2,1)}, bf16[256,1024]{1,0:T(8,128)(2,1)}, u32[]{:S(2)}, u32[]{:S(2)}) collective-permute-start(bf16[256,1024]{1,0:T(8,128)(2,1)} %get-tuple-element.203), channel_id=1, source_target_pairs={{0,1},{1,0},{2,3},{3,2},{4,5},{5,4},{6,7},{7,6},{8,9},{9,8},{10,11... | collective-permute-start | bytes 1572872 | tf_op jit(solution)/shard_map/ppermute | solution.py:748
  258.3 22.9 %all-to-all-start.3 = ((bf16[8,272,128]{2,1,0:T(8,128)(2,1)}), bf16[8,272,128]{2,1,0:T(8,128)(2,1)}, u32[]{:S(2)}, u32[]{:S(2)}) async-start(bf16[8,272,128]{2,1,0:T(8,128)(2,1)} %get-tuple-element.197), calls=%async_computation.3 | async-start | bytes 1114112 | tf_op jit(solution)/shard_map/all_to_all | solution.py:744
  264.0 134.8 %reduce-scatter.2.cloned.1.call-start = ((), (), s32[]{:S(2)}) async-start(), calls=%async_computation.8 | async-start | bytes 4718592 | tf_op jit(solution)/shard_map/reduce_scatter | solution.py:1039
  266.0 14.1 %collective-permute-start.29 = (bf16[8,1,32,1024]{3,2,0,1:T(8,128)(2,1)S(1)}, bf16[8,1,32,1024]{3,2,0,1:T(8,128)(2,1)S(1)}, u32[]{:S(2)}, u32[]{:S(2)}) collective-permute-start(bf16[8,1,32,1024]{3,2,0,1:T(8,128)(2,1)S(1)} %dynamic-slice_bitcast_fusion.1), channel_id=1, source_target_pairs={{0,2},{2,0},{1,3},{3,1},{4,6},{6,4},{5,7},{7,5},{8,10},{10,8},{9,1... | collective-permute-start | bytes 1572872 | tf_op jit(solution)/shard_map/ppermute | solution.py:748
  281.2 14.3 %collective-permute-start.32 = (bf16[1,8,272,128]{3,2,1,0:T(8,128)(2,1)}, bf16[1,8,272,128]{3,2,1,0:T(8,128)(2,1)S(1)}, u32[]{:S(2)}, u32[]{:S(2)}) collective-permute-start(bf16[1,8,272,128]{3,2,1,0:T(8,128)(2,1)} %bitcast.58), channel_id=1, source_target_pairs={{0,2},{2,0},{1,3},{3,1},{4,6},{6,4},{5,7},{7,5},{8,10},{10,8},{9,1... | collective-permute-start | bytes 1671176 | tf_op jit(solution)/shard_map/ppermute | solution.py:748
  296.7 48.2 %collective-permute-start.34 = (bf16[2,8,1,32,1024]{4,3,0,1,2:T(8,128)(2,1)S(1)}, bf16[2,8,1,32,1024]{4,3,0,1,2:T(8,128)(2,1)S(1)}, u32[]{:S(2)}, u32[]{:S(2)}) collective-permute-start(bf16[2,8,1,32,1024]{4,3,0,1,2:T(8,128)(2,1)S(1)} %bitcast.243), channel_id=1, source_target_pairs={{0,2},{2,0},{1,3},{3,1},{4,6},{6,4},{5,7},{7,5},{8,10},{10,8},{9,1... | collective-permute-start | bytes 3145736 | tf_op jit(solution)/shard_map/ppermute | solution.py:748
  298.3 46.6 %collective-permute-start.35 = (bf16[256,1024]{1,0:T(8,128)(2,1)S(1)}, bf16[256,1024]{1,0:T(8,128)(2,1)}, u32[]{:S(2)}, u32[]{:S(2)}) collective-permute-start(bf16[256,1024]{1,0:T(8,128)(2,1)S(1)} %copy-done.28), channel_id=1, source_target_pairs={{0,2},{2,0},{1,3},{3,1},{4,6},{6,4},{5,7},{7,5},{8,10},{10,8},{9,1... | collective-permute-start | bytes 1572872 | tf_op jit(solution)/shard_map/ppermute | solution.py:748
  344.9 4.4 %collective-permute-start.36 = (bf16[2,1,8,256,256]{4,3,2,1,0:T(8,128)(2,1)}, bf16[2,1,8,256,256]{4,3,2,1,0:T(8,128)(2,1)S(1)}, u32[]{:S(2)}, u32[]{:S(2)}) collective-permute-start(bf16[2,1,8,256,256]{4,3,2,1,0:T(8,128)(2,1)} %bitcast.295), channel_id=1, source_target_pairs={{0,1},{1,0},{2,3},{3,2},{4,5},{5,4},{6,7},{7,6},{8,9},{9,8},{10,11... | collective-permute-start | bytes 6291464 | tf_op jit(solution)/shard_map/ppermute | solution.py:748
  354.4 10.5 %collective-permute-start.38 = (bf16[2,8,1,2,32,1024]{5,4,0,1,3,2:T(8,128)(2,1)}, bf16[2,8,1,2,32,1024]{5,4,0,1,3,2:T(8,128)(2,1)}, u32[]{:S(2)}, u32[]{:S(2)}) collective-permute-start(bf16[2,8,1,2,32,1024]{5,4,0,1,3,2:T(8,128)(2,1)} %pad_maximum_fusion.2), channel_id=1, source_target_pairs={{0,1},{1,0},{2,3},{3,2},{4,5},{5,4},{6,7},{7,6},{8,9},{9,8},{10,11... | collective-permute-start | bytes 6291464 | tf_op jit(solution)/shard_map/ppermute | solution.py:748
  356.0 25.9 %collective-permute-start.37 = (bf16[1,8,256,256]{3,2,1,0:T(8,128)(2,1)}, bf16[1,8,256,256]{3,2,1,0:T(8,128)(2,1)}, u32[]{:S(2)}, u32[]{:S(2)}) collective-permute-start(bf16[1,8,256,256]{3,2,1,0:T(8,128)(2,1)} %get-tuple-element.249), channel_id=1, source_target_pairs={{0,2},{2,0},{1,3},{3,1},{4,6},{6,4},{5,7},{7,5},{8,10},{10,8},{9,1... | collective-permute-start | bytes 3145736 | tf_op jit(solution)/shard_map/ppermute | solution.py:748
  357.6 24.4 %all-to-all-start.4 = ((bf16[8,32,1024]{2,1,0:T(8,128)(2,1)}), bf16[8,32,1024]{2,1,0:T(8,128)(2,1)S(1)}, u32[]{:S(2)}, u32[]{:S(2)}) async-start(bf16[8,32,1024]{2,1,0:T(8,128)(2,1)} %bitcast.70), calls=%async_computation.4 | async-start | bytes 1048576 | tf_op jit(solution)/shard_map/all_to_all | solution.py:744
  364.4 34.4 %collective-permute-start.44 = (f32[8,128]{1,0:T(8,128)S(1)}, f32[8,128]{1,0:T(8,128)S(1)}, u32[]{:S(2)}, u32[]{:S(2)}) collective-permute-start(f32[8,128]{1,0:T(8,128)S(1)} %bitcast.288), channel_id=1, source_target_pairs={{0,2},{2,0},{1,3},{3,1},{4,6},{6,4},{5,7},{7,5},{8,10},{10,8},{9,1... | collective-permute-start | bytes 12296 | tf_op jit(solution)/shard_map/ppermute | solution.py:748
  384.4 30.7 %all-to-all-start.5 = ((bf16[8,256,256]{2,1,0:T(8,128)(2,1)}), bf16[8,256,256]{2,1,0:T(8,128)(2,1)S(1)}, u32[]{:S(2)}, u32[]{:S(2)}) async-start(bf16[8,256,256]{2,1,0:T(8,128)(2,1)} %bitcast.235), calls=%async_computation.5 | async-start | bytes 2097152 | tf_op jit(solution)/shard_map/all_to_all | solution.py:744
  396.5 5.7 %collective-permute-start.39 = (bf16[8,1,2,48,256]{4,3,2,0,1:T(8,128)(2,1)S(1)}, bf16[8,1,2,48,256]{4,3,2,0,1:T(8,128)(2,1)S(1)}, u32[]{:S(2)}, u32[]{:S(2)}) collective-permute-start(bf16[8,1,2,48,256]{4,3,2,0,1:T(8,128)(2,1)S(1)} %fusion.35), channel_id=1, source_target_pairs={{0,1},{1,0},{2,3},{3,2},{4,5},{5,4},{6,7},{7,6},{8,9},{9,8},{10,11... | collective-permute-start | bytes 1179656 | tf_op jit(solution)/shard_map/ppermute | solution.py:748
  400.7 6.4 %collective-permute-start.41 = (bf16[1,2,32,1024]{3,2,1,0:T(8,128)(2,1)S(1)}, bf16[1,2,32,1024]{3,2,1,0:T(8,128)(2,1)S(1)}, u32[]{:S(2)}, u32[]{:S(2)}) collective-permute-start(bf16[1,2,32,1024]{3,2,1,0:T(8,128)(2,1)S(1)} %constant_dynamic-slice_fusion.1), channel_id=1, source_target_pairs={{0,2},{2,0},{1,3},{3,1},{4,6},{6,4},{5,7},{7,5},{8,10},{10,8},{9,1... | collective-permute-start | bytes 393224 | tf_op jit(solution)/shard_map/ppermute | solution.py:748
  402.4 8.4 %collective-permute-start.40 = (bf16[8,1,48,256]{3,2,0,1:T(8,128)(2,1)S(1)}, bf16[8,1,48,256]{3,2,0,1:T(8,128)(2,1)S(1)}, u32[]{:S(2)}, u32[]{:S(2)}) collective-permute-start(bf16[8,1,48,256]{3,2,0,1:T(8,128)(2,1)S(1)} %dynamic-slice_bitcast_fusion.2), channel_id=1, source_target_pairs={{0,2},{2,0},{1,3},{3,1},{4,6},{6,4},{5,7},{7,5},{8,10},{10,8},{9,1... | collective-permute-start | bytes 589832 | tf_op jit(solution)/shard_map/ppermute | solution.py:748
  407.1 4.5 %collective-permute-start.42 = (bf16[2,1,32,1024]{3,2,1,0:T(8,128)(2,1)S(1)}, bf16[2,1,32,1024]{3,2,1,0:T(8,128)(2,1)S(1)}, u32[]{:S(2)}, u32[]{:S(2)}) collective-permute-start(bf16[2,1,32,1024]{3,2,1,0:T(8,128)(2,1)S(1)} %constant_dynamic-slice_fusion), channel_id=1, source_target_pairs={{0,1},{1,0},{2,3},{3,2},{4,5},{5,4},{6,7},{7,6},{8,9},{9,8},{10,11... | collective-permute-start | bytes 393224 | tf_op jit(solution)/shard_map/ppermute | solution.py:748
  415.1 11.8 %all-to-all-start.6 = ((bf16[8,48,256]{2,1,0:T(8,128)(2,1)}), bf16[8,48,256]{2,1,0:T(8,128)(2,1)S(1)}, u32[]{:S(2)}, u32[]{:S(2)}) async-start(bf16[8,48,256]{2,1,0:T(8,128)(2,1)} %fusion.42), calls=%async_computation.7 | async-start | bytes 393216 | tf_op jit(solution)/shard_map/all_to_all | solution.py:744
  (59 other events, 662.3 us)
Sparse Core Ops, SparseCore 0:
  80.2 101.0 all-gather.2
  282.8 91.4 reduce-scatter.1

commit v4 on v3

--- a/solution.py
+++ b/solution.py
@@ -16,6 +16,7 @@
 PAD = 16
 UNROLL = 17
 TOKB = 128
+BUCKETS = 32
 CHUNK = 4096
 VMEM_LIMIT = 60 * 2**20
 KEY_EPS = 1e-06
@@ -83,17 +84,33 @@
     peer_ref,
     pay_own_ref,
     pay_peer_ref,
+    query_out,
+    key_out,
+    value_out,
+    prob_out,
+    sum_ref,
     query_ref,
     key_ref,
     value_ref,
     prob_ref,
-    sum_ref,
     wide_a,
     wide_b,
     stage_a,
     stage_b,
+    sems,
 ):
     step = pl.program_id(0)
+    leaving = [
+        pltpu.make_async_copy(source, target, sems.at[number])
+        for number, (source, target) in enumerate(
+            [
+                (query_ref, query_out),
+                (key_ref, key_out),
+                (value_ref, value_out),
+                (prob_ref, prob_out),
+            ]
+        )
+    ]
     own_spans = prob_ref.shape[0] // SPAN
     tail = SPAN * (own_spans + 1)
 
@@ -185,6 +202,8 @@
             return carry
 
         lax.fori_loop(0, own_spans // UNROLL, spans, 0)
+        for copy in leaving:
+            copy.start()
         wide_a[pl.ds(tail, SPAN), :] = jnp.zeros((SPAN, HEADD), f32)
         wide_b[pl.ds(tail, SPAN), :] = jnp.zeros((SPAN, HEADD), f32)
 
@@ -216,6 +235,11 @@
     half = load_steps + 1 + load_steps // 2
     pl.when((step > load_steps) & (step < half))(lambda: collect_to(pay_own_ref))
     pl.when(step >= half)(lambda: collect_to(pay_peer_ref))
+
+    @pl.when(step == 2 * load_steps)
+    def _():
+        for copy in leaving:
+            copy.wait()
 
 
 def part_spec(shape, first, count):
@@ -258,13 +282,17 @@
         out_specs=(
             part_spec((pay_rows, HEADD), steps + 1, half),
             part_spec((pay_rows, HEADD), steps + 1 + half, half),
-            whole((rows, HEADD)),
-            whole((rows, HEADD)),
-            whole((rows, HEADD)),
-            whole((own_spans * SPAN, 2 * SPAN)),
+            pl.BlockSpec(memory_space=pl.ANY),
+            pl.BlockSpec(memory_space=pl.ANY),
+            pl.BlockSpec(memory_space=pl.ANY),
+            pl.BlockSpec(memory_space=pl.ANY),
             part_spec((CHUNK // TOKB, TOKB), steps + 1, steps),
         ),
-        scratch_shapes=[pltpu.VMEM((rows, HEADD), f32)] * 2 + [pltpu.VMEM((TOKB, HEADD), f32)] * 2,
+        scratch_shapes=[pltpu.VMEM((rows, HEADD), bf)] * 3
+        + [pltpu.VMEM((own_spans * SPAN, 2 * SPAN), bf)]
+        + [pltpu.VMEM((rows, HEADD), f32)] * 2
+        + [pltpu.VMEM((TOKB, HEADD), f32)] * 2
+        + [pltpu.SemaphoreType.DMA((4,))],
         compiler_params=pltpu.CompilerParams(vmem_limit_bytes=VMEM_LIMIT),
         name="attend_forward",
         cost_estimate=takes(35),
@@ -279,24 +307,37 @@
     pay_own_ref,
     pay_peer_ref,
     sum_ref,
+    query_in,
+    key_in,
+    value_in,
+    prob_in,
+    out_own_ref,
+    out_peer_ref,
     query_ref,
     key_ref,
     value_ref,
     prob_ref,
-    out_own_ref,
-    out_peer_ref,
     wide_a,
     wide_b,
     wide_c,
     stage_a,
     stage_b,
+    sems,
 ):
     step = pl.program_id(0)
+    coming = [
+        pltpu.make_async_copy(source, target, sems.at[number])
+        for number, (source, target) in enumerate(
+            [(query_in, query_ref), (key_in, key_ref), (value_in, value_ref), (prob_in, prob_ref)]
+        )
+    ]
     own_spans = prob_ref.shape[0] // SPAN
     tail = SPAN * (own_spans + 1)
 
     @pl.when(step == 0)
     def _():
+        for copy in coming:
+            copy.start()
         fill(wide_a, 0.0)
         fill(wide_b, 0.0)
 
@@ -338,6 +379,8 @@
 
     @pl.when(step == load_steps)
     def _():
+        for copy in coming:
+            copy.wait()
         for ref in (wide_a, wide_b, wide_c):
             ref[:SPAN, :] = jnp.zeros((SPAN, HEADD), f32)
         zero = jnp.zeros((SPAN, HEADD), bf)
@@ -421,11 +464,6 @@
     half = steps // 2
     rows = query.shape[0]
     pay_rows = CHUNK // own_rows * (own_rows + PAD)
-    once = pl.Buffered(1)
-
-    def whole(shape):
-        return pl.BlockSpec(shape, lambda step: (0, 0), pipeline_mode=once)
-
     out_half = jax.ShapeDtypeStruct((tokens // 2, 2 * HEADD), bf)
     return pl.pallas_call(
         functools.partial(backward_kernel, own_rows, steps),
@@ -437,16 +475,20 @@
             part_spec((pay_rows, HEADD), 0, half),
             part_spec((pay_rows, HEADD), half, half),
             part_spec((CHUNK // TOKB, TOKB), 0, steps),
-            whole((rows, HEADD)),
-            whole((rows, HEADD)),
-            whole((rows, HEADD)),
-            whole(probs.shape),
+            pl.BlockSpec(memory_space=pl.ANY),
+            pl.BlockSpec(memory_space=pl.ANY),
+            pl.BlockSpec(memory_space=pl.ANY),
+            pl.BlockSpec(memory_space=pl.ANY),
         ],
         out_specs=(
             part_spec((CHUNK, 2 * HEADD), steps + 1, half),
             part_spec((CHUNK, 2 * HEADD), steps + 1 + half, half),
         ),
-        scratch_shapes=[pltpu.VMEM((rows, HEADD), f32)] * 3 + [pltpu.VMEM((TOKB, HEADD), f32)] * 2,
+        scratch_shapes=[pltpu.VMEM((rows, HEADD), bf)] * 3
+        + [pltpu.VMEM(probs.shape, bf)]
+        + [pltpu.VMEM((rows, HEADD), f32)] * 3
+        + [pltpu.VMEM((TOKB, HEADD), f32)] * 2
+        + [pltpu.SemaphoreType.DMA((4,))],
         compiler_params=pltpu.CompilerParams(vmem_limit_bytes=VMEM_LIMIT),
         name="attend_backward",
         cost_estimate=takes(44),
@@ -713,6 +755,96 @@
     )(order, back, *pieces)
 
 
+def layout_kernel(
+    heads, slot_rows, first_ref, code_ref, place_ref, bucket_ref, start_ref, low_ref, end_ref
+):
+    sources = code_ref.shape[0]
+    rows = place_ref.shape[0] // sources
+    own_spans = bucket_ref.shape[0]
+    categories = BUCKETS + 1
+    before = first_ref[0].astype(f32)
+    codes = code_ref[...].astype(f32)[:, :rows].reshape(sources * rows, 3 * TOKB)
+    slots = codes[:, :TOKB] * 256.0 + codes[:, TOKB : 2 * TOKB]
+    buckets = codes[:, 2 * TOKB :]
+    target = jnp.floor(slots * (1.0 / slot_rows))
+    block = target - before
+    local = slots - target * slot_rows
+    block_ids = lax.broadcasted_iota(jnp.int32, (16, TOKB), 0).astype(f32)
+    bucket_ids = lax.broadcasted_iota(jnp.int32, (TOKB, TOKB), 0).astype(f32)
+    counts = jnp.zeros((16, TOKB), f32)
+    for row in range(sources * rows):
+        left = jnp.where(block_ids == block[row : row + 1], 1.0, 0.0).astype(bf)
+        right = jnp.where(bucket_ids == buckets[row : row + 1], 1.0, 0.0).astype(bf)
+        counts += through(left, right)
+    lane_ids = lax.broadcasted_iota(jnp.int32, (16, TOKB), 1)
+    row_ids = lax.broadcasted_iota(jnp.int32, (16, TOKB), 0)
+    total = jnp.broadcast_to(jnp.sum(counts, axis=1, keepdims=True), counts.shape)
+    step = 1
+    while step < categories:
+        counts += jnp.where(lane_ids >= step, pltpu.roll(counts, step, 1), 0.0)
+        step *= 2
+    spans = jnp.where(row_ids == 0, 0.0, jnp.floor((total + (SPAN - 1)) * (1.0 / SPAN)))
+    start = spans
+    step = 1
+    while step < 16:
+        start += jnp.where(row_ids >= step, pltpu.roll(start, step, 0), 0.0)
+        step *= 2
+    start = (start - spans + 1.0) * SPAN
+    last_start = jnp.floor(jnp.maximum(total - 1.0, 0.0) * (1.0 / SPAN)) * SPAN
+    start = jnp.where(row_ids == 0, -last_start, start)
+    start_ref[...] = start
+    low_ref[...] = jnp.where(row_ids == 0, last_start, 0.0)
+    unused = (row_ids > heads) | (lane_ids >= categories)
+    ends = jnp.where(unused, 1e9, start + counts)
+    for bucket in range(categories):
+        wide = jnp.sum(jnp.where(lane_ids == bucket, ends, 0.0), axis=1, keepdims=True)
+        end_ref[bucket] = jnp.broadcast_to(wide, ends.shape)
+    place = jnp.full(local.shape, (own_spans + 1.0) * SPAN, f32)
+    for number in range(heads + 1):
+        here = (block == float(number)) & (local >= low_ref[number : number + 1, :])
+        place = jnp.where(here, local + start_ref[number : number + 1, :], place)
+    place_ref[...] = place.astype(jnp.int32)
+    shape = (own_spans, TOKB)
+    at = lax.broadcasted_iota(jnp.int32, shape, 0) * SPAN + lax.broadcasted_iota(jnp.int32, shape, 1)
+    at = at.astype(f32)
+    block_number = jnp.zeros(shape, f32)
+    for number in range(1, heads + 1):
+        block_number += jnp.where(at >= start_ref[number : number + 1, :], 1.0, 0.0)
+    passed = -block_number * categories
+
+    def count(bucket, passed):
+        for number in range(heads + 1):
+            passed += jnp.where(at >= end_ref[bucket, number : number + 1, :], 1.0, 0.0)
+        return passed
+
+    passed = lax.fori_loop(0, categories, count, passed)
+    bucket_ref[...] = jnp.where(
+        passed <= BUCKETS, (before + block_number) * BUCKETS + passed, -1.0
+    )
+
+
+def sorted_layout(first, codes, heads, slot_rows, own_spans, rows):
+    sources = codes.shape[0]
+    vm = pl.BlockSpec(memory_space=pltpu.VMEM)
+    return pl.pallas_call(
+        functools.partial(layout_kernel, heads, slot_rows),
+        out_shape=(
+            jax.ShapeDtypeStruct((sources * rows, TOKB), jnp.int32),
+            jax.ShapeDtypeStruct((own_spans, 2 * SPAN), f32),
+        ),
+        in_specs=[pl.BlockSpec(memory_space=pltpu.SMEM), vm],
+        out_specs=(vm, vm),
+        scratch_shapes=[
+            pltpu.VMEM((16, TOKB), f32),
+            pltpu.VMEM((16, TOKB), f32),
+            pltpu.VMEM((BUCKETS + 1, 16, TOKB), f32),
+        ],
+        compiler_params=pltpu.CompilerParams(vmem_limit_bytes=VMEM_LIMIT),
+        name="sorted_layout",
+        cost_estimate=takes(5),
+    )(first, codes)
+
+
 ALL = ("hd", "kk", "ry", "rc")
 SEQ = ("hd", "kk")
 ROUND = ("ry", "rc")
@@ -920,9 +1052,6 @@
     blocks = own_rows // TOKB
     both = 2 * HEADD
 
-    second_in = second_half.astype(f32)
-    unit, unit_scale = normalised(second_in)
-    unit_low = unit.astype(bf)
     vectors = jnp.stack([attn_gain, attn_shift, ffn_gain, ffn_shift], axis=1)
     vectors = jnp.pad(vectors, ((0, 0), (0, HEADD - 4)))
     wide = both + HEADD
@@ -940,12 +1069,19 @@
     codes = jnp.broadcast_to(codes[None], (heads,) + codes.shape)
     starter = jnp.concatenate([jnp.transpose(head_shard, (1, 0, 2)), codes], axis=1)
 
+    second_later, starter = together(second_half, starter)
+    second_in = second_later.astype(f32)
+    unit, unit_scale = normalised(second_in)
+    unit_low = unit.astype(bf)
     inner_split = inner_weight.reshape(weight_rows, seq_count, round_count, piece)
     inner_split = jnp.transpose(inner_split, (2, 0, 1, 3)).reshape(2, 2, weight_rows, -1)
-    unit_low, starter = together(unit_low, starter)
     ring = [(unit_low,)]
     up, down = ring_step(unit_low, unit_low)
-    up, down, starter, inner_split = together(up, down, exchange(starter), inner_split)
+    inner_rows = traded(traded(inner_split, "rc", 1), "ry", 0)
+    cut = round_count * weight_rows
+    output_rows = ordered(ordered(output_weight, "rc", 0), "ry", 0).reshape(cut, model_width)
+    shard = jnp.stack([inner_rows.reshape(cut, -1), outer_weight, output_rows])
+    up, down, starter, shard = together(up, down, exchange(starter), shard)
     ring.append((up, down))
 
     up, down = ring_step(up, down)
@@ -959,10 +1095,6 @@
     head_float = head_weight[:, :both].astype(f32)
     head_scaled = (head_float * attn_gain_col).astype(bf)
     head_offset = jnp.sum(head_float * attn_shift_col, axis=0, keepdims=True)
-    inner_rows = traded(traded(inner_split, "rc", 1), "ry", 0)
-    cut = round_count * weight_rows
-    output_rows = ordered(ordered(output_weight, "rc", 0), "ry", 0).reshape(cut, model_width)
-    shard = jnp.stack([inner_rows.reshape(cut, -1), outer_weight, output_rows])
     up, down, head_scaled, head_offset, shard, second_later = together(
         up, down, head_scaled, head_offset, shard, second_grad
     )
@@ -974,16 +1106,15 @@
 
     up, down = ring_step(up, down)
     first_heads = head_part([part for step in ring for part in step])
-    up, down, first_heads, codes, shard = together(up, down, first_heads, codes, shard)
+    up, down, codes, shard = together(up, down, codes, shard)
     ring.append((up, down))
 
     half = own_rows // 2
     up, down = ring_step(up[:half], down[half:])
+    up, down, first_swapped = together(up, down, swapped(first_heads, "ry"))
     ring.append((up, down))
     last_heads = head_part(ring[3] + ring[4])
-    head_own = []
-    for rows in (first_heads, last_heads):
-        head_own += [rows, swapped(rows, "ry")]
+    head_own = [first_heads, first_swapped, last_heads, swapped(last_heads, "ry")]
     head_own = jnp.concatenate([part.reshape(-1, both) for part in head_own], axis=0)
     place, key_bucket = sorted_layout(codes, slot_rows, own_spans)
     in_table, out_table = chunk_tables(groups)
@@ -1057,7 +1188,10 @@
     )
     qkv_rows = jnp.transpose(over_groups(qkv_rows), (2, 1, 0, 3, 4))
     back_own, back_peer = spread_pair(over_groups(back_parts))
-    back_own, second_far, qkv_rows = together(back_own, second_far, qkv_rows)
+    back_own, second_far, qkv_rows, output_part = together(
+        back_own, second_far, qkv_rows, output_part
+    )
+    output_rows = exchange(sum_groups(jnp.transpose(output_part, (1, 0, 2, 3))))
     second_far = swapped(second_far, "ry")
     qkv_got = swapped(qkv_rows, "ry")
     query_value_own, query_value_peer = attend_backward(
@@ -1076,20 +1210,25 @@
     packed = (2, groups, heads, own_rows, both)
     vector_rows = back_parts[:, own_rows + 2 * blocks : own_rows + 2 * blocks + 2]
     packed = (2, groups, heads, own_rows, both)
-    query_value_peer, qkv_got, second_far = together(query_value_peer, qkv_got, second_far)
+    query_value_peer, qkv_got, second_far, output_rows = together(
+        query_value_peer, qkv_got, second_far, output_rows
+    )
     second_sum = second_in + second_pair.astype(f32) + second_far.astype(f32)
-    head_back = pair_sum(query_value_own.reshape(packed), query_value_peer.reshape(packed), "rc")
-    head_back, output_part, vector_rows, qkv_rows, qkv_got = together(
-        head_back, output_part, vector_rows, qkv_rows, qkv_got
+    query_value_own = query_value_own.reshape(packed)
+    query_value_peer = swapped(query_value_peer.reshape(packed), "rc")
+
+    def summed(part):
+        return (query_value_own[part].astype(f32) + query_value_peer[part].astype(f32)).astype(bf)
+
+    head_send = summed(1)
+    head_send, output_rows, vector_rows, qkv_rows, qkv_got = together(
+        head_send, output_rows, vector_rows, qkv_rows, qkv_got
     )
     qkv_rows = pair_order(qkv_rows, qkv_got, "ry", 3)
     qkv_full = ordered(qkv_rows, "rc", 4).reshape(2, model_width, model_width)
-    output_rows = exchange(sum_groups(jnp.transpose(output_part, (1, 0, 2, 3))))
-    head_got, output_rows, qkv_full = together(
-        swapped(head_back[1], "ry"), output_rows, qkv_full
-    )
+    head_got, qkv_full, head_keep = together(swapped(head_send, "ry"), qkv_full, summed(0))
     output_grad = jnp.sum(output_rows.astype(f32), axis=0)
-    head_back = sum_groups(add_rows(head_back[0], head_got))
+    head_back = sum_groups(add_rows(head_keep, head_got))
     own_back = exchange(head_back)
     vector_sums = jnp.sum(vector_rows.astype(f32), axis=0)
     if groups > 1:

time: 445 us -> 437 us (0.982)
  waiting for transfers between devices: 141 us -> 132 us
  Pallas kernels: 123 us -> 117 us
  matrix products: 11.8 us -> 16.9 us
    all_to_all x7, waiting for transfers between devices: 45.1 us -> 22.7 us  [exchange(): return lax.all_to_all(parts, axes, split_axis=0, concat_axis=0, tiled=True)]
    ppermute x37, waiting for transfers between devices: 79.6 us -> 94.6 us  [swapped(): return lax.ppermute(value, axis, SWAP)]
    convert_element_type x9 -> x8, other arithmetic: 12.8 us -> 9.58 us  [pair_sum(): return (keep.astype(f32) + swapped(give, axis).astype(f32)).astype(bf)]
    unnamed x113 -> x118, local copies, waits for them, and re-layouts: 8.72 us -> 11.3 us
  transfers between devices with their start and end apart: 54 -> 54, of which waited for: 25 -> 27; matrix products, arithmetic and copies ran while one was open for 16% -> 18% of each run, Pallas kernels for 27% -> 26%
where the time goes in v4:
time: 437 us; the launch traced here: 429 us
  waiting for transfers between devices  132 us (30%)
  Pallas kernels  117 us (27%)
  starting transfers between devices  72.4 us (17%)
  other arithmetic  45.6 us (10%)
  local copies, waits for them, and re-layouts  30.3 us (7%)
  matrix products  16.9 us (4%)
  between operations  15.7 us (4%)
    ppermute x37, waiting for transfers between devices, swapped(): return lax.ppermute(value, axis, SWAP)  94.6 us
    pallas_call x1, Pallas kernels, attend_backward(): pl.pallas_call(functools.partial(backward_kernel, own_rows, steps), grid=...  41.5 us
    all_to_all x7, starting transfers between devices, exchange(): return lax.all_to_all(parts, axes, split_axis=0, concat_axis=0, tiled=True)  37 us
    pallas_call x1, Pallas kernels, attend_forward(): pl.pallas_call(functools.partial(forward_kernel, own_rows, steps), grid=(...  32.4 us
    ppermute x37, starting transfers between devices, swapped(): return lax.ppermute(value, axis, SWAP)  25.8 us
    all_to_all x7, waiting for transfers between devices, exchange(): return lax.all_to_all(parts, axes, split_axis=0, concat_axis=0, tiled=True)  22.7 us
    pallas_call x2, Pallas kernels, feed_forward(): pl.pallas_call(feed_kernel, grid=(2,), out_shape=(by_width, by_width, by_...  20.6 us
    ppermute x8, waiting for transfers between devices, ring_step(): return (lax.ppermute(up, 'hd', UP), lax.ppermute(down, 'hd', DOWN))  14.5 us
  transfers between devices with their start and end apart: 54, of which 27 were waited for; matrix products, arithmetic and copies ran while one was open for 18% of the time, Pallas kernels for 26%

profile of v4, /device:TPU:0, one launch (start us, length us, event | category | flops | bytes accessed | tf_op | source)
XLA Modules:
  0.0 429.3 jit_solution(7473815561106568741)
XLA Ops:
  13.6 2.9 collective-permute-start.1
  17.3 6.3 %all-to-all-start = ((bf16[8,48,384]{2,1,0:T(8,128)(2,1)}), bf16[8,48,384]{2,1,0:T(8,128)(2,1)S(1)}, u32[]{:S(2)}, u32[]{:S(2)}) async-start(bf16[8,48,384]{2,1,0:T(8,128)(2,1)} %copy.88), calls=%async_computation | async-start | bytes 589824 | tf_op jit(solution)/shard_map/all_to_all | solution.py:876
  27.4 4.2 collective-permute-done.5
  31.7 2.1 collective-permute-done.3
  34.8 2.5 all-to-all-done
  38.9 4.2 collective-permute-done.8
  49.5 9.3 %collective-permute-done.6.refs_3_ = bf16[256,1024]{1,0:T(8,128)(2,1)S(1)} collective-permute-done((bf16[256,1024]{1,0:T(8,128)(2,1)S(1)}, bf16[256,1024]{1,0:T(8,128)(2,1)S(1)}, u32[]{:S(2)}, u32[]{:S(2)}) %collective-permute-start.6) | collective-permute-done | bytes 524320 | tf_op jit(solution)/shard_map/ppermute | solution.py:930
  83.7 2.0 collective-permute-done.14
  85.8 2.6 collective-permute-done.12.refs_7_
  88.3 2.1 bitcast_dynamic-update-slice_fusion
  97.4 4.5 %collective-permute-done.15 = bf16[1,768,256]{2,1,0:T(8,128)(2,1)S(1)} collective-permute-done((bf16[1,768,256]{2,1,0:T(8,128)(2,1)S(1)}, bf16[1,768,256]{2,1,0:T(8,128)(2,1)S(1)}, u32[]{:S(2)}, u32[]{:S(2)}) %collective-permute-start.15) | collective-permute-done | bytes 393248 | tf_op jit(solution)/shard_map/ppermute | solution.py:880
  102.7 4.4 %collective-permute-done.16.peer_ref = bf16[4096,256]{1,0:T(8,128)(2,1)S(1)} collective-permute-done((bf16[4096,256]{1,0:T(8,128)(2,1)}, bf16[4096,256]{1,0:T(8,128)(2,1)S(1)}, u32[]{:S(2)}, u32[]{:S(2)}) %collective-permute-start.16) | collective-permute-done | bytes 2097184 | tf_op jit(solution)/shard_map/ppermute | solution.py:880
  108.5 32.4 %attend_forward.1 = (bf16[4352,128]{1,0:T(8,128)(2,1)}, bf16[4352,128]{1,0:T(8,128)(2,1)}, bf16[8832,128]{1,0:T(8,128)(2,1)}, bf16[8832,128]{1,0:T(8,128)(2,1)},...) custom-call(s32[32]{0:T(128)} %get-tuple-element.146.in_ref, ...), custom_call_target="tpu_custom_call" | custom-call | flops 3500000000 | bytes 105000000 | tf_op jit(solution)/shard_map/attend_forward/pallas_call | solution.py:262
  141.1 2.8 collective-permute-done.17
  147.3 13.1 %collective-permute-done.18 = bf16[1,8,272,128]{3,2,1,0:T(8,128)(2,1)S(1)} collective-permute-done((bf16[1,8,272,128]{3,2,1,0:T(8,128)(2,1)S(1)}, bf16[1,8,272,128]{3,2,1,0:T(8,128)(2,1)S(1)}, u32[]{:S(2)}, u32[]{:S(2)}) %collective-permute-start.18) | collective-permute-done | bytes 557088 | tf_op jit(solution)/shard_map/ppermute | solution.py:880
  161.3 5.3 %all-to-all-start.1 = ((bf16[8,272,128]{2,1,0:T(8,128)(2,1)}), bf16[8,272,128]{2,1,0:T(8,128)(2,1)S(1)}, u32[]{:S(2)}, u32[]{:S(2)}) async-start(bf16[8,272,128]{2,1,0:T(8,128)(2,1)} %fusion.23), calls=%async_computation.1 | async-start | bytes 1114112 | tf_op jit(solution)/shard_map/all_to_all | solution.py:876
  168.2 15.8 %all-to-all-done.1.parts_ref = bf16[8,272,128]{2,1,0:T(8,128)(2,1)S(1)} async-done(((bf16[8,272,128]{2,1,0:T(8,128)(2,1)}), bf16[8,272,128]{2,1,0:T(8,128)(2,1)S(1)}, u32[]{:S(2)}, u32[]{:S(2)}) %all-to-all-start.1) | async-done | bytes 557088 | tf_op jit(solution)/shard_map/all_to_all | solution.py:876
  184.8 4.3 %mix_rows.1 = (f32[256,1024]{1,0:T(8,128)}, bf16[256,1024]{1,0:T(8,128)(2,1)}, bf16[256,1024]{1,0:T(8,128)(2,1)}, f32[256,1024]{1,0:T(8,128)}, f32[256,1]{1,0:T(8,128)}, /*index=5*/bf16[256,1024]{1,0:T(8,128)(2,1)}) custom-call(bf16[8,272,128]{2,1,0:T(8,128)(2,1)} %copy-done.3, bf16[8,3,128,1024]{3,2,1,0:T(8,128)(2,1)} %bitcast.223, ...), custom_call_target="tpu_custom_call" | custom-call | flops 500000000 | bytes 15000000 | tf_op jit(solution)/shard_map/mix_rows/pallas_call | solution.py:608
  192.4 10.3 %feed_forward.2 = (bf16[512,1024]{1,0:T(8,128)(2,1)}, bf16[512,1024]{1,0:T(8,128)(2,1)}, bf16[512,1024]{1,0:T(8,128)(2,1)}, bf16[512,1024]{1,0:T(8,128)(2,1)}, b...) custom-call(bf16[256,1024]{1,0:T(8,128)(2,1)} %get-tuple-element.158, ...), custom_call_target="tpu_custom_call" | custom-call | flops 900000000 | bytes 27000000 | tf_op jit(solution)/shard_map/feed_forward/pallas_call | solution.py:565
  204.9 3.8 all-to-all-start.2
  208.7 10.3 %feed_forward.3 = (bf16[512,1024]{1,0:T(8,128)(2,1)}, bf16[512,1024]{1,0:T(8,128)(2,1)}, bf16[512,1024]{1,0:T(8,128)(2,1)}, bf16[512,1024]{1,0:T(8,128)(2,1)}, b...) custom-call(bf16[256,1024]{1,0:T(8,128)(2,1)} %collective-permute-do, ...), custom_call_target="tpu_custom_call" | custom-call | flops 900000000 | bytes 27000000 | tf_op jit(solution)/shard_map/feed_forward/pallas_call | solution.py:565
  219.7 2.5 fusion.45
  229.1 2.4 pad_maximum_fusion
  232.5 2.8 all-to-all-done.2
  235.3 5.4 %collective-permute-done.27.far_ref = bf16[256,1024]{1,0:T(8,128)(2,1)S(1)} collective-permute-done((bf16[256,1024]{1,0:T(8,128)(2,1)}, bf16[256,1024]{1,0:T(8,128)(2,1)S(1)}, u32[]{:S(2)}, u32[]{:S(2)}) %collective-permute-start.27) | collective-permute-done | bytes 524320 | tf_op jit(solution)/shard_map/ppermute | solution.py:880
  241.5 5.2 %carry_rows.1 = (bf16[256,1024]{1,0:T(8,128)(2,1)}, bf16[8,272,128]{2,1,0:T(8,128)(2,1)}) custom-call(bf16[256,1024]{1,0:T(8,128)(2,1)} %add_convert_fusion.5.near_ref, bf16[256,1024]{1,0:T(8,128)(2,1)} %copy-done.35, f32[1,1024]{1,0:T(1,128)} %bitcast.277, f32[256,1024]{1,0:T(8,128)} %get-tuple-element.200.unit_ref, f32[256,1]{1,0:T(8,128)} %get-tuple-element.201.scale_ref, ...), custom_call_target="tpu_custom_call" | custom-call | flops 500000000 | bytes 15000000 | tf_op jit(solution)/shard_map/carry_rows/pallas_call | solution.py:657
  250.1 5.7 %all-to-all-start.3 = ((bf16[8,272,128]{2,1,0:T(8,128)(2,1)}), bf16[8,272,128]{2,1,0:T(8,128)(2,1)S(1)}, u32[]{:S(2)}, u32[]{:S(2)}) async-start(bf16[8,272,128]{2,1,0:T(8,128)(2,1)} %get-tuple-element.203), calls=%async_computation.3 | async-start | bytes 1114112 | tf_op jit(solution)/shard_map/all_to_all | solution.py:876
  260.6 2.0 add_convert_fusion.2
  262.7 9.3 %collective-permute-done.29 = bf16[8,1,32,1024]{3,2,0,1:T(8,128)(2,1)S(1)} collective-permute-done((bf16[8,1,32,1024]{3,2,0,1:T(8,128)(2,1)S(1)}, bf16[8,1,32,1024]{3,2,0,1:T(8,128)(2,1)S(1)}, u32[]{:S(2)}, u32[]{:S(2)}) %collective-permute-start.29) | collective-permute-done | bytes 524320 | tf_op jit(solution)/shard_map/ppermute | solution.py:880
  274.5 12.5 %collective-permute-done.32 = bf16[1,8,272,128]{3,2,1,0:T(8,128)(2,1)} collective-permute-done((bf16[1,8,272,128]{3,2,1,0:T(8,128)(2,1)S(1)}, bf16[1,8,272,128]{3,2,1,0:T(8,128)(2,1)}, u32[]{:S(2)}, u32[]{:S(2)}) %collective-permute-start.32) | collective-permute-done | bytes 557088 | tf_op jit(solution)/shard_map/ppermute | solution.py:880
  287.0 2.2 pad_maximum_fusion.3
  290.6 5.4 %all-to-all-start.4 = ((bf16[8,32,1024]{2,1,0:T(8,128)(2,1)}), bf16[8,32,1024]{2,1,0:T(8,128)(2,1)S(1)}, u32[]{:S(2)}, u32[]{:S(2)}) async-start(bf16[8,32,1024]{2,1,0:T(8,128)(2,1)} %bitcast.251), calls=%async_computation.4 | async-start | bytes 1048576 | tf_op jit(solution)/shard_map/all_to_all | solution.py:876
  296.5 41.5 %attend_backward.1 = (bf16[4096,256]{1,0:T(8,128)(2,1)}, bf16[4096,256]{1,0:T(8,128)(2,1)}) custom-call(s32[32]{0:T(128)} %get-tuple-element.147.out_ref.table_ref, s32[8192]{0:T(1024)} %broadcast_add_fusion.place_ref, bf16[4352,128]{1,0:T(8,128)(2,1)} %bitcast.61.pay_own_ref, bf16[4352,128]{1,0:T(8,128)(2,1)} %bitcast.62.pay_peer_ref, ...), custom_call_target="tpu_custom_call" | custom-call | flops 4400000000 | bytes 132000000 | tf_op jit(solution)/shard_map/attend_backward/pallas_call | solution.py:468
  338.2 1.8 fusion.43
  340.0 2.5 collective-permute-done.36
  342.5 2.0 fusion.1
  351.9 1.9 select_bitcast_fusion.1
  354.2 2.4 copy.95
  356.6 16.7 %collective-permute-done.37 = bf16[1,8,256,256]{3,2,1,0:T(8,128)(2,1)} collective-permute-done((bf16[1,8,256,256]{3,2,1,0:T(8,128)(2,1)}, bf16[1,8,256,256]{3,2,1,0:T(8,128)(2,1)}, u32[]{:S(2)}, u32[]{:S(2)}) %collective-permute-start.37) | collective-permute-done | bytes 1048608 | tf_op jit(solution)/shard_map/ppermute | solution.py:880
  373.3 2.4 add_rows.1
  375.8 6.0 %all-to-all-start.5 = ((bf16[8,256,256]{2,1,0:T(8,128)(2,1)}), bf16[8,256,256]{2,1,0:T(8,128)(2,1)S(1)}, u32[]{:S(2)}, u32[]{:S(2)}) async-start(bf16[8,256,256]{2,1,0:T(8,128)(2,1)} %bitcast.230), calls=%async_computation.5 | async-start | bytes 2097152 | tf_op jit(solution)/shard_map/all_to_all | solution.py:876
  381.8 2.1 fusion.20
  383.9 4.9 %weight_part.1 = (f32[1024,256]{1,0:T(8,128)}, f32[8,256]{1,0:T(8,128)}) custom-call(s32[8]{0:T(128)} %copy-done, bf16[8,256,256]{2,1,0:T(8,128)(2,1)} %bitcast.231, bf16[256,1024]{1,0:T(8,128)(2,1)} %copy-done.4, bf16[256,1024]{1,0:T(8,128)(2,1)} %copy-done.15, bf16[256,1024]{1,0:T(8,128)(2,1)} %copy-done.14, bf16[256,1024]{1,0:T(8,128)(2,1)} %copy-done.17, ...), custom_call_target="tpu_custom_call" | custom-call | flops 500000000 | bytes 15000000 | tf_op jit(solution)/shard_map/weight_part/pallas_call | solution.py:744
  393.2 1.9 fusion.32
  397.4 4.1 collective-permute-done.41
  401.6 3.4 collective-permute-done.40
  407.4 4.7 %all-to-all-start.6 = ((bf16[8,48,256]{2,1,0:T(8,128)(2,1)}), bf16[8,48,256]{2,1,0:T(8,128)(2,1)S(1)}, u32[]{:S(2)}, u32[]{:S(2)}) async-start(bf16[8,48,256]{2,1,0:T(8,128)(2,1)} %fusion.33), calls=%async_computation.7 | async-start | bytes 393216 | tf_op jit(solution)/shard_map/all_to_all | solution.py:876
  414.8 5.3 %last_rows.1 = bf16[256,1024]{1,0:T(8,128)(2,1)} custom-call(bf16[8,256,256]{2,1,0:T(8,128)(2,1)} %copy-done.8, bf16[2,1024,1024]{2,1,0:T(8,128)(2,1)} %bitcast.229, f32[1,1024]{1,0:T(1,128)} %bitcast.278, f32[256,1024]{1,0:T(8,128)} %get-tuple-element.265.unit_ref, f32[256,1]{1,0:T(8,128)} %copy.96.scale_ref, bf16[256,1024]{1,0:T(8,128)(2,1)} %grad_ref.3), custom_call_target="tpu_custom_call" | custom-call | flops 600000000 | bytes 18000000 | tf_op jit(solution)/shard_map/last_rows/pallas_call | solution.py:713
  (331 shorter events, 109.7 us)
Async XLA Ops:
  13.6 23.7 %collective-permute-start.1 = (bf16[256,1024]{1,0:T(8,128)(2,1)S(1)}, bf16[256,1024]{1,0:T(8,128)(2,1)S(1)}, u32[]{:S(2)}, u32[]{:S(2)}) collective-permute-start(bf16[256,1024]{1,0:T(8,128)(2,1)S(1)} %get-tuple-element.266.refs_0_), channel_id=1, source_target_pairs={{8,0},{16,8},{24,16},{28,24},{20,28},{12,20},{4,12},{0,4},{9,1},{1... | collective-permute-start | bytes 1572872 | tf_op jit(solution)/shard_map/ppermute | solution.py:930
  16.5 20.8 %collective-permute-start = (bf16[256,1024]{1,0:T(8,128)(2,1)S(1)}, bf16[256,1024]{1,0:T(8,128)(2,1)S(1)}, u32[]{:S(2)}, u32[]{:S(2)}) collective-permute-start(bf16[256,1024]{1,0:T(8,128)(2,1)S(1)} %get-tuple-element.266.refs_0_), channel_id=1, source_target_pairs={{0,8},{8,16},{16,24},{24,28},{28,20},{20,12},{12,4},{4,0},{1,9},{9... | collective-permute-start | bytes 1572872 | tf_op jit(solution)/shard_map/ppermute | solution.py:930
  16.6 7.7 %collective-permute-start.4 = (bf16[32,1024]{1,0:T(8,128)(2,1)S(1)}, bf16[32,1024]{1,0:T(8,128)(2,1)}, u32[]{:S(2)}, u32[]{:S(2)}) collective-permute-start(bf16[32,1024]{1,0:T(8,128)(2,1)S(1)} %copy-done.42), channel_id=1, source_target_pairs={{0,1},{1,0},{2,3},{3,2},{4,5},{5,4},{6,7},{7,6},{8,9},{9,8},{10,11... | collective-permute-start | bytes 196616 | tf_op jit(solution)/shard_map/ppermute | solution.py:880
  17.3 19.9 %all-to-all-start = ((bf16[8,48,384]{2,1,0:T(8,128)(2,1)}), bf16[8,48,384]{2,1,0:T(8,128)(2,1)S(1)}, u32[]{:S(2)}, u32[]{:S(2)}) async-start(bf16[8,48,384]{2,1,0:T(8,128)(2,1)} %copy.88), calls=%async_computation | async-start | bytes 589824 | tf_op jit(solution)/shard_map/all_to_all | solution.py:876
  23.6 160.3 %all-gather.3.cloned.1.call-start = ((), (), s32[]{:S(2)}) async-start(), calls=%async_computation.9 | async-start | bytes 7077888 | tf_op jit(solution)/shard_map/all_gather | solution.py:1129
  25.2 6.4 %collective-permute-start.5 = (bf16[2,32,1024]{2,1,0:T(8,128)(2,1)S(1)}, bf16[2,32,1024]{2,1,0:T(8,128)(2,1)S(1)}, u32[]{:S(2)}, u32[]{:S(2)}) collective-permute-start(bf16[2,32,1024]{2,1,0:T(8,128)(2,1)S(1)} %pad_maximum_fusion.10), channel_id=1, source_target_pairs={{0,2},{2,0},{1,3},{3,1},{4,6},{6,4},{5,7},{7,5},{8,10},{10,8},{9,1... | collective-permute-start | bytes 393224 | tf_op jit(solution)/shard_map/ppermute | solution.py:880
  26.8 6.9 %collective-permute-start.3 = (bf16[1,2,32,1024]{3,2,1,0:T(8,128)(2,1)S(1)}, bf16[1,2,32,1024]{3,2,1,0:T(8,128)(2,1)S(1)}, u32[]{:S(2)}, u32[]{:S(2)}) collective-permute-start(bf16[1,2,32,1024]{3,2,1,0:T(8,128)(2,1)S(1)} %constant_dynamic-slice_fusion.3), channel_id=1, source_target_pairs={{0,2},{2,0},{1,3},{3,1},{4,6},{6,4},{5,7},{7,5},{8,10},{10,8},{9,1... | collective-permute-start | bytes 393224 | tf_op jit(solution)/shard_map/ppermute | solution.py:880
  37.3 5.7 %collective-permute-start.8 = (bf16[8,1,32,384]{3,2,0,1:T(8,128)(2,1)S(1)}, bf16[8,1,32,384]{3,2,0,1:T(8,128)(2,1)S(1)}, u32[]{:S(2)}, u32[]{:S(2)}) collective-permute-start(bf16[8,1,32,384]{3,2,0,1:T(8,128)(2,1)S(1)} %slice.149), channel_id=1, source_target_pairs={{0,2},{2,0},{1,3},{3,1},{4,6},{6,4},{5,7},{7,5},{8,10},{10,8},{9,1... | collective-permute-start | bytes 589832 | tf_op jit(solution)/shard_map/ppermute | solution.py:880
  44.5 14.3 %collective-permute-start.6 = (bf16[256,1024]{1,0:T(8,128)(2,1)S(1)}, bf16[256,1024]{1,0:T(8,128)(2,1)S(1)}, u32[]{:S(2)}, u32[]{:S(2)}) collective-permute-start(bf16[256,1024]{1,0:T(8,128)(2,1)S(1)} %collective-permute-done.refs_1_), channel_id=1, source_target_pairs={{0,8},{8,16},{16,24},{24,28},{28,20},{20,12},{12,4},{4,0},{1,9},{9... | collective-permute-start | bytes 1572872 | tf_op jit(solution)/shard_map/ppermute | solution.py:930
  45.7 14.0 %collective-permute-start.7 = (bf16[256,1024]{1,0:T(8,128)(2,1)S(1)}, bf16[256,1024]{1,0:T(8,128)(2,1)S(1)}, u32[]{:S(2)}, u32[]{:S(2)}) collective-permute-start(bf16[256,1024]{1,0:T(8,128)(2,1)S(1)} %collective-permute-done.1.refs_2_), channel_id=1, source_target_pairs={{8,0},{16,8},{24,16},{28,24},{20,28},{12,20},{4,12},{0,4},{9,1},{1... | collective-permute-start | bytes 1572872 | tf_op jit(solution)/shard_map/ppermute | solution.py:930
  59.7 13.2 %collective-permute-start.10 = (bf16[256,1024]{1,0:T(8,128)(2,1)S(1)}, bf16[256,1024]{1,0:T(8,128)(2,1)S(1)}, u32[]{:S(2)}, u32[]{:S(2)}) collective-permute-start(bf16[256,1024]{1,0:T(8,128)(2,1)S(1)} %collective-permute-done.6.refs_3_), channel_id=1, source_target_pairs={{0,8},{8,16},{16,24},{24,28},{28,20},{20,12},{12,4},{4,0},{1,9},{9... | collective-permute-start | bytes 1572872 | tf_op jit(solution)/shard_map/ppermute | solution.py:930
  60.4 12.9 %collective-permute-start.11 = (bf16[256,1024]{1,0:T(8,128)(2,1)S(1)}, bf16[256,1024]{1,0:T(8,128)(2,1)S(1)}, u32[]{:S(2)}, u32[]{:S(2)}) collective-permute-start(bf16[256,1024]{1,0:T(8,128)(2,1)S(1)} %collective-permute-done.7.refs_4_), channel_id=1, source_target_pairs={{8,0},{16,8},{24,16},{28,24},{20,28},{12,20},{4,12},{0,4},{9,1},{1... | collective-permute-start | bytes 1572872 | tf_op jit(solution)/shard_map/ppermute | solution.py:930
  69.9 15.8 %collective-permute-start.14 = (bf16[1,1280,256]{2,1,0:T(8,128)(2,1)}, bf16[1,1280,256]{2,1,0:T(8,128)(2,1)}, u32[]{:S(2)}, u32[]{:S(2)}) collective-permute-start(bf16[1,1280,256]{2,1,0:T(8,128)(2,1)} %bitcast_dynamic-update-slice_fusion.2), channel_id=1, source_target_pairs={{0,2},{2,0},{1,3},{3,1},{4,6},{6,4},{5,7},{7,5},{8,10},{10,8},{9,1... | collective-permute-start | bytes 1966088 | tf_op jit(solution)/shard_map/ppermute | solution.py:880
  77.4 8.3 %collective-permute-start.13 = (bf16[128,1024]{1,0:T(8,128)(2,1)}, bf16[128,1024]{1,0:T(8,128)(2,1)S(1)}, u32[]{:S(2)}, u32[]{:S(2)}) collective-permute-start(bf16[128,1024]{1,0:T(8,128)(2,1)} %slice.117), channel_id=1, source_target_pairs={{8,0},{16,8},{24,16},{28,24},{20,28},{12,20},{4,12},{0,4},{9,1},{1... | collective-permute-start | bytes 786440 | tf_op jit(solution)/shard_map/ppermute | solution.py:930
  78.8 9.6 %collective-permute-start.12 = (bf16[128,1024]{1,0:T(8,128)(2,1)S(1)}, bf16[128,1024]{1,0:T(8,128)(2,1)S(1)}, u32[]{:S(2)}, u32[]{:S(2)}) collective-permute-start(bf16[128,1024]{1,0:T(8,128)(2,1)S(1)} %slice.116), channel_id=1, source_target_pairs={{0,8},{8,16},{16,24},{24,28},{28,20},{20,12},{12,4},{4,0},{1,9},{9... | collective-permute-start | bytes 786440 | tf_op jit(solution)/shard_map/ppermute | solution.py:930
  94.1 7.8 %collective-permute-start.15 = (bf16[1,768,256]{2,1,0:T(8,128)(2,1)S(1)}, bf16[1,768,256]{2,1,0:T(8,128)(2,1)S(1)}, u32[]{:S(2)}, u32[]{:S(2)}) collective-permute-start(bf16[1,768,256]{2,1,0:T(8,128)(2,1)S(1)} %pad_maximum_fusion.7), channel_id=1, source_target_pairs={{0,2},{2,0},{1,3},{3,1},{4,6},{6,4},{5,7},{7,5},{8,10},{10,8},{9,1... | collective-permute-start | bytes 1179656 | tf_op jit(solution)/shard_map/ppermute | solution.py:880
  102.7 4.4 %collective-permute-start.16 = (bf16[4096,256]{1,0:T(8,128)(2,1)}, bf16[4096,256]{1,0:T(8,128)(2,1)S(1)}, u32[]{:S(2)}, u32[]{:S(2)}) collective-permute-start(bf16[4096,256]{1,0:T(8,128)(2,1)} %bitcast_dynamic-update-slice_fusion.1.own_ref), channel_id=1, source_target_pairs={{0,1},{1,0},{2,3},{3,2},{4,5},{5,4},{6,7},{7,6},{8,9},{9,8},{10,11... | collective-permute-start | bytes 6291464 | tf_op jit(solution)/shard_map/ppermute | solution.py:880
  145.6 14.7 %collective-permute-start.18 = (bf16[1,8,272,128]{3,2,1,0:T(8,128)(2,1)S(1)}, bf16[1,8,272,128]{3,2,1,0:T(8,128)(2,1)S(1)}, u32[]{:S(2)}, u32[]{:S(2)}) collective-permute-start(bf16[1,8,272,128]{3,2,1,0:T(8,128)(2,1)S(1)} %slice_bitcast_fusion.2), channel_id=1, source_target_pairs={{0,2},{2,0},{1,3},{3,1},{4,6},{6,4},{5,7},{7,5},{8,10},{10,8},{9,1... | collective-permute-start | bytes 1671176 | tf_op jit(solution)/shard_map/ppermute | solution.py:880
  161.3 22.6 %all-to-all-start.1 = ((bf16[8,272,128]{2,1,0:T(8,128)(2,1)}), bf16[8,272,128]{2,1,0:T(8,128)(2,1)S(1)}, u32[]{:S(2)}, u32[]{:S(2)}) async-start(bf16[8,272,128]{2,1,0:T(8,128)(2,1)} %fusion.23), calls=%async_computation.1 | async-start | bytes 1114112 | tf_op jit(solution)/shard_map/all_to_all | solution.py:876
  166.6 24.0 %collective-permute-start.23 = (bf16[256,1024]{1,0:T(8,128)(2,1)S(1)}, bf16[256,1024]{1,0:T(8,128)(2,1)S(1)}, u32[]{:S(2)}, u32[]{:S(2)}) collective-permute-start(bf16[256,1024]{1,0:T(8,128)(2,1)S(1)} %copy-done.11), channel_id=1, source_target_pairs={{0,2},{2,0},{1,3},{3,1},{4,6},{6,4},{5,7},{7,5},{8,10},{10,8},{9,1... | collective-permute-start | bytes 1572872 | tf_op jit(solution)/shard_map/ppermute | solution.py:880
  168.2 22.6 %collective-permute-start.21 = (bf16[256,1024]{1,0:T(8,128)(2,1)S(1)}, bf16[256,1024]{1,0:T(8,128)(2,1)S(1)}, u32[]{:S(2)}, u32[]{:S(2)}) collective-permute-start(bf16[256,1024]{1,0:T(8,128)(2,1)S(1)} %copy-done.11), channel_id=1, source_target_pairs={{0,1},{1,0},{2,3},{3,2},{4,5},{5,4},{6,7},{7,6},{8,9},{9,8},{10,11... | collective-permute-start | bytes 1572872 | tf_op jit(solution)/shard_map/ppermute | solution.py:880
  189.1 14.7 %collective-permute-start.19 = (bf16[256,1024]{1,0:T(8,128)(2,1)}, bf16[256,1024]{1,0:T(8,128)(2,1)}, u32[]{:S(2)}, u32[]{:S(2)}) collective-permute-start(bf16[256,1024]{1,0:T(8,128)(2,1)} %get-tuple-element.158.own_ref), channel_id=1, source_target_pairs={{0,2},{2,0},{1,3},{3,1},{4,6},{6,4},{5,7},{7,5},{8,10},{10,8},{9,1... | collective-permute-start | bytes 1572872 | tf_op jit(solution)/shard_map/ppermute | solution.py:880
  190.6 18.1 %collective-permute-start.24 = (bf16[256,1024]{1,0:T(8,128)(2,1)S(1)}, bf16[256,1024]{1,0:T(8,128)(2,1)}, u32[]{:S(2)}, u32[]{:S(2)}) collective-permute-start(bf16[256,1024]{1,0:T(8,128)(2,1)S(1)} %collective-permute-done.23.grad_own_ref), channel_id=1, source_target_pairs={{0,1},{1,0},{2,3},{3,2},{4,5},{5,4},{6,7},{7,6},{8,9},{9,8},{10,11... | collective-permute-start | bytes 1572872 | tf_op jit(solution)/shard_map/ppermute | solution.py:880
  203.7 4.9 %collective-permute-start.22 = (bf16[256,1024]{1,0:T(8,128)(2,1)}, bf16[256,1024]{1,0:T(8,128)(2,1)}, u32[]{:S(2)}, u32[]{:S(2)}) collective-permute-start(bf16[256,1024]{1,0:T(8,128)(2,1)} %collective-permute-done.19.own_ref), channel_id=1, source_target_pairs={{0,1},{1,0},{2,3},{3,2},{4,5},{5,4},{6,7},{7,6},{8,9},{9,8},{10,11... | collective-permute-start | bytes 1572872 | tf_op jit(solution)/shard_map/ppermute | solution.py:880
  204.9 30.4 %all-to-all-start.2 = ((bf16[8,2,32,1024]{3,2,1,0:T(8,128)(2,1)}), bf16[8,2,32,1024]{3,2,1,0:T(8,128)(2,1)S(1)}, u32[]{:S(2)}, u32[]{:S(2)}) async-start(bf16[8,2,32,1024]{3,2,1,0:T(8,128)(2,1)} %broadcast_in_dim.32), calls=%async_computation.2 | async-start | bytes 2097152 | tf_op jit(solution)/shard_map/all_to_all | solution.py:876
  219.0 12.5 %collective-permute-start.25 = (bf16[256,1024]{1,0:T(8,128)(2,1)}, bf16[256,1024]{1,0:T(8,128)(2,1)S(1)}, u32[]{:S(2)}, u32[]{:S(2)}) collective-permute-start(bf16[256,1024]{1,0:T(8,128)(2,1)} %get-tuple-element.186), channel_id=1, source_target_pairs={{0,1},{1,0},{2,3},{3,2},{4,5},{5,4},{6,7},{7,6},{8,9},{9,8},{10,11... | collective-permute-start | bytes 1572872 | tf_op jit(solution)/shard_map/ppermute | solution.py:880
  219.6 5.6 %collective-permute-start.26 = (bf16[256,1024]{1,0:T(8,128)(2,1)}, bf16[256,1024]{1,0:T(8,128)(2,1)S(1)}, u32[]{:S(2)}, u32[]{:S(2)}) collective-permute-start(bf16[256,1024]{1,0:T(8,128)(2,1)} %get-tuple-element.188), channel_id=1, source_target_pairs={{0,1},{1,0},{2,3},{3,2},{4,5},{5,4},{6,7},{7,6},{8,9},{9,8},{10,11... | collective-permute-start | bytes 1572872 | tf_op jit(solution)/shard_map/ppermute | solution.py:880
  226.2 14.5 %collective-permute-start.27 = (bf16[256,1024]{1,0:T(8,128)(2,1)}, bf16[256,1024]{1,0:T(8,128)(2,1)S(1)}, u32[]{:S(2)}, u32[]{:S(2)}) collective-permute-start(bf16[256,1024]{1,0:T(8,128)(2,1)} %add_convert_fusion.4), channel_id=1, source_target_pairs={{0,2},{2,0},{1,3},{3,1},{4,6},{6,4},{5,7},{7,5},{8,10},{10,8},{9,1... | collective-permute-start | bytes 1572872 | tf_op jit(solution)/shard_map/ppermute | solution.py:880
  249.6 6.5 %collective-permute-start.28 = (bf16[8,1,2,32,1024]{4,3,2,0,1:T(8,128)(2,1)}, bf16[8,1,2,32,1024]{4,3,2,0,1:T(8,128)(2,1)}, u32[]{:S(2)}, u32[]{:S(2)}) collective-permute-start(bf16[8,1,2,32,1024]{4,3,2,0,1:T(8,128)(2,1)} %dynamic-slice_bitcast_fusion), channel_id=1, source_target_pairs={{0,1},{1,0},{2,3},{3,2},{4,5},{5,4},{6,7},{7,6},{8,9},{9,8},{10,11... | collective-permute-start | bytes 3145736 | tf_op jit(solution)/shard_map/ppermute | solution.py:880
  249.6 9.8 %collective-permute-start.30 = (bf16[256,1024]{1,0:T(8,128)(2,1)}, bf16[256,1024]{1,0:T(8,128)(2,1)}, u32[]{:S(2)}, u32[]{:S(2)}) collective-permute-start(bf16[256,1024]{1,0:T(8,128)(2,1)} %get-tuple-element.207), channel_id=1, source_target_pairs={{0,1},{1,0},{2,3},{3,2},{4,5},{5,4},{6,7},{7,6},{8,9},{9,8},{10,11... | collective-permute-start | bytes 1572872 | tf_op jit(solution)/shard_map/ppermute | solution.py:880
  250.1 10.5 %collective-permute-start.31 = (bf16[256,1024]{1,0:T(8,128)(2,1)}, bf16[256,1024]{1,0:T(8,128)(2,1)}, u32[]{:S(2)}, u32[]{:S(2)}) collective-permute-start(bf16[256,1024]{1,0:T(8,128)(2,1)} %get-tuple-element.209), channel_id=1, source_target_pairs={{0,1},{1,0},{2,3},{3,2},{4,5},{5,4},{6,7},{7,6},{8,9},{9,8},{10,11... | collective-permute-start | bytes 1572872 | tf_op jit(solution)/shard_map/ppermute | solution.py:880
  250.1 22.9 %all-to-all-start.3 = ((bf16[8,272,128]{2,1,0:T(8,128)(2,1)}), bf16[8,272,128]{2,1,0:T(8,128)(2,1)S(1)}, u32[]{:S(2)}, u32[]{:S(2)}) async-start(bf16[8,272,128]{2,1,0:T(8,128)(2,1)} %get-tuple-element.203), calls=%async_computation.3 | async-start | bytes 1114112 | tf_op jit(solution)/shard_map/all_to_all | solution.py:876
  255.8 137.4 %reduce-scatter.2.cloned.1.call-start = ((), (), s32[]{:S(2)}) async-start(), calls=%async_computation.8 | async-start | bytes 4718592 | tf_op jit(solution)/shard_map/reduce_scatter | solution.py:1170
  257.8 14.1 %collective-permute-start.29 = (bf16[8,1,32,1024]{3,2,0,1:T(8,128)(2,1)S(1)}, bf16[8,1,32,1024]{3,2,0,1:T(8,128)(2,1)S(1)}, u32[]{:S(2)}, u32[]{:S(2)}) collective-permute-start(bf16[8,1,32,1024]{3,2,0,1:T(8,128)(2,1)S(1)} %dynamic-slice_bitcast_fusion.1), channel_id=1, source_target_pairs={{0,2},{2,0},{1,3},{3,1},{4,6},{6,4},{5,7},{7,5},{8,10},{10,8},{9,1... | collective-permute-start | bytes 1572872 | tf_op jit(solution)/shard_map/ppermute | solution.py:880
  272.9 14.0 %collective-permute-start.32 = (bf16[1,8,272,128]{3,2,1,0:T(8,128)(2,1)S(1)}, bf16[1,8,272,128]{3,2,1,0:T(8,128)(2,1)}, u32[]{:S(2)}, u32[]{:S(2)}) collective-permute-start(bf16[1,8,272,128]{3,2,1,0:T(8,128)(2,1)S(1)} %bitcast.249), channel_id=1, source_target_pairs={{0,2},{2,0},{1,3},{3,1},{4,6},{6,4},{5,7},{7,5},{8,10},{10,8},{9,1... | collective-permute-start | bytes 1671176 | tf_op jit(solution)/shard_map/ppermute | solution.py:880
  289.1 7.4 %collective-permute-start.33 = (bf16[2,1,8,272,128]{4,3,2,1,0:T(8,128)(2,1)}, bf16[2,1,8,272,128]{4,3,2,1,0:T(8,128)(2,1)}, u32[]{:S(2)}, u32[]{:S(2)}) collective-permute-start(bf16[2,1,8,272,128]{4,3,2,1,0:T(8,128)(2,1)} %pad_maximum_fusion.3), channel_id=1, source_target_pairs={{0,1},{1,0},{2,3},{3,2},{4,5},{5,4},{6,7},{7,6},{8,9},{9,8},{10,11... | collective-permute-start | bytes 3342344 | tf_op jit(solution)/shard_map/ppermute | solution.py:880
  289.2 49.0 %collective-permute-start.34 = (bf16[2,8,1,32,1024]{4,3,0,1,2:T(8,128)(2,1)S(1)}, bf16[2,8,1,32,1024]{4,3,0,1,2:T(8,128)(2,1)}, u32[]{:S(2)}, u32[]{:S(2)}) collective-permute-start(bf16[2,8,1,32,1024]{4,3,0,1,2:T(8,128)(2,1)S(1)} %bitcast.238), channel_id=1, source_target_pairs={{0,2},{2,0},{1,3},{3,1},{4,6},{6,4},{5,7},{7,5},{8,10},{10,8},{9,1... | collective-permute-start | bytes 3145736 | tf_op jit(solution)/shard_map/ppermute | solution.py:880
  290.6 47.5 %all-to-all-start.4 = ((bf16[8,32,1024]{2,1,0:T(8,128)(2,1)}), bf16[8,32,1024]{2,1,0:T(8,128)(2,1)S(1)}, u32[]{:S(2)}, u32[]{:S(2)}) async-start(bf16[8,32,1024]{2,1,0:T(8,128)(2,1)} %bitcast.251), calls=%async_computation.4 | async-start | bytes 1048576 | tf_op jit(solution)/shard_map/all_to_all | solution.py:876
  296.0 42.1 %collective-permute-start.35 = (bf16[256,1024]{1,0:T(8,128)(2,1)}, bf16[256,1024]{1,0:T(8,128)(2,1)}, u32[]{:S(2)}, u32[]{:S(2)}) collective-permute-start(bf16[256,1024]{1,0:T(8,128)(2,1)} %add_convert_fusion.2), channel_id=1, source_target_pairs={{0,2},{2,0},{1,3},{3,1},{4,6},{6,4},{5,7},{7,5},{8,10},{10,8},{9,1... | collective-permute-start | bytes 1572872 | tf_op jit(solution)/shard_map/ppermute | solution.py:880
  338.1 4.4 %collective-permute-start.36 = (bf16[2,1,8,256,256]{4,3,2,1,0:T(8,128)(2,1)}, bf16[2,1,8,256,256]{4,3,2,1,0:T(8,128)(2,1)S(1)}, u32[]{:S(2)}, u32[]{:S(2)}) collective-permute-start(bf16[2,1,8,256,256]{4,3,2,1,0:T(8,128)(2,1)} %bitcast.292), channel_id=1, source_target_pairs={{0,1},{1,0},{2,3},{3,2},{4,5},{5,4},{6,7},{7,6},{8,9},{9,8},{10,11... | collective-permute-start | bytes 6291464 | tf_op jit(solution)/shard_map/ppermute | solution.py:880
  347.4 4.5 %collective-permute-start.38 = (bf16[2,8,1,2,32,1024]{5,4,0,1,3,2:T(8,128)(2,1)}, bf16[2,8,1,2,32,1024]{5,4,0,1,3,2:T(8,128)(2,1)}, u32[]{:S(2)}, u32[]{:S(2)}) collective-permute-start(bf16[2,8,1,2,32,1024]{5,4,0,1,3,2:T(8,128)(2,1)} %pad_maximum_fusion.2), channel_id=1, source_target_pairs={{0,1},{1,0},{2,3},{3,2},{4,5},{5,4},{6,7},{7,6},{8,9},{9,8},{10,11... | collective-permute-start | bytes 6291464 | tf_op jit(solution)/shard_map/ppermute | solution.py:880
  347.6 25.7 %collective-permute-start.37 = (bf16[1,8,256,256]{3,2,1,0:T(8,128)(2,1)}, bf16[1,8,256,256]{3,2,1,0:T(8,128)(2,1)}, u32[]{:S(2)}, u32[]{:S(2)}) collective-permute-start(bf16[1,8,256,256]{3,2,1,0:T(8,128)(2,1)} %get-tuple-element.231), channel_id=1, source_target_pairs={{0,2},{2,0},{1,3},{3,1},{4,6},{6,4},{5,7},{7,5},{8,10},{10,8},{9,1... | collective-permute-start | bytes 3145736 | tf_op jit(solution)/shard_map/ppermute | solution.py:880
  350.0 33.9 %collective-permute-start.43 = (f32[8,2,128]{2,1,0:T(2,128)S(1)}, f32[8,2,128]{2,1,0:T(2,128)S(1)}, u32[]{:S(2)}, u32[]{:S(2)}) collective-permute-start(f32[8,2,128]{2,1,0:T(2,128)S(1)} %bitcast.284), channel_id=1, source_target_pairs={{0,1},{1,0},{2,3},{3,2},{4,5},{5,4},{6,7},{7,6},{8,9},{9,8},{10,11... | collective-permute-start | bytes 24584 | tf_op jit(solution)/shard_map/ppermute | solution.py:880
  375.8 31.6 %all-to-all-start.5 = ((bf16[8,256,256]{2,1,0:T(8,128)(2,1)}), bf16[8,256,256]{2,1,0:T(8,128)(2,1)S(1)}, u32[]{:S(2)}, u32[]{:S(2)}) async-start(bf16[8,256,256]{2,1,0:T(8,128)(2,1)} %bitcast.230), calls=%async_computation.5 | async-start | bytes 2097152 | tf_op jit(solution)/shard_map/all_to_all | solution.py:876
  391.7 21.2 %collective-permute-start.44 = (f32[8,128]{1,0:T(8,128)S(1)}, f32[8,128]{1,0:T(8,128)S(1)}, u32[]{:S(2)}, u32[]{:S(2)}) collective-permute-start(f32[8,128]{1,0:T(8,128)S(1)} %bitcast.285), channel_id=1, source_target_pairs={{0,2},{2,0},{1,3},{3,1},{4,6},{6,4},{5,7},{7,5},{8,10},{10,8},{9,1... | collective-permute-start | bytes 12296 | tf_op jit(solution)/shard_map/ppermute | solution.py:880
  395.1 6.4 %collective-permute-start.41 = (bf16[1,2,32,1024]{3,2,1,0:T(8,128)(2,1)S(1)}, bf16[1,2,32,1024]{3,2,1,0:T(8,128)(2,1)S(1)}, u32[]{:S(2)}, u32[]{:S(2)}) collective-permute-start(bf16[1,2,32,1024]{3,2,1,0:T(8,128)(2,1)S(1)} %constant_dynamic-slice_fusion.1), channel_id=1, source_target_pairs={{0,2},{2,0},{1,3},{3,1},{4,6},{6,4},{5,7},{7,5},{8,10},{10,8},{9,1... | collective-permute-start | bytes 393224 | tf_op jit(solution)/shard_map/ppermute | solution.py:880
  395.9 9.1 %collective-permute-start.40 = (bf16[8,1,48,256]{3,2,0,1:T(8,128)(2,1)S(1)}, bf16[8,1,48,256]{3,2,0,1:T(8,128)(2,1)S(1)}, u32[]{:S(2)}, u32[]{:S(2)}) collective-permute-start(bf16[8,1,48,256]{3,2,0,1:T(8,128)(2,1)S(1)} %dynamic-slice_bitcast_fusion.2), channel_id=1, source_target_pairs={{0,2},{2,0},{1,3},{3,1},{4,6},{6,4},{5,7},{7,5},{8,10},{10,8},{9,1... | collective-permute-start | bytes 589832 | tf_op jit(solution)/shard_map/ppermute | solution.py:880
  407.4 12.7 %all-to-all-start.6 = ((bf16[8,48,256]{2,1,0:T(8,128)(2,1)}), bf16[8,48,256]{2,1,0:T(8,128)(2,1)S(1)}, u32[]{:S(2)}, u32[]{:S(2)}) async-start(bf16[8,48,256]{2,1,0:T(8,128)(2,1)} %fusion.33), calls=%async_computation.7 | async-start | bytes 393216 | tf_op jit(solution)/shard_map/all_to_all | solution.py:876
  (60 other events, 534.9 us)
Sparse Core Ops, SparseCore 0:
  73.4 100.9 all-gather.2
  274.6 99.3 reduce-scatter.1

commit v5 on v4

--- a/solution.py
+++ b/solution.py
@@ -14,7 +14,7 @@
 SPAN = 64
 HEADD = 128
 PAD = 16
-UNROLL = 17
+UNROLL = 34
 TOKB = 128
 BUCKETS = 32
 CHUNK = 4096
@@ -61,10 +61,6 @@
 def diagonal():
     rows = lax.broadcasted_iota(jnp.int32, (TOKB, TOKB), 0)
     return rows == lax.broadcasted_iota(jnp.int32, (TOKB, TOKB), 1)
-
-
-def chunk_start(table_ref, own_rows, position):
-    return table_ref[position // own_rows] * own_rows + position % own_rows
 
 
 def lanes(row, eye, ones):
@@ -120,18 +116,18 @@
         fill(wide_b, 0.0)
 
     def scatter_from(token_ref):
-        def scatter(block, carry):
-            both = token_ref[aligned(block * TOKB, TOKB, TOKB), :].astype(f32)
+        def scatter(chunk, carry):
+            both = token_ref[aligned(chunk * own_rows, own_rows, TOKB), :].astype(f32)
             stage_a[...] = both[:, :HEADD]
             stage_b[...] = both[:, HEADD:]
-            first = chunk_start(in_ref, own_rows, step * CHUNK + block * TOKB)
-            for row in range(TOKB):
+            first = in_ref[step * (CHUNK // own_rows) + chunk] * own_rows
+            for row in range(own_rows):
                 place = place_ref[first + row]
                 wide_a[pl.ds(place, 1), :] = stage_a[row : row + 1, :]
                 wide_b[pl.ds(place, 1), :] = stage_b[row : row + 1, :]
             return carry
 
-        lax.fori_loop(0, CHUNK // TOKB, scatter, 0)
+        lax.fori_loop(0, CHUNK // own_rows, scatter, 0)
 
     pl.when(step < load_steps // 2)(lambda: scatter_from(own_ref))
     pl.when((step >= load_steps // 2) & (step < load_steps))(lambda: scatter_from(peer_ref))
@@ -212,19 +208,20 @@
         per_step = CHUNK // own_rows
         eye = diagonal()
         sum_rows = lax.broadcasted_iota(jnp.int32, (PAD, TOKB), 0)
-        offset = (step - load_steps - 1) * CHUNK
+        offset = (step - load_steps - 1) * per_step
 
         def collect(chunk, carry):
             first = chunk * (own_rows + PAD)
             sums = jnp.zeros((PAD, TOKB), f32)
+            start = out_ref[offset + chunk] * own_rows
+            for row in range(own_rows):
+                place = place_ref[start + row]
+                stage_a[row : row + 1, :] = wide_a[pl.ds(place, 1), :]
+                stage_b[row : row + 1, :] = wide_b[pl.ds(place, 1), :]
+            pay_ref[aligned(first, own_rows, PAD), :] = stage_a[...].astype(bf)
             for block in range(blocks):
-                start = chunk_start(out_ref, own_rows, offset + chunk * own_rows + block * TOKB)
-                for row in range(TOKB):
-                    place = place_ref[start + row]
-                    stage_a[row : row + 1, :] = wide_a[pl.ds(place, 1), :]
-                    stage_b[row : row + 1, :] = wide_b[pl.ds(place, 1), :]
-                pay_ref[aligned(first + block * TOKB, TOKB, PAD), :] = stage_a[...].astype(bf)
-                packed = jnp.sum(jnp.where(eye, stage_b[...], 0.0), axis=0, keepdims=True)
+                wide_sums = stage_b[block * TOKB : (block + 1) * TOKB, :]
+                packed = jnp.sum(jnp.where(eye, wide_sums, 0.0), axis=0, keepdims=True)
                 sum_ref[pl.ds(chunk * blocks + block, 1), :] = packed
                 sums = jnp.where(sum_rows == block, packed, sums)
             pay_ref[aligned(first + own_rows, PAD, PAD), :] = sums.astype(bf)
@@ -291,7 +288,7 @@
         scratch_shapes=[pltpu.VMEM((rows, HEADD), bf)] * 3
         + [pltpu.VMEM((own_spans * SPAN, 2 * SPAN), bf)]
         + [pltpu.VMEM((rows, HEADD), f32)] * 2
-        + [pltpu.VMEM((TOKB, HEADD), f32)] * 2
+        + [pltpu.VMEM((own_rows, HEADD), f32)] * 2
         + [pltpu.SemaphoreType.DMA((4,))],
         compiler_params=pltpu.CompilerParams(vmem_limit_bytes=VMEM_LIMIT),
         name="attend_forward",
@@ -353,14 +350,14 @@
                 share = sum_ref[pl.ds(chunk * blocks + block, 1), :]
                 share = share / extra[blocks + block : blocks + block + 1, :]
                 rows = pay_ref[aligned(first + block * TOKB, TOKB, PAD), :].astype(f32)
-                stage_a[...] = rows * lanes(share, eye, ones)
-                stage_b[...] = lanes(share * extra[block : block + 1, :], eye, ones)
-                start = step * CHUNK + chunk * own_rows + block * TOKB
-                start = chunk_start(table_ref, own_rows, start)
-                for row in range(TOKB):
-                    place = place_ref[start + row]
-                    wide_a[pl.ds(place, 1), :] = stage_a[row : row + 1, :]
-                    wide_b[pl.ds(place, 1), :] = stage_b[row : row + 1, :]
+                here = slice(block * TOKB, (block + 1) * TOKB)
+                stage_a[here, :] = rows * lanes(share, eye, ones)
+                stage_b[here, :] = lanes(share * extra[block : block + 1, :], eye, ones)
+            start = table_ref[step * (CHUNK // own_rows) + chunk] * own_rows
+            for row in range(own_rows):
+                place = place_ref[start + row]
+                wide_a[pl.ds(place, 1), :] = stage_a[row : row + 1, :]
+                wide_b[pl.ds(place, 1), :] = stage_b[row : row + 1, :]
             return carry
 
         lax.fori_loop(0, CHUNK // own_rows, scatter, 0)
@@ -438,20 +435,20 @@
         wide_c[pl.ds(tail, SPAN), :] = jnp.zeros((SPAN, HEADD), f32)
 
     def collect_to(out_ref):
-        offset = (step - load_steps - 1) * CHUNK
-
-        def collect(block, carry):
-            start = chunk_start(table_ref, own_rows, offset + block * TOKB)
-            for row in range(TOKB):
+        offset = (step - load_steps - 1) * (CHUNK // own_rows)
+
+        def collect(chunk, carry):
+            start = table_ref[offset + chunk] * own_rows
+            for row in range(own_rows):
                 place = place_ref[start + row]
                 stage_a[row : row + 1, :] = wide_a[pl.ds(place, 1), :]
                 stage_b[row : row + 1, :] = wide_c[pl.ds(place, 1), :]
-            here = aligned(block * TOKB, TOKB, TOKB)
+            here = aligned(chunk * own_rows, own_rows, TOKB)
             out_ref[here, :HEADD] = stage_a[...].astype(bf)
             out_ref[here, HEADD:] = stage_b[...].astype(bf)
             return carry
 
-        lax.fori_loop(0, CHUNK // TOKB, collect, 0)
+        lax.fori_loop(0, CHUNK // own_rows, collect, 0)
 
     half = load_steps + 1 + load_steps // 2
     pl.when((step > load_steps) & (step < half))(lambda: collect_to(out_own_ref))
@@ -487,7 +484,7 @@
         scratch_shapes=[pltpu.VMEM((rows, HEADD), bf)] * 3
         + [pltpu.VMEM(probs.shape, bf)]
         + [pltpu.VMEM((rows, HEADD), f32)] * 3
-        + [pltpu.VMEM((TOKB, HEADD), f32)] * 2
+        + [pltpu.VMEM((own_rows, HEADD), f32)] * 2
         + [pltpu.SemaphoreType.DMA((4,))],
         compiler_params=pltpu.CompilerParams(vmem_limit_bytes=VMEM_LIMIT),
         name="attend_backward",
@@ -578,7 +575,7 @@
 
 def mix_kernel(
     parts_ref, weight_ref, first_ref, gain_ref, shift_ref,
-    mixed_ref, low_ref, sum_ref, unit_ref, scale_ref, feed_ref,
+    low_ref, sum_ref, unit_ref, scale_ref, feed_ref,
 ):
     heads, rows = parts_ref.shape[0], first_ref.shape[0]
     eye = diagonal()
@@ -589,7 +586,6 @@
             here = slice(block * TOKB, (block + 1) * TOKB)
             sums = parts_ref[head, rows : rows + PAD, :].astype(f32)[block : block + 1]
             mixed = parts_ref[head, here, :].astype(f32) / lanes(sums, eye, ones)
-            mixed_ref[here, columns] = mixed
             low_ref[here, columns] = mixed.astype(bf)
     total = first_ref[...].astype(f32) + product(low_ref[...], whole_weight(weight_ref))
     sum_ref[...] = total.astype(bf)
@@ -607,10 +603,10 @@
     wide, low = jax.ShapeDtypeStruct((rows, width), f32), jax.ShapeDtypeStruct((rows, width), bf)
     return pl.pallas_call(
         mix_kernel,
-        out_shape=(wide, low, low, wide, jax.ShapeDtypeStruct((rows, 1), f32), low),
+        out_shape=(low, low, wide, jax.ShapeDtypeStruct((rows, 1), f32), low),
         grid=(1,),
         in_specs=[vm, shard_spec(shards, 2), vm, vm, vm],
-        out_specs=(vm,) * 6,
+        out_specs=(vm,) * 5,
         compiler_params=pltpu.CompilerParams(vmem_limit_bytes=VMEM_LIMIT),
         name="mix_rows",
         cost_estimate=takes(5),
@@ -642,7 +638,8 @@
             here = slice(block * TOKB, (block + 1) * TOKB)
             wide = wide_ref[here, columns]
             pay_ref[head, here, :] = wide.astype(bf)
-            dot = jnp.sum(wide * mixed_ref[here, columns], axis=-1, keepdims=True)
+            mixed = mixed_ref[here, columns].astype(f32)
+            dot = jnp.sum(wide * mixed, axis=-1, keepdims=True)
             packed = jnp.sum(jnp.where(eye, dot, 0.0), axis=0, keepdims=True)
             tails = jnp.where(pad_rows == block, packed, tails)
             tails = jnp.where(pad_rows == blocks + block, sums[block : block + 1], tails)
@@ -845,6 +842,39 @@
     )(first, codes)
 
 
+def parts_kernel(
+    row_pair_ref, row_far_ref, inner_pair_ref, inner_far_ref,
+    hidden_pair_ref, hidden_far_ref, grad_pair_ref, grad_far_ref, out_ref,
+):
+    inner = against(row_pair_ref[...], inner_pair_ref[...])
+    inner += against(row_far_ref[...], inner_far_ref[...])
+    out_ref[0, 0] = inner.astype(bf)
+    outer = against(hidden_pair_ref[...], grad_pair_ref[...])
+    outer += against(hidden_far_ref[...], grad_far_ref[...])
+    out_ref[0, 1] = outer.astype(bf)
+
+
+def parts_product(row_pair, row_far, inner_pair, inner_far, hidden_pair, hidden_far, grads):
+    rows, width = row_pair.shape
+    units = hidden_pair.shape[1]
+    block = pl.BlockSpec((rows, TOKB), lambda i: (0, i))
+
+    def whole(columns):
+        return pl.BlockSpec((rows, columns), lambda i: (0, 0), pipeline_mode=pl.Buffered(1))
+
+    return pl.pallas_call(
+        parts_kernel,
+        grid=(width // TOKB,),
+        out_shape=jax.ShapeDtypeStruct((width // TOKB, 2, TOKB, width), bf),
+        in_specs=[block, block, whole(units), whole(units), block, block]
+        + [whole(width), whole(width)],
+        out_specs=pl.BlockSpec((1, 2, TOKB, width), lambda i: (i, 0, 0, 0)),
+        compiler_params=pltpu.CompilerParams(vmem_limit_bytes=VMEM_LIMIT),
+        name="parts_product",
+        cost_estimate=takes(0),
+    )(row_pair, row_far, inner_pair, inner_far, hidden_pair, hidden_far, *grads)
+
+
 ALL = ("hd", "kk", "ry", "rc")
 SEQ = ("hd", "kk")
 ROUND = ("ry", "rc")
@@ -1141,7 +1171,7 @@
     head_sums = sum_pair(payload_own.reshape(packed), payload_peer.reshape(packed))
     mixed_parts = exchange(sum_groups(head_sums))
     mixed_parts, shards = together(mixed_parts, shards)
-    mixed, mixed_low, first_sum, ffn_unit, ffn_scale, ffn_low = mix_rows(
+    mixed_low, first_sum, ffn_unit, ffn_scale, ffn_low = mix_rows(
         mixed_parts, shards, first_half, ffn_gain_row, ffn_shift_row
     )
     ffn_low, qkv_rows = together(ffn_low, jnp.stack([qk_weight, value_weight]))
@@ -1157,15 +1187,17 @@
     near_sum = pair_sum(back_pair[0], back_pair[1], "rc")
     second_far = pair_sum(back_far[2], back_far[3], "rc")
     second_pair = pair_sum(back_pair[2], back_pair[3], "rc")
-    outer_part = (against(hidden_pair, grad_pair) + against(hidden_far, grad_far)).astype(bf)
-    inner_part = (against(ffn_pair, inner_pair) + against(ffn_far, inner_far)).astype(bf)
-    part_sums = jnp.stack(
-        [
-            inner_part.reshape(seq_count, cut, -1),
-            outer_part.reshape(seq_count, -1, model_width),
-        ],
-        axis=1,
-    )
+    part_sums = parts_product(
+        ffn_pair,
+        ffn_far,
+        inner_pair,
+        inner_far,
+        hidden_pair,
+        hidden_far,
+        (grad_pair, grad_far),
+    )
+    part_sums = part_sums.reshape(-1, 2, TOKB // cut, cut, model_width)
+    part_sums = jnp.transpose(part_sums, (0, 2, 1, 3, 4)).reshape(seq_count, 2, cut, model_width)
     near_sum, far_sum, part_sums, qkv_rows = together(near_sum, far_sum, part_sums, qkv_rows)
     part_grads = lax.psum_scatter(part_sums, SEQ, scatter_dimension=0, tiled=False)
     carry_low, back_parts = carry_rows(
@@ -1176,7 +1208,7 @@
         ffn_scale,
         first_grad,
         shards,
-        mixed,
+        mixed_low,
         mixed_parts,
     )
     back_parts = exchange(back_parts)

time: 437 us -> 429 us (0.982)
  matrix products: 16.9 us -> 10.2 us
    pallas_call x1 -> x2, Pallas kernels: 4.31 us -> 15.3 us  [the longest x1 11 us: parts_product(): pl.pallas_call(parts_kernel, grid=(width // TOKB,), out_shape=jax.ShapeDt...]
    dot_general x5 -> x1, matrix products: 8.39 us -> 1.79 us  [against(): lax.dot_general(left_side, right_side, (((0,), (0,)), ((), ())), preferre...]
    pallas_call x1, Pallas kernels: 41.5 us -> 37 us  [attend_backward(): pl.pallas_call(functools.partial(backward_kernel, own_rows, steps), grid=...]
    unnamed x118 -> x104, local copies, waits for them, and re-layouts: 11.3 us -> 11.3 us
  transfers between devices with their start and end apart: 54 -> 54, of which waited for: 27 -> 26; matrix products, arithmetic and copies ran while one was open for 18% -> 16% of each run, Pallas kernels for 26% -> 28%
where the time goes in v5:
time: 429 us; the launch traced here: 421 us
  waiting for transfers between devices  130 us (30%)
  Pallas kernels  121 us (28%)
  starting transfers between devices  69.8 us (16%)
  other arithmetic  44.5 us (10%)
  local copies, waits for them, and re-layouts  30.5 us (7%)
  between operations  15.6 us (4%)
  matrix products  10.2 us (2%)
    ppermute x37, waiting for transfers between devices, swapped(): return lax.ppermute(value, axis, SWAP)  92.8 us
    pallas_call x1, Pallas kernels, attend_backward(): pl.pallas_call(functools.partial(backward_kernel, own_rows, steps), grid=...  37 us
    all_to_all x7, starting transfers between devices, exchange(): return lax.all_to_all(parts, axes, split_axis=0, concat_axis=0, tiled=True)  36.7 us
    pallas_call x1, Pallas kernels, attend_forward(): pl.pallas_call(functools.partial(forward_kernel, own_rows, steps), grid=(...  30.6 us
    ppermute x37, starting transfers between devices, swapped(): return lax.ppermute(value, axis, SWAP)  23.7 us
    all_to_all x7, waiting for transfers between devices, exchange(): return lax.all_to_all(parts, axes, split_axis=0, concat_axis=0, tiled=True)  22.5 us
    pallas_call x2, Pallas kernels, feed_forward(): pl.pallas_call(feed_kernel, grid=(2,), out_shape=(by_width, by_width, by_...  20.4 us
    ppermute x8, waiting for transfers between devices, ring_step(): return (lax.ppermute(up, 'hd', UP), lax.ppermute(down, 'hd', DOWN))  14.6 us
  transfers between devices with their start and end apart: 54, of which 26 were waited for; matrix products, arithmetic and copies ran while one was open for 16% of the time, Pallas kernels for 28%

profile of v5, /device:TPU:0, one launch (start us, length us, event | category | flops | bytes accessed | tf_op | source)
XLA Modules:
  0.0 421.5 jit_solution(10799240977994615062)
XLA Ops:
  13.5 2.9 collective-permute-start.1
  17.3 6.3 %all-to-all-start = ((bf16[8,48,384]{2,1,0:T(8,128)(2,1)}), bf16[8,48,384]{2,1,0:T(8,128)(2,1)S(1)}, u32[]{:S(2)}, u32[]{:S(2)}) async-start(bf16[8,48,384]{2,1,0:T(8,128)(2,1)} %copy.80), calls=%async_computation | async-start | bytes 589824 | tf_op jit(solution)/shard_map/all_to_all | solution.py:906
  27.4 4.2 collective-permute-done.5
  31.7 2.1 collective-permute-done.3
  34.8 2.5 all-to-all-done
  38.9 4.2 collective-permute-done.8
  49.5 9.3 %collective-permute-done.6.refs_3_ = bf16[256,1024]{1,0:T(8,128)(2,1)S(1)} collective-permute-done((bf16[256,1024]{1,0:T(8,128)(2,1)S(1)}, bf16[256,1024]{1,0:T(8,128)(2,1)S(1)}, u32[]{:S(2)}, u32[]{:S(2)}) %collective-permute-start.6) | collective-permute-done | bytes 524320 | tf_op jit(solution)/shard_map/ppermute | solution.py:960
  83.7 2.0 collective-permute-done.14
  85.7 2.6 collective-permute-done.12.refs_7_
  88.3 2.1 bitcast_dynamic-update-slice_fusion
  97.3 4.5 %collective-permute-done.15 = bf16[1,768,256]{2,1,0:T(8,128)(2,1)S(1)} collective-permute-done((bf16[1,768,256]{2,1,0:T(8,128)(2,1)S(1)}, bf16[1,768,256]{2,1,0:T(8,128)(2,1)S(1)}, u32[]{:S(2)}, u32[]{:S(2)}) %collective-permute-start.15) | collective-permute-done | bytes 393248 | tf_op jit(solution)/shard_map/ppermute | solution.py:910
  102.7 4.4 %collective-permute-done.16.peer_ref = bf16[4096,256]{1,0:T(8,128)(2,1)S(1)} collective-permute-done((bf16[4096,256]{1,0:T(8,128)(2,1)}, bf16[4096,256]{1,0:T(8,128)(2,1)S(1)}, u32[]{:S(2)}, u32[]{:S(2)}) %collective-permute-start.16) | collective-permute-done | bytes 2097184 | tf_op jit(solution)/shard_map/ppermute | solution.py:910
  108.4 30.6 %attend_forward.1 = (bf16[4352,128]{1,0:T(8,128)(2,1)}, bf16[4352,128]{1,0:T(8,128)(2,1)}, bf16[8832,128]{1,0:T(8,128)(2,1)}, bf16[8832,128]{1,0:T(8,128)(2,1)},...) custom-call(s32[32]{0:T(128)} %get-tuple-element.145.in_ref, ...), custom_call_target="tpu_custom_call" | custom-call | flops 3500000000 | bytes 105000000 | tf_op jit(solution)/shard_map/attend_forward/pallas_call | solution.py:259
  139.2 2.8 collective-permute-done.17
  145.3 13.0 %collective-permute-done.18 = bf16[1,8,272,128]{3,2,1,0:T(8,128)(2,1)S(1)} collective-permute-done((bf16[1,8,272,128]{3,2,1,0:T(8,128)(2,1)S(1)}, bf16[1,8,272,128]{3,2,1,0:T(8,128)(2,1)S(1)}, u32[]{:S(2)}, u32[]{:S(2)}) %collective-permute-start.18) | collective-permute-done | bytes 557088 | tf_op jit(solution)/shard_map/ppermute | solution.py:910
  159.4 5.3 %all-to-all-start.1 = ((bf16[8,272,128]{2,1,0:T(8,128)(2,1)}), bf16[8,272,128]{2,1,0:T(8,128)(2,1)S(1)}, u32[]{:S(2)}, u32[]{:S(2)}) async-start(bf16[8,272,128]{2,1,0:T(8,128)(2,1)} %fusion.23), calls=%async_computation.1 | async-start | bytes 1114112 | tf_op jit(solution)/shard_map/all_to_all | solution.py:906
  166.2 17.7 %all-to-all-done.1.parts_ref = bf16[8,272,128]{2,1,0:T(8,128)(2,1)S(1)} async-done(((bf16[8,272,128]{2,1,0:T(8,128)(2,1)}), bf16[8,272,128]{2,1,0:T(8,128)(2,1)S(1)}, u32[]{:S(2)}, u32[]{:S(2)}) %all-to-all-start.1) | async-done | bytes 557088 | tf_op jit(solution)/shard_map/all_to_all | solution.py:906
  184.7 4.3 %mix_rows.1 = (bf16[256,1024]{1,0:T(8,128)(2,1)}, bf16[256,1024]{1,0:T(8,128)(2,1)}, f32[256,1024]{1,0:T(8,128)}, f32[256,1]{1,0:T(8,128)}, bf16[256,1024]{1,0:T(8,128)(2,1)}) custom-call(bf16[8,272,128]{2,1,0:T(8,128)(2,1)} %copy-done.3, bf16[8,3,128,1024]{3,2,1,0:T(8,128)(2,1)} %bitcast.209, bf16[256,1024]{1,0:T(8,128)(2,1)} %first_ref.1, ...), custom_call_target="tpu_custom_call" | custom-call | flops 500000000 | bytes 15000000 | tf_op jit(solution)/shard_map/mix_rows/pallas_call | solution.py:604
  192.0 10.2 %feed_forward.2 = (bf16[512,1024]{1,0:T(8,128)(2,1)}, bf16[512,1024]{1,0:T(8,128)(2,1)}, bf16[512,1024]{1,0:T(8,128)(2,1)}, bf16[512,1024]{1,0:T(8,128)(2,1)}, b...) custom-call(bf16[256,1024]{1,0:T(8,128)(2,1)} %get-tuple-element.157, ...), custom_call_target="tpu_custom_call" | custom-call | flops 900000000 | bytes 27000000 | tf_op jit(solution)/shard_map/feed_forward/pallas_call | solution.py:562
  204.8 3.8 all-to-all-start.2
  209.4 10.2 %feed_forward.3 = (bf16[512,1024]{1,0:T(8,128)(2,1)}, bf16[512,1024]{1,0:T(8,128)(2,1)}, bf16[512,1024]{1,0:T(8,128)(2,1)}, bf16[512,1024]{1,0:T(8,128)(2,1)}, b...) custom-call(bf16[256,1024]{1,0:T(8,128)(2,1)} %copy-done.28, ...), custom_call_target="tpu_custom_call" | custom-call | flops 900000000 | bytes 27000000 | tf_op jit(solution)/shard_map/feed_forward/pallas_call | solution.py:562
  224.7 11.0 %parts_product.1 = bf16[8,2,128,1024]{3,2,1,0:T(8,128)(2,1)} custom-call(bf16[512,1024]{1,0:T(8,128)(2,1)} %get-tuple-element.188.row_pair_ref, bf16[512,1024]{1,0:T(8,128)(2,1)} %get-tuple-element.189.row_far_ref, bf16[512,1024]{1,0:T(8,128)(2,1)} %get-tuple-element.190.inner_pair_ref, bf16[512,1024]{1,0:T(8,128)(2,1)} %get-tuple-element.191.inner_far_ref, ...), custom_call_target="tpu_custom_call" | custom-call | tf_op jit(solution)/shard_map/parts_product/pallas_call | solution.py:865
  235.7 2.0 add_convert_fusion.3.near_ref
  238.6 5.0 %carry_rows.1 = (bf16[256,1024]{1,0:T(8,128)(2,1)}, bf16[8,272,128]{2,1,0:T(8,128)(2,1)}) custom-call(bf16[256,1024]{1,0:T(8,128)(2,1)} %add_convert_fusion.3.near_ref, bf16[256,1024]{1,0:T(8,128)(2,1)} %copy-done.30, f32[1,1024]{1,0:T(1,128)} %bitcast.262, f32[256,1024]{1,0:T(8,128)} %get-tuple-element.199.unit_ref, f32[256,1]{1,0:T(8,128)} %get-tuple-element.200.scale_ref, ...), custom_call_target="tpu_custom_call" | custom-call | flops 500000000 | bytes 15000000 | tf_op jit(solution)/shard_map/carry_rows/pallas_call | solution.py:654
  243.6 1.8 convolution_convert_fusion
  247.1 5.8 %all-to-all-start.3 = ((bf16[8,272,128]{2,1,0:T(8,128)(2,1)}), bf16[8,272,128]{2,1,0:T(8,128)(2,1)S(1)}, u32[]{:S(2)}, u32[]{:S(2)}) async-start(bf16[8,272,128]{2,1,0:T(8,128)(2,1)} %get-tuple-element.202), calls=%async_computation.3 | async-start | bytes 1114112 | tf_op jit(solution)/shard_map/all_to_all | solution.py:906
  256.9 2.0 add_convert_fusion
  258.9 9.8 %collective-permute-done.29 = bf16[8,1,32,1024]{3,2,0,1:T(8,128)(2,1)S(1)} collective-permute-done((bf16[8,1,32,1024]{3,2,0,1:T(8,128)(2,1)S(1)}, bf16[8,1,32,1024]{3,2,0,1:T(8,128)(2,1)S(1)}, u32[]{:S(2)}, u32[]{:S(2)}) %collective-permute-start.29) | collective-permute-done | bytes 524320 | tf_op jit(solution)/shard_map/ppermute | solution.py:910
  270.7 13.1 %collective-permute-done.32 = bf16[1,8,272,128]{3,2,1,0:T(8,128)(2,1)} collective-permute-done((bf16[1,8,272,128]{3,2,1,0:T(8,128)(2,1)S(1)}, bf16[1,8,272,128]{3,2,1,0:T(8,128)(2,1)}, u32[]{:S(2)}, u32[]{:S(2)}) %collective-permute-start.32) | collective-permute-done | bytes 557088 | tf_op jit(solution)/shard_map/ppermute | solution.py:910
  283.8 2.2 pad_maximum_fusion.2
  286.9 5.6 %all-to-all-start.4 = ((bf16[8,32,1024]{2,1,0:T(8,128)(2,1)}), bf16[8,32,1024]{2,1,0:T(8,128)(2,1)S(1)}, u32[]{:S(2)}, u32[]{:S(2)}) async-start(bf16[8,32,1024]{2,1,0:T(8,128)(2,1)} %bitcast.235), calls=%async_computation.4 | async-start | bytes 1048576 | tf_op jit(solution)/shard_map/all_to_all | solution.py:906
  293.8 37.0 %attend_backward.1 = (bf16[4096,256]{1,0:T(8,128)(2,1)}, bf16[4096,256]{1,0:T(8,128)(2,1)}) custom-call(s32[32]{0:T(128)} %get-tuple-element.146.out_ref.table_ref, s32[8192]{0:T(1024)} %broadcast_add_fusion.place_ref, bf16[4352,128]{1,0:T(8,128)(2,1)} %bitcast.57.pay_own_ref, bf16[4352,128]{1,0:T(8,128)(2,1)} %bitcast.58.pay_peer_ref, ...), custom_call_target="tpu_custom_call" | custom-call | flops 4400000000 | bytes 132000000 | tf_op jit(solution)/shard_map/attend_backward/pallas_call | solution.py:465
  332.7 2.6 collective-permute-done.36
  335.3 2.0 fusion.1
  342.3 2.3 collective-permute-done.38
  344.7 1.9 select_bitcast_fusion.1
  346.9 2.5 copy.85
  349.4 16.7 %collective-permute-done.37 = bf16[1,8,256,256]{3,2,1,0:T(8,128)(2,1)} collective-permute-done((bf16[1,8,256,256]{3,2,1,0:T(8,128)(2,1)}, bf16[1,8,256,256]{3,2,1,0:T(8,128)(2,1)}, u32[]{:S(2)}, u32[]{:S(2)}) %collective-permute-start.37) | collective-permute-done | bytes 1048608 | tf_op jit(solution)/shard_map/ppermute | solution.py:910
  366.1 2.5 add_rows.1
  368.6 6.0 %all-to-all-start.5 = ((bf16[8,256,256]{2,1,0:T(8,128)(2,1)}), bf16[8,256,256]{2,1,0:T(8,128)(2,1)S(1)}, u32[]{:S(2)}, u32[]{:S(2)}) async-start(bf16[8,256,256]{2,1,0:T(8,128)(2,1)} %bitcast.216), calls=%async_computation.5 | async-start | bytes 2097152 | tf_op jit(solution)/shard_map/all_to_all | solution.py:906
  374.6 2.1 fusion.20
  376.7 4.9 %weight_part.1 = (f32[1024,256]{1,0:T(8,128)}, f32[8,256]{1,0:T(8,128)}) custom-call(s32[8]{0:T(128)} %copy-done, bf16[8,256,256]{2,1,0:T(8,128)(2,1)} %bitcast.217, bf16[256,1024]{1,0:T(8,128)(2,1)} %copy-done.4, bf16[256,1024]{1,0:T(8,128)(2,1)} %copy-done.16, bf16[256,1024]{1,0:T(8,128)(2,1)} %copy-done.15, bf16[256,1024]{1,0:T(8,128)(2,1)} %copy-done.18, ...), custom_call_target="tpu_custom_call" | custom-call | flops 500000000 | bytes 15000000 | tf_op jit(solution)/shard_map/weight_part/pallas_call | solution.py:741
  385.3 1.9 fusion.32
  389.5 4.1 collective-permute-done.41
  393.7 3.4 collective-permute-done.40
  397.9 2.3 all-to-all-done.5.back_ref
  400.2 4.0 all-to-all-start.6
  406.9 5.3 %last_rows.1 = bf16[256,1024]{1,0:T(8,128)(2,1)} custom-call(bf16[8,256,256]{2,1,0:T(8,128)(2,1)} %copy-done.8, bf16[2,1024,1024]{2,1,0:T(8,128)(2,1)} %bitcast.215, f32[1,1024]{1,0:T(1,128)} %bitcast.260, f32[256,1024]{1,0:T(8,128)} %get-tuple-element.263.unit_ref, f32[256,1]{1,0:T(8,128)} %copy.86.scale_ref, bf16[256,1024]{1,0:T(8,128)(2,1)} %grad_ref.3), custom_call_target="tpu_custom_call" | custom-call | flops 600000000 | bytes 18000000 | tf_op jit(solution)/shard_map/last_rows/pallas_call | solution.py:710
  (313 shorter events, 101.2 us)
Async XLA Ops:
  13.5 23.7 %collective-permute-start.1 = (bf16[256,1024]{1,0:T(8,128)(2,1)S(1)}, bf16[256,1024]{1,0:T(8,128)(2,1)S(1)}, u32[]{:S(2)}, u32[]{:S(2)}) collective-permute-start(bf16[256,1024]{1,0:T(8,128)(2,1)S(1)} %get-tuple-element.264.refs_0_), channel_id=1, source_target_pairs={{8,0},{16,8},{24,16},{28,24},{20,28},{12,20},{4,12},{0,4},{9,1},{1... | collective-permute-start | bytes 1572872 | tf_op jit(solution)/shard_map/ppermute | solution.py:960
  16.5 20.8 %collective-permute-start = (bf16[256,1024]{1,0:T(8,128)(2,1)S(1)}, bf16[256,1024]{1,0:T(8,128)(2,1)S(1)}, u32[]{:S(2)}, u32[]{:S(2)}) collective-permute-start(bf16[256,1024]{1,0:T(8,128)(2,1)S(1)} %get-tuple-element.264.refs_0_), channel_id=1, source_target_pairs={{0,8},{8,16},{16,24},{24,28},{28,20},{20,12},{12,4},{4,0},{1,9},{9... | collective-permute-start | bytes 1572872 | tf_op jit(solution)/shard_map/ppermute | solution.py:960
  16.6 7.7 %collective-permute-start.4 = (bf16[32,1024]{1,0:T(8,128)(2,1)S(1)}, bf16[32,1024]{1,0:T(8,128)(2,1)}, u32[]{:S(2)}, u32[]{:S(2)}) collective-permute-start(bf16[32,1024]{1,0:T(8,128)(2,1)S(1)} %copy-done.35), channel_id=1, source_target_pairs={{0,1},{1,0},{2,3},{3,2},{4,5},{5,4},{6,7},{7,6},{8,9},{9,8},{10,11... | collective-permute-start | bytes 196616 | tf_op jit(solution)/shard_map/ppermute | solution.py:910
  17.3 19.9 %all-to-all-start = ((bf16[8,48,384]{2,1,0:T(8,128)(2,1)}), bf16[8,48,384]{2,1,0:T(8,128)(2,1)S(1)}, u32[]{:S(2)}, u32[]{:S(2)}) async-start(bf16[8,48,384]{2,1,0:T(8,128)(2,1)} %copy.80), calls=%async_computation | async-start | bytes 589824 | tf_op jit(solution)/shard_map/all_to_all | solution.py:906
  23.6 160.3 %all-gather.3.cloned.1.call-start = ((), (), s32[]{:S(2)}) async-start(), calls=%async_computation.9 | async-start | bytes 7077888 | tf_op jit(solution)/shard_map/all_gather | solution.py:1159
  25.2 6.4 %collective-permute-start.5 = (bf16[2,32,1024]{2,1,0:T(8,128)(2,1)S(1)}, bf16[2,32,1024]{2,1,0:T(8,128)(2,1)S(1)}, u32[]{:S(2)}, u32[]{:S(2)}) collective-permute-start(bf16[2,32,1024]{2,1,0:T(8,128)(2,1)S(1)} %pad_maximum_fusion.9), channel_id=1, source_target_pairs={{0,2},{2,0},{1,3},{3,1},{4,6},{6,4},{5,7},{7,5},{8,10},{10,8},{9,1... | collective-permute-start | bytes 393224 | tf_op jit(solution)/shard_map/ppermute | solution.py:910
  26.8 6.9 %collective-permute-start.3 = (bf16[1,2,32,1024]{3,2,1,0:T(8,128)(2,1)S(1)}, bf16[1,2,32,1024]{3,2,1,0:T(8,128)(2,1)S(1)}, u32[]{:S(2)}, u32[]{:S(2)}) collective-permute-start(bf16[1,2,32,1024]{3,2,1,0:T(8,128)(2,1)S(1)} %constant_dynamic-slice_fusion.3), channel_id=1, source_target_pairs={{0,2},{2,0},{1,3},{3,1},{4,6},{6,4},{5,7},{7,5},{8,10},{10,8},{9,1... | collective-permute-start | bytes 393224 | tf_op jit(solution)/shard_map/ppermute | solution.py:910
  37.3 5.7 %collective-permute-start.8 = (bf16[8,1,32,384]{3,2,0,1:T(8,128)(2,1)S(1)}, bf16[8,1,32,384]{3,2,0,1:T(8,128)(2,1)S(1)}, u32[]{:S(2)}, u32[]{:S(2)}) collective-permute-start(bf16[8,1,32,384]{3,2,0,1:T(8,128)(2,1)S(1)} %slice.149), channel_id=1, source_target_pairs={{0,2},{2,0},{1,3},{3,1},{4,6},{6,4},{5,7},{7,5},{8,10},{10,8},{9,1... | collective-permute-start | bytes 589832 | tf_op jit(solution)/shard_map/ppermute | solution.py:910
  44.5 14.3 %collective-permute-start.6 = (bf16[256,1024]{1,0:T(8,128)(2,1)S(1)}, bf16[256,1024]{1,0:T(8,128)(2,1)S(1)}, u32[]{:S(2)}, u32[]{:S(2)}) collective-permute-start(bf16[256,1024]{1,0:T(8,128)(2,1)S(1)} %collective-permute-done.refs_1_), channel_id=1, source_target_pairs={{0,8},{8,16},{16,24},{24,28},{28,20},{20,12},{12,4},{4,0},{1,9},{9... | collective-permute-start | bytes 1572872 | tf_op jit(solution)/shard_map/ppermute | solution.py:960
  45.6 14.0 %collective-permute-start.7 = (bf16[256,1024]{1,0:T(8,128)(2,1)S(1)}, bf16[256,1024]{1,0:T(8,128)(2,1)S(1)}, u32[]{:S(2)}, u32[]{:S(2)}) collective-permute-start(bf16[256,1024]{1,0:T(8,128)(2,1)S(1)} %collective-permute-done.1.refs_2_), channel_id=1, source_target_pairs={{8,0},{16,8},{24,16},{28,24},{20,28},{12,20},{4,12},{0,4},{9,1},{1... | collective-permute-start | bytes 1572872 | tf_op jit(solution)/shard_map/ppermute | solution.py:960
  59.7 13.2 %collective-permute-start.10 = (bf16[256,1024]{1,0:T(8,128)(2,1)S(1)}, bf16[256,1024]{1,0:T(8,128)(2,1)S(1)}, u32[]{:S(2)}, u32[]{:S(2)}) collective-permute-start(bf16[256,1024]{1,0:T(8,128)(2,1)S(1)} %collective-permute-done.6.refs_3_), channel_id=1, source_target_pairs={{0,8},{8,16},{16,24},{24,28},{28,20},{20,12},{12,4},{4,0},{1,9},{9... | collective-permute-start | bytes 1572872 | tf_op jit(solution)/shard_map/ppermute | solution.py:960
  60.3 12.9 %collective-permute-start.11 = (bf16[256,1024]{1,0:T(8,128)(2,1)S(1)}, bf16[256,1024]{1,0:T(8,128)(2,1)S(1)}, u32[]{:S(2)}, u32[]{:S(2)}) collective-permute-start(bf16[256,1024]{1,0:T(8,128)(2,1)S(1)} %collective-permute-done.7.refs_4_), channel_id=1, source_target_pairs={{8,0},{16,8},{24,16},{28,24},{20,28},{12,20},{4,12},{0,4},{9,1},{1... | collective-permute-start | bytes 1572872 | tf_op jit(solution)/shard_map/ppermute | solution.py:960
  69.8 15.8 %collective-permute-start.14 = (bf16[1,1280,256]{2,1,0:T(8,128)(2,1)}, bf16[1,1280,256]{2,1,0:T(8,128)(2,1)}, u32[]{:S(2)}, u32[]{:S(2)}) collective-permute-start(bf16[1,1280,256]{2,1,0:T(8,128)(2,1)} %bitcast_dynamic-update-slice_fusion.2), channel_id=1, source_target_pairs={{0,2},{2,0},{1,3},{3,1},{4,6},{6,4},{5,7},{7,5},{8,10},{10,8},{9,1... | collective-permute-start | bytes 1966088 | tf_op jit(solution)/shard_map/ppermute | solution.py:910
  77.4 8.3 %collective-permute-start.13 = (bf16[128,1024]{1,0:T(8,128)(2,1)}, bf16[128,1024]{1,0:T(8,128)(2,1)S(1)}, u32[]{:S(2)}, u32[]{:S(2)}) collective-permute-start(bf16[128,1024]{1,0:T(8,128)(2,1)} %slice.117), channel_id=1, source_target_pairs={{8,0},{16,8},{24,16},{28,24},{20,28},{12,20},{4,12},{0,4},{9,1},{1... | collective-permute-start | bytes 786440 | tf_op jit(solution)/shard_map/ppermute | solution.py:960
  78.8 9.6 %collective-permute-start.12 = (bf16[128,1024]{1,0:T(8,128)(2,1)S(1)}, bf16[128,1024]{1,0:T(8,128)(2,1)S(1)}, u32[]{:S(2)}, u32[]{:S(2)}) collective-permute-start(bf16[128,1024]{1,0:T(8,128)(2,1)S(1)} %slice.116), channel_id=1, source_target_pairs={{0,8},{8,16},{16,24},{24,28},{28,20},{20,12},{12,4},{4,0},{1,9},{9... | collective-permute-start | bytes 786440 | tf_op jit(solution)/shard_map/ppermute | solution.py:960
  94.0 7.8 %collective-permute-start.15 = (bf16[1,768,256]{2,1,0:T(8,128)(2,1)S(1)}, bf16[1,768,256]{2,1,0:T(8,128)(2,1)S(1)}, u32[]{:S(2)}, u32[]{:S(2)}) collective-permute-start(bf16[1,768,256]{2,1,0:T(8,128)(2,1)S(1)} %pad_maximum_fusion.6), channel_id=1, source_target_pairs={{0,2},{2,0},{1,3},{3,1},{4,6},{6,4},{5,7},{7,5},{8,10},{10,8},{9,1... | collective-permute-start | bytes 1179656 | tf_op jit(solution)/shard_map/ppermute | solution.py:910
  102.6 4.4 %collective-permute-start.16 = (bf16[4096,256]{1,0:T(8,128)(2,1)}, bf16[4096,256]{1,0:T(8,128)(2,1)S(1)}, u32[]{:S(2)}, u32[]{:S(2)}) collective-permute-start(bf16[4096,256]{1,0:T(8,128)(2,1)} %bitcast_dynamic-update-slice_fusion.1.own_ref), channel_id=1, source_target_pairs={{0,1},{1,0},{2,3},{3,2},{4,5},{5,4},{6,7},{7,6},{8,9},{9,8},{10,11... | collective-permute-start | bytes 6291464 | tf_op jit(solution)/shard_map/ppermute | solution.py:910
  143.7 14.7 %collective-permute-start.18 = (bf16[1,8,272,128]{3,2,1,0:T(8,128)(2,1)S(1)}, bf16[1,8,272,128]{3,2,1,0:T(8,128)(2,1)S(1)}, u32[]{:S(2)}, u32[]{:S(2)}) collective-permute-start(bf16[1,8,272,128]{3,2,1,0:T(8,128)(2,1)S(1)} %slice_bitcast_fusion.2), channel_id=1, source_target_pairs={{0,2},{2,0},{1,3},{3,1},{4,6},{6,4},{5,7},{7,5},{8,10},{10,8},{9,1... | collective-permute-start | bytes 1671176 | tf_op jit(solution)/shard_map/ppermute | solution.py:910
  159.4 24.5 %all-to-all-start.1 = ((bf16[8,272,128]{2,1,0:T(8,128)(2,1)}), bf16[8,272,128]{2,1,0:T(8,128)(2,1)S(1)}, u32[]{:S(2)}, u32[]{:S(2)}) async-start(bf16[8,272,128]{2,1,0:T(8,128)(2,1)} %fusion.23), calls=%async_computation.1 | async-start | bytes 1114112 | tf_op jit(solution)/shard_map/all_to_all | solution.py:906
  164.7 25.9 %collective-permute-start.23 = (bf16[256,1024]{1,0:T(8,128)(2,1)S(1)}, bf16[256,1024]{1,0:T(8,128)(2,1)S(1)}, u32[]{:S(2)}, u32[]{:S(2)}) collective-permute-start(bf16[256,1024]{1,0:T(8,128)(2,1)S(1)} %copy-done.11), channel_id=1, source_target_pairs={{0,2},{2,0},{1,3},{3,1},{4,6},{6,4},{5,7},{7,5},{8,10},{10,8},{9,1... | collective-permute-start | bytes 1572872 | tf_op jit(solution)/shard_map/ppermute | solution.py:910
  166.2 24.6 %collective-permute-start.21 = (bf16[256,1024]{1,0:T(8,128)(2,1)S(1)}, bf16[256,1024]{1,0:T(8,128)(2,1)}, u32[]{:S(2)}, u32[]{:S(2)}) collective-permute-start(bf16[256,1024]{1,0:T(8,128)(2,1)S(1)} %copy-done.11), channel_id=1, source_target_pairs={{0,1},{1,0},{2,3},{3,2},{4,5},{5,4},{6,7},{7,6},{8,9},{9,8},{10,11... | collective-permute-start | bytes 1572872 | tf_op jit(solution)/shard_map/ppermute | solution.py:910
  189.1 14.5 %collective-permute-start.19 = (bf16[256,1024]{1,0:T(8,128)(2,1)}, bf16[256,1024]{1,0:T(8,128)(2,1)S(1)}, u32[]{:S(2)}, u32[]{:S(2)}) collective-permute-start(bf16[256,1024]{1,0:T(8,128)(2,1)} %get-tuple-element.157.own_ref), channel_id=1, source_target_pairs={{0,2},{2,0},{1,3},{3,1},{4,6},{6,4},{5,7},{7,5},{8,10},{10,8},{9,1... | collective-permute-start | bytes 1572872 | tf_op jit(solution)/shard_map/ppermute | solution.py:910
  190.6 18.0 %collective-permute-start.24 = (bf16[256,1024]{1,0:T(8,128)(2,1)S(1)}, bf16[256,1024]{1,0:T(8,128)(2,1)S(1)}, u32[]{:S(2)}, u32[]{:S(2)}) collective-permute-start(bf16[256,1024]{1,0:T(8,128)(2,1)S(1)} %collective-permute-done.23.grad_own_ref), channel_id=1, source_target_pairs={{0,1},{1,0},{2,3},{3,2},{4,5},{5,4},{6,7},{7,6},{8,9},{9,8},{10,11... | collective-permute-start | bytes 1572872 | tf_op jit(solution)/shard_map/ppermute | solution.py:910
  203.6 5.0 %collective-permute-start.22 = (bf16[256,1024]{1,0:T(8,128)(2,1)S(1)}, bf16[256,1024]{1,0:T(8,128)(2,1)}, u32[]{:S(2)}, u32[]{:S(2)}) collective-permute-start(bf16[256,1024]{1,0:T(8,128)(2,1)S(1)} %collective-permute-done.19.own_ref), channel_id=1, source_target_pairs={{0,1},{1,0},{2,3},{3,2},{4,5},{5,4},{6,7},{7,6},{8,9},{9,8},{10,11... | collective-permute-start | bytes 1572872 | tf_op jit(solution)/shard_map/ppermute | solution.py:910
  204.8 32.9 %all-to-all-start.2 = ((bf16[8,2,32,1024]{3,2,1,0:T(8,128)(2,1)}), bf16[8,2,32,1024]{3,2,1,0:T(8,128)(2,1)S(1)}, u32[]{:S(2)}, u32[]{:S(2)}) async-start(bf16[8,2,32,1024]{3,2,1,0:T(8,128)(2,1)} %broadcast_in_dim.32), calls=%async_computation.2 | async-start | bytes 2097152 | tf_op jit(solution)/shard_map/all_to_all | solution.py:906
  220.1 15.6 %collective-permute-start.25 = (bf16[256,1024]{1,0:T(8,128)(2,1)}, bf16[256,1024]{1,0:T(8,128)(2,1)}, u32[]{:S(2)}, u32[]{:S(2)}) collective-permute-start(bf16[256,1024]{1,0:T(8,128)(2,1)} %get-tuple-element.185), channel_id=1, source_target_pairs={{0,1},{1,0},{2,3},{3,2},{4,5},{5,4},{6,7},{7,6},{8,9},{9,8},{10,11... | collective-permute-start | bytes 1572872 | tf_op jit(solution)/shard_map/ppermute | solution.py:910
  223.1 14.6 %collective-permute-start.27 = (bf16[256,1024]{1,0:T(8,128)(2,1)S(1)}, bf16[256,1024]{1,0:T(8,128)(2,1)S(1)}, u32[]{:S(2)}, u32[]{:S(2)}) collective-permute-start(bf16[256,1024]{1,0:T(8,128)(2,1)S(1)} %add_convert_fusion.2), channel_id=1, source_target_pairs={{0,2},{2,0},{1,3},{3,1},{4,6},{6,4},{5,7},{7,5},{8,10},{10,8},{9,1... | collective-permute-start | bytes 1572872 | tf_op jit(solution)/shard_map/ppermute | solution.py:910
  246.5 6.4 %collective-permute-start.28 = (bf16[8,1,2,32,1024]{4,3,2,0,1:T(8,128)(2,1)}, bf16[8,1,2,32,1024]{4,3,2,0,1:T(8,128)(2,1)}, u32[]{:S(2)}, u32[]{:S(2)}) collective-permute-start(bf16[8,1,2,32,1024]{4,3,2,0,1:T(8,128)(2,1)} %dynamic-slice_bitcast_fusion), channel_id=1, source_target_pairs={{0,1},{1,0},{2,3},{3,2},{4,5},{5,4},{6,7},{7,6},{8,9},{9,8},{10,11... | collective-permute-start | bytes 3145736 | tf_op jit(solution)/shard_map/ppermute | solution.py:910
  246.6 9.1 %collective-permute-start.30 = (bf16[256,1024]{1,0:T(8,128)(2,1)}, bf16[256,1024]{1,0:T(8,128)(2,1)}, u32[]{:S(2)}, u32[]{:S(2)}) collective-permute-start(bf16[256,1024]{1,0:T(8,128)(2,1)} %get-tuple-element.205), channel_id=1, source_target_pairs={{0,1},{1,0},{2,3},{3,2},{4,5},{5,4},{6,7},{7,6},{8,9},{9,8},{10,11... | collective-permute-start | bytes 1572872 | tf_op jit(solution)/shard_map/ppermute | solution.py:910
  247.0 9.9 %collective-permute-start.31 = (bf16[256,1024]{1,0:T(8,128)(2,1)}, bf16[256,1024]{1,0:T(8,128)(2,1)}, u32[]{:S(2)}, u32[]{:S(2)}) collective-permute-start(bf16[256,1024]{1,0:T(8,128)(2,1)} %get-tuple-element.207), channel_id=1, source_target_pairs={{0,1},{1,0},{2,3},{3,2},{4,5},{5,4},{6,7},{7,6},{8,9},{9,8},{10,11... | collective-permute-start | bytes 1572872 | tf_op jit(solution)/shard_map/ppermute | solution.py:910
  247.1 22.7 %all-to-all-start.3 = ((bf16[8,272,128]{2,1,0:T(8,128)(2,1)}), bf16[8,272,128]{2,1,0:T(8,128)(2,1)S(1)}, u32[]{:S(2)}, u32[]{:S(2)}) async-start(bf16[8,272,128]{2,1,0:T(8,128)(2,1)} %get-tuple-element.202), calls=%async_computation.3 | async-start | bytes 1114112 | tf_op jit(solution)/shard_map/all_to_all | solution.py:906
  252.9 132.5 %reduce-scatter.2.cloned.1.call-start = ((), (), s32[]{:S(2)}) async-start(), calls=%async_computation.8 | async-start | bytes 4718592 | tf_op jit(solution)/shard_map/reduce_scatter | solution.py:1202
  254.7 14.1 %collective-permute-start.29 = (bf16[8,1,32,1024]{3,2,0,1:T(8,128)(2,1)S(1)}, bf16[8,1,32,1024]{3,2,0,1:T(8,128)(2,1)S(1)}, u32[]{:S(2)}, u32[]{:S(2)}) collective-permute-start(bf16[8,1,32,1024]{3,2,0,1:T(8,128)(2,1)S(1)} %dynamic-slice_bitcast_fusion.1), channel_id=1, source_target_pairs={{0,2},{2,0},{1,3},{3,1},{4,6},{6,4},{5,7},{7,5},{8,10},{10,8},{9,1... | collective-permute-start | bytes 1572872 | tf_op jit(solution)/shard_map/ppermute | solution.py:910
  269.8 14.0 %collective-permute-start.32 = (bf16[1,8,272,128]{3,2,1,0:T(8,128)(2,1)S(1)}, bf16[1,8,272,128]{3,2,1,0:T(8,128)(2,1)}, u32[]{:S(2)}, u32[]{:S(2)}) collective-permute-start(bf16[1,8,272,128]{3,2,1,0:T(8,128)(2,1)S(1)} %bitcast.233), channel_id=1, source_target_pairs={{0,2},{2,0},{1,3},{3,1},{4,6},{6,4},{5,7},{7,5},{8,10},{10,8},{9,1... | collective-permute-start | bytes 1671176 | tf_op jit(solution)/shard_map/ppermute | solution.py:910
  286.0 7.7 %collective-permute-start.33 = (bf16[2,1,8,272,128]{4,3,2,1,0:T(8,128)(2,1)}, bf16[2,1,8,272,128]{4,3,2,1,0:T(8,128)(2,1)}, u32[]{:S(2)}, u32[]{:S(2)}) collective-permute-start(bf16[2,1,8,272,128]{4,3,2,1,0:T(8,128)(2,1)} %pad_maximum_fusion.2), channel_id=1, source_target_pairs={{0,1},{1,0},{2,3},{3,2},{4,5},{5,4},{6,7},{7,6},{8,9},{9,8},{10,11... | collective-permute-start | bytes 3342344 | tf_op jit(solution)/shard_map/ppermute | solution.py:910
  286.0 44.8 %collective-permute-start.34 = (bf16[2,8,1,32,1024]{4,3,0,1,2:T(8,128)(2,1)S(1)}, bf16[2,8,1,32,1024]{4,3,0,1,2:T(8,128)(2,1)}, u32[]{:S(2)}, u32[]{:S(2)}) collective-permute-start(bf16[2,8,1,32,1024]{4,3,0,1,2:T(8,128)(2,1)S(1)} %bitcast.222), channel_id=1, source_target_pairs={{0,2},{2,0},{1,3},{3,1},{4,6},{6,4},{5,7},{7,5},{8,10},{10,8},{9,1... | collective-permute-start | bytes 3145736 | tf_op jit(solution)/shard_map/ppermute | solution.py:910
  286.9 43.8 %all-to-all-start.4 = ((bf16[8,32,1024]{2,1,0:T(8,128)(2,1)}), bf16[8,32,1024]{2,1,0:T(8,128)(2,1)S(1)}, u32[]{:S(2)}, u32[]{:S(2)}) async-start(bf16[8,32,1024]{2,1,0:T(8,128)(2,1)} %bitcast.235), calls=%async_computation.4 | async-start | bytes 1048576 | tf_op jit(solution)/shard_map/all_to_all | solution.py:906
  292.6 38.2 %collective-permute-start.35 = (bf16[256,1024]{1,0:T(8,128)(2,1)}, bf16[256,1024]{1,0:T(8,128)(2,1)}, u32[]{:S(2)}, u32[]{:S(2)}) collective-permute-start(bf16[256,1024]{1,0:T(8,128)(2,1)} %add_convert_fusion), channel_id=1, source_target_pairs={{0,2},{2,0},{1,3},{3,1},{4,6},{6,4},{5,7},{7,5},{8,10},{10,8},{9,1... | collective-permute-start | bytes 1572872 | tf_op jit(solution)/shard_map/ppermute | solution.py:910
  330.8 4.4 %collective-permute-start.36 = (bf16[2,1,8,256,256]{4,3,2,1,0:T(8,128)(2,1)}, bf16[2,1,8,256,256]{4,3,2,1,0:T(8,128)(2,1)S(1)}, u32[]{:S(2)}, u32[]{:S(2)}) collective-permute-start(bf16[2,1,8,256,256]{4,3,2,1,0:T(8,128)(2,1)} %bitcast.276), channel_id=1, source_target_pairs={{0,1},{1,0},{2,3},{3,2},{4,5},{5,4},{6,7},{7,6},{8,9},{9,8},{10,11... | collective-permute-start | bytes 6291464 | tf_op jit(solution)/shard_map/ppermute | solution.py:910
  340.2 4.5 %collective-permute-start.38 = (bf16[2,8,1,2,32,1024]{5,4,0,1,3,2:T(8,128)(2,1)}, bf16[2,8,1,2,32,1024]{5,4,0,1,3,2:T(8,128)(2,1)}, u32[]{:S(2)}, u32[]{:S(2)}) collective-permute-start(bf16[2,8,1,2,32,1024]{5,4,0,1,3,2:T(8,128)(2,1)} %pad_maximum_fusion.1), channel_id=1, source_target_pairs={{0,1},{1,0},{2,3},{3,2},{4,5},{5,4},{6,7},{7,6},{8,9},{9,8},{10,11... | collective-permute-start | bytes 6291464 | tf_op jit(solution)/shard_map/ppermute | solution.py:910
  340.3 25.8 %collective-permute-start.37 = (bf16[1,8,256,256]{3,2,1,0:T(8,128)(2,1)}, bf16[1,8,256,256]{3,2,1,0:T(8,128)(2,1)}, u32[]{:S(2)}, u32[]{:S(2)}) collective-permute-start(bf16[1,8,256,256]{3,2,1,0:T(8,128)(2,1)} %get-tuple-element.229), channel_id=1, source_target_pairs={{0,2},{2,0},{1,3},{3,1},{4,6},{6,4},{5,7},{7,5},{8,10},{10,8},{9,1... | collective-permute-start | bytes 3145736 | tf_op jit(solution)/shard_map/ppermute | solution.py:910
  342.2 34.5 %collective-permute-start.43 = (f32[8,2,128]{2,1,0:T(2,128)S(1)}, f32[8,2,128]{2,1,0:T(2,128)S(1)}, u32[]{:S(2)}, u32[]{:S(2)}) collective-permute-start(f32[8,2,128]{2,1,0:T(2,128)S(1)} %bitcast.268), channel_id=1, source_target_pairs={{0,1},{1,0},{2,3},{3,2},{4,5},{5,4},{6,7},{7,6},{8,9},{9,8},{10,11... | collective-permute-start | bytes 24584 | tf_op jit(solution)/shard_map/ppermute | solution.py:910
  368.6 31.6 %all-to-all-start.5 = ((bf16[8,256,256]{2,1,0:T(8,128)(2,1)}), bf16[8,256,256]{2,1,0:T(8,128)(2,1)S(1)}, u32[]{:S(2)}, u32[]{:S(2)}) async-start(bf16[8,256,256]{2,1,0:T(8,128)(2,1)} %bitcast.216), calls=%async_computation.5 | async-start | bytes 2097152 | tf_op jit(solution)/shard_map/all_to_all | solution.py:906
  384.4 20.6 %collective-permute-start.44 = (f32[8,128]{1,0:T(8,128)S(1)}, f32[8,128]{1,0:T(8,128)S(1)}, u32[]{:S(2)}, u32[]{:S(2)}) collective-permute-start(f32[8,128]{1,0:T(8,128)S(1)} %bitcast.269), channel_id=1, source_target_pairs={{0,2},{2,0},{1,3},{3,1},{4,6},{6,4},{5,7},{7,5},{8,10},{10,8},{9,1... | collective-permute-start | bytes 12296 | tf_op jit(solution)/shard_map/ppermute | solution.py:910
  387.2 6.4 %collective-permute-start.41 = (bf16[1,2,32,1024]{3,2,1,0:T(8,128)(2,1)S(1)}, bf16[1,2,32,1024]{3,2,1,0:T(8,128)(2,1)S(1)}, u32[]{:S(2)}, u32[]{:S(2)}) collective-permute-start(bf16[1,2,32,1024]{3,2,1,0:T(8,128)(2,1)S(1)} %constant_dynamic-slice_fusion.1), channel_id=1, source_target_pairs={{0,2},{2,0},{1,3},{3,1},{4,6},{6,4},{5,7},{7,5},{8,10},{10,8},{9,1... | collective-permute-start | bytes 393224 | tf_op jit(solution)/shard_map/ppermute | solution.py:910
  388.6 8.5 %collective-permute-start.40 = (bf16[8,1,48,256]{3,2,0,1:T(8,128)(2,1)S(1)}, bf16[8,1,48,256]{3,2,0,1:T(8,128)(2,1)S(1)}, u32[]{:S(2)}, u32[]{:S(2)}) collective-permute-start(bf16[8,1,48,256]{3,2,0,1:T(8,128)(2,1)S(1)} %dynamic-slice_bitcast_fusion.2), channel_id=1, source_target_pairs={{0,2},{2,0},{1,3},{3,1},{4,6},{6,4},{5,7},{7,5},{8,10},{10,8},{9,1... | collective-permute-start | bytes 589832 | tf_op jit(solution)/shard_map/ppermute | solution.py:910
  393.7 4.2 collective-permute-start.42
  400.2 12.0 %all-to-all-start.6 = ((bf16[8,48,256]{2,1,0:T(8,128)(2,1)}), bf16[8,48,256]{2,1,0:T(8,128)(2,1)S(1)}, u32[]{:S(2)}, u32[]{:S(2)}) async-start(bf16[8,48,256]{2,1,0:T(8,128)(2,1)} %fusion.33), calls=%async_computation.7 | async-start | bytes 393216 | tf_op jit(solution)/shard_map/all_to_all | solution.py:906
  (53 other events, 510.2 us)
Sparse Core Ops, SparseCore 0:
  73.4 103.0 all-gather.2
  270.8 99.9 reduce-scatter.1

commit v6 on v5

--- a/solution.py
+++ b/solution.py
@@ -108,6 +108,7 @@
         )
     ]
     own_spans = prob_ref.shape[0] // SPAN
+    unroll = 2 * UNROLL if own_spans == 4 * UNROLL else UNROLL
     tail = SPAN * (own_spans + 1)
 
     @pl.when(step == 0)
@@ -152,24 +153,24 @@
         before, itself = lane_ids == row_ids, lane_ids == row_ids + SPAN
 
         def spans(group, carry):
-            first = group * (UNROLL * SPAN)
+            first = group * (unroll * SPAN)
             prev = aligned(first, SPAN)
-            here = aligned(first + SPAN, UNROLL * SPAN)
+            here = aligned(first + SPAN, unroll * SPAN)
             query_wide = wide_a[here, :]
             values = wide_b[here, :].astype(bf)
             keys = jnp.concatenate([key_ref[prev, :], unit_keys(query_wide)], axis=0)
             seen = jnp.concatenate([value_ref[prev, :], values], axis=0)
             query = query_wide.astype(bf)
             key_buckets, columns = [], []
-            for span in range(UNROLL):
-                row = bucket_ref[pl.ds(group * UNROLL + span, 1), :]
+            for span in range(unroll):
+                row = bucket_ref[pl.ds(group * unroll + span, 1), :]
                 high = row.astype(bf).astype(f32)
                 low = pltpu.roll(row - high, SPAN, 1)
                 key_buckets.append(row)
                 columns.append(jnp.where(itself, high, jnp.where(before, low, 0.0)).astype(bf))
             columns = product(jnp.concatenate(columns, axis=0), ones)
             raised = []
-            for span in range(UNROLL):
+            for span in range(unroll):
                 mine = slice(span * SPAN, (span + 1) * SPAN)
                 both = slice(span * SPAN, (span + 2) * SPAN)
                 same = columns[mine] == key_buckets[span]
@@ -180,7 +181,7 @@
             lows = [member.astype(bf) for member in raised]
             totals = product(jnp.concatenate(lows, axis=0), ones)
             results = []
-            for span in range(UNROLL):
+            for span in range(unroll):
                 mine = slice(span * SPAN, (span + 1) * SPAN)
                 both = slice(span * SPAN, (span + 2) * SPAN)
                 total = totals[mine]
@@ -197,7 +198,7 @@
                 prob_ref[aligned(first + span * SPAN, SPAN), :] = probs
             return carry
 
-        lax.fori_loop(0, own_spans // UNROLL, spans, 0)
+        lax.fori_loop(0, own_spans // unroll, spans, 0)
         for copy in leaving:
             copy.start()
         wide_a[pl.ds(tail, SPAN), :] = jnp.zeros((SPAN, HEADD), f32)
@@ -329,6 +330,7 @@
         )
     ]
     own_spans = prob_ref.shape[0] // SPAN
+    unroll = 2 * UNROLL if own_spans == 4 * UNROLL else UNROLL
     tail = SPAN * (own_spans + 1)
 
     @pl.when(step == 0)
@@ -383,11 +385,11 @@
         zero = jnp.zeros((SPAN, HEADD), bf)
 
         def spans(group, carry):
-            first = group * (UNROLL * SPAN)
+            first = group * (unroll * SPAN)
             prev = aligned(first, SPAN)
-            own = aligned(first, UNROLL * SPAN)
-            here = aligned(first + SPAN, UNROLL * SPAN)
-            around = aligned(first, (UNROLL + 1) * SPAN)
+            own = aligned(first, unroll * SPAN)
+            here = aligned(first + SPAN, unroll * SPAN)
+            around = aligned(first, (unroll + 1) * SPAN)
             query = query_ref[around, :]
             keys = key_ref[around, :]
             values = value_ref[around, :]
@@ -397,7 +399,7 @@
             d_query = [wide_a[prev, :]]
             d_keys = [wide_b[prev, :]]
             d_values = [wide_c[prev, :]]
-            for span in range(UNROLL):
+            for span in range(unroll):
                 mine = slice(span * SPAN, (span + 1) * SPAN)
                 after = slice((span + 1) * SPAN, (span + 2) * SPAN)
                 both = slice(span * SPAN, (span + 2) * SPAN)
@@ -417,10 +419,10 @@
                 d_values[-1] = d_values[-1] + pair[:SPAN, HEADD:]
                 d_keys.append(pair[SPAN:, :HEADD])
                 d_values.append(pair[SPAN:, HEADD:])
-            for span in range(UNROLL + 1):
+            for span in range(unroll + 1):
                 at = aligned(first + span * SPAN, SPAN)
                 wide_c[at, :] = d_values[span]
-                if span < UNROLL:
+                if span < unroll:
                     rows = slice(span * SPAN, (span + 1) * SPAN)
                     wide_a[at, :] = pulled(query[rows], d_query[span], d_keys[span])
                 else:
@@ -428,7 +430,7 @@
                     wide_b[at, :] = d_keys[span]
             return carry
 
-        lax.fori_loop(0, own_spans // UNROLL, spans, 0)
+        lax.fori_loop(0, own_spans // unroll, spans, 0)
         last = pl.ds(tail - SPAN, SPAN)
         wide_a[last, :] = pulled(query_ref[last, :], wide_a[last, :], wide_b[last, :])
         wide_a[pl.ds(tail, SPAN), :] = jnp.zeros((SPAN, HEADD), f32)

time: 429 us -> 428 us (level)
  transfers between devices with their start and end apart: 54 -> 54, of which waited for: 26 -> 26; matrix products, arithmetic and copies ran while one was open for 16% -> 16% of each run, Pallas kernels for 28% -> 27%
where the time goes in v6:
time: 428 us; the launch traced here: 420 us
  waiting for transfers between devices  130 us (30%)
  Pallas kernels  120 us (28%)
  starting transfers between devices  70 us (16%)
  other arithmetic  44.6 us (10%)
  local copies, waits for them, and re-layouts  30.5 us (7%)
  between operations  15.6 us (4%)
  matrix products  10.2 us (2%)
    ppermute x37, waiting for transfers between devices, swapped(): return lax.ppermute(value, axis, SWAP)  92.7 us
    all_to_all x7, starting transfers between devices, exchange(): return lax.all_to_all(parts, axes, split_axis=0, concat_axis=0, tiled=True)  36.6 us
    pallas_call x1, Pallas kernels, attend_backward(): pl.pallas_call(functools.partial(backward_kernel, own_rows, steps), grid=...  36.2 us
    pallas_call x1, Pallas kernels, attend_forward(): pl.pallas_call(functools.partial(forward_kernel, own_rows, steps), grid=(...  30.2 us
    ppermute x37, starting transfers between devices, swapped(): return lax.ppermute(value, axis, SWAP)  23.8 us
    all_to_all x7, waiting for transfers between devices, exchange(): return lax.all_to_all(parts, axes, split_axis=0, concat_axis=0, tiled=True)  22.5 us
    pallas_call x2, Pallas kernels, feed_forward(): pl.pallas_call(feed_kernel, grid=(2,), out_shape=(by_width, by_width, by_...  20.4 us
    ppermute x8, waiting for transfers between devices, ring_step(): return (lax.ppermute(up, 'hd', UP), lax.ppermute(down, 'hd', DOWN))  14.6 us
  transfers between devices with their start and end apart: 54, of which 26 were waited for; matrix products, arithmetic and copies ran while one was open for 16% of the time, Pallas kernels for 27%

profile of v6, /device:TPU:0, one launch (start us, length us, event | category | flops | bytes accessed | tf_op | source)
XLA Modules:
  0.0 420.4 jit_solution(2784385707835817179)
XLA Ops:
  13.5 2.9 collective-permute-start.1
  17.3 6.3 %all-to-all-start = ((bf16[8,48,384]{2,1,0:T(8,128)(2,1)}), bf16[8,48,384]{2,1,0:T(8,128)(2,1)S(1)}, u32[]{:S(2)}, u32[]{:S(2)}) async-start(bf16[8,48,384]{2,1,0:T(8,128)(2,1)} %copy.80), calls=%async_computation | async-start | bytes 589824 | tf_op jit(solution)/shard_map/all_to_all | solution.py:908
  27.4 4.2 collective-permute-done.5
  31.7 2.1 collective-permute-done.3
  34.8 2.5 all-to-all-done
  38.9 4.2 collective-permute-done.8
  49.5 9.3 %collective-permute-done.6.refs_3_ = bf16[256,1024]{1,0:T(8,128)(2,1)S(1)} collective-permute-done((bf16[256,1024]{1,0:T(8,128)(2,1)S(1)}, bf16[256,1024]{1,0:T(8,128)(2,1)S(1)}, u32[]{:S(2)}, u32[]{:S(2)}) %collective-permute-start.6) | collective-permute-done | bytes 524320 | tf_op jit(solution)/shard_map/ppermute | solution.py:962
  83.7 2.0 collective-permute-done.14
  85.7 2.6 collective-permute-done.12.refs_7_
  88.3 2.1 bitcast_dynamic-update-slice_fusion
  97.3 4.5 %collective-permute-done.15 = bf16[1,768,256]{2,1,0:T(8,128)(2,1)S(1)} collective-permute-done((bf16[1,768,256]{2,1,0:T(8,128)(2,1)S(1)}, bf16[1,768,256]{2,1,0:T(8,128)(2,1)S(1)}, u32[]{:S(2)}, u32[]{:S(2)}) %collective-permute-start.15) | collective-permute-done | bytes 393248 | tf_op jit(solution)/shard_map/ppermute | solution.py:912
  102.7 4.4 %collective-permute-done.16.peer_ref = bf16[4096,256]{1,0:T(8,128)(2,1)S(1)} collective-permute-done((bf16[4096,256]{1,0:T(8,128)(2,1)}, bf16[4096,256]{1,0:T(8,128)(2,1)S(1)}, u32[]{:S(2)}, u32[]{:S(2)}) %collective-permute-start.16) | collective-permute-done | bytes 2097184 | tf_op jit(solution)/shard_map/ppermute | solution.py:912
  108.4 30.2 %attend_forward.1 = (bf16[4352,128]{1,0:T(8,128)(2,1)}, bf16[4352,128]{1,0:T(8,128)(2,1)}, bf16[8832,128]{1,0:T(8,128)(2,1)}, bf16[8832,128]{1,0:T(8,128)(2,1)},...) custom-call(s32[32]{0:T(128)} %get-tuple-element.145.in_ref, ...), custom_call_target="tpu_custom_call" | custom-call | flops 3500000000 | bytes 105000000 | tf_op jit(solution)/shard_map/attend_forward/pallas_call | solution.py:260
  138.8 2.8 collective-permute-done.17
  144.9 13.0 %collective-permute-done.18 = bf16[1,8,272,128]{3,2,1,0:T(8,128)(2,1)S(1)} collective-permute-done((bf16[1,8,272,128]{3,2,1,0:T(8,128)(2,1)S(1)}, bf16[1,8,272,128]{3,2,1,0:T(8,128)(2,1)S(1)}, u32[]{:S(2)}, u32[]{:S(2)}) %collective-permute-start.18) | collective-permute-done | bytes 557088 | tf_op jit(solution)/shard_map/ppermute | solution.py:912
  158.9 5.5 %all-to-all-start.1 = ((bf16[8,272,128]{2,1,0:T(8,128)(2,1)}), bf16[8,272,128]{2,1,0:T(8,128)(2,1)S(1)}, u32[]{:S(2)}, u32[]{:S(2)}) async-start(bf16[8,272,128]{2,1,0:T(8,128)(2,1)} %fusion.23), calls=%async_computation.1 | async-start | bytes 1114112 | tf_op jit(solution)/shard_map/all_to_all | solution.py:908
  166.0 17.8 %all-to-all-done.1.parts_ref = bf16[8,272,128]{2,1,0:T(8,128)(2,1)S(1)} async-done(((bf16[8,272,128]{2,1,0:T(8,128)(2,1)}), bf16[8,272,128]{2,1,0:T(8,128)(2,1)S(1)}, u32[]{:S(2)}, u32[]{:S(2)}) %all-to-all-start.1) | async-done | bytes 557088 | tf_op jit(solution)/shard_map/all_to_all | solution.py:908
  184.7 4.3 %mix_rows.1 = (bf16[256,1024]{1,0:T(8,128)(2,1)}, bf16[256,1024]{1,0:T(8,128)(2,1)}, f32[256,1024]{1,0:T(8,128)}, f32[256,1]{1,0:T(8,128)}, bf16[256,1024]{1,0:T(8,128)(2,1)}) custom-call(bf16[8,272,128]{2,1,0:T(8,128)(2,1)} %copy-done.3, bf16[8,3,128,1024]{3,2,1,0:T(8,128)(2,1)} %bitcast.209, bf16[256,1024]{1,0:T(8,128)(2,1)} %first_ref.1, ...), custom_call_target="tpu_custom_call" | custom-call | flops 500000000 | bytes 15000000 | tf_op jit(solution)/shard_map/mix_rows/pallas_call | solution.py:606
  192.0 10.2 %feed_forward.2 = (bf16[512,1024]{1,0:T(8,128)(2,1)}, bf16[512,1024]{1,0:T(8,128)(2,1)}, bf16[512,1024]{1,0:T(8,128)(2,1)}, bf16[512,1024]{1,0:T(8,128)(2,1)}, b...) custom-call(bf16[256,1024]{1,0:T(8,128)(2,1)} %get-tuple-element.157, ...), custom_call_target="tpu_custom_call" | custom-call | flops 900000000 | bytes 27000000 | tf_op jit(solution)/shard_map/feed_forward/pallas_call | solution.py:564
  204.8 3.6 all-to-all-start.2
  209.2 10.2 %feed_forward.3 = (bf16[512,1024]{1,0:T(8,128)(2,1)}, bf16[512,1024]{1,0:T(8,128)(2,1)}, bf16[512,1024]{1,0:T(8,128)(2,1)}, bf16[512,1024]{1,0:T(8,128)(2,1)}, b...) custom-call(bf16[256,1024]{1,0:T(8,128)(2,1)} %copy-done.28, ...), custom_call_target="tpu_custom_call" | custom-call | flops 900000000 | bytes 27000000 | tf_op jit(solution)/shard_map/feed_forward/pallas_call | solution.py:564
  224.5 11.0 %parts_product.1 = bf16[8,2,128,1024]{3,2,1,0:T(8,128)(2,1)} custom-call(bf16[512,1024]{1,0:T(8,128)(2,1)} %get-tuple-element.188.row_pair_ref, bf16[512,1024]{1,0:T(8,128)(2,1)} %get-tuple-element.189.row_far_ref, bf16[512,1024]{1,0:T(8,128)(2,1)} %get-tuple-element.190.inner_pair_ref, bf16[512,1024]{1,0:T(8,128)(2,1)} %get-tuple-element.191.inner_far_ref, ...), custom_call_target="tpu_custom_call" | custom-call | tf_op jit(solution)/shard_map/parts_product/pallas_call | solution.py:867
  235.5 2.0 add_convert_fusion.3.near_ref
  238.4 5.0 %carry_rows.1 = (bf16[256,1024]{1,0:T(8,128)(2,1)}, bf16[8,272,128]{2,1,0:T(8,128)(2,1)}) custom-call(bf16[256,1024]{1,0:T(8,128)(2,1)} %add_convert_fusion.3.near_ref, bf16[256,1024]{1,0:T(8,128)(2,1)} %copy-done.30, f32[1,1024]{1,0:T(1,128)} %bitcast.262, f32[256,1024]{1,0:T(8,128)} %get-tuple-element.199.unit_ref, f32[256,1]{1,0:T(8,128)} %get-tuple-element.200.scale_ref, ...), custom_call_target="tpu_custom_call" | custom-call | flops 500000000 | bytes 15000000 | tf_op jit(solution)/shard_map/carry_rows/pallas_call | solution.py:656
  243.4 1.8 convolution_convert_fusion
  246.9 5.7 %all-to-all-start.3 = ((bf16[8,272,128]{2,1,0:T(8,128)(2,1)}), bf16[8,272,128]{2,1,0:T(8,128)(2,1)S(1)}, u32[]{:S(2)}, u32[]{:S(2)}) async-start(bf16[8,272,128]{2,1,0:T(8,128)(2,1)} %get-tuple-element.202), calls=%async_computation.3 | async-start | bytes 1114112 | tf_op jit(solution)/shard_map/all_to_all | solution.py:908
  256.9 2.0 add_convert_fusion
  258.9 9.8 %collective-permute-done.29 = bf16[8,1,32,1024]{3,2,0,1:T(8,128)(2,1)S(1)} collective-permute-done((bf16[8,1,32,1024]{3,2,0,1:T(8,128)(2,1)S(1)}, bf16[8,1,32,1024]{3,2,0,1:T(8,128)(2,1)S(1)}, u32[]{:S(2)}, u32[]{:S(2)}) %collective-permute-start.29) | collective-permute-done | bytes 524320 | tf_op jit(solution)/shard_map/ppermute | solution.py:912
  270.7 13.1 %collective-permute-done.32 = bf16[1,8,272,128]{3,2,1,0:T(8,128)(2,1)} collective-permute-done((bf16[1,8,272,128]{3,2,1,0:T(8,128)(2,1)S(1)}, bf16[1,8,272,128]{3,2,1,0:T(8,128)(2,1)}, u32[]{:S(2)}, u32[]{:S(2)}) %collective-permute-start.32) | collective-permute-done | bytes 557088 | tf_op jit(solution)/shard_map/ppermute | solution.py:912
  283.8 2.2 pad_maximum_fusion.2
  286.9 5.4 %all-to-all-start.4 = ((bf16[8,32,1024]{2,1,0:T(8,128)(2,1)}), bf16[8,32,1024]{2,1,0:T(8,128)(2,1)S(1)}, u32[]{:S(2)}, u32[]{:S(2)}) async-start(bf16[8,32,1024]{2,1,0:T(8,128)(2,1)} %bitcast.235), calls=%async_computation.4 | async-start | bytes 1048576 | tf_op jit(solution)/shard_map/all_to_all | solution.py:908
  293.4 36.2 %attend_backward.1 = (bf16[4096,256]{1,0:T(8,128)(2,1)}, bf16[4096,256]{1,0:T(8,128)(2,1)}) custom-call(s32[32]{0:T(128)} %get-tuple-element.146.out_ref.table_ref, s32[8192]{0:T(1024)} %broadcast_add_fusion.place_ref, bf16[4352,128]{1,0:T(8,128)(2,1)} %bitcast.57.pay_own_ref, bf16[4352,128]{1,0:T(8,128)(2,1)} %bitcast.58.pay_peer_ref, ...), custom_call_target="tpu_custom_call" | custom-call | flops 4400000000 | bytes 132000000 | tf_op jit(solution)/shard_map/attend_backward/pallas_call | solution.py:467
  331.6 2.6 collective-permute-done.36
  334.2 2.0 fusion.1
  341.2 2.3 collective-permute-done.38
  343.6 1.9 select_bitcast_fusion.1
  345.9 2.5 copy.85
  348.4 16.6 %collective-permute-done.37 = bf16[1,8,256,256]{3,2,1,0:T(8,128)(2,1)} collective-permute-done((bf16[1,8,256,256]{3,2,1,0:T(8,128)(2,1)}, bf16[1,8,256,256]{3,2,1,0:T(8,128)(2,1)}, u32[]{:S(2)}, u32[]{:S(2)}) %collective-permute-start.37) | collective-permute-done | bytes 1048608 | tf_op jit(solution)/shard_map/ppermute | solution.py:912
  365.0 2.5 add_rows.1
  367.4 6.3 %all-to-all-start.5 = ((bf16[8,256,256]{2,1,0:T(8,128)(2,1)}), bf16[8,256,256]{2,1,0:T(8,128)(2,1)S(1)}, u32[]{:S(2)}, u32[]{:S(2)}) async-start(bf16[8,256,256]{2,1,0:T(8,128)(2,1)} %bitcast.216), calls=%async_computation.5 | async-start | bytes 2097152 | tf_op jit(solution)/shard_map/all_to_all | solution.py:908
  373.7 2.1 fusion.20
  375.8 4.9 %weight_part.1 = (f32[1024,256]{1,0:T(8,128)}, f32[8,256]{1,0:T(8,128)}) custom-call(s32[8]{0:T(128)} %copy-done, bf16[8,256,256]{2,1,0:T(8,128)(2,1)} %bitcast.217, bf16[256,1024]{1,0:T(8,128)(2,1)} %copy-done.4, bf16[256,1024]{1,0:T(8,128)(2,1)} %copy-done.16, bf16[256,1024]{1,0:T(8,128)(2,1)} %copy-done.15, bf16[256,1024]{1,0:T(8,128)(2,1)} %copy-done.18, ...), custom_call_target="tpu_custom_call" | custom-call | flops 500000000 | bytes 15000000 | tf_op jit(solution)/shard_map/weight_part/pallas_call | solution.py:743
  384.6 1.9 fusion.32
  388.8 4.1 collective-permute-done.41
  393.0 3.4 collective-permute-done.40
  397.2 2.1 all-to-all-done.5.back_ref
  399.3 3.9 all-to-all-start.6
  405.9 5.3 %last_rows.1 = bf16[256,1024]{1,0:T(8,128)(2,1)} custom-call(bf16[8,256,256]{2,1,0:T(8,128)(2,1)} %copy-done.8, bf16[2,1024,1024]{2,1,0:T(8,128)(2,1)} %bitcast.215, f32[1,1024]{1,0:T(1,128)} %bitcast.260, f32[256,1024]{1,0:T(8,128)} %get-tuple-element.263.unit_ref, f32[256,1]{1,0:T(8,128)} %copy.86.scale_ref, bf16[256,1024]{1,0:T(8,128)(2,1)} %grad_ref.3), custom_call_target="tpu_custom_call" | custom-call | flops 600000000 | bytes 18000000 | tf_op jit(solution)/shard_map/last_rows/pallas_call | solution.py:712
  (313 shorter events, 101.5 us)
Async XLA Ops:
  13.5 23.7 %collective-permute-start.1 = (bf16[256,1024]{1,0:T(8,128)(2,1)S(1)}, bf16[256,1024]{1,0:T(8,128)(2,1)S(1)}, u32[]{:S(2)}, u32[]{:S(2)}) collective-permute-start(bf16[256,1024]{1,0:T(8,128)(2,1)S(1)} %get-tuple-element.264.refs_0_), channel_id=1, source_target_pairs={{8,0},{16,8},{24,16},{28,24},{20,28},{12,20},{4,12},{0,4},{9,1},{1... | collective-permute-start | bytes 1572872 | tf_op jit(solution)/shard_map/ppermute | solution.py:962
  16.5 20.8 %collective-permute-start = (bf16[256,1024]{1,0:T(8,128)(2,1)S(1)}, bf16[256,1024]{1,0:T(8,128)(2,1)S(1)}, u32[]{:S(2)}, u32[]{:S(2)}) collective-permute-start(bf16[256,1024]{1,0:T(8,128)(2,1)S(1)} %get-tuple-element.264.refs_0_), channel_id=1, source_target_pairs={{0,8},{8,16},{16,24},{24,28},{28,20},{20,12},{12,4},{4,0},{1,9},{9... | collective-permute-start | bytes 1572872 | tf_op jit(solution)/shard_map/ppermute | solution.py:962
  16.6 7.7 %collective-permute-start.4 = (bf16[32,1024]{1,0:T(8,128)(2,1)S(1)}, bf16[32,1024]{1,0:T(8,128)(2,1)}, u32[]{:S(2)}, u32[]{:S(2)}) collective-permute-start(bf16[32,1024]{1,0:T(8,128)(2,1)S(1)} %copy-done.35), channel_id=1, source_target_pairs={{0,1},{1,0},{2,3},{3,2},{4,5},{5,4},{6,7},{7,6},{8,9},{9,8},{10,11... | collective-permute-start | bytes 196616 | tf_op jit(solution)/shard_map/ppermute | solution.py:912
  17.3 19.9 %all-to-all-start = ((bf16[8,48,384]{2,1,0:T(8,128)(2,1)}), bf16[8,48,384]{2,1,0:T(8,128)(2,1)S(1)}, u32[]{:S(2)}, u32[]{:S(2)}) async-start(bf16[8,48,384]{2,1,0:T(8,128)(2,1)} %copy.80), calls=%async_computation | async-start | bytes 589824 | tf_op jit(solution)/shard_map/all_to_all | solution.py:908
  23.6 160.3 %all-gather.3.cloned.1.call-start = ((), (), s32[]{:S(2)}) async-start(), calls=%async_computation.9 | async-start | bytes 7077888 | tf_op jit(solution)/shard_map/all_gather | solution.py:1161
  25.2 6.4 %collective-permute-start.5 = (bf16[2,32,1024]{2,1,0:T(8,128)(2,1)S(1)}, bf16[2,32,1024]{2,1,0:T(8,128)(2,1)S(1)}, u32[]{:S(2)}, u32[]{:S(2)}) collective-permute-start(bf16[2,32,1024]{2,1,0:T(8,128)(2,1)S(1)} %pad_maximum_fusion.9), channel_id=1, source_target_pairs={{0,2},{2,0},{1,3},{3,1},{4,6},{6,4},{5,7},{7,5},{8,10},{10,8},{9,1... | collective-permute-start | bytes 393224 | tf_op jit(solution)/shard_map/ppermute | solution.py:912
  26.8 6.9 %collective-permute-start.3 = (bf16[1,2,32,1024]{3,2,1,0:T(8,128)(2,1)S(1)}, bf16[1,2,32,1024]{3,2,1,0:T(8,128)(2,1)S(1)}, u32[]{:S(2)}, u32[]{:S(2)}) collective-permute-start(bf16[1,2,32,1024]{3,2,1,0:T(8,128)(2,1)S(1)} %constant_dynamic-slice_fusion.3), channel_id=1, source_target_pairs={{0,2},{2,0},{1,3},{3,1},{4,6},{6,4},{5,7},{7,5},{8,10},{10,8},{9,1... | collective-permute-start | bytes 393224 | tf_op jit(solution)/shard_map/ppermute | solution.py:912
  37.3 5.7 %collective-permute-start.8 = (bf16[8,1,32,384]{3,2,0,1:T(8,128)(2,1)S(1)}, bf16[8,1,32,384]{3,2,0,1:T(8,128)(2,1)S(1)}, u32[]{:S(2)}, u32[]{:S(2)}) collective-permute-start(bf16[8,1,32,384]{3,2,0,1:T(8,128)(2,1)S(1)} %slice.149), channel_id=1, source_target_pairs={{0,2},{2,0},{1,3},{3,1},{4,6},{6,4},{5,7},{7,5},{8,10},{10,8},{9,1... | collective-permute-start | bytes 589832 | tf_op jit(solution)/shard_map/ppermute | solution.py:912
  44.5 14.3 %collective-permute-start.6 = (bf16[256,1024]{1,0:T(8,128)(2,1)S(1)}, bf16[256,1024]{1,0:T(8,128)(2,1)S(1)}, u32[]{:S(2)}, u32[]{:S(2)}) collective-permute-start(bf16[256,1024]{1,0:T(8,128)(2,1)S(1)} %collective-permute-done.refs_1_), channel_id=1, source_target_pairs={{0,8},{8,16},{16,24},{24,28},{28,20},{20,12},{12,4},{4,0},{1,9},{9... | collective-permute-start | bytes 1572872 | tf_op jit(solution)/shard_map/ppermute | solution.py:962
  45.6 14.0 %collective-permute-start.7 = (bf16[256,1024]{1,0:T(8,128)(2,1)S(1)}, bf16[256,1024]{1,0:T(8,128)(2,1)S(1)}, u32[]{:S(2)}, u32[]{:S(2)}) collective-permute-start(bf16[256,1024]{1,0:T(8,128)(2,1)S(1)} %collective-permute-done.1.refs_2_), channel_id=1, source_target_pairs={{8,0},{16,8},{24,16},{28,24},{20,28},{12,20},{4,12},{0,4},{9,1},{1... | collective-permute-start | bytes 1572872 | tf_op jit(solution)/shard_map/ppermute | solution.py:962
  59.7 13.2 %collective-permute-start.10 = (bf16[256,1024]{1,0:T(8,128)(2,1)S(1)}, bf16[256,1024]{1,0:T(8,128)(2,1)S(1)}, u32[]{:S(2)}, u32[]{:S(2)}) collective-permute-start(bf16[256,1024]{1,0:T(8,128)(2,1)S(1)} %collective-permute-done.6.refs_3_), channel_id=1, source_target_pairs={{0,8},{8,16},{16,24},{24,28},{28,20},{20,12},{12,4},{4,0},{1,9},{9... | collective-permute-start | bytes 1572872 | tf_op jit(solution)/shard_map/ppermute | solution.py:962
  60.3 12.9 %collective-permute-start.11 = (bf16[256,1024]{1,0:T(8,128)(2,1)S(1)}, bf16[256,1024]{1,0:T(8,128)(2,1)S(1)}, u32[]{:S(2)}, u32[]{:S(2)}) collective-permute-start(bf16[256,1024]{1,0:T(8,128)(2,1)S(1)} %collective-permute-done.7.refs_4_), channel_id=1, source_target_pairs={{8,0},{16,8},{24,16},{28,24},{20,28},{12,20},{4,12},{0,4},{9,1},{1... | collective-permute-start | bytes 1572872 | tf_op jit(solution)/shard_map/ppermute | solution.py:962
  69.8 15.8 %collective-permute-start.14 = (bf16[1,1280,256]{2,1,0:T(8,128)(2,1)}, bf16[1,1280,256]{2,1,0:T(8,128)(2,1)}, u32[]{:S(2)}, u32[]{:S(2)}) collective-permute-start(bf16[1,1280,256]{2,1,0:T(8,128)(2,1)} %bitcast_dynamic-update-slice_fusion.2), channel_id=1, source_target_pairs={{0,2},{2,0},{1,3},{3,1},{4,6},{6,4},{5,7},{7,5},{8,10},{10,8},{9,1... | collective-permute-start | bytes 1966088 | tf_op jit(solution)/shard_map/ppermute | solution.py:912
  77.4 8.3 %collective-permute-start.13 = (bf16[128,1024]{1,0:T(8,128)(2,1)}, bf16[128,1024]{1,0:T(8,128)(2,1)S(1)}, u32[]{:S(2)}, u32[]{:S(2)}) collective-permute-start(bf16[128,1024]{1,0:T(8,128)(2,1)} %slice.117), channel_id=1, source_target_pairs={{8,0},{16,8},{24,16},{28,24},{20,28},{12,20},{4,12},{0,4},{9,1},{1... | collective-permute-start | bytes 786440 | tf_op jit(solution)/shard_map/ppermute | solution.py:962
  78.8 9.6 %collective-permute-start.12 = (bf16[128,1024]{1,0:T(8,128)(2,1)S(1)}, bf16[128,1024]{1,0:T(8,128)(2,1)S(1)}, u32[]{:S(2)}, u32[]{:S(2)}) collective-permute-start(bf16[128,1024]{1,0:T(8,128)(2,1)S(1)} %slice.116), channel_id=1, source_target_pairs={{0,8},{8,16},{16,24},{24,28},{28,20},{20,12},{12,4},{4,0},{1,9},{9... | collective-permute-start | bytes 786440 | tf_op jit(solution)/shard_map/ppermute | solution.py:962
  94.0 7.8 %collective-permute-start.15 = (bf16[1,768,256]{2,1,0:T(8,128)(2,1)S(1)}, bf16[1,768,256]{2,1,0:T(8,128)(2,1)S(1)}, u32[]{:S(2)}, u32[]{:S(2)}) collective-permute-start(bf16[1,768,256]{2,1,0:T(8,128)(2,1)S(1)} %pad_maximum_fusion.6), channel_id=1, source_target_pairs={{0,2},{2,0},{1,3},{3,1},{4,6},{6,4},{5,7},{7,5},{8,10},{10,8},{9,1... | collective-permute-start | bytes 1179656 | tf_op jit(solution)/shard_map/ppermute | solution.py:912
  102.6 4.4 %collective-permute-start.16 = (bf16[4096,256]{1,0:T(8,128)(2,1)}, bf16[4096,256]{1,0:T(8,128)(2,1)S(1)}, u32[]{:S(2)}, u32[]{:S(2)}) collective-permute-start(bf16[4096,256]{1,0:T(8,128)(2,1)} %bitcast_dynamic-update-slice_fusion.1.own_ref), channel_id=1, source_target_pairs={{0,1},{1,0},{2,3},{3,2},{4,5},{5,4},{6,7},{7,6},{8,9},{9,8},{10,11... | collective-permute-start | bytes 6291464 | tf_op jit(solution)/shard_map/ppermute | solution.py:912
  143.2 14.7 %collective-permute-start.18 = (bf16[1,8,272,128]{3,2,1,0:T(8,128)(2,1)S(1)}, bf16[1,8,272,128]{3,2,1,0:T(8,128)(2,1)S(1)}, u32[]{:S(2)}, u32[]{:S(2)}) collective-permute-start(bf16[1,8,272,128]{3,2,1,0:T(8,128)(2,1)S(1)} %slice_bitcast_fusion.2), channel_id=1, source_target_pairs={{0,2},{2,0},{1,3},{3,1},{4,6},{6,4},{5,7},{7,5},{8,10},{10,8},{9,1... | collective-permute-start | bytes 1671176 | tf_op jit(solution)/shard_map/ppermute | solution.py:912
  158.9 25.0 %all-to-all-start.1 = ((bf16[8,272,128]{2,1,0:T(8,128)(2,1)}), bf16[8,272,128]{2,1,0:T(8,128)(2,1)S(1)}, u32[]{:S(2)}, u32[]{:S(2)}) async-start(bf16[8,272,128]{2,1,0:T(8,128)(2,1)} %fusion.23), calls=%async_computation.1 | async-start | bytes 1114112 | tf_op jit(solution)/shard_map/all_to_all | solution.py:908
  164.5 26.1 %collective-permute-start.23 = (bf16[256,1024]{1,0:T(8,128)(2,1)S(1)}, bf16[256,1024]{1,0:T(8,128)(2,1)S(1)}, u32[]{:S(2)}, u32[]{:S(2)}) collective-permute-start(bf16[256,1024]{1,0:T(8,128)(2,1)S(1)} %copy-done.11), channel_id=1, source_target_pairs={{0,2},{2,0},{1,3},{3,1},{4,6},{6,4},{5,7},{7,5},{8,10},{10,8},{9,1... | collective-permute-start | bytes 1572872 | tf_op jit(solution)/shard_map/ppermute | solution.py:912
  166.0 24.7 %collective-permute-start.21 = (bf16[256,1024]{1,0:T(8,128)(2,1)S(1)}, bf16[256,1024]{1,0:T(8,128)(2,1)}, u32[]{:S(2)}, u32[]{:S(2)}) collective-permute-start(bf16[256,1024]{1,0:T(8,128)(2,1)S(1)} %copy-done.11), channel_id=1, source_target_pairs={{0,1},{1,0},{2,3},{3,2},{4,5},{5,4},{6,7},{7,6},{8,9},{9,8},{10,11... | collective-permute-start | bytes 1572872 | tf_op jit(solution)/shard_map/ppermute | solution.py:912
  189.1 14.5 %collective-permute-start.19 = (bf16[256,1024]{1,0:T(8,128)(2,1)}, bf16[256,1024]{1,0:T(8,128)(2,1)S(1)}, u32[]{:S(2)}, u32[]{:S(2)}) collective-permute-start(bf16[256,1024]{1,0:T(8,128)(2,1)} %get-tuple-element.157.own_ref), channel_id=1, source_target_pairs={{0,2},{2,0},{1,3},{3,1},{4,6},{6,4},{5,7},{7,5},{8,10},{10,8},{9,1... | collective-permute-start | bytes 1572872 | tf_op jit(solution)/shard_map/ppermute | solution.py:912
  190.6 17.8 %collective-permute-start.24 = (bf16[256,1024]{1,0:T(8,128)(2,1)S(1)}, bf16[256,1024]{1,0:T(8,128)(2,1)S(1)}, u32[]{:S(2)}, u32[]{:S(2)}) collective-permute-start(bf16[256,1024]{1,0:T(8,128)(2,1)S(1)} %collective-permute-done.23.grad_own_ref), channel_id=1, source_target_pairs={{0,1},{1,0},{2,3},{3,2},{4,5},{5,4},{6,7},{7,6},{8,9},{9,8},{10,11... | collective-permute-start | bytes 1572872 | tf_op jit(solution)/shard_map/ppermute | solution.py:912
  203.6 4.7 %collective-permute-start.22 = (bf16[256,1024]{1,0:T(8,128)(2,1)S(1)}, bf16[256,1024]{1,0:T(8,128)(2,1)}, u32[]{:S(2)}, u32[]{:S(2)}) collective-permute-start(bf16[256,1024]{1,0:T(8,128)(2,1)S(1)} %collective-permute-done.19.own_ref), channel_id=1, source_target_pairs={{0,1},{1,0},{2,3},{3,2},{4,5},{5,4},{6,7},{7,6},{8,9},{9,8},{10,11... | collective-permute-start | bytes 1572872 | tf_op jit(solution)/shard_map/ppermute | solution.py:912
  204.8 32.7 %all-to-all-start.2 = ((bf16[8,2,32,1024]{3,2,1,0:T(8,128)(2,1)}), bf16[8,2,32,1024]{3,2,1,0:T(8,128)(2,1)S(1)}, u32[]{:S(2)}, u32[]{:S(2)}) async-start(bf16[8,2,32,1024]{3,2,1,0:T(8,128)(2,1)} %broadcast_in_dim.32), calls=%async_computation.2 | async-start | bytes 2097152 | tf_op jit(solution)/shard_map/all_to_all | solution.py:908
  219.9 15.6 %collective-permute-start.25 = (bf16[256,1024]{1,0:T(8,128)(2,1)}, bf16[256,1024]{1,0:T(8,128)(2,1)}, u32[]{:S(2)}, u32[]{:S(2)}) collective-permute-start(bf16[256,1024]{1,0:T(8,128)(2,1)} %get-tuple-element.185), channel_id=1, source_target_pairs={{0,1},{1,0},{2,3},{3,2},{4,5},{5,4},{6,7},{7,6},{8,9},{9,8},{10,11... | collective-permute-start | bytes 1572872 | tf_op jit(solution)/shard_map/ppermute | solution.py:912
  222.9 14.6 %collective-permute-start.27 = (bf16[256,1024]{1,0:T(8,128)(2,1)S(1)}, bf16[256,1024]{1,0:T(8,128)(2,1)S(1)}, u32[]{:S(2)}, u32[]{:S(2)}) collective-permute-start(bf16[256,1024]{1,0:T(8,128)(2,1)S(1)} %add_convert_fusion.2), channel_id=1, source_target_pairs={{0,2},{2,0},{1,3},{3,1},{4,6},{6,4},{5,7},{7,5},{8,10},{10,8},{9,1... | collective-permute-start | bytes 1572872 | tf_op jit(solution)/shard_map/ppermute | solution.py:912
  246.3 6.6 %collective-permute-start.28 = (bf16[8,1,2,32,1024]{4,3,2,0,1:T(8,128)(2,1)}, bf16[8,1,2,32,1024]{4,3,2,0,1:T(8,128)(2,1)}, u32[]{:S(2)}, u32[]{:S(2)}) collective-permute-start(bf16[8,1,2,32,1024]{4,3,2,0,1:T(8,128)(2,1)} %dynamic-slice_bitcast_fusion), channel_id=1, source_target_pairs={{0,1},{1,0},{2,3},{3,2},{4,5},{5,4},{6,7},{7,6},{8,9},{9,8},{10,11... | collective-permute-start | bytes 3145736 | tf_op jit(solution)/shard_map/ppermute | solution.py:912
  246.3 9.3 %collective-permute-start.30 = (bf16[256,1024]{1,0:T(8,128)(2,1)}, bf16[256,1024]{1,0:T(8,128)(2,1)}, u32[]{:S(2)}, u32[]{:S(2)}) collective-permute-start(bf16[256,1024]{1,0:T(8,128)(2,1)} %get-tuple-element.205), channel_id=1, source_target_pairs={{0,1},{1,0},{2,3},{3,2},{4,5},{5,4},{6,7},{7,6},{8,9},{9,8},{10,11... | collective-permute-start | bytes 1572872 | tf_op jit(solution)/shard_map/ppermute | solution.py:912
  246.8 10.1 %collective-permute-start.31 = (bf16[256,1024]{1,0:T(8,128)(2,1)}, bf16[256,1024]{1,0:T(8,128)(2,1)}, u32[]{:S(2)}, u32[]{:S(2)}) collective-permute-start(bf16[256,1024]{1,0:T(8,128)(2,1)} %get-tuple-element.207), channel_id=1, source_target_pairs={{0,1},{1,0},{2,3},{3,2},{4,5},{5,4},{6,7},{7,6},{8,9},{9,8},{10,11... | collective-permute-start | bytes 1572872 | tf_op jit(solution)/shard_map/ppermute | solution.py:912
  246.9 22.9 %all-to-all-start.3 = ((bf16[8,272,128]{2,1,0:T(8,128)(2,1)}), bf16[8,272,128]{2,1,0:T(8,128)(2,1)S(1)}, u32[]{:S(2)}, u32[]{:S(2)}) async-start(bf16[8,272,128]{2,1,0:T(8,128)(2,1)} %get-tuple-element.202), calls=%async_computation.3 | async-start | bytes 1114112 | tf_op jit(solution)/shard_map/all_to_all | solution.py:908
  252.6 132.0 %reduce-scatter.2.cloned.1.call-start = ((), (), s32[]{:S(2)}) async-start(), calls=%async_computation.8 | async-start | bytes 4718592 | tf_op jit(solution)/shard_map/reduce_scatter | solution.py:1204
  254.7 14.1 %collective-permute-start.29 = (bf16[8,1,32,1024]{3,2,0,1:T(8,128)(2,1)S(1)}, bf16[8,1,32,1024]{3,2,0,1:T(8,128)(2,1)S(1)}, u32[]{:S(2)}, u32[]{:S(2)}) collective-permute-start(bf16[8,1,32,1024]{3,2,0,1:T(8,128)(2,1)S(1)} %dynamic-slice_bitcast_fusion.1), channel_id=1, source_target_pairs={{0,2},{2,0},{1,3},{3,1},{4,6},{6,4},{5,7},{7,5},{8,10},{10,8},{9,1... | collective-permute-start | bytes 1572872 | tf_op jit(solution)/shard_map/ppermute | solution.py:912
  269.8 14.0 %collective-permute-start.32 = (bf16[1,8,272,128]{3,2,1,0:T(8,128)(2,1)S(1)}, bf16[1,8,272,128]{3,2,1,0:T(8,128)(2,1)}, u32[]{:S(2)}, u32[]{:S(2)}) collective-permute-start(bf16[1,8,272,128]{3,2,1,0:T(8,128)(2,1)S(1)} %bitcast.233), channel_id=1, source_target_pairs={{0,2},{2,0},{1,3},{3,1},{4,6},{6,4},{5,7},{7,5},{8,10},{10,8},{9,1... | collective-permute-start | bytes 1671176 | tf_op jit(solution)/shard_map/ppermute | solution.py:912
  286.0 7.4 %collective-permute-start.33 = (bf16[2,1,8,272,128]{4,3,2,1,0:T(8,128)(2,1)}, bf16[2,1,8,272,128]{4,3,2,1,0:T(8,128)(2,1)}, u32[]{:S(2)}, u32[]{:S(2)}) collective-permute-start(bf16[2,1,8,272,128]{4,3,2,1,0:T(8,128)(2,1)} %pad_maximum_fusion.2), channel_id=1, source_target_pairs={{0,1},{1,0},{2,3},{3,2},{4,5},{5,4},{6,7},{7,6},{8,9},{9,8},{10,11... | collective-permute-start | bytes 3342344 | tf_op jit(solution)/shard_map/ppermute | solution.py:912
  286.0 43.7 %collective-permute-start.34 = (bf16[2,8,1,32,1024]{4,3,0,1,2:T(8,128)(2,1)S(1)}, bf16[2,8,1,32,1024]{4,3,0,1,2:T(8,128)(2,1)}, u32[]{:S(2)}, u32[]{:S(2)}) collective-permute-start(bf16[2,8,1,32,1024]{4,3,0,1,2:T(8,128)(2,1)S(1)} %bitcast.222), channel_id=1, source_target_pairs={{0,2},{2,0},{1,3},{3,1},{4,6},{6,4},{5,7},{7,5},{8,10},{10,8},{9,1... | collective-permute-start | bytes 3145736 | tf_op jit(solution)/shard_map/ppermute | solution.py:912
  286.9 42.8 %all-to-all-start.4 = ((bf16[8,32,1024]{2,1,0:T(8,128)(2,1)}), bf16[8,32,1024]{2,1,0:T(8,128)(2,1)S(1)}, u32[]{:S(2)}, u32[]{:S(2)}) async-start(bf16[8,32,1024]{2,1,0:T(8,128)(2,1)} %bitcast.235), calls=%async_computation.4 | async-start | bytes 1048576 | tf_op jit(solution)/shard_map/all_to_all | solution.py:908
  292.3 37.4 %collective-permute-start.35 = (bf16[256,1024]{1,0:T(8,128)(2,1)}, bf16[256,1024]{1,0:T(8,128)(2,1)}, u32[]{:S(2)}, u32[]{:S(2)}) collective-permute-start(bf16[256,1024]{1,0:T(8,128)(2,1)} %add_convert_fusion), channel_id=1, source_target_pairs={{0,2},{2,0},{1,3},{3,1},{4,6},{6,4},{5,7},{7,5},{8,10},{10,8},{9,1... | collective-permute-start | bytes 1572872 | tf_op jit(solution)/shard_map/ppermute | solution.py:912
  329.7 4.4 %collective-permute-start.36 = (bf16[2,1,8,256,256]{4,3,2,1,0:T(8,128)(2,1)}, bf16[2,1,8,256,256]{4,3,2,1,0:T(8,128)(2,1)S(1)}, u32[]{:S(2)}, u32[]{:S(2)}) collective-permute-start(bf16[2,1,8,256,256]{4,3,2,1,0:T(8,128)(2,1)} %bitcast.276), channel_id=1, source_target_pairs={{0,1},{1,0},{2,3},{3,2},{4,5},{5,4},{6,7},{7,6},{8,9},{9,8},{10,11... | collective-permute-start | bytes 6291464 | tf_op jit(solution)/shard_map/ppermute | solution.py:912
  339.1 4.5 %collective-permute-start.38 = (bf16[2,8,1,2,32,1024]{5,4,0,1,3,2:T(8,128)(2,1)}, bf16[2,8,1,2,32,1024]{5,4,0,1,3,2:T(8,128)(2,1)}, u32[]{:S(2)}, u32[]{:S(2)}) collective-permute-start(bf16[2,8,1,2,32,1024]{5,4,0,1,3,2:T(8,128)(2,1)} %pad_maximum_fusion.1), channel_id=1, source_target_pairs={{0,1},{1,0},{2,3},{3,2},{4,5},{5,4},{6,7},{7,6},{8,9},{9,8},{10,11... | collective-permute-start | bytes 6291464 | tf_op jit(solution)/shard_map/ppermute | solution.py:912
  339.2 25.8 %collective-permute-start.37 = (bf16[1,8,256,256]{3,2,1,0:T(8,128)(2,1)}, bf16[1,8,256,256]{3,2,1,0:T(8,128)(2,1)}, u32[]{:S(2)}, u32[]{:S(2)}) collective-permute-start(bf16[1,8,256,256]{3,2,1,0:T(8,128)(2,1)} %get-tuple-element.229), channel_id=1, source_target_pairs={{0,2},{2,0},{1,3},{3,1},{4,6},{6,4},{5,7},{7,5},{8,10},{10,8},{9,1... | collective-permute-start | bytes 3145736 | tf_op jit(solution)/shard_map/ppermute | solution.py:912
  341.1 34.7 %collective-permute-start.43 = (f32[8,2,128]{2,1,0:T(2,128)S(1)}, f32[8,2,128]{2,1,0:T(2,128)S(1)}, u32[]{:S(2)}, u32[]{:S(2)}) collective-permute-start(f32[8,2,128]{2,1,0:T(2,128)S(1)} %bitcast.268), channel_id=1, source_target_pairs={{0,1},{1,0},{2,3},{3,2},{4,5},{5,4},{6,7},{7,6},{8,9},{9,8},{10,11... | collective-permute-start | bytes 24584 | tf_op jit(solution)/shard_map/ppermute | solution.py:912
  367.4 31.9 %all-to-all-start.5 = ((bf16[8,256,256]{2,1,0:T(8,128)(2,1)}), bf16[8,256,256]{2,1,0:T(8,128)(2,1)S(1)}, u32[]{:S(2)}, u32[]{:S(2)}) async-start(bf16[8,256,256]{2,1,0:T(8,128)(2,1)} %bitcast.216), calls=%async_computation.5 | async-start | bytes 2097152 | tf_op jit(solution)/shard_map/all_to_all | solution.py:908
  383.6 20.4 %collective-permute-start.44 = (f32[8,128]{1,0:T(8,128)S(1)}, f32[8,128]{1,0:T(8,128)S(1)}, u32[]{:S(2)}, u32[]{:S(2)}) collective-permute-start(f32[8,128]{1,0:T(8,128)S(1)} %bitcast.269), channel_id=1, source_target_pairs={{0,2},{2,0},{1,3},{3,1},{4,6},{6,4},{5,7},{7,5},{8,10},{10,8},{9,1... | collective-permute-start | bytes 12296 | tf_op jit(solution)/shard_map/ppermute | solution.py:912
  386.5 6.4 %collective-permute-start.41 = (bf16[1,2,32,1024]{3,2,1,0:T(8,128)(2,1)S(1)}, bf16[1,2,32,1024]{3,2,1,0:T(8,128)(2,1)S(1)}, u32[]{:S(2)}, u32[]{:S(2)}) collective-permute-start(bf16[1,2,32,1024]{3,2,1,0:T(8,128)(2,1)S(1)} %constant_dynamic-slice_fusion.1), channel_id=1, source_target_pairs={{0,2},{2,0},{1,3},{3,1},{4,6},{6,4},{5,7},{7,5},{8,10},{10,8},{9,1... | collective-permute-start | bytes 393224 | tf_op jit(solution)/shard_map/ppermute | solution.py:912
  387.8 8.7 %collective-permute-start.40 = (bf16[8,1,48,256]{3,2,0,1:T(8,128)(2,1)S(1)}, bf16[8,1,48,256]{3,2,0,1:T(8,128)(2,1)S(1)}, u32[]{:S(2)}, u32[]{:S(2)}) collective-permute-start(bf16[8,1,48,256]{3,2,0,1:T(8,128)(2,1)S(1)} %dynamic-slice_bitcast_fusion.2), channel_id=1, source_target_pairs={{0,2},{2,0},{1,3},{3,1},{4,6},{6,4},{5,7},{7,5},{8,10},{10,8},{9,1... | collective-permute-start | bytes 589832 | tf_op jit(solution)/shard_map/ppermute | solution.py:912
  393.0 4.2 collective-permute-start.42
  399.3 11.9 %all-to-all-start.6 = ((bf16[8,48,256]{2,1,0:T(8,128)(2,1)}), bf16[8,48,256]{2,1,0:T(8,128)(2,1)S(1)}, u32[]{:S(2)}, u32[]{:S(2)}) async-start(bf16[8,48,256]{2,1,0:T(8,128)(2,1)} %fusion.33), calls=%async_computation.7 | async-start | bytes 393216 | tf_op jit(solution)/shard_map/all_to_all | solution.py:908
  (53 other events, 510.2 us)
Sparse Core Ops, SparseCore 0:
  73.4 103.2 all-gather.2
  270.8 99.8 reduce-scatter.1
